TPU v7x, 32 devices: a whole 2x2x4 slice. The times are simulated.
32 devices in a mesh: col: 8 (over z, x), rhs: 4 (over y, core).
Axes of the slice: x: 2, y: 2, z: 4, core: 2. Of those that a mesh axis runs over, the one named last changes fastest.
Arguments:
- rhs_block: bfloat16 [2048, 4096], P('col', 'rhs'), may hold values from -6 to 6
- solution: bfloat16 [24576, 4096], P('col', 'rhs'), may hold values from -6 to 6
- factor: bfloat16 [8, 6, 256, 3072], P('col', None, 'rhs'), may hold values from -0.109375 to 0.109375
- tile_list: int32 [8, 6], P('col'), may hold values 0 or 1
- diag_inverse: bfloat16 [8, 256, 256], P('col'), may hold values from -0.375 to 0.375
Outputs:
- solved_rows: bfloat16 [2048, 4096], P('col', 'rhs')
All inputs are finite; a program needn't handle non-finite values. No bound on the sum of `tile_list` on one device may be relied on, other than what follows from the above.
Results may differ from a plain program's by a relative error of at most 0.0049.
Values may be sent and summed in bfloat16 or wider, within the bound.
No kernel may reach another device: no remote copies, remote signals or barrier semaphores. Data moves between devices by JAX's collectives and lax.ppermute only.
A program may use at most 64 MiB of HBM per device.

v0:
```python
import jax
import jax.numpy as jnp
from jax import lax
from jax.sharding import PartitionSpec as P


def from_behind(block, axis, distance):
    devices = range(lax.axis_size(axis))
    route = [((i - distance) % len(devices), i) for i in devices]
    return lax.ppermute(block, axis, route)


def per_device(rhs_block, solution, factor, tile_list, diag_inverse):
    hop_count = factor.shape[1]
    carried = jnp.zeros((rhs_block.shape[0], rhs_block.shape[1]), jnp.float32)
    for offset in reversed(range(hop_count)):
        product_term = jnp.dot(
            lax.all_gather(factor[0, offset], "rhs", axis=0, tiled=True),
            solution,
            preferred_element_type=jnp.float32,
        )
        carried = carried + product_term * tile_list[0, offset].astype(jnp.float32)
        carried = from_behind(carried, "col", 1)
    remaining = (rhs_block.astype(jnp.float32) - carried).astype(jnp.bfloat16)
    return jnp.dot(diag_inverse[0], remaining, preferred_element_type=jnp.float32).astype(
        jnp.bfloat16
    )


def solution(mesh):
    in_specs = (
        P("col", "rhs"),
        P("col", "rhs"),
        P("col", None, "rhs", None),
        P("col", None),
        P("col", None, None),
    )
    out_specs = P("col", "rhs")
    return jax.shard_map(
        per_device, mesh=mesh, in_specs=in_specs, out_specs=out_specs, check_vma=False
    )
```

profile of v0, /device:TPU:0, one launch (start us, length us, event | category | flops | bytes accessed | tf_op | source)
XLA Modules:
  0.0 206.1 jit_solution(4537024455786390463)
XLA Ops:
  6.5 0.0 copy-start
  6.5 0.0 all-gather.13.cloned.1.call-start
  6.5 3.0 %fusion.35 = (bf16[1,1,64,3072]{3,2,1,0:T(8,128)(2,1)}, bf16[1,1,64,3072]{3,2,1,0:T(8,128)(2,1)}, bf16[1,1,64,3072]{3,2,1,0:T(8,128)(2,1)}, bf16[1,1,64,3072]{3,...) fusion(bf16[1,6,64,3072]{3,2,1,0:T(8,128)(2,1)} %param.7), kind=kLoop, calls=%fused_computation.23 | loop fusion | bytes 4718592 | tf_op jit(solution)/shard_map/slice | solution.py:18
  9.6 0.0 copy-start.2
  9.6 0.0 all-gather.13.cloned.1.call-update
  9.6 0.0 all-gather.15.cloned.1.call-start
  9.7 0.7 all-gather.15.cloned.1.call-update
  10.4 0.0 all-gather.17.cloned.1.call-start
  10.4 0.7 all-gather.17.cloned.1.call-update
  11.1 0.0 all-gather.19.cloned.1.call-start
  11.1 0.5 all-gather.19.cloned.1.call-update
  11.7 0.0 all-gather.21.cloned.1.call-start
  11.7 0.0 copy-done.2
  11.7 0.7 fusion.36
  13.0 19.1 %all-gather.13.cloned.1.call-done = bf16[1,1,256,3072]{3,2,1,0:T(8,128)(2,1)} async-done(((bf16[1,1,64,3072]{3,2,1,0:T(8,128)(2,1)}), bf16[1,1,256,3072]{3,2,1,0:T(8,128)(2,1)}) %all-gather.13.cloned.1.call-update) | async-done | bytes 1572880 | tf_op jit(solution)/shard_map/all_gather | solution.py:18
  32.1 5.1 %fusion.12 = f32[256,1024]{1,0:T(8,128)S(1)} fusion(bf16[3072,1024]{1,0:T(8,128)(2,1)} %param.6, bf16[1,1,256,3072]{3,2,1,0:T(8,128)(2,1)} %all-gather.13.cloned.1.call-done, f32[]{:T(128)} %bitcast.1), kind=kOutput, calls=%fused_computation.12 | convolution fusion | flops 1610874880 | bytes 8912900 | tf_op jit(solution)/shard_map/dot_general | solution.py:17
  37.2 1.5 collective-permute-start
  38.7 0.0 all-gather.21.cloned.1.call-update
  38.7 0.0 all-gather.23.cloned.1.call-start
  39.3 14.0 %all-gather.15.cloned.1.call-done = bf16[1,1,256,3072]{3,2,1,0:T(8,128)(2,1)} async-done(((bf16[1,1,64,3072]{3,2,1,0:T(8,128)(2,1)}), bf16[1,1,256,3072]{3,2,1,0:T(8,128)(2,1)}) %all-gather.15.cloned.1.call-update) | async-done | bytes 1572880 | tf_op jit(solution)/shard_map/all_gather | solution.py:18
  53.4 11.9 %collective-permute-done = f32[256,1024]{1,0:T(8,128)S(1)} collective-permute-done((f32[256,1024]{1,0:T(8,128)S(1)}, f32[256,1024]{1,0:T(8,128)S(1)}, u32[]{:S(2)}, u32[]{:S(2)}) %collective-permute-start) | collective-permute-done | bytes 1048608 | tf_op jit(solution)/shard_map/ppermute | solution.py:10
  65.2 5.1 %fusion.30 = f32[256,1024]{1,0:T(8,128)S(1)} fusion(f32[256,1024]{1,0:T(8,128)S(1)} %collective-permute-done, bf16[3072,1024]{1,0:T(8,128)(2,1)} %param.6, bf16[1,1,256,3072]{3,2,1,0:T(8,128)(2,1)} %all-gather.15.cloned.1.call-done, f32[]{:T(128)} %bitcast.3), kind=kOutput, calls=%fused_computation.18 | convolution fusion | flops 1611137024 | bytes 9961476 | tf_op jit(solution)/shard_map/dot_general | solution.py:17
  70.3 0.1 collective-permute-start.1
  71.0 3.6 %all-gather.17.cloned.1.call-done = bf16[1,1,256,3072]{3,2,1,0:T(8,128)(2,1)} async-done(((bf16[1,1,64,3072]{3,2,1,0:T(8,128)(2,1)}), bf16[1,1,256,3072]{3,2,1,0:T(8,128)(2,1)}) %all-gather.17.cloned.1.call-update) | async-done | bytes 1572880 | tf_op jit(solution)/shard_map/all_gather | solution.py:18
  74.6 5.1 %fusion.18 = f32[256,1024]{1,0:T(8,128)S(1)} fusion(bf16[3072,1024]{1,0:T(8,128)(2,1)} %param.6, bf16[1,1,256,3072]{3,2,1,0:T(8,128)(2,1)} %all-gather.17.cloned.1.call-done, f32[]{:T(128)} %bitcast.5), kind=kOutput, calls=%fused_computation.14 | convolution fusion | flops 1610874880 | bytes 8912900 | tf_op jit(solution)/shard_map/dot_general | solution.py:17
  79.7 17.9 %collective-permute-done.1 = f32[256,1024]{1,0:T(8,128)S(1)} collective-permute-done((f32[256,1024]{1,0:T(8,128)S(1)}, f32[256,1024]{1,0:T(8,128)S(1)}, u32[]{:S(2)}, u32[]{:S(2)}) %collective-permute-start.1) | collective-permute-done | bytes 1048608 | tf_op jit(solution)/shard_map/ppermute | solution.py:10
  97.6 0.2 add.16
  97.7 0.1 collective-permute-start.2
  97.8 0.0 all-gather.23.cloned.1.call-update
  98.4 0.0 all-gather.19.cloned.1.call-done
  98.4 5.1 %fusion.21 = f32[256,1024]{1,0:T(8,128)S(1)} fusion(bf16[3072,1024]{1,0:T(8,128)(2,1)} %param.6, bf16[1,1,256,3072]{3,2,1,0:T(8,128)(2,1)} %all-gather.19.cloned.1.call-done, f32[]{:T(128)} %bitcast.7), kind=kOutput, calls=%fused_computation.15 | convolution fusion | flops 1610874880 | bytes 8912900 | tf_op jit(solution)/shard_map/dot_general | solution.py:17
  103.5 20.5 %collective-permute-done.2 = f32[256,1024]{1,0:T(8,128)S(1)} collective-permute-done((f32[256,1024]{1,0:T(8,128)S(1)}, f32[256,1024]{1,0:T(8,128)S(1)}, u32[]{:S(2)}, u32[]{:S(2)}) %collective-permute-start.2) | collective-permute-done | bytes 1048608 | tf_op jit(solution)/shard_map/ppermute | solution.py:10
  124.0 0.2 add.17
  124.2 0.1 collective-permute-start.3
  124.9 0.0 all-gather.21.cloned.1.call-done
  124.9 5.3 %fusion.24 = f32[256,1024]{1,0:T(8,128)S(1)} fusion(bf16[3072,1024]{1,0:T(8,128)(2,1)} %param.6, bf16[1,1,256,3072]{3,2,1,0:T(8,128)(2,1)} %all-gather.21.cloned.1.call-done, f32[]{:T(128)} %bitcast.9), kind=kOutput, calls=%fused_computation.16 | convolution fusion | flops 1610874880 | bytes 8912900 | tf_op jit(solution)/shard_map/dot_general | solution.py:17
  130.3 19.3 %collective-permute-done.3 = f32[256,1024]{1,0:T(8,128)S(1)} collective-permute-done((f32[256,1024]{1,0:T(8,128)S(1)}, f32[256,1024]{1,0:T(8,128)S(1)}, u32[]{:S(2)}, u32[]{:S(2)}) %collective-permute-start.3) | collective-permute-done | bytes 1048608 | tf_op jit(solution)/shard_map/ppermute | solution.py:10
  149.5 0.2 add.18
  149.7 0.1 collective-permute-start.4
  150.4 0.0 all-gather.23.cloned.1.call-done
  150.4 5.1 %fusion.27 = f32[256,1024]{1,0:T(8,128)S(1)} fusion(bf16[3072,1024]{1,0:T(8,128)(2,1)} %param.6, bf16[1,1,256,3072]{3,2,1,0:T(8,128)(2,1)} %all-gather.23.cloned.1.call-done, f32[]{:T(128)} %bitcast.11), kind=kOutput, calls=%fused_computation.17 | convolution fusion | flops 1610874880 | bytes 8912900 | tf_op jit(solution)/shard_map/dot_general | solution.py:17
  155.5 0.0 copy-start.1
  155.5 18.7 %collective-permute-done.4 = f32[256,1024]{1,0:T(8,128)S(1)} collective-permute-done((f32[256,1024]{1,0:T(8,128)S(1)}, f32[256,1024]{1,0:T(8,128)S(1)}, u32[]{:S(2)}, u32[]{:S(2)}) %collective-permute-start.4) | collective-permute-done | bytes 1048608 | tf_op jit(solution)/shard_map/ppermute | solution.py:10
  174.2 0.2 add.19
  174.3 0.1 collective-permute-start.5
  174.4 23.5 %collective-permute-done.5 = f32[256,1024]{1,0:T(8,128)S(1)} collective-permute-done((f32[256,1024]{1,0:T(8,128)S(1)}, f32[256,1024]{1,0:T(8,128)S(1)}, u32[]{:S(2)}, u32[]{:S(2)}) %collective-permute-start.5) | collective-permute-done | bytes 1048608 | tf_op jit(solution)/shard_map/ppermute | solution.py:10
  197.8 0.0 copy-done
  197.8 0.0 copy-done.1
  197.8 0.4 fusion.33
  198.3 1.0 copy.6
Async XLA Ops:
  6.5 191.3 %copy-start = (bf16[1,256,256]{2,1,0:T(8,128)(2,1)S(1)}, bf16[1,256,256]{2,1,0:T(8,128)(2,1)}, u32[]{:S(2)}) copy-start(bf16[1,256,256]{2,1,0:T(8,128)(2,1)} %param.9) | copy-start | bytes 393220
  6.5 25.6 %all-gather.13.cloned.1.call-start = ((), (), s32[]{:S(2)}) async-start(), calls=%async_computation | async-start | bytes 1966080 | tf_op jit(solution)/shard_map/all_gather | solution.py:18
  9.6 2.1 %copy-start.2 = (s32[1,6]{1,0:T(1,128)S(1)}, s32[1,6]{1,0:T(1,128)}, u32[]{:S(2)}) copy-start(s32[1,6]{1,0:T(1,128)} %param.8) | copy-start | bytes 76
  9.6 43.8 %all-gather.15.cloned.1.call-start = ((), (), s32[]{:S(2)}) async-start(), calls=%async_computation.1 | async-start | bytes 1966080 | tf_op jit(solution)/shard_map/all_gather | solution.py:18
  10.4 64.3 %all-gather.17.cloned.1.call-start = ((), (), s32[]{:S(2)}) async-start(), calls=%async_computation.2 | async-start | bytes 1966080 | tf_op jit(solution)/shard_map/all_gather | solution.py:18
  11.1 87.3 %all-gather.19.cloned.1.call-start = ((), (), s32[]{:S(2)}) async-start(), calls=%async_computation.3 | async-start | bytes 1966080 | tf_op jit(solution)/shard_map/all_gather | solution.py:18
  11.7 113.3 %all-gather.21.cloned.1.call-start = ((), (), s32[]{:S(2)}) async-start(), calls=%async_computation.4 | async-start | bytes 1966080 | tf_op jit(solution)/shard_map/all_gather | solution.py:18
  37.2 28.0 %collective-permute-start = (f32[256,1024]{1,0:T(8,128)S(1)}, f32[256,1024]{1,0:T(8,128)S(1)}, u32[]{:S(2)}, u32[]{:S(2)}) collective-permute-start(f32[256,1024]{1,0:T(8,128)S(1)} %fusion.12), channel_id=1, source_target_pairs={{28,0},{0,4},{4,8},{8,12},{12,16},{16,20},{20,24},{24,28},{29,1},{... | collective-permute-start | bytes 3145736 | tf_op jit(solution)/shard_map/ppermute | solution.py:10
  38.7 111.7 %all-gather.23.cloned.1.call-start = ((), (), s32[]{:S(2)}) async-start(), calls=%async_computation.5 | async-start | bytes 1966080 | tf_op jit(solution)/shard_map/all_gather | solution.py:18
  70.3 27.2 %collective-permute-start.1 = (f32[256,1024]{1,0:T(8,128)S(1)}, f32[256,1024]{1,0:T(8,128)S(1)}, u32[]{:S(2)}, u32[]{:S(2)}) collective-permute-start(f32[256,1024]{1,0:T(8,128)S(1)} %fusion.30), channel_id=1, source_target_pairs={{28,0},{0,4},{4,8},{8,12},{12,16},{16,20},{20,24},{24,28},{29,1},{... | collective-permute-start | bytes 3145736 | tf_op jit(solution)/shard_map/ppermute | solution.py:10
  97.7 26.3 %collective-permute-start.2 = (f32[256,1024]{1,0:T(8,128)S(1)}, f32[256,1024]{1,0:T(8,128)S(1)}, u32[]{:S(2)}, u32[]{:S(2)}) collective-permute-start(f32[256,1024]{1,0:T(8,128)S(1)} %add.16), channel_id=1, source_target_pairs={{28,0},{0,4},{4,8},{8,12},{12,16},{16,20},{20,24},{24,28},{29,1},{... | collective-permute-start | bytes 3145736 | tf_op jit(solution)/shard_map/ppermute | solution.py:10
  124.2 25.4 %collective-permute-start.3 = (f32[256,1024]{1,0:T(8,128)S(1)}, f32[256,1024]{1,0:T(8,128)S(1)}, u32[]{:S(2)}, u32[]{:S(2)}) collective-permute-start(f32[256,1024]{1,0:T(8,128)S(1)} %add.17), channel_id=1, source_target_pairs={{28,0},{0,4},{4,8},{8,12},{12,16},{16,20},{20,24},{24,28},{29,1},{... | collective-permute-start | bytes 3145736 | tf_op jit(solution)/shard_map/ppermute | solution.py:10
  149.7 24.5 %collective-permute-start.4 = (f32[256,1024]{1,0:T(8,128)S(1)}, f32[256,1024]{1,0:T(8,128)S(1)}, u32[]{:S(2)}, u32[]{:S(2)}) collective-permute-start(f32[256,1024]{1,0:T(8,128)S(1)} %add.18), channel_id=1, source_target_pairs={{28,0},{0,4},{4,8},{8,12},{12,16},{16,20},{20,24},{24,28},{29,1},{... | collective-permute-start | bytes 3145736 | tf_op jit(solution)/shard_map/ppermute | solution.py:10
  155.5 42.4 %copy-start.1 = (bf16[256,1024]{1,0:T(8,128)(2,1)S(1)}, bf16[256,1024]{1,0:T(8,128)(2,1)}, u32[]{:S(2)}) copy-start(bf16[256,1024]{1,0:T(8,128)(2,1)} %param.5) | copy-start | bytes 1572868
  174.3 23.5 %collective-permute-start.5 = (f32[256,1024]{1,0:T(8,128)S(1)}, f32[256,1024]{1,0:T(8,128)S(1)}, u32[]{:S(2)}, u32[]{:S(2)}) collective-permute-start(f32[256,1024]{1,0:T(8,128)S(1)} %add.19), channel_id=1, source_target_pairs={{28,0},{0,4},{4,8},{8,12},{12,16},{16,20},{20,24},{24,28},{29,1},{... | collective-permute-start | bytes 3145736 | tf_op jit(solution)/shard_map/ppermute | solution.py:10
Sparse Core Ops, SparseCore 0:
  9.7 22.3 all-gather.12
  33.7 19.6 all-gather.14
  54.9 19.6 all-gather.16
  76.1 19.6 all-gather.18
  97.2 19.6 all-gather.20
  118.3 19.6 all-gather.22
where the time goes:
time: 206 us
  waiting for transfers between devices  150 us (73%)
  matrix products  31.1 us (15%)
  between operations  17.3 us (8%)
  local copies, waits for them, and re-layouts  4.73 us (2%)
    ppermute x6, waiting for transfers between devices, from_behind(): return lax.ppermute(block, axis, route)  112 us
    all_gather x6, waiting for transfers between devices, per_device(): lax.all_gather(factor[0, offset], 'rhs', axis=0, tiled=True)  36.8 us
    dot_general x6, matrix products, per_device(): jnp.dot(lax.all_gather(factor[0, offset], 'rhs', axis=0, tiled=True), sol...  30.7 us
  transfers between devices with their start and end apart: 12, of which 9 were waited for; matrix products, arithmetic and copies ran while one was open for 15% of the time, Pallas kernels for 0%

commit v1 on v0

v1 whole, which is shorter than its diff:
```python
import jax
import jax.numpy as jnp
from jax import lax
from jax.sharding import PartitionSpec as P


def shift(block, axis, distance):
    size = lax.axis_size(axis)
    return lax.ppermute(block, axis, [(i, (i + distance) % size) for i in range(size)])


def pair_swap(block, axis):
    size = lax.axis_size(axis)
    return lax.ppermute(block, axis, [(i, i ^ 1) for i in range(size)])


def across(block, axis):
    return shift(block, axis, lax.axis_size(axis) // 2)


def half_gather(block, axis):
    size = lax.axis_size(axis)
    half = size // 2
    parts = [block]
    for j in range(1, half):
        route = [(i // half * half + (i % half + j) % half, i) for i in range(size)]
        parts.append(lax.ppermute(block, axis, route))
    return parts


def per_device(rhs_block, solution, factor, tile_list, diag_inverse):
    hops, quarter, depth = factor.shape[1:]
    rows, cols = rhs_block.shape
    stages = hops // 2
    odd = lax.axis_index("col") % 2 == 1
    size = lax.axis_size("rhs")
    half = size // 2
    me = lax.axis_index("rhs")
    tiles = factor[0]
    weight = tile_list[0].astype(jnp.float32)

    def give(array, d):
        return jnp.where(odd, array[2 * (d - 1)], array[2 * (d % stages)])

    def own(array, d):
        return array[2 * d - 1]

    def product(left, scale):
        out = jnp.dot(left, solution, preferred_element_type=jnp.float32)
        return out * scale

    order = [2, 3, 1] if stages == 3 else list(range(stages, 0, -1))
    far = {}
    for d in order:
        far[d] = (across(give(tiles, d), "rhs"), across(own(tiles, d), "rhs"))

    near = [product(part, jnp.repeat(weight, quarter)[:, None]).reshape(hops, quarter, cols)
            for part in half_gather(tiles.reshape(hops * quarter, depth), "rhs")]
    near_give = {d: jnp.concatenate([give(p, d) for p in near]).astype(jnp.bfloat16) for d in order}
    near_own = {d: jnp.concatenate([own(p, d) for p in near]) for d in order}

    def far_products(d):
        g = jnp.concatenate(half_gather(far[d][0], "rhs"))
        o = jnp.concatenate(half_gather(far[d][1], "rhs"))
        return product(g, give(weight, d)).astype(jnp.bfloat16), product(o, own(weight, d))

    def combine(d, mine, received, extra=None):
        received = received.astype(jnp.float32)
        stay = None
        if d == stages:
            stay = jnp.where(odd, received, 0.0)
            received = jnp.where(odd, 0.0, received)
        total = mine + received
        if extra is not None:
            total = total + extra.astype(jnp.float32)
        return total.astype(jnp.bfloat16), stay

    def reduce(gives, owns):
        arrived = jnp.zeros((half * quarter, cols), jnp.float32)
        chained = None
        for d in order:
            received = pair_swap(gives[d], "col")
            total, stay = combine(d, owns[d], received, chained if d == 1 else None)
            if d == 2:
                chained = shift(total, "col", 2)
            else:
                arrived = arrived + shift(total, "col", 2 * d).astype(jnp.float32)
            if stay is not None:
                arrived = arrived + stay
        return arrived

    near_sum = reduce(near_give, near_own)
    far_give, far_own = {}, {}
    for d in order:
        far_give[d], far_own[d] = far_products(d)
    far_sum = reduce(far_give, far_own)

    place = jnp.concatenate([
        (((me // half + s) % 2) * half + (me % half + j) % half) * quarter + jnp.arange(quarter)
        for s in range(2) for j in range(half)
    ])
    pick = (lax.broadcasted_iota(jnp.int32, (rows, rows), 0) == place[None, :]).astype(jnp.bfloat16)
    rhs_local = jnp.dot(pick.T, rhs_block, preferred_element_type=jnp.float32)
    diag_local = jnp.dot(diag_inverse[0], pick, preferred_element_type=jnp.float32).astype(jnp.bfloat16)
    acc = jnp.concatenate([near_sum, far_sum])
    remaining = (rhs_local - acc).astype(jnp.bfloat16)
    return jnp.dot(diag_local, remaining, preferred_element_type=jnp.float32).astype(jnp.bfloat16)


def solution(mesh):
    in_specs = (
        P("col", "rhs"),
        P("col", "rhs"),
        P("col", None, "rhs", None),
        P("col", None),
        P("col", None, None),
    )
    out_specs = P("col", "rhs")
    return jax.shard_map(
        per_device, mesh=mesh, in_specs=in_specs, out_specs=out_specs, check_vma=False
    )
```

time: 206 us -> 119 us (0.58)
  waiting for transfers between devices: 150 us -> 54.7 us
  starting transfers between devices: 2.01 us -> 26.2 us
  between operations: 17.3 us -> 4.04 us
  matrix products: 31.1 us -> 26.7 us
  other arithmetic: 0.61 us -> 4.86 us
  local copies, waits for them, and re-layouts: 4.73 us -> 2.07 us
    ppermute x6 -> x25, waiting for transfers between devices: 112 us -> 54.7 us  [the longest x12 38.1 us: shift(): lax.ppermute(block, axis, [(i, (i + distance) % size) for i in range(size)])]
    all_gather x6 -> x0, waiting for transfers between devices: 36.8 us -> none  [per_device(): lax.all_gather(factor[0, offset], 'rhs', axis=0, tiled=True)]
    ppermute x6 -> x25, starting transfers between devices: 1.81 us -> 26.2 us  [the longest x12 18.4 us: shift(): lax.ppermute(block, axis, [(i, (i + distance) % size) for i in range(size)])]
    dot_general x7 -> x10, matrix products: 31.1 us -> 26.7 us  [the longest x8 25 us: product(): out = jnp.dot(left, solution, preferred_element_type=jnp.float32)]
    squeeze x0 -> x1, other arithmetic: none -> 3.04 us  [own(): return array[2 * d - 1]]
  transfers between devices with their start and end apart: 12 -> 25, of which waited for: 9 -> 11; matrix products, arithmetic and copies ran while one was open for 15% -> 27% of each run, Pallas kernels for 0% -> 0%
where the time goes in v1:
time: 119 us
  waiting for transfers between devices  54.7 us (46%)
  matrix products  26.7 us (22%)
  starting transfers between devices  26.2 us (22%)
  other arithmetic  4.86 us (4%)
  between operations  4.04 us (3%)
  local copies, waits for them, and re-layouts  2.07 us (2%)
    ppermute x12, waiting for transfers between devices, shift(): lax.ppermute(block, axis, [(i, (i + distance) % size) for i in range(size)])  38.1 us
    dot_general x8, matrix products, product(): out = jnp.dot(left, solution, preferred_element_type=jnp.float32)  25 us
    ppermute x12, starting transfers between devices, shift(): lax.ppermute(block, axis, [(i, (i + distance) % size) for i in range(size)])  18.4 us
    ppermute x6, waiting for transfers between devices, pair_swap(): return lax.ppermute(block, axis, [(i, i ^ 1) for i in range(size)])  16.6 us
    ppermute x6, starting transfers between devices, pair_swap(): return lax.ppermute(block, axis, [(i, i ^ 1) for i in range(size)])  6.8 us
    squeeze x1, other arithmetic, own(): return array[2 * d - 1]  3.04 us
  transfers between devices with their start and end apart: 25, of which 11 were waited for; matrix products, arithmetic and copies ran while one was open for 27% of the time, Pallas kernels for 0%

profile of v1, /device:TPU:0, one launch (start us, length us, event | category | flops | bytes accessed | tf_op | source)
XLA Modules:
  0.0 118.6 jit_solution(2151538628650027589)
XLA Ops:
  0.0 0.5 collective-permute-start
  0.5 3.0 %slice_bitcast_fusion.2 = (bf16[64,3072]{1,0:T(8,128)(2,1)}, bf16[64,3072]{1,0:T(8,128)(2,1)S(1)}, bf16[64,3072]{1,0:T(8,128)(2,1)}, bf16[64,3072]{1,0:T(8,128)(...) fusion(bf16[1,6,64,3072]{3,2,1,0:T(8,128)(2,1)} %param.7, pred[]{:T(512)S(6)} %eq.27), kind=kLoop, calls=%fused_computation.60 | loop fusion | flops 589824 | bytes 4718593 | tf_op jit(solution)/shard_map/squeeze | solution.py:46
  3.5 2.6 %collective-permute-start.9 = (bf16[64,3072]{1,0:T(8,128)(2,1)}, bf16[64,3072]{1,0:T(8,128)(2,1)}, u32[]{:S(2)}, u32[]{:S(2)}) collective-permute-start(bf16[64,3072]{1,0:T(8,128)(2,1)} %get-tuple-element.7), channel_id=1, source_target_pairs={{0,2},{1,3},{2,0},{3,1},{4,6},{5,7},{6,4},{7,5},{8,10},{9,11},{10,... | collective-permute-start | bytes 1179656 | tf_op jit(solution)/shard_map/ppermute | solution.py:9
  6.1 0.0 collective-permute-start.7
  6.1 2.0 %collective-permute-start.20 = (bf16[64,3072]{1,0:T(8,128)(2,1)}, bf16[64,3072]{1,0:T(8,128)(2,1)}, u32[]{:S(2)}, u32[]{:S(2)}) collective-permute-start(bf16[64,3072]{1,0:T(8,128)(2,1)} %get-tuple-element.8), channel_id=1, source_target_pairs={{0,2},{1,3},{2,0},{3,1},{4,6},{5,7},{6,4},{7,5},{8,10},{9,11},{10,... | collective-permute-start | bytes 1179656 | tf_op jit(solution)/shard_map/ppermute | solution.py:9
  8.1 0.0 collective-permute-start.18
  8.1 0.1 broadcast_in_dim.13
  8.2 0.1 mul.78
  8.3 6.5 %convolution_multiply_fusion.1 = f32[384,1024]{1,0:T(8,128)} fusion(bf16[384,3072]{1,0:T(8,128)(2,1)S(1)} %bitcast.37, bf16[3072,1024]{1,0:T(8,128)(2,1)} %param.6, f32[384]{0:T(512)S(1)} %mul.78), kind=kOutput, calls=%fused_computation.1 | convolution fusion | flops 2416312320 | bytes 10225152 | tf_op jit(solution)/shard_map/dot_general | solution.py:49
  14.8 0.7 fusion.57
  15.5 1.2 select_convert_fusion.3
  16.7 0.1 collective-permute-start.10
  16.8 1.2 fusion.55
  17.9 0.1 pad_add_fusion
  21.8 3.0 %collective-permute-done.7 = bf16[64,3072]{1,0:T(8,128)(2,1)} collective-permute-done((bf16[64,3072]{1,0:T(8,128)(2,1)}, bf16[64,3072]{1,0:T(8,128)(2,1)}, u32[]{:S(2)}, u32[]{:S(2)}) %collective-permute-start.7) | collective-permute-done | bytes 393248 | tf_op jit(solution)/shard_map/ppermute | solution.py:9
  24.8 2.0 %collective-permute-start.15 = (bf16[64,3072]{1,0:T(8,128)(2,1)S(1)}, bf16[64,3072]{1,0:T(8,128)(2,1)S(1)}, u32[]{:S(2)}, u32[]{:S(2)}) collective-permute-start(bf16[64,3072]{1,0:T(8,128)(2,1)S(1)} %copy-done.3), channel_id=1, source_target_pairs={{0,2},{1,3},{2,0},{3,1},{4,6},{5,7},{6,4},{7,5},{8,10},{9,11},{10,... | collective-permute-start | bytes 1179656 | tf_op jit(solution)/shard_map/ppermute | solution.py:9
  26.7 6.5 %collective-permute-done.20 = bf16[64,3072]{1,0:T(8,128)(2,1)} collective-permute-done((bf16[64,3072]{1,0:T(8,128)(2,1)}, bf16[64,3072]{1,0:T(8,128)(2,1)}, u32[]{:S(2)}, u32[]{:S(2)}) %collective-permute-start.20) | collective-permute-done | bytes 393248 | tf_op jit(solution)/shard_map/ppermute | solution.py:9
  33.2 2.0 %collective-permute-start.13 = (bf16[64,3072]{1,0:T(8,128)(2,1)S(1)}, bf16[64,3072]{1,0:T(8,128)(2,1)S(1)}, u32[]{:S(2)}, u32[]{:S(2)}) collective-permute-start(bf16[64,3072]{1,0:T(8,128)(2,1)S(1)} %get-tuple-element.6), channel_id=1, source_target_pairs={{0,2},{1,3},{2,0},{3,1},{4,6},{5,7},{6,4},{7,5},{8,10},{9,11},{10,... | collective-permute-start | bytes 1179656 | tf_op jit(solution)/shard_map/ppermute | solution.py:9
  35.2 3.9 %fusion.7 = bf16[128,1024]{1,0:T(8,128)(2,1)S(1)} fusion(bf16[3072,1024]{1,0:T(8,128)(2,1)} %param.6, bf16[64,3072]{1,0:T(8,128)(2,1)S(1)} %collective-permute-done.10, bf16[64,3072]{1,0:T(8,128)(2,1)} %collective-permute-done.9, f32[]{:T(128)S(6)} %select_n.153), kind=kOutput, calls=%fused_computation.16 | convolution fusion | flops 807141376 | bytes 7340036 | tf_op jit(solution)/shard_map/dot_general | solution.py:49
  39.1 2.5 %collective-permute-done.18 = bf16[64,3072]{1,0:T(8,128)(2,1)} collective-permute-done((bf16[64,3072]{1,0:T(8,128)(2,1)}, bf16[64,3072]{1,0:T(8,128)(2,1)}, u32[]{:S(2)}, u32[]{:S(2)}) %collective-permute-start.18) | collective-permute-done | bytes 393248 | tf_op jit(solution)/shard_map/ppermute | solution.py:9
  41.6 0.0 collective-permute-start.8
  41.6 8.3 %collective-permute-done.15 = bf16[64,3072]{1,0:T(8,128)(2,1)S(1)} collective-permute-done((bf16[64,3072]{1,0:T(8,128)(2,1)S(1)}, bf16[64,3072]{1,0:T(8,128)(2,1)S(1)}, u32[]{:S(2)}, u32[]{:S(2)}) %collective-permute-start.15) | collective-permute-done | bytes 393248 | tf_op jit(solution)/shard_map/ppermute | solution.py:9
  49.9 0.0 collective-permute-start.19
  49.9 8.2 %collective-permute-done.13 = bf16[64,3072]{1,0:T(8,128)(2,1)S(1)} collective-permute-done((bf16[64,3072]{1,0:T(8,128)(2,1)S(1)}, bf16[64,3072]{1,0:T(8,128)(2,1)S(1)}, u32[]{:S(2)}, u32[]{:S(2)}) %collective-permute-start.13) | collective-permute-done | bytes 393248 | tf_op jit(solution)/shard_map/ppermute | solution.py:9
  58.1 0.0 collective-permute-start.16
  58.2 0.0 collective-permute-done.21
  58.2 0.5 collective-permute-start.14
  58.7 2.0 %fusion.9 = bf16[128,1024]{1,0:T(8,128)(2,1)S(1)} fusion(bf16[3072,1024]{1,0:T(8,128)(2,1)S(1)} %copy-done.1, bf16[64,3072]{1,0:T(8,128)(2,1)S(1)} %collective-permute-done.21, bf16[64,3072]{1,0:T(8,128)(2,1)} %collective-permute-done.20, f32[]{:T(128)S(6)} %select_n.161), kind=kOutput, calls=%fused_computation.18 | convolution fusion | flops 807141376 | bytes 7340036 | tf_op jit(solution)/shard_map/dot_general | solution.py:49
  60.7 0.0 collective-permute-done.16
  60.7 1.8 %collective-permute-start.11 = (bf16[128,1024]{1,0:T(8,128)(2,1)S(1)}, bf16[128,1024]{1,0:T(8,128)(2,1)S(1)}, u32[]{:S(2)}, u32[]{:S(2)}) collective-permute-start(bf16[128,1024]{1,0:T(8,128)(2,1)S(1)} %fusion.7), channel_id=1, source_target_pairs={{0,4},{4,0},{8,12},{12,8},{16,20},{20,16},{24,28},{28,24},{1,5},{5... | collective-permute-start | bytes 786440 | tf_op jit(solution)/shard_map/ppermute | solution.py:14
  62.5 1.0 fusion.8
  63.5 0.4 collective-permute-start.22
  63.9 6.0 %collective-permute-done.11 = bf16[128,1024]{1,0:T(8,128)(2,1)S(1)} collective-permute-done((bf16[128,1024]{1,0:T(8,128)(2,1)S(1)}, bf16[128,1024]{1,0:T(8,128)(2,1)S(1)}, u32[]{:S(2)}, u32[]{:S(2)}) %collective-permute-start.11) | collective-permute-done | bytes 262176 | tf_op jit(solution)/shard_map/ppermute | solution.py:14
  70.0 1.7 %collective-permute-start.17 = (bf16[128,1024]{1,0:T(8,128)(2,1)S(1)}, bf16[128,1024]{1,0:T(8,128)(2,1)S(1)}, u32[]{:S(2)}, u32[]{:S(2)}) collective-permute-start(bf16[128,1024]{1,0:T(8,128)(2,1)S(1)} %fusion.8), channel_id=1, source_target_pairs={{0,4},{4,0},{8,12},{12,8},{16,20},{20,16},{24,28},{28,24},{1,5},{5... | collective-permute-start | bytes 786440 | tf_op jit(solution)/shard_map/ppermute | solution.py:14
  71.7 2.7 %fusion.6 = bf16[128,1024]{1,0:T(8,128)(2,1)S(1)} fusion(bf16[3072,1024]{1,0:T(8,128)(2,1)S(1)} %copy-done.1, bf16[64,3072]{1,0:T(8,128)(2,1)S(1)} %collective-permute-done.8, bf16[64,3072]{1,0:T(8,128)(2,1)} %collective-permute-done.7, bf16[128,1024]{1,0:T(8,128)(2,1)S(1)} %collective-permute-done.11, f32[]{:T(128)} %bitcast.4, pred[]{:T(512)S(6)} %eq.27), kind=kOutput, calls=%fused_computation.15 | convolution fusion | flops 807534592 | bytes 7602181 | tf_op jit(solution)/shard_map/dot_general | solution.py:49
  74.4 3.7 %collective-permute-start.12 = (bf16[128,1024]{1,0:T(8,128)(2,1)S(1)}, bf16[128,1024]{1,0:T(8,128)(2,1)S(1)}, u32[]{:S(2)}, u32[]{:S(2)}) collective-permute-start(bf16[128,1024]{1,0:T(8,128)(2,1)S(1)} %fusion.6), channel_id=1, source_target_pairs={{0,24},{4,28},{8,0},{12,4},{16,8},{20,12},{24,16},{28,20},{1,25},{... | collective-permute-start | bytes 786440 | tf_op jit(solution)/shard_map/ppermute | solution.py:9
  78.1 2.7 %fusion.4 = bf16[128,1024]{1,0:T(8,128)(2,1)S(1)} fusion(bf16[3072,1024]{1,0:T(8,128)(2,1)S(1)} %copy-done.1, bf16[64,3072]{1,0:T(8,128)(2,1)S(1)} %collective-permute-done.19, bf16[64,3072]{1,0:T(8,128)(2,1)} %collective-permute-done.18, bf16[128,1024]{1,0:T(8,128)(2,1)S(1)} %collective-permute-done.22, f32[]{:T(128)} %bitcast.13), kind=kOutput, calls=%fused_computation.13 | convolution fusion | flops 807403520 | bytes 7602180 | tf_op jit(solution)/shard_map/dot_general | solution.py:49
  80.7 0.1 collective-permute-start.23
  80.8 0.0 collective-permute-done
  80.8 4.3 %convolution_multiply_fusion = f32[384,1024]{1,0:T(8,128)S(1)} fusion(bf16[384,3072]{1,0:T(8,128)(2,1)} %collective-permute-done, bf16[3072,1024]{1,0:T(8,128)(2,1)S(1)} %copy-done.1, f32[384]{0:T(512)S(1)} %mul.78), kind=kOutput, calls=%fused_computation | convolution fusion | flops 2416312320 | bytes 10225152 | tf_op jit(solution)/shard_map/dot_general | solution.py:49
  85.2 0.8 collective-permute-start.4
  86.0 0.1 fusion.56
  86.2 6.0 %collective-permute-done.4 = bf16[128,1024]{1,0:T(8,128)(2,1)S(1)} collective-permute-done((bf16[128,1024]{1,0:T(8,128)(2,1)S(1)}, bf16[128,1024]{1,0:T(8,128)(2,1)S(1)}, u32[]{:S(2)}, u32[]{:S(2)}) %collective-permute-start.4) | collective-permute-done | bytes 262176 | tf_op jit(solution)/shard_map/ppermute | solution.py:14
  92.2 0.5 collective-permute-start.3
  92.7 0.1 fusion.38
  92.7 0.0 collective-permute-done.14
  92.8 1.6 %collective-permute-start.1 = (bf16[128,1024]{1,0:T(8,128)(2,1)S(1)}, bf16[128,1024]{1,0:T(8,128)(2,1)S(1)}, u32[]{:S(2)}, u32[]{:S(2)}) collective-permute-start(bf16[128,1024]{1,0:T(8,128)(2,1)S(1)} %pad_maximum_fusion), channel_id=1, source_target_pairs={{0,4},{4,0},{8,12},{12,8},{16,20},{20,16},{24,28},{28,24},{1,5},{5... | collective-permute-start | bytes 786440 | tf_op jit(solution)/shard_map/ppermute | solution.py:14
  94.4 0.0 collective-permute-done.17
  94.4 0.6 collective-permute-start.5
  95.0 1.8 %fusion.5 = bf16[128,1024]{1,0:T(8,128)(2,1)S(1)} fusion(bf16[3072,1024]{1,0:T(8,128)(2,1)S(1)} %copy-done.1, bf16[64,3072]{1,0:T(8,128)(2,1)S(1)} %collective-permute-done.14, bf16[64,3072]{1,0:T(8,128)(2,1)S(1)} %collective-permute-done.13, bf16[128,1024]{1,0:T(8,128)(2,1)S(1)} %collective-permute-done.23, ...), kind=kOutput, calls=%fused_computation.14 | convolution fusion | flops 807665664 | bytes 7864324 | tf_op jit(solution)/shard_map/dot_general | solution.py:49
  96.7 1.6 %collective-permute-start.24 = (bf16[128,1024]{1,0:T(8,128)(2,1)S(1)}, bf16[128,1024]{1,0:T(8,128)(2,1)S(1)}, u32[]{:S(2)}, u32[]{:S(2)}) collective-permute-start(bf16[128,1024]{1,0:T(8,128)(2,1)S(1)} %fusion.5), channel_id=1, source_target_pairs={{0,8},{4,12},{8,16},{12,20},{16,24},{20,28},{24,0},{28,4},{1,9},{5... | collective-permute-start | bytes 786440 | tf_op jit(solution)/shard_map/ppermute | solution.py:9
  98.4 4.5 %collective-permute-done.1 = bf16[128,1024]{1,0:T(8,128)(2,1)S(1)} collective-permute-done((bf16[128,1024]{1,0:T(8,128)(2,1)S(1)}, bf16[128,1024]{1,0:T(8,128)(2,1)S(1)}, u32[]{:S(2)}, u32[]{:S(2)}) %collective-permute-start.1) | collective-permute-done | bytes 262176 | tf_op jit(solution)/shard_map/ppermute | solution.py:14
  102.9 0.1 fusion.30
  103.0 3.9 %collective-permute-start.2 = (bf16[128,1024]{1,0:T(8,128)(2,1)S(1)}, bf16[128,1024]{1,0:T(8,128)(2,1)S(1)}, u32[]{:S(2)}, u32[]{:S(2)}) collective-permute-start(bf16[128,1024]{1,0:T(8,128)(2,1)S(1)} %fusion.30), channel_id=1, source_target_pairs={{0,24},{4,28},{8,0},{12,4},{16,8},{20,12},{24,16},{28,20},{1,25},{... | collective-permute-start | bytes 786440 | tf_op jit(solution)/shard_map/ppermute | solution.py:9
  106.8 0.1 fusion.37
  106.9 0.0 copy-start.4
  106.9 0.1 collective-permute-start.6
  107.0 0.3 fusion.39
  107.4 1.0 collective-permute-done.24
  108.4 0.1 fusion.34
  108.6 5.5 %collective-permute-done.2 = bf16[128,1024]{1,0:T(8,128)(2,1)S(1)} collective-permute-done((bf16[128,1024]{1,0:T(8,128)(2,1)S(1)}, bf16[128,1024]{1,0:T(8,128)(2,1)S(1)}, u32[]{:S(2)}, u32[]{:S(2)}) %collective-permute-start.2) | collective-permute-done | bytes 262176 | tf_op jit(solution)/shard_map/ppermute | solution.py:9
  114.1 3.0 %collective-permute-done.6 = bf16[128,1024]{1,0:T(8,128)(2,1)S(1)} collective-permute-done((bf16[128,1024]{1,0:T(8,128)(2,1)S(1)}, bf16[128,1024]{1,0:T(8,128)(2,1)S(1)}, u32[]{:S(2)}, u32[]{:S(2)}) %collective-permute-start.6) | collective-permute-done | bytes 262176 | tf_op jit(solution)/shard_map/ppermute | solution.py:9
  117.1 0.1 fusion.32
  117.2 1.4 %convolution_convert_fusion = bf16[256,1024]{1,0:T(8,128)(2,1)} fusion(f32[256,1024]{1,0:T(8,128)S(1)} %fusion.39, f32[128,1024]{1,0:T(8,128)S(1)} %fusion.34, f32[128,1024]{1,0:T(8,128)S(1)} %fusion.32, bf16[1,256,256]{2,1,0:T(8,128)(2,1)S(1)} %copy-done.4, s32[256]{0:T(256)S(1)} %pad_add_fusion), kind=kOutput, calls=%fused_computation.2 | convolution fusion | flops 169017344 | bytes 2753536 | tf_op jit(solution)/shard_map/dot_general | solution.py:107
  (28 shorter events, 0.2 us)
Async XLA Ops:
  0.0 107.0 %copy-start = (bf16[256,1024]{1,0:T(8,128)(2,1)S(1)}, bf16[256,1024]{1,0:T(8,128)(2,1)}, u32[]{:S(2)}) copy-start(bf16[256,1024]{1,0:T(8,128)(2,1)} %param.5) | copy-start | bytes 1572868
  0.0 80.8 %collective-permute-start = (bf16[384,3072]{1,0:T(8,128)(2,1)}, bf16[384,3072]{1,0:T(8,128)(2,1)}, u32[]{:S(2)}, u32[]{:S(2)}) collective-permute-start(bf16[384,3072]{1,0:T(8,128)(2,1)} %bitcast.36), channel_id=1, source_target_pairs={{1,0},{0,1},{3,2},{2,3},{5,4},{4,5},{7,6},{6,7},{9,8},{8,9},{11,10... | collective-permute-start | bytes 7077896 | tf_op jit(solution)/shard_map/ppermute | solution.py:27
  0.5 7.7 %copy-start.5 = (s32[1,6]{1,0:T(1,128)S(1)}, s32[1,6]{1,0:T(1,128)}, u32[]{:S(2)}) copy-start(s32[1,6]{1,0:T(1,128)} %param.8) | copy-start | bytes 76
  0.5 7.8 %copy-start.2 = (bf16[1,6,64,3072]{3,2,1,0:T(8,128)(2,1)S(1)}, bf16[1,6,64,3072]{3,2,1,0:T(8,128)(2,1)}, u32[]{:S(2)}) copy-start(bf16[1,6,64,3072]{3,2,1,0:T(8,128)(2,1)} %param.7) | copy-start | bytes 7077892
  3.5 13.1 %collective-permute-start.9 = (bf16[64,3072]{1,0:T(8,128)(2,1)}, bf16[64,3072]{1,0:T(8,128)(2,1)}, u32[]{:S(2)}, u32[]{:S(2)}) collective-permute-start(bf16[64,3072]{1,0:T(8,128)(2,1)} %get-tuple-element.7), channel_id=1, source_target_pairs={{0,2},{1,3},{2,0},{3,1},{4,6},{5,7},{6,4},{7,5},{8,10},{9,11},{10,... | collective-permute-start | bytes 1179656 | tf_op jit(solution)/shard_map/ppermute | solution.py:9
  6.1 18.7 %collective-permute-start.7 = (bf16[64,3072]{1,0:T(8,128)(2,1)}, bf16[64,3072]{1,0:T(8,128)(2,1)}, u32[]{:S(2)}, u32[]{:S(2)}) collective-permute-start(bf16[64,3072]{1,0:T(8,128)(2,1)} %get-tuple-element.5), channel_id=1, source_target_pairs={{0,2},{1,3},{2,0},{3,1},{4,6},{5,7},{6,4},{7,5},{8,10},{9,11},{10,... | collective-permute-start | bytes 1179656 | tf_op jit(solution)/shard_map/ppermute | solution.py:9
  6.1 27.1 %collective-permute-start.20 = (bf16[64,3072]{1,0:T(8,128)(2,1)}, bf16[64,3072]{1,0:T(8,128)(2,1)}, u32[]{:S(2)}, u32[]{:S(2)}) collective-permute-start(bf16[64,3072]{1,0:T(8,128)(2,1)} %get-tuple-element.8), channel_id=1, source_target_pairs={{0,2},{1,3},{2,0},{3,1},{4,6},{5,7},{6,4},{7,5},{8,10},{9,11},{10,... | collective-permute-start | bytes 1179656 | tf_op jit(solution)/shard_map/ppermute | solution.py:9
  8.1 33.5 %collective-permute-start.18 = (bf16[64,3072]{1,0:T(8,128)(2,1)}, bf16[64,3072]{1,0:T(8,128)(2,1)}, u32[]{:S(2)}, u32[]{:S(2)}) collective-permute-start(bf16[64,3072]{1,0:T(8,128)(2,1)} %get-tuple-element.9), channel_id=1, source_target_pairs={{0,2},{1,3},{2,0},{3,1},{4,6},{5,7},{6,4},{7,5},{8,10},{9,11},{10,... | collective-permute-start | bytes 1179656 | tf_op jit(solution)/shard_map/ppermute | solution.py:9
  14.8 10.0 %copy-start.3 = (bf16[64,3072]{1,0:T(8,128)(2,1)S(1)}, bf16[64,3072]{1,0:T(8,128)(2,1)}, u32[]{:S(2)}) copy-start(bf16[64,3072]{1,0:T(8,128)(2,1)} %get-tuple-element.10) | copy-start | bytes 1179652
  16.7 18.5 %collective-permute-start.10 = (bf16[64,3072]{1,0:T(8,128)(2,1)}, bf16[64,3072]{1,0:T(8,128)(2,1)S(1)}, u32[]{:S(2)}, u32[]{:S(2)}) collective-permute-start(bf16[64,3072]{1,0:T(8,128)(2,1)} %collective-permute-done.9), channel_id=1, source_target_pairs={{1,0},{0,1},{3,2},{2,3},{5,4},{4,5},{7,6},{6,7},{9,8},{8,9},{11,10... | collective-permute-start | bytes 1179656 | tf_op jit(solution)/shard_map/ppermute | solution.py:27
  24.8 25.2 %collective-permute-start.15 = (bf16[64,3072]{1,0:T(8,128)(2,1)S(1)}, bf16[64,3072]{1,0:T(8,128)(2,1)S(1)}, u32[]{:S(2)}, u32[]{:S(2)}) collective-permute-start(bf16[64,3072]{1,0:T(8,128)(2,1)S(1)} %copy-done.3), channel_id=1, source_target_pairs={{0,2},{1,3},{2,0},{3,1},{4,6},{5,7},{6,4},{7,5},{8,10},{9,11},{10,... | collective-permute-start | bytes 1179656 | tf_op jit(solution)/shard_map/ppermute | solution.py:9
  33.2 25.5 %copy-start.1 = (bf16[3072,1024]{1,0:T(8,128)(2,1)S(1)}, bf16[3072,1024]{1,0:T(8,128)(2,1)}, u32[]{:S(2)}) copy-start(bf16[3072,1024]{1,0:T(8,128)(2,1)} %param.6) | copy-start | bytes 18874372
  33.2 25.0 %collective-permute-start.13 = (bf16[64,3072]{1,0:T(8,128)(2,1)S(1)}, bf16[64,3072]{1,0:T(8,128)(2,1)S(1)}, u32[]{:S(2)}, u32[]{:S(2)}) collective-permute-start(bf16[64,3072]{1,0:T(8,128)(2,1)S(1)} %get-tuple-element.6), channel_id=1, source_target_pairs={{0,2},{1,3},{2,0},{3,1},{4,6},{5,7},{6,4},{7,5},{8,10},{9,11},{10,... | collective-permute-start | bytes 1179656 | tf_op jit(solution)/shard_map/ppermute | solution.py:9
  35.2 23.0 %collective-permute-start.21 = (bf16[64,3072]{1,0:T(8,128)(2,1)}, bf16[64,3072]{1,0:T(8,128)(2,1)S(1)}, u32[]{:S(2)}, u32[]{:S(2)}) collective-permute-start(bf16[64,3072]{1,0:T(8,128)(2,1)} %collective-permute-done.20), channel_id=1, source_target_pairs={{1,0},{0,1},{3,2},{2,3},{5,4},{4,5},{7,6},{6,7},{9,8},{8,9},{11,10... | collective-permute-start | bytes 1179656 | tf_op jit(solution)/shard_map/ppermute | solution.py:27
  41.6 21.9 %collective-permute-start.8 = (bf16[64,3072]{1,0:T(8,128)(2,1)}, bf16[64,3072]{1,0:T(8,128)(2,1)S(1)}, u32[]{:S(2)}, u32[]{:S(2)}) collective-permute-start(bf16[64,3072]{1,0:T(8,128)(2,1)} %collective-permute-done.7), channel_id=1, source_target_pairs={{1,0},{0,1},{3,2},{2,3},{5,4},{4,5},{7,6},{6,7},{9,8},{8,9},{11,10... | collective-permute-start | bytes 1179656 | tf_op jit(solution)/shard_map/ppermute | solution.py:27
  49.9 24.5 %collective-permute-start.19 = (bf16[64,3072]{1,0:T(8,128)(2,1)}, bf16[64,3072]{1,0:T(8,128)(2,1)S(1)}, u32[]{:S(2)}, u32[]{:S(2)}) collective-permute-start(bf16[64,3072]{1,0:T(8,128)(2,1)} %collective-permute-done.18), channel_id=1, source_target_pairs={{1,0},{0,1},{3,2},{2,3},{5,4},{4,5},{7,6},{6,7},{9,8},{8,9},{11,10... | collective-permute-start | bytes 1179656 | tf_op jit(solution)/shard_map/ppermute | solution.py:27
  58.1 2.6 %collective-permute-start.16 = (bf16[64,3072]{1,0:T(8,128)(2,1)S(1)}, bf16[64,3072]{1,0:T(8,128)(2,1)S(1)}, u32[]{:S(2)}, u32[]{:S(2)}) collective-permute-start(bf16[64,3072]{1,0:T(8,128)(2,1)S(1)} %collective-permute-done.15), channel_id=1, source_target_pairs={{1,0},{0,1},{3,2},{2,3},{5,4},{4,5},{7,6},{6,7},{9,8},{8,9},{11,10... | collective-permute-start | bytes 1179656 | tf_op jit(solution)/shard_map/ppermute | solution.py:27
  58.2 34.6 %collective-permute-start.14 = (bf16[64,3072]{1,0:T(8,128)(2,1)S(1)}, bf16[64,3072]{1,0:T(8,128)(2,1)S(1)}, u32[]{:S(2)}, u32[]{:S(2)}) collective-permute-start(bf16[64,3072]{1,0:T(8,128)(2,1)S(1)} %collective-permute-done.13), channel_id=1, source_target_pairs={{1,0},{0,1},{3,2},{2,3},{5,4},{4,5},{7,6},{6,7},{9,8},{8,9},{11,10... | collective-permute-start | bytes 1179656 | tf_op jit(solution)/shard_map/ppermute | solution.py:27
  60.7 9.2 %collective-permute-start.11 = (bf16[128,1024]{1,0:T(8,128)(2,1)S(1)}, bf16[128,1024]{1,0:T(8,128)(2,1)S(1)}, u32[]{:S(2)}, u32[]{:S(2)}) collective-permute-start(bf16[128,1024]{1,0:T(8,128)(2,1)S(1)} %fusion.7), channel_id=1, source_target_pairs={{0,4},{4,0},{8,12},{12,8},{16,20},{20,16},{24,28},{28,24},{1,5},{5... | collective-permute-start | bytes 786440 | tf_op jit(solution)/shard_map/ppermute | solution.py:14
  63.5 14.5 %collective-permute-start.22 = (bf16[128,1024]{1,0:T(8,128)(2,1)S(1)}, bf16[128,1024]{1,0:T(8,128)(2,1)S(1)}, u32[]{:S(2)}, u32[]{:S(2)}) collective-permute-start(bf16[128,1024]{1,0:T(8,128)(2,1)S(1)} %fusion.9), channel_id=1, source_target_pairs={{0,4},{4,0},{8,12},{12,8},{16,20},{20,16},{24,28},{28,24},{1,5},{5... | collective-permute-start | bytes 786440 | tf_op jit(solution)/shard_map/ppermute | solution.py:14
  70.0 24.4 %collective-permute-start.17 = (bf16[128,1024]{1,0:T(8,128)(2,1)S(1)}, bf16[128,1024]{1,0:T(8,128)(2,1)S(1)}, u32[]{:S(2)}, u32[]{:S(2)}) collective-permute-start(bf16[128,1024]{1,0:T(8,128)(2,1)S(1)} %fusion.8), channel_id=1, source_target_pairs={{0,4},{4,0},{8,12},{12,8},{16,20},{20,16},{24,28},{28,24},{1,5},{5... | collective-permute-start | bytes 786440 | tf_op jit(solution)/shard_map/ppermute | solution.py:14
  74.4 33.0 %collective-permute-start.12 = (bf16[128,1024]{1,0:T(8,128)(2,1)S(1)}, bf16[128,1024]{1,0:T(8,128)(2,1)S(1)}, u32[]{:S(2)}, u32[]{:S(2)}) collective-permute-start(bf16[128,1024]{1,0:T(8,128)(2,1)S(1)} %fusion.6), channel_id=1, source_target_pairs={{0,24},{4,28},{8,0},{12,4},{16,8},{20,12},{24,16},{28,20},{1,25},{... | collective-permute-start | bytes 786440 | tf_op jit(solution)/shard_map/ppermute | solution.py:9
  80.7 14.2 %collective-permute-start.23 = (bf16[128,1024]{1,0:T(8,128)(2,1)S(1)}, bf16[128,1024]{1,0:T(8,128)(2,1)S(1)}, u32[]{:S(2)}, u32[]{:S(2)}) collective-permute-start(bf16[128,1024]{1,0:T(8,128)(2,1)S(1)} %fusion.4), channel_id=1, source_target_pairs={{0,8},{4,12},{8,16},{12,20},{16,24},{20,28},{24,0},{28,4},{1,9},{5... | collective-permute-start | bytes 786440 | tf_op jit(solution)/shard_map/ppermute | solution.py:9
  85.2 7.0 %collective-permute-start.4 = (bf16[128,1024]{1,0:T(8,128)(2,1)S(1)}, bf16[128,1024]{1,0:T(8,128)(2,1)S(1)}, u32[]{:S(2)}, u32[]{:S(2)}) collective-permute-start(bf16[128,1024]{1,0:T(8,128)(2,1)S(1)} %pad_maximum_fusion.2), channel_id=1, source_target_pairs={{0,4},{4,0},{8,12},{12,8},{16,20},{20,16},{24,28},{28,24},{1,5},{5... | collective-permute-start | bytes 786440 | tf_op jit(solution)/shard_map/ppermute | solution.py:14
  92.2 14.6 %collective-permute-start.3 = (bf16[128,1024]{1,0:T(8,128)(2,1)S(1)}, bf16[128,1024]{1,0:T(8,128)(2,1)S(1)}, u32[]{:S(2)}, u32[]{:S(2)}) collective-permute-start(bf16[128,1024]{1,0:T(8,128)(2,1)S(1)} %pad_maximum_fusion.1), channel_id=1, source_target_pairs={{0,4},{4,0},{8,12},{12,8},{16,20},{20,16},{24,28},{28,24},{1,5},{5... | collective-permute-start | bytes 786440 | tf_op jit(solution)/shard_map/ppermute | solution.py:14
  92.8 10.1 %collective-permute-start.1 = (bf16[128,1024]{1,0:T(8,128)(2,1)S(1)}, bf16[128,1024]{1,0:T(8,128)(2,1)S(1)}, u32[]{:S(2)}, u32[]{:S(2)}) collective-permute-start(bf16[128,1024]{1,0:T(8,128)(2,1)S(1)} %pad_maximum_fusion), channel_id=1, source_target_pairs={{0,4},{4,0},{8,12},{12,8},{16,20},{20,16},{24,28},{28,24},{1,5},{5... | collective-permute-start | bytes 786440 | tf_op jit(solution)/shard_map/ppermute | solution.py:14
  94.4 12.5 %collective-permute-start.5 = (bf16[128,1024]{1,0:T(8,128)(2,1)S(1)}, bf16[128,1024]{1,0:T(8,128)(2,1)S(1)}, u32[]{:S(2)}, u32[]{:S(2)}) collective-permute-start(bf16[128,1024]{1,0:T(8,128)(2,1)S(1)} %fusion.38), channel_id=1, source_target_pairs={{0,8},{4,12},{8,16},{12,20},{16,24},{20,28},{24,0},{28,4},{1,9},{5... | collective-permute-start | bytes 786440 | tf_op jit(solution)/shard_map/ppermute | solution.py:9
  96.7 11.7 %collective-permute-start.24 = (bf16[128,1024]{1,0:T(8,128)(2,1)S(1)}, bf16[128,1024]{1,0:T(8,128)(2,1)S(1)}, u32[]{:S(2)}, u32[]{:S(2)}) collective-permute-start(bf16[128,1024]{1,0:T(8,128)(2,1)S(1)} %fusion.5), channel_id=1, source_target_pairs={{0,8},{4,12},{8,16},{12,20},{16,24},{20,28},{24,0},{28,4},{1,9},{5... | collective-permute-start | bytes 786440 | tf_op jit(solution)/shard_map/ppermute | solution.py:9
  103.0 11.1 %collective-permute-start.2 = (bf16[128,1024]{1,0:T(8,128)(2,1)S(1)}, bf16[128,1024]{1,0:T(8,128)(2,1)S(1)}, u32[]{:S(2)}, u32[]{:S(2)}) collective-permute-start(bf16[128,1024]{1,0:T(8,128)(2,1)S(1)} %fusion.30), channel_id=1, source_target_pairs={{0,24},{4,28},{8,0},{12,4},{16,8},{20,12},{24,16},{28,20},{1,25},{... | collective-permute-start | bytes 786440 | tf_op jit(solution)/shard_map/ppermute | solution.py:9
  106.9 10.2 %copy-start.4 = (bf16[1,256,256]{2,1,0:T(8,128)(2,1)S(1)}, bf16[1,256,256]{2,1,0:T(8,128)(2,1)}, u32[]{:S(2)}) copy-start(bf16[1,256,256]{2,1,0:T(8,128)(2,1)} %param.9) | copy-start | bytes 393220
  106.9 10.1 %collective-permute-start.6 = (bf16[128,1024]{1,0:T(8,128)(2,1)S(1)}, bf16[128,1024]{1,0:T(8,128)(2,1)S(1)}, u32[]{:S(2)}, u32[]{:S(2)}) collective-permute-start(bf16[128,1024]{1,0:T(8,128)(2,1)S(1)} %fusion.37), channel_id=1, source_target_pairs={{0,8},{4,12},{8,16},{12,20},{16,24},{20,28},{24,0},{28,4},{1,9},{5... | collective-permute-start | bytes 786440 | tf_op jit(solution)/shard_map/ppermute | solution.py:9

commit v2 on v0

v2 whole, which is shorter than its diff:
```python
import functools

import jax
import jax.numpy as jnp
from jax import lax
from jax.experimental import pallas as pl
from jax.experimental.pallas import tpu as pltpu
from jax.sharding import PartitionSpec as P

F32, BF16 = jnp.float32, jnp.bfloat16
VMEM = pl.BlockSpec(memory_space=pltpu.VMEM)
SMEM = pl.BlockSpec(memory_space=pltpu.SMEM)
ANY = pl.BlockSpec(memory_space=pl.ANY)
HBM = pl.BlockSpec(memory_space=pltpu.HBM)


WIDE = 256
PIECES = 4


def shift(block, axis, distance):
    size = lax.axis_size(axis)
    return lax.ppermute(block, axis, [(i, (i + distance) % size) for i in range(size)])


def pair_swap(block, axis):
    size = lax.axis_size(axis)
    return lax.ppermute(block, axis, [(i, i ^ 1) for i in range(size)])


def across(block, axis):
    return shift(block, axis, lax.axis_size(axis) // 2)


def inner(i, j, half):
    return i // half * half + (i % half + j) % half


def half_gather(block, axis):
    size = lax.axis_size(axis)
    half = size // 2
    parts = [block]
    for j in range(1, half):
        parts.append(lax.ppermute(block, axis, [(inner(i, j, half), i) for i in range(size)]))
    return parts


def to_columns(blocks, distance):
    n, size = lax.axis_size("col"), lax.axis_size("rhs")
    out = []
    for j, block in enumerate(blocks):
        route = [(c * size + r, (c + distance) % n * size + inner(r, j, size // 2))
                 for c in range(n) for r in range(size)]
        out.append(lax.ppermute(block, ("col", "rhs"), route) if distance or j else block)
    return out


def pinned(*shape, dtype=BF16):
    return pltpu.VMEM(shape, dtype)


def call(body, outs, specs, args, flops=0, space=12, out_specs=None, **more):
    moved = sum(a.size * a.dtype.itemsize for a in args)
    return pl.pallas_call(
        body,
        out_shape=outs,
        in_specs=specs,
        out_specs=out_specs or [VMEM] * len(outs),
        compiler_params=pltpu.CompilerParams(vmem_limit_bytes=space << 20),
        cost_estimate=pl.CostEstimate(flops=flops, bytes_accessed=moved, transcendentals=0),
        **more,
    )(*args)


def take(tiles, groups, *earlier):
    n, rows = len(groups), tiles.shape[1]

    def body(*refs):
        src, dsts, sems = refs[0], refs[-1 - n:-1], refs[-1]
        copies = []
        for group, dst in zip(groups, dsts):
            for i, k in enumerate(group):
                for at in range(0, rows, rows // PIECES):
                    cut = pl.ds(at, rows // PIECES)
                    copies.append(pltpu.make_async_copy(src.at[k, cut], dst.at[i, cut], sems.at[len(copies)]))
        for c in copies:
            c.start()
        for c in copies:
            c.wait()

    outs = [pinned(len(g), *tiles.shape[1:]) for g in groups]
    return call(body, outs, [HBM] + [ANY] * len(earlier), [in_hbm(tiles), *earlier], space=2,
                scratch_shapes=[pltpu.SemaphoreType.DMA((PIECES * sum(map(len, groups)),))])


def in_hbm(array):
    return pltpu.with_memory_space_constraint(array, pltpu.HBM)


def on_odd():
    return lax.rem(lax.axis_index("col"), 2) == 1


def gate(block, *earlier):
    def body(*refs):
        pass

    return call(body, [jax.ShapeDtypeStruct(block.shape, block.dtype)], [ANY] * (1 + len(earlier)), [block, *earlier],
                space=1, out_specs=[ANY], input_output_aliases={0: 0})[0]


def column_cuts(cols):
    wide = min(WIDE, cols)
    return [slice(at, at + wide) for at in range(0, cols, wide)]


def per_device(rhs_block, solution, factor, tile_list, diag_inverse):
    hops, quarter, depth = factor.shape[1:]
    rows, cols = rhs_block.shape
    size = lax.axis_size("rhs")
    half = size // 2
    tiles = factor[0]
    gives, owns = (2, 4, 0), (3, 5, 1)
    cuts = column_cuts(cols)
    strip = (half, quarter, cols)
    one = pinned(*strip)

    s24, = take(tiles, [(2, 4)])
    y24 = across(s24, "rhs")
    others = half_gather(solution, "rhs")[1:]
    s35, s0, s1 = take(tiles, [(3, 5), (0,), (1,)], s24)
    y35 = across(s35, "rhs")
    y0 = across(s0, "rhs")
    y1 = across(s1, "rhs")

    def near(left_ref, sol, weights, *refs):
        give, own = refs[-2:]
        left = left_ref[...].reshape(hops * quarter, depth)
        for cut in cuts:
            total = jnp.dot(left, sol[:, cut], preferred_element_type=F32)
            for i in range(len(gives)):
                g = total[gives[i] * quarter:(gives[i] + 1) * quarter]
                give[i, :, cut] = (g * weights[0, gives[i]].astype(F32)).astype(BF16)
                o = total[owns[i] * quarter:(owns[i] + 1) * quarter]
                own[i, :, cut] = o * weights[0, owns[i]].astype(F32)

    sols = [solution, *others]
    near_own, got_near = [], []
    token = s35
    for sol in sols:
        give, own = call(near, [pinned(3, quarter, cols), pinned(3, quarter, cols, dtype=F32)],
                         [VMEM, VMEM, SMEM, ANY], [tiles, sol, tile_list, token],
                         flops=2 * hops * quarter * depth * cols)
        got_near.append(pair_swap(give, "col"))
        near_own.append(own)
        token = own

    def products(far, ks, epilogue, outs, extra, earlier, which=None):
        which = list(range(half)) if which is None else which
        n_sol, n_extra = len(which), len(extra)

        def body(far_ref, *refs):
            sol_refs, weights = refs[:n_sol], refs[n_sol]
            more = refs[n_sol + 1:n_sol + 1 + n_extra]
            out = refs[len(refs) - len(outs):]
            is_odd = on_odd()
            left = far_ref[...].reshape(len(ks) * quarter, depth)
            for part, sol_ref in zip(which, sol_refs):
                for cut in cuts:
                    total = jnp.dot(left, sol_ref[:, cut], preferred_element_type=F32)
                    for i, k in enumerate(ks):
                        term = total[i * quarter:(i + 1) * quarter] * weights[0, k].astype(F32)
                        epilogue(out, more, is_odd, i, part, cut, term)

        args = [far, *[sols[p] for p in which], tile_list, *extra, *earlier]
        specs = [VMEM] * (n_sol + 1) + [SMEM] + [VMEM] * n_extra + [ANY] * len(earlier)
        return call(body, outs, specs, args, flops=2 * len(ks) * quarter * depth * cols * n_sol)

    def store(out, more, is_odd, i, part, cut, total):
        out[0][i, part, :, cut] = total.astype(out[0].dtype)

    far_give, = products(y24, (2, 4), store, [pinned(2, *strip)], [], [token])
    got_far = pair_swap(far_give, "col")

    def near23(*refs):
        owns, gots, (d2, d3) = refs[:half], refs[half:2 * half], refs[-2:]
        is_odd = on_odd()
        for part, (own, got) in enumerate(zip(owns, gots)):
            r4 = got[1].astype(F32)
            d2[part] = (own[0] + jnp.where(is_odd, r4, got[0].astype(F32))).astype(BF16)
            d3[part] = (own[1] + jnp.where(is_odd, 0.0, r4)).astype(BF16)

    d2n, d3n = call(near23, [one, one], [VMEM] * (2 * half) + [ANY], [*near_own, *got_near, far_give])
    d2n_in = shift(d2n, "col", 2)
    d3n_in = shift(d3n, "col", 6)

    def near1(chained, *refs):
        owns, gots, d1 = refs[:half], refs[half:2 * half], refs[-1]
        is_odd = on_odd()
        for part, (own, got) in enumerate(zip(owns, gots)):
            r = jnp.where(is_odd, got[0].astype(F32), got[2].astype(F32))
            d1[part] = (own[2] + r + chained[part].astype(F32)).astype(BF16)

    d1n, = call(near1, [one], [VMEM] * (1 + 2 * half), [d2n_in, *near_own, *got_near])
    d1n_in = shift(d1n, "col", 2)

    def far23(out, more, is_odd, i, part, cut, total):
        got, = more
        r4 = got[1, part, :, cut].astype(F32)
        if i == 0:
            total = total + jnp.where(is_odd, r4, got[0, part, :, cut].astype(F32))
        else:
            total = total + jnp.where(is_odd, 0.0, r4)
        out[i][part, :, cut] = total.astype(BF16)

    d2f, d3f = products(y35, (3, 5), far23, [one, one], [got_far], [d1n])
    d2f_in = shift(d2f, "col", 2)
    d3f_in = shift(d3f, "col", 6)

    last_give, = products(y0, (0,), store, [pinned(1, *strip)], [], [d2f])
    got_last = pair_swap(last_give, "col")

    def collect(d1, d3, gl, d3far, *refs):
        gots, outs = refs[:half], refs[-half:]
        is_odd = on_odd()
        for part, (got, out) in enumerate(zip(gots, outs)):
            upper = d1[part].astype(F32) + d3[part].astype(F32)
            out[0] = upper + jnp.where(is_odd, got[2].astype(F32), 0.0)
            out[1] = d3far[part].astype(F32) + jnp.where(is_odd, gl[0, part].astype(F32), 0.0)

    sums = call(collect, [pinned(2, quarter, cols, dtype=F32)] * half, [VMEM] * (4 + half) + [ANY],
                [d1n_in, d3n_in, got_last, d3f_in, *got_near, last_give])
    sums_in = to_columns(sums, 0)

    def far1(out, more, is_odd, i, part, cut, total):
        got, got0, chained = more
        r = jnp.where(is_odd, got[0, part, :, cut].astype(F32), got0[0, part, :, cut].astype(F32))
        out[0][:, cut] = (total + r + chained[part, :, cut].astype(F32)).astype(BF16)

    d1f = [None] * half
    token = sums[-1]
    for part in list(range(1, half)) + [0]:
        d1f[part], = products(y1, (1,), far1, [pinned(quarter, cols)], [got_far, got_last, d2f_in], [token], [part])
        token = d1f[part]
    d1f_in = to_columns(d1f, 2)

    def arrange(rhs, diag, _, rhs_out, diag_out):
        me = lax.axis_index("rhs")
        upper, mine = lax.div(me, half), lax.rem(me, half)
        column = lax.broadcasted_iota(jnp.int32, (rows, rows), 1)
        source = column
        for s in range(2):
            for j in range(half):
                at = (s * half + j) * quarter
                block = lax.rem(upper + s, 2) * half + lax.rem(mine + half - j, half)
                start = pl.multiple_of(block * quarter, quarter)
                rhs_out[at:at + quarter] = rhs[pl.ds(start, quarter)]
                source = jnp.where((column >= at) & (column < at + quarter), column - at + start, source)
        pick = (lax.broadcasted_iota(jnp.int32, (rows, rows), 0) == source).astype(BF16)
        diag_out[...] = jnp.dot(diag[0], pick, preferred_element_type=F32).astype(BF16)

    rhs_local, diag_local = call(arrange, [pinned(rows, cols), pinned(rows, rows)], [VMEM, VMEM, ANY],
                                 [rhs_block, diag_inverse, near_own[-1]], flops=2 * rows * rows * rows)

    def final(rhs, diag, *refs):
        acc, last, out = refs[:half], refs[half:2 * half], refs[-1]
        total = jnp.concatenate([a[0] for a in acc] + [a[1] + l[...].astype(F32) for a, l in zip(acc, last)])
        remaining = (rhs[...].astype(F32) - total).astype(BF16)
        out[...] = jnp.dot(diag[...], remaining, preferred_element_type=F32).astype(BF16)

    return call(final, [jax.ShapeDtypeStruct((rows, cols), BF16)], [VMEM] * (2 + 2 * half),
                [rhs_local, diag_local, *sums_in, *d1f_in], flops=2 * rows * rows * cols)[0]


def solution(mesh):
    in_specs = (
        P("col", "rhs"),
        P("col", "rhs"),
        P("col", None, "rhs", None),
        P("col", None),
        P("col", None, None),
    )
    out_specs = P("col", "rhs")
    return jax.shard_map(
        per_device, mesh=mesh, in_specs=in_specs, out_specs=out_specs, check_vma=False
    )
```

time: 206 us -> 85.1 us (0.41)
  waiting for transfers between devices: 150 us -> 38.3 us
  matrix products: 31.1 us -> 0 us
  Pallas kernels: 0 us -> 22.6 us
  starting transfers between devices: 2.01 us -> 21.5 us
  between operations: 17.3 us -> 0.16 us
  local copies, waits for them, and re-layouts: 4.73 us -> 1.69 us
    ppermute x6 -> x17, waiting for transfers between devices: 112 us -> 38.3 us  [the longest x9 22.4 us: shift(): lax.ppermute(block, axis, [(i, (i + distance) % size) for i in range(size)])]
    all_gather x6 -> x0, waiting for transfers between devices: 36.8 us -> none  [per_device(): lax.all_gather(factor[0, offset], 'rhs', axis=0, tiled=True)]
    dot_general x7 -> x0, matrix products: 31.1 us -> none  [the longest x6 30.7 us: per_device(): jnp.dot(lax.all_gather(factor[0, offset], 'rhs', axis=0, tiled=True), sol...]
    pallas_call x0 -> x14, Pallas kernels: none -> 22.6 us  [call(): pl.pallas_call(body, out_shape=outs, in_specs=specs, out_specs=out_specs...]
    ppermute x6 -> x17, starting transfers between devices: 1.81 us -> 21.5 us  [the longest x9 15.1 us: shift(): lax.ppermute(block, axis, [(i, (i + distance) % size) for i in range(size)])]
    slice x2 -> x0, local copies, waits for them, and re-layouts: 3.71 us -> none  [the longest x1 3.04 us: per_device(): factor[0, offset]]
  transfers between devices with their start and end apart: 12 -> 17, of which waited for: 9 -> 9; matrix products, arithmetic and copies ran while one was open for 15% -> 0% of each run, Pallas kernels for 0% -> 25%
where the time goes in v2:
time: 85.1 us; the launch traced here: 84.2 us
  waiting for transfers between devices  38.3 us (45%)
  Pallas kernels  22.6 us (27%)
  starting transfers between devices  21.5 us (25%)
  local copies, waits for them, and re-layouts  1.69 us (2%)
    pallas_call x14, Pallas kernels, call(): pl.pallas_call(body, out_shape=outs, in_specs=specs, out_specs=out_specs...  22.6 us
    ppermute x9, waiting for transfers between devices, shift(): lax.ppermute(block, axis, [(i, (i + distance) % size) for i in range(size)])  22.4 us
    ppermute x9, starting transfers between devices, shift(): lax.ppermute(block, axis, [(i, (i + distance) % size) for i in range(size)])  15.1 us
    ppermute x3, waiting for transfers between devices, to_columns(): lax.ppermute(block, ('col', 'rhs'), route)  7.97 us
    ppermute x4, waiting for transfers between devices, pair_swap(): return lax.ppermute(block, axis, [(i, i ^ 1) for i in range(size)])  7.88 us
    ppermute x4, starting transfers between devices, pair_swap(): return lax.ppermute(block, axis, [(i, i ^ 1) for i in range(size)])  5.78 us
  transfers between devices with their start and end apart: 17, of which 9 were waited for; matrix products, arithmetic and copies ran while one was open for 0% of the time, Pallas kernels for 25%

profile of v2, /device:TPU:0, one launch (start us, length us, event | category | flops | bytes accessed | tf_op | source)
XLA Modules:
  0.0 84.2 jit_solution(13779370593262599258)
XLA Ops:
  0.0 0.0 copy-start
  0.0 0.0 copy-start.4
  0.0 0.5 collective-permute-start
  0.5 1.5 %shard_map.55.refs_1_ = bf16[2,64,3072]{2,1,0:T(8,128)(2,1)S(1)} custom-call(bf16[6,64,3072]{2,1,0:T(8,128)(2,1)} %bitcast.1), custom_call_target="tpu_custom_call" | custom-call | bytes 2359296 | tf_op jit(solution)/shard_map/pallas_call | solution.py:64
  1.9 2.5 %collective-permute-start.3 = (bf16[2,64,3072]{2,1,0:T(8,128)(2,1)S(1)}, bf16[2,64,3072]{2,1,0:T(8,128)(2,1)S(1)}, u32[]{:S(2)}, u32[]{:S(2)}) collective-permute-start(bf16[2,64,3072]{2,1,0:T(8,128)(2,1)S(1)} %shard_map.55.refs_1_), channel_id=1, source_target_pairs={{0,2},{1,3},{2,0},{3,1},{4,6},{5,7},{6,4},{7,5},{8,10},{9,11},{10,... | collective-permute-start | bytes 2359304 | tf_op jit(solution)/shard_map/ppermute | solution.py:23
  4.5 1.6 %shard_map.56 = (bf16[2,64,3072]{2,1,0:T(8,128)(2,1)S(1)}, bf16[1,64,3072]{2,1,0:T(8,128)(2,1)S(1)}, bf16[1,64,3072]{2,1,0:T(8,128)(2,1)S(1)}) custom-call(bf16[6,64,3072]{2,1,0:T(8,128)(2,1)} %bitcast.2, bf16[2,64,3072]{2,1,0:T(8,128)(2,1)S(1)} %shard_map.55.refs_1_), custom_call_target="tpu_custom_call" | custom-call | bytes 3145728 | tf_op jit(solution)/shard_map/pallas_call | solution.py:64
  6.1 0.7 collective-permute-start.8
  6.8 0.0 copy-done
  6.8 0.0 copy-done.4
  6.8 0.0 copy-start.1
  6.8 1.7 %copy-done.1 = bf16[1,6,64,3072]{3,2,1,0:T(8,128)(2,1)S(1)} copy-done((bf16[1,6,64,3072]{3,2,1,0:T(8,128)(2,1)S(1)}, bf16[1,6,64,3072]{3,2,1,0:T(8,128)(2,1)}, u32[]{:S(2)}) %copy-start.1) | copy-done | bytes 2359320
  8.5 3.2 %shard_map.57 = (bf16[3,64,1024]{2,1,0:T(8,128)(2,1)S(1)}, f32[3,64,1024]{2,1,0:T(8,128)S(1)}) custom-call(bf16[6,64,3072]{2,1,0:T(8,128)(2,1)S(1)} %bitcast.3, bf16[3072,1024]{1,0:T(8,128)(2,1)S(1)} %copy-done, s32[1,6]{1,0:T(1,128)S(1)} %copy-done.4, bf16[2,64,3072]{2,1,0:T(8,128)(2,1)S(1)} %get-tuple-element.20.refs_0_), custom_call_target="tpu_custom_call" | custom-call | flops 2415919104 | bytes 9437208 | tf_op jit(solution)/shard_map/pallas_call | solution.py:64
  11.7 1.6 %collective-permute-start.1 = (bf16[3,64,1024]{2,1,0:T(8,128)(2,1)S(1)}, bf16[3,64,1024]{2,1,0:T(8,128)(2,1)S(1)}, u32[]{:S(2)}, u32[]{:S(2)}) collective-permute-start(bf16[3,64,1024]{2,1,0:T(8,128)(2,1)S(1)} %get-tuple-element.25), channel_id=1, source_target_pairs={{0,4},{4,0},{8,12},{12,8},{16,20},{20,16},{24,28},{28,24},{1,5},{5... | collective-permute-start | bytes 1179656 | tf_op jit(solution)/shard_map/ppermute | solution.py:28
  13.2 0.0 collective-permute-done.sol.refs_1_.refs_0_
  13.2 3.2 %shard_map.58 = (bf16[3,64,1024]{2,1,0:T(8,128)(2,1)S(1)}, f32[3,64,1024]{2,1,0:T(8,128)S(1)}) custom-call(bf16[6,64,3072]{2,1,0:T(8,128)(2,1)S(1)} %bitcast.4, bf16[3072,1024]{1,0:T(8,128)(2,1)S(1)} %collective-permute-done.sol.refs_1_.refs_0_, s32[1,6]{1,0:T(1,128)S(1)} %copy-done.4, f32[3,64,1024]{2,1,0:T(8,128)S(1)} %get-tuple-element.21.refs_0_), custom_call_target="tpu_custom_call" | custom-call | flops 2415919104 | bytes 9437208 | tf_op jit(solution)/shard_map/pallas_call | solution.py:64
  16.4 0.6 collective-permute-start.2
  17.0 5.9 %collective-permute-done.3.far_ref = bf16[2,64,3072]{2,1,0:T(8,128)(2,1)S(1)} collective-permute-done((bf16[2,64,3072]{2,1,0:T(8,128)(2,1)S(1)}, bf16[2,64,3072]{2,1,0:T(8,128)(2,1)S(1)}, u32[]{:S(2)}, u32[]{:S(2)}) %collective-permute-start.3) | collective-permute-done | bytes 786464 | tf_op jit(solution)/shard_map/ppermute | solution.py:23
  22.9 2.4 %shard_map.60.refs_4_ = bf16[2,2,64,1024]{3,2,1,0:T(8,128)(2,1)S(1)} custom-call(bf16[2,64,3072]{2,1,0:T(8,128)(2,1)S(1)} %collective-permute-done.3.far_ref, bf16[3072,1024]{1,0:T(8,128)(2,1)S(1)} %copy-done, bf16[3072,1024]{1,0:T(8,128)(2,1)S(1)} %collective-permute-done.sol.refs_1_.refs_0_, s32[1,6]{1,0:T(1,128)S(1)} %copy-done.4, ...), custom_call_target="tpu_custom_call" | custom-call | flops 1610612736 | bytes 14155800 | tf_op jit(solution)/shard_map/pallas_call | solution.py:64
  25.3 2.1 %collective-permute-start.9 = (bf16[2,2,64,1024]{3,2,1,0:T(8,128)(2,1)S(1)}, bf16[2,2,64,1024]{3,2,1,0:T(8,128)(2,1)S(1)}, u32[]{:S(2)}, u32[]{:S(2)}) collective-permute-start(bf16[2,2,64,1024]{3,2,1,0:T(8,128)(2,1)S(1)} %shard_map.60.refs_4_), channel_id=1, source_target_pairs={{0,4},{4,0},{8,12},{12,8},{16,20},{20,16},{24,28},{28,24},{1,5},{5... | collective-permute-start | bytes 1572872 | tf_op jit(solution)/shard_map/ppermute | solution.py:28
  27.3 0.0 collective-permute-done.1.refs_2_.refs_0_
  27.3 4.8 %collective-permute-done.2.refs_3_.refs_1_ = bf16[3,64,1024]{2,1,0:T(8,128)(2,1)S(1)} collective-permute-done((bf16[3,64,1024]{2,1,0:T(8,128)(2,1)S(1)}, bf16[3,64,1024]{2,1,0:T(8,128)(2,1)S(1)}, u32[]{:S(2)}, u32[]{:S(2)}) %collective-permute-start.2) | collective-permute-done | bytes 393248 | tf_op jit(solution)/shard_map/ppermute | solution.py:28
  32.2 0.2 shard_map.61
  32.3 1.6 %collective-permute-start.4 = (bf16[2,64,1024]{2,1,0:T(8,128)(2,1)S(1)}, bf16[2,64,1024]{2,1,0:T(8,128)(2,1)S(1)}, u32[]{:S(2)}, u32[]{:S(2)}) collective-permute-start(bf16[2,64,1024]{2,1,0:T(8,128)(2,1)S(1)} %get-tuple-element.27), channel_id=1, source_target_pairs={{0,8},{4,12},{8,16},{12,20},{16,24},{20,28},{24,0},{28,4},{1,9},{5... | collective-permute-start | bytes 786440 | tf_op jit(solution)/shard_map/ppermute | solution.py:23
  33.9 1.4 %collective-permute-start.7 = (bf16[1,64,3072]{2,1,0:T(8,128)(2,1)S(1)}, bf16[1,64,3072]{2,1,0:T(8,128)(2,1)S(1)}, u32[]{:S(2)}, u32[]{:S(2)}) collective-permute-start(bf16[1,64,3072]{2,1,0:T(8,128)(2,1)S(1)} %get-tuple-element.29), channel_id=1, source_target_pairs={{0,2},{1,3},{2,0},{3,1},{4,6},{5,7},{6,4},{7,5},{8,10},{9,11},{10,... | collective-permute-start | bytes 1179656 | tf_op jit(solution)/shard_map/ppermute | solution.py:23
  35.3 2.2 %collective-permute-start.6 = (bf16[2,64,1024]{2,1,0:T(8,128)(2,1)S(1)}, bf16[2,64,1024]{2,1,0:T(8,128)(2,1)S(1)}, u32[]{:S(2)}, u32[]{:S(2)}) collective-permute-start(bf16[2,64,1024]{2,1,0:T(8,128)(2,1)S(1)} %get-tuple-element.28), channel_id=1, source_target_pairs={{0,24},{4,28},{8,0},{12,4},{16,8},{20,12},{24,16},{28,20},{1,25},{... | collective-permute-start | bytes 786440 | tf_op jit(solution)/shard_map/ppermute | solution.py:23
  37.5 5.8 %collective-permute-done.4.chained = bf16[2,64,1024]{2,1,0:T(8,128)(2,1)S(1)} collective-permute-done((bf16[2,64,1024]{2,1,0:T(8,128)(2,1)S(1)}, bf16[2,64,1024]{2,1,0:T(8,128)(2,1)S(1)}, u32[]{:S(2)}, u32[]{:S(2)}) %collective-permute-start.4) | collective-permute-done | bytes 262176 | tf_op jit(solution)/shard_map/ppermute | solution.py:23
  43.4 0.1 shard_map.62.refs_4_
  43.5 1.3 %collective-permute-start.5 = (bf16[2,64,1024]{2,1,0:T(8,128)(2,1)S(1)}, bf16[2,64,1024]{2,1,0:T(8,128)(2,1)S(1)}, u32[]{:S(2)}, u32[]{:S(2)}) collective-permute-start(bf16[2,64,1024]{2,1,0:T(8,128)(2,1)S(1)} %shard_map.62.refs_4_), channel_id=1, source_target_pairs={{0,8},{4,12},{8,16},{12,20},{16,24},{20,28},{24,0},{28,4},{1,9},{5... | collective-permute-start | bytes 786440 | tf_op jit(solution)/shard_map/ppermute | solution.py:23
  44.8 0.0 collective-permute-done.8.far_ref
  44.8 0.0 collective-permute-done.9.refs_3_.refs_2_
  44.8 2.5 %shard_map.63 = (bf16[2,64,1024]{2,1,0:T(8,128)(2,1)S(1)}, bf16[2,64,1024]{2,1,0:T(8,128)(2,1)S(1)}) custom-call(bf16[2,64,3072]{2,1,0:T(8,128)(2,1)S(1)} %collective-permute-done.8.far_ref, bf16[3072,1024]{1,0:T(8,128)(2,1)S(1)} %copy-done, bf16[3072,1024]{1,0:T(8,128)(2,1)S(1)} %collective-permute-done.sol.refs_1_.refs_0_, s32[1,6]{1,0:T(1,128)S(1)} %copy-done.4, ...), custom_call_target="tpu_custom_call" | custom-call | flops 1610612736 | bytes 14155800 | tf_op jit(solution)/shard_map/pallas_call | solution.py:64
  47.3 3.7 %collective-permute-start.11 = (bf16[2,64,1024]{2,1,0:T(8,128)(2,1)S(1)}, bf16[2,64,1024]{2,1,0:T(8,128)(2,1)S(1)}, u32[]{:S(2)}, u32[]{:S(2)}) collective-permute-start(bf16[2,64,1024]{2,1,0:T(8,128)(2,1)S(1)} %get-tuple-element.31), channel_id=1, source_target_pairs={{0,24},{4,28},{8,0},{12,4},{16,8},{20,12},{24,16},{28,20},{1,25},{... | collective-permute-start | bytes 786440 | tf_op jit(solution)/shard_map/ppermute | solution.py:23
  51.0 0.0 collective-permute-done.7.far_ref
  51.0 2.9 %shard_map.64.refs_2_ = bf16[1,2,64,1024]{3,2,1,0:T(8,128)(2,1)S(1)} custom-call(bf16[1,64,3072]{2,1,0:T(8,128)(2,1)S(1)} %collective-permute-done.7.far_ref, bf16[3072,1024]{1,0:T(8,128)(2,1)S(1)} %copy-done, bf16[3072,1024]{1,0:T(8,128)(2,1)S(1)} %collective-permute-done.sol.refs_1_.refs_0_, s32[1,6]{1,0:T(1,128)S(1)} %copy-done.4, ...), custom_call_target="tpu_custom_call" | custom-call | flops 805306368 | bytes 13238296 | tf_op jit(solution)/shard_map/pallas_call | solution.py:64
  53.9 1.6 %collective-permute-start.10 = (bf16[1,2,64,1024]{3,2,1,0:T(8,128)(2,1)S(1)}, bf16[1,2,64,1024]{3,2,1,0:T(8,128)(2,1)S(1)}, u32[]{:S(2)}, u32[]{:S(2)}) collective-permute-start(bf16[1,2,64,1024]{3,2,1,0:T(8,128)(2,1)S(1)} %shard_map.64.refs_2_), channel_id=1, source_target_pairs={{0,4},{4,0},{8,12},{12,8},{16,20},{20,16},{24,28},{28,24},{1,5},{5... | collective-permute-start | bytes 786440 | tf_op jit(solution)/shard_map/ppermute | solution.py:28
  55.5 1.1 %collective-permute-start.13 = (bf16[1,64,3072]{2,1,0:T(8,128)(2,1)S(1)}, bf16[1,64,3072]{2,1,0:T(8,128)(2,1)S(1)}, u32[]{:S(2)}, u32[]{:S(2)}) collective-permute-start(bf16[1,64,3072]{2,1,0:T(8,128)(2,1)S(1)} %get-tuple-element.34), channel_id=1, source_target_pairs={{0,2},{1,3},{2,0},{3,1},{4,6},{5,7},{6,4},{7,5},{8,10},{9,11},{10,... | collective-permute-start | bytes 1179656 | tf_op jit(solution)/shard_map/ppermute | solution.py:23
  56.5 0.0 collective-permute-done.6.d3
  56.5 0.0 collective-permute-done.5.d1
  56.5 0.8 collective-permute-done.11.d3far
  57.3 3.0 %collective-permute-done.10.gl.refs_3_ = bf16[1,2,64,1024]{3,2,1,0:T(8,128)(2,1)S(1)} collective-permute-done((bf16[1,2,64,1024]{3,2,1,0:T(8,128)(2,1)S(1)}, bf16[1,2,64,1024]{3,2,1,0:T(8,128)(2,1)S(1)}, u32[]{:S(2)}, u32[]{:S(2)}) %collective-permute-start.10) | collective-permute-done | bytes 262176 | tf_op jit(solution)/shard_map/ppermute | solution.py:28
  60.3 0.2 shard_map.65
  60.5 0.0 copy-start.2
  60.5 0.0 copy-start.3
  60.5 0.1 collective-permute-start.12
  60.6 0.5 collective-permute-start.14
  61.1 2.1 %collective-permute-done.13.far_ref = bf16[1,64,3072]{2,1,0:T(8,128)(2,1)S(1)} collective-permute-done((bf16[1,64,3072]{2,1,0:T(8,128)(2,1)S(1)}, bf16[1,64,3072]{2,1,0:T(8,128)(2,1)S(1)}, u32[]{:S(2)}, u32[]{:S(2)}) %collective-permute-start.13) | collective-permute-done | bytes 393248 | tf_op jit(solution)/shard_map/ppermute | solution.py:23
  63.3 7.9 %collective-permute-done.14.refs_4_ = bf16[2,64,1024]{2,1,0:T(8,128)(2,1)S(1)} collective-permute-done((bf16[2,64,1024]{2,1,0:T(8,128)(2,1)S(1)}, bf16[2,64,1024]{2,1,0:T(8,128)(2,1)S(1)}, u32[]{:S(2)}, u32[]{:S(2)}) %collective-permute-start.14) | collective-permute-done | bytes 262176 | tf_op jit(solution)/shard_map/ppermute | solution.py:23
  71.1 1.8 %shard_map.66.refs_5_ = bf16[64,1024]{1,0:T(8,128)(2,1)S(1)} custom-call(bf16[1,64,3072]{2,1,0:T(8,128)(2,1)S(1)} %collective-permute-done.13.far_ref, bf16[3072,1024]{1,0:T(8,128)(2,1)S(1)} %collective-permute-done.sol.refs_1_.refs_0_, s32[1,6]{1,0:T(1,128)S(1)} %copy-done.4, bf16[2,2,64,1024]{3,2,1,0:T(8,128)(2,1)S(1)} %collective-permute-done.9.refs_3_.refs_2_, ...), custom_call_target="tpu_custom_call" | custom-call | flops 402653184 | bytes 8257560 | tf_op jit(solution)/shard_map/pallas_call | solution.py:64
  72.9 1.8 %shard_map.67 = bf16[64,1024]{1,0:T(8,128)(2,1)S(1)} custom-call(bf16[1,64,3072]{2,1,0:T(8,128)(2,1)S(1)} %collective-permute-done.13.far_ref, bf16[3072,1024]{1,0:T(8,128)(2,1)S(1)} %copy-done, s32[1,6]{1,0:T(1,128)S(1)} %copy-done.4, bf16[2,2,64,1024]{3,2,1,0:T(8,128)(2,1)S(1)} %collective-permute-done.9.refs_3_.refs_2_, ...), custom_call_target="tpu_custom_call" | custom-call | flops 402653184 | bytes 7864344 | tf_op jit(solution)/shard_map/pallas_call | solution.py:64
  74.7 0.1 collective-permute-start.15
  74.8 0.1 collective-permute-start.16
  74.8 0.0 copy-done.2
  74.9 0.0 copy-done.3
  74.9 0.2 shard_map.59
  75.1 7.9 %collective-permute-done.15.refs_2_ = bf16[64,1024]{1,0:T(8,128)(2,1)S(1)} collective-permute-done((bf16[64,1024]{1,0:T(8,128)(2,1)S(1)}, bf16[64,1024]{1,0:T(8,128)(2,1)S(1)}, u32[]{:S(2)}, u32[]{:S(2)}) %collective-permute-start.15) | collective-permute-done | bytes 131104 | tf_op jit(solution)/shard_map/ppermute | solution.py:54
  83.0 0.1 collective-permute-done.16.refs_3_
  83.1 0.0 collective-permute-done.12.refs_1_
  83.1 1.1 %shard_map.68 = bf16[256,1024]{1,0:T(8,128)(2,1)} custom-call(bf16[256,1024]{1,0:T(8,128)(2,1)S(1)} %get-tuple-element.23.rhs, bf16[256,256]{1,0:T(8,128)(2,1)S(1)} %get-tuple-element.24.diag, f32[2,64,1024]{2,1,0:T(8,128)S(1)} %get-tuple-element.32.refs_0_, f32[2,64,1024]{2,1,0:T(8,128)S(1)} %collective-permute-done.12.refs_1_, ...), custom_call_target="tpu_custom_call" | custom-call | flops 134217728 | bytes 1966080 | tf_op jit(solution)/shard_map/pallas_call | solution.py:64
Async XLA Ops:
  0.0 6.8 %copy-start = (bf16[3072,1024]{1,0:T(8,128)(2,1)S(1)}, bf16[3072,1024]{1,0:T(8,128)(2,1)}, u32[]{:S(2)}) copy-start(bf16[3072,1024]{1,0:T(8,128)(2,1)} %refs_0_.7) | copy-start | bytes 18874372
  0.0 6.8 %copy-start.4 = (s32[1,6]{1,0:T(1,128)S(1)}, s32[1,6]{1,0:T(1,128)}, u32[]{:S(2)}) copy-start(s32[1,6]{1,0:T(1,128)} %refs_1_.3) | copy-start | bytes 76
  0.0 13.2 %collective-permute-start = (bf16[3072,1024]{1,0:T(8,128)(2,1)}, bf16[3072,1024]{1,0:T(8,128)(2,1)S(1)}, u32[]{:S(2)}, u32[]{:S(2)}) collective-permute-start(bf16[3072,1024]{1,0:T(8,128)(2,1)} %refs_0_.7), channel_id=1, source_target_pairs={{1,0},{0,1},{3,2},{2,3},{5,4},{4,5},{7,6},{6,7},{9,8},{8,9},{11,10... | collective-permute-start | bytes 18874376 | tf_op jit(solution)/shard_map/ppermute | solution.py:44
  1.9 20.9 %collective-permute-start.3 = (bf16[2,64,3072]{2,1,0:T(8,128)(2,1)S(1)}, bf16[2,64,3072]{2,1,0:T(8,128)(2,1)S(1)}, u32[]{:S(2)}, u32[]{:S(2)}) collective-permute-start(bf16[2,64,3072]{2,1,0:T(8,128)(2,1)S(1)} %shard_map.55.refs_1_), channel_id=1, source_target_pairs={{0,2},{1,3},{2,0},{3,1},{4,6},{5,7},{6,4},{7,5},{8,10},{9,11},{10,... | collective-permute-start | bytes 2359304 | tf_op jit(solution)/shard_map/ppermute | solution.py:23
  6.1 38.8 %collective-permute-start.8 = (bf16[2,64,3072]{2,1,0:T(8,128)(2,1)S(1)}, bf16[2,64,3072]{2,1,0:T(8,128)(2,1)S(1)}, u32[]{:S(2)}, u32[]{:S(2)}) collective-permute-start(bf16[2,64,3072]{2,1,0:T(8,128)(2,1)S(1)} %get-tuple-element.20.refs_0_), channel_id=1, source_target_pairs={{0,2},{1,3},{2,0},{3,1},{4,6},{5,7},{6,4},{7,5},{8,10},{9,11},{10,... | collective-permute-start | bytes 2359304 | tf_op jit(solution)/shard_map/ppermute | solution.py:23
  6.8 1.7 %copy-start.1 = (bf16[1,6,64,3072]{3,2,1,0:T(8,128)(2,1)S(1)}, bf16[1,6,64,3072]{3,2,1,0:T(8,128)(2,1)}, u32[]{:S(2)}) copy-start(bf16[1,6,64,3072]{3,2,1,0:T(8,128)(2,1)} %param.7) | copy-start | bytes 7077892
  11.7 15.7 %collective-permute-start.1 = (bf16[3,64,1024]{2,1,0:T(8,128)(2,1)S(1)}, bf16[3,64,1024]{2,1,0:T(8,128)(2,1)S(1)}, u32[]{:S(2)}, u32[]{:S(2)}) collective-permute-start(bf16[3,64,1024]{2,1,0:T(8,128)(2,1)S(1)} %get-tuple-element.25), channel_id=1, source_target_pairs={{0,4},{4,0},{8,12},{12,8},{16,20},{20,16},{24,28},{28,24},{1,5},{5... | collective-permute-start | bytes 1179656 | tf_op jit(solution)/shard_map/ppermute | solution.py:28
  16.4 15.8 %collective-permute-start.2 = (bf16[3,64,1024]{2,1,0:T(8,128)(2,1)S(1)}, bf16[3,64,1024]{2,1,0:T(8,128)(2,1)S(1)}, u32[]{:S(2)}, u32[]{:S(2)}) collective-permute-start(bf16[3,64,1024]{2,1,0:T(8,128)(2,1)S(1)} %get-tuple-element.26), channel_id=1, source_target_pairs={{0,4},{4,0},{8,12},{12,8},{16,20},{20,16},{24,28},{28,24},{1,5},{5... | collective-permute-start | bytes 1179656 | tf_op jit(solution)/shard_map/ppermute | solution.py:28
  25.3 19.6 %collective-permute-start.9 = (bf16[2,2,64,1024]{3,2,1,0:T(8,128)(2,1)S(1)}, bf16[2,2,64,1024]{3,2,1,0:T(8,128)(2,1)S(1)}, u32[]{:S(2)}, u32[]{:S(2)}) collective-permute-start(bf16[2,2,64,1024]{3,2,1,0:T(8,128)(2,1)S(1)} %shard_map.60.refs_4_), channel_id=1, source_target_pairs={{0,4},{4,0},{8,12},{12,8},{16,20},{20,16},{24,28},{28,24},{1,5},{5... | collective-permute-start | bytes 1572872 | tf_op jit(solution)/shard_map/ppermute | solution.py:28
  32.3 11.0 %collective-permute-start.4 = (bf16[2,64,1024]{2,1,0:T(8,128)(2,1)S(1)}, bf16[2,64,1024]{2,1,0:T(8,128)(2,1)S(1)}, u32[]{:S(2)}, u32[]{:S(2)}) collective-permute-start(bf16[2,64,1024]{2,1,0:T(8,128)(2,1)S(1)} %get-tuple-element.27), channel_id=1, source_target_pairs={{0,8},{4,12},{8,16},{12,20},{16,24},{20,28},{24,0},{28,4},{1,9},{5... | collective-permute-start | bytes 786440 | tf_op jit(solution)/shard_map/ppermute | solution.py:23
  33.9 17.1 %collective-permute-start.7 = (bf16[1,64,3072]{2,1,0:T(8,128)(2,1)S(1)}, bf16[1,64,3072]{2,1,0:T(8,128)(2,1)S(1)}, u32[]{:S(2)}, u32[]{:S(2)}) collective-permute-start(bf16[1,64,3072]{2,1,0:T(8,128)(2,1)S(1)} %get-tuple-element.29), channel_id=1, source_target_pairs={{0,2},{1,3},{2,0},{3,1},{4,6},{5,7},{6,4},{7,5},{8,10},{9,11},{10,... | collective-permute-start | bytes 1179656 | tf_op jit(solution)/shard_map/ppermute | solution.py:23
  35.3 21.2 %collective-permute-start.6 = (bf16[2,64,1024]{2,1,0:T(8,128)(2,1)S(1)}, bf16[2,64,1024]{2,1,0:T(8,128)(2,1)S(1)}, u32[]{:S(2)}, u32[]{:S(2)}) collective-permute-start(bf16[2,64,1024]{2,1,0:T(8,128)(2,1)S(1)} %get-tuple-element.28), channel_id=1, source_target_pairs={{0,24},{4,28},{8,0},{12,4},{16,8},{20,12},{24,16},{28,20},{1,25},{... | collective-permute-start | bytes 786440 | tf_op jit(solution)/shard_map/ppermute | solution.py:23
  43.5 13.0 %collective-permute-start.5 = (bf16[2,64,1024]{2,1,0:T(8,128)(2,1)S(1)}, bf16[2,64,1024]{2,1,0:T(8,128)(2,1)S(1)}, u32[]{:S(2)}, u32[]{:S(2)}) collective-permute-start(bf16[2,64,1024]{2,1,0:T(8,128)(2,1)S(1)} %shard_map.62.refs_4_), channel_id=1, source_target_pairs={{0,8},{4,12},{8,16},{12,20},{16,24},{20,28},{24,0},{28,4},{1,9},{5... | collective-permute-start | bytes 786440 | tf_op jit(solution)/shard_map/ppermute | solution.py:23
  47.3 10.0 %collective-permute-start.11 = (bf16[2,64,1024]{2,1,0:T(8,128)(2,1)S(1)}, bf16[2,64,1024]{2,1,0:T(8,128)(2,1)S(1)}, u32[]{:S(2)}, u32[]{:S(2)}) collective-permute-start(bf16[2,64,1024]{2,1,0:T(8,128)(2,1)S(1)} %get-tuple-element.31), channel_id=1, source_target_pairs={{0,24},{4,28},{8,0},{12,4},{16,8},{20,12},{24,16},{28,20},{1,25},{... | collective-permute-start | bytes 786440 | tf_op jit(solution)/shard_map/ppermute | solution.py:23
  53.9 6.4 %collective-permute-start.10 = (bf16[1,2,64,1024]{3,2,1,0:T(8,128)(2,1)S(1)}, bf16[1,2,64,1024]{3,2,1,0:T(8,128)(2,1)S(1)}, u32[]{:S(2)}, u32[]{:S(2)}) collective-permute-start(bf16[1,2,64,1024]{3,2,1,0:T(8,128)(2,1)S(1)} %shard_map.64.refs_2_), channel_id=1, source_target_pairs={{0,4},{4,0},{8,12},{12,8},{16,20},{20,16},{24,28},{28,24},{1,5},{5... | collective-permute-start | bytes 786440 | tf_op jit(solution)/shard_map/ppermute | solution.py:28
  55.5 7.8 %collective-permute-start.13 = (bf16[1,64,3072]{2,1,0:T(8,128)(2,1)S(1)}, bf16[1,64,3072]{2,1,0:T(8,128)(2,1)S(1)}, u32[]{:S(2)}, u32[]{:S(2)}) collective-permute-start(bf16[1,64,3072]{2,1,0:T(8,128)(2,1)S(1)} %get-tuple-element.34), channel_id=1, source_target_pairs={{0,2},{1,3},{2,0},{3,1},{4,6},{5,7},{6,4},{7,5},{8,10},{9,11},{10,... | collective-permute-start | bytes 1179656 | tf_op jit(solution)/shard_map/ppermute | solution.py:23
  60.5 14.3 %copy-start.2 = (bf16[256,1024]{1,0:T(8,128)(2,1)S(1)}, bf16[256,1024]{1,0:T(8,128)(2,1)}, u32[]{:S(2)}) copy-start(bf16[256,1024]{1,0:T(8,128)(2,1)} %rhs.1) | copy-start | bytes 1572868
  60.5 14.3 %copy-start.3 = (bf16[1,256,256]{2,1,0:T(8,128)(2,1)S(1)}, bf16[1,256,256]{2,1,0:T(8,128)(2,1)}, u32[]{:S(2)}) copy-start(bf16[1,256,256]{2,1,0:T(8,128)(2,1)} %diag.1) | copy-start | bytes 393220
  60.5 22.5 %collective-permute-start.12 = (f32[2,64,1024]{2,1,0:T(8,128)S(1)}, f32[2,64,1024]{2,1,0:T(8,128)S(1)}, u32[]{:S(2)}, u32[]{:S(2)}) collective-permute-start(f32[2,64,1024]{2,1,0:T(8,128)S(1)} %get-tuple-element.33.refs_5_), channel_id=1, source_target_pairs={{0,1},{1,0},{2,3},{3,2},{4,5},{5,4},{6,7},{7,6},{8,9},{9,8},{10,11... | collective-permute-start | bytes 1572872 | tf_op jit(solution)/shard_map/ppermute | solution.py:54
  60.6 10.5 %collective-permute-start.14 = (bf16[2,64,1024]{2,1,0:T(8,128)(2,1)S(1)}, bf16[2,64,1024]{2,1,0:T(8,128)(2,1)S(1)}, u32[]{:S(2)}, u32[]{:S(2)}) collective-permute-start(bf16[2,64,1024]{2,1,0:T(8,128)(2,1)S(1)} %get-tuple-element.30.refs_3_), channel_id=1, source_target_pairs={{0,8},{4,12},{8,16},{12,20},{16,24},{20,28},{24,0},{28,4},{1,9},{5... | collective-permute-start | bytes 786440 | tf_op jit(solution)/shard_map/ppermute | solution.py:23
  74.7 8.3 %collective-permute-start.15 = (bf16[64,1024]{1,0:T(8,128)(2,1)S(1)}, bf16[64,1024]{1,0:T(8,128)(2,1)S(1)}, u32[]{:S(2)}, u32[]{:S(2)}) collective-permute-start(bf16[64,1024]{1,0:T(8,128)(2,1)S(1)} %shard_map.67), channel_id=1, source_target_pairs={{0,8},{1,9},{2,10},{3,11},{4,12},{5,13},{6,14},{7,15},{8,16},{9,17... | collective-permute-start | bytes 393224 | tf_op jit(solution)/shard_map/ppermute | solution.py:54
  74.8 8.3 %collective-permute-start.16 = (bf16[64,1024]{1,0:T(8,128)(2,1)S(1)}, bf16[64,1024]{1,0:T(8,128)(2,1)S(1)}, u32[]{:S(2)}, u32[]{:S(2)}) collective-permute-start(bf16[64,1024]{1,0:T(8,128)(2,1)S(1)} %shard_map.66.refs_5_), channel_id=1, source_target_pairs={{0,9},{1,8},{2,11},{3,10},{4,13},{5,12},{6,15},{7,14},{8,17},{9,16... | collective-permute-start | bytes 393224 | tf_op jit(solution)/shard_map/ppermute | solution.py:54

commit v3 on v2

--- a/solution.py
+++ b/solution.py
@@ -132,24 +132,26 @@
     y35 = across(s35, "rhs")
     y0 = across(s0, "rhs")
     y1 = across(s1, "rhs")
-
-    def near(left_ref, sol, weights, *refs):
-        give, own = refs[-2:]
-        left = left_ref[...].reshape(hops * quarter, depth)
+    taken, order = [s24, s35, s0, s1], (2, 4, 3, 5, 0, 1)
+
+    def near(*refs):
+        lefts, (sol, weights), (give, own) = refs[:len(taken)], refs[len(taken):len(taken) + 2], refs[-2:]
+        left = jnp.concatenate([r[i] for r in lefts for i in range(r.shape[0])])
         for cut in cuts:
             total = jnp.dot(left, sol[:, cut], preferred_element_type=F32)
-            for i in range(len(gives)):
-                g = total[gives[i] * quarter:(gives[i] + 1) * quarter]
-                give[i, :, cut] = (g * weights[0, gives[i]].astype(F32)).astype(BF16)
-                o = total[owns[i] * quarter:(owns[i] + 1) * quarter]
-                own[i, :, cut] = o * weights[0, owns[i]].astype(F32)
+            for at, k in enumerate(order):
+                term = total[at * quarter:(at + 1) * quarter] * weights[0, k].astype(F32)
+                if k in gives:
+                    give[gives.index(k), :, cut] = term.astype(BF16)
+                else:
+                    own[owns.index(k), :, cut] = term
 
     sols = [solution, *others]
     near_own, got_near = [], []
     token = s35
     for sol in sols:
         give, own = call(near, [pinned(3, quarter, cols), pinned(3, quarter, cols, dtype=F32)],
-                         [VMEM, VMEM, SMEM, ANY], [tiles, sol, tile_list, token],
+                         [VMEM] * (len(taken) + 1) + [SMEM, ANY], [*taken, sol, tile_list, token],
                          flops=2 * hops * quarter * depth * cols)
         got_near.append(pair_swap(give, "col"))
         near_own.append(own)
@@ -217,59 +219,100 @@
     d2f_in = shift(d2f, "col", 2)
     d3f_in = shift(d3f, "col", 6)
 
-    last_give, = products(y0, (0,), store, [pinned(1, *strip)], [], [d2f])
+    def near3(d3, *refs):
+        gots, sums = refs[:half], refs[-1]
+        is_odd = on_odd()
+        for part, got in enumerate(gots):
+            sums[part] = d3[part].astype(F32) + jnp.where(is_odd, got[2].astype(F32), 0.0)
+
+    wide_one = pinned(*strip, dtype=F32)
+    near_sum, = call(near3, [wide_one], [VMEM] * (1 + half) + [ANY], [d3n_in, *got_near, d2f])
+
+    last_give, = products(y0, (0,), store, [pinned(1, *strip)], [], [near_sum])
     got_last = pair_swap(last_give, "col")
 
-    def collect(d1, d3, gl, d3far, *refs):
-        gots, outs = refs[:half], refs[-half:]
-        is_odd = on_odd()
-        for part, (got, out) in enumerate(zip(gots, outs)):
-            upper = d1[part].astype(F32) + d3[part].astype(F32)
-            out[0] = upper + jnp.where(is_odd, got[2].astype(F32), 0.0)
-            out[1] = d3far[part].astype(F32) + jnp.where(is_odd, gl[0, part].astype(F32), 0.0)
-
-    sums = call(collect, [pinned(2, quarter, cols, dtype=F32)] * half, [VMEM] * (4 + half) + [ANY],
-                [d1n_in, d3n_in, got_last, d3f_in, *got_near, last_give])
+    def near_all(d1, sums, d2far, gf, _, total, pre):
+        is_odd = on_odd()
+        for part in range(half):
+            total[part] = d1[part].astype(F32) + sums[part]
+            pre[part] = d2far[part].astype(F32) + jnp.where(is_odd, gf[0, part].astype(F32), 0.0)
+
+    near_total, pre = call(near_all, [wide_one, wide_one], [VMEM] * 4 + [ANY],
+                           [d1n_in, near_sum, d2f_in, got_far, last_give])
+
+    def plain(out, more, is_odd, i, part, cut, total):
+        out[0][:, cut] = total
+
+    raw, token = [], pre
+    for part in range(1, half):
+        term, = products(y1, (1,), plain, [pinned(quarter, cols, dtype=F32)], [], [token], [part])
+        raw.append(term)
+        token = term
+
+    def collect(total, pre, gl, d3far, *refs):
+        raws, refs = refs[:half - 1], refs[half:]
+        pre0, sums, lasts = refs[0], refs[1:1 + half], refs[1 + half:]
+        is_odd = on_odd()
+        for part in range(half):
+            r0 = gl[0, part].astype(F32)
+            sums[part][0] = total[part]
+            sums[part][1] = d3far[part].astype(F32) + jnp.where(is_odd, r0, 0.0)
+            chained = pre[part] + jnp.where(is_odd, 0.0, r0)
+            if part:
+                lasts[part - 1][...] = (raws[part - 1][...] + chained).astype(BF16)
+            else:
+                pre0[...] = chained
+
+    flat = pinned(quarter, cols, dtype=F32)
+    pre0, *outs = call(
+        collect, [flat] + [pinned(2, quarter, cols, dtype=F32)] * half + [pinned(quarter, cols)] * (half - 1),
+        [VMEM] * (4 + half - 1) + [ANY], [near_total, pre, got_last, d3f_in, *raw, token])
+    sums, lasts = outs[:half], outs[half:]
     sums_in = to_columns(sums, 0)
 
     def far1(out, more, is_odd, i, part, cut, total):
-        got, got0, chained = more
-        r = jnp.where(is_odd, got[0, part, :, cut].astype(F32), got0[0, part, :, cut].astype(F32))
-        out[0][:, cut] = (total + r + chained[part, :, cut].astype(F32)).astype(BF16)
-
-    d1f = [None] * half
-    token = sums[-1]
-    for part in list(range(1, half)) + [0]:
-        d1f[part], = products(y1, (1,), far1, [pinned(quarter, cols)], [got_far, got_last, d2f_in], [token], [part])
-        token = d1f[part]
-    d1f_in = to_columns(d1f, 2)
+        out[0][:, cut] = (total + more[0][:, cut]).astype(BF16)
+
+    own_last, = products(y1, (1,), far1, [pinned(quarter, cols)], [pre0], [], [0])
+    last_in = to_columns([own_last, *lasts], 2)
+
+    places = [(0, j) for j in range(half)] + [(1, j) for j in range(1, half)] + [(1, 0)]
 
     def arrange(rhs, diag, _, rhs_out, diag_out):
         me = lax.axis_index("rhs")
         upper, mine = lax.div(me, half), lax.rem(me, half)
         column = lax.broadcasted_iota(jnp.int32, (rows, rows), 1)
         source = column
-        for s in range(2):
-            for j in range(half):
-                at = (s * half + j) * quarter
-                block = lax.rem(upper + s, 2) * half + lax.rem(mine + half - j, half)
-                start = pl.multiple_of(block * quarter, quarter)
-                rhs_out[at:at + quarter] = rhs[pl.ds(start, quarter)]
-                source = jnp.where((column >= at) & (column < at + quarter), column - at + start, source)
+        for slot, (s, j) in enumerate(places):
+            at = slot * quarter
+            block = lax.rem(upper + s, 2) * half + lax.rem(mine + half - j, half)
+            start = pl.multiple_of(block * quarter, quarter)
+            rhs_out[at:at + quarter] = rhs[pl.ds(start, quarter)]
+            source = jnp.where((column >= at) & (column < at + quarter), column - at + start, source)
         pick = (lax.broadcasted_iota(jnp.int32, (rows, rows), 0) == source).astype(BF16)
         diag_out[...] = jnp.dot(diag[0], pick, preferred_element_type=F32).astype(BF16)
 
     rhs_local, diag_local = call(arrange, [pinned(rows, cols), pinned(rows, rows)], [VMEM, VMEM, ANY],
                                  [rhs_block, diag_inverse, near_own[-1]], flops=2 * rows * rows * rows)
 
-    def final(rhs, diag, *refs):
-        acc, last, out = refs[:half], refs[half:2 * half], refs[-1]
-        total = jnp.concatenate([a[0] for a in acc] + [a[1] + l[...].astype(F32) for a, l in zip(acc, last)])
-        remaining = (rhs[...].astype(F32) - total).astype(BF16)
-        out[...] = jnp.dot(diag[...], remaining, preferred_element_type=F32).astype(BF16)
-
-    return call(final, [jax.ShapeDtypeStruct((rows, cols), BF16)], [VMEM] * (2 + 2 * half),
-                [rhs_local, diag_local, *sums_in, *d1f_in], flops=2 * rows * rows * cols)[0]
+    early = rows - quarter
+
+    def most(rhs, diag, *refs):
+        acc, last, out = refs[:half], refs[half:2 * half - 1], refs[-1]
+        total = jnp.concatenate([a[0] for a in acc] + [a[1] + l[...].astype(F32) for a, l in zip(acc[1:], last)])
+        remaining = (rhs[:early].astype(F32) - total).astype(BF16)
+        out[...] = jnp.dot(diag[:, :early], remaining, preferred_element_type=F32)
+
+    partial, = call(most, [pinned(rows, cols, dtype=F32)], [VMEM] * (2 + 2 * half - 1) + [ANY],
+                    [rhs_local, diag_local, *sums_in, *last_in[1:], own_last], flops=2 * rows * early * cols)
+
+    def final(rhs, diag, acc, last, part, out):
+        total = acc[1] + last[...].astype(F32)
+        remaining = (rhs[early:].astype(F32) - total).astype(BF16)
+        out[...] = (part[...] + jnp.dot(diag[:, early:], remaining, preferred_element_type=F32)).astype(BF16)
+
+    return call(final, [jax.ShapeDtypeStruct((rows, cols), BF16)], [VMEM] * 5,
+                [rhs_local, diag_local, sums_in[0], last_in[0], partial], flops=2 * rows * quarter * cols)[0]
 
 
 def solution(mesh):

time: 85.1 us -> 74.3 us (0.87)
  waiting for transfers between devices: 38.3 us -> 25.3 us
  starting transfers between devices: 21.5 us -> 25.7 us
  local copies, waits for them, and re-layouts: 1.69 us -> 0.02 us
    ppermute x9, waiting for transfers between devices: 22.4 us -> 14.7 us  [shift(): lax.ppermute(block, axis, [(i, (i + distance) % size) for i in range(size)])]
    ppermute x4, waiting for transfers between devices: 7.88 us -> 3.87 us  [pair_swap(): return lax.ppermute(block, axis, [(i, i ^ 1) for i in range(size)])]
    ppermute x3, starting transfers between devices: 0.19 us -> 1.89 us  [to_columns(): lax.ppermute(block, ('col', 'rhs'), route)]
    unnamed x10 -> x8, local copies, waits for them, and re-layouts: 1.69 us -> 0.02 us
    ppermute x3, waiting for transfers between devices: 7.97 us -> 6.72 us  [to_columns(): lax.ppermute(block, ('col', 'rhs'), route)]
    ppermute x4, starting transfers between devices: 5.78 us -> 7.03 us  [pair_swap(): return lax.ppermute(block, axis, [(i, i ^ 1) for i in range(size)])]
    ppermute x9, starting transfers between devices: 15.1 us -> 16.4 us  [shift(): lax.ppermute(block, axis, [(i, (i + distance) % size) for i in range(size)])]
    pallas_call x14 -> x17, Pallas kernels: 22.6 us -> 22.9 us  [call(): pl.pallas_call(body, out_shape=outs, in_specs=specs, out_specs=out_specs...]
  transfers between devices with their start and end apart: 17 -> 17, of which waited for: 9 -> 7; matrix products, arithmetic and copies ran while one was open for 0% -> 0% of each run, Pallas kernels for 25% -> 29%
where the time goes in v3:
time: 74.3 us; the launch traced here: 74.2 us
  starting transfers between devices  25.7 us (35%)
  waiting for transfers between devices  25.3 us (34%)
  Pallas kernels  22.9 us (31%)
    pallas_call x17, Pallas kernels, call(): pl.pallas_call(body, out_shape=outs, in_specs=specs, out_specs=out_specs...  22.9 us
    ppermute x9, starting transfers between devices, shift(): lax.ppermute(block, axis, [(i, (i + distance) % size) for i in range(size)])  16.4 us
    ppermute x9, waiting for transfers between devices, shift(): lax.ppermute(block, axis, [(i, (i + distance) % size) for i in range(size)])  14.7 us
    ppermute x4, starting transfers between devices, pair_swap(): return lax.ppermute(block, axis, [(i, i ^ 1) for i in range(size)])  7.03 us
    ppermute x3, waiting for transfers between devices, to_columns(): lax.ppermute(block, ('col', 'rhs'), route)  6.72 us
    ppermute x4, waiting for transfers between devices, pair_swap(): return lax.ppermute(block, axis, [(i, i ^ 1) for i in range(size)])  3.87 us
    ppermute x3, starting transfers between devices, to_columns(): lax.ppermute(block, ('col', 'rhs'), route)  1.89 us
  transfers between devices with their start and end apart: 17, of which 7 were waited for; matrix products, arithmetic and copies ran while one was open for 0% of the time, Pallas kernels for 29%

profile of v3, /device:TPU:0, one launch (start us, length us, event | category | flops | bytes accessed | tf_op | source)
XLA Modules:
  0.0 74.2 jit_solution(1326065924919336909)
XLA Ops:
  0.0 0.0 copy-start
  0.0 0.0 copy-start.3
  0.0 0.5 collective-permute-start
  0.5 1.5 %shard_map.55.refs_1_.refs_0_ = bf16[2,64,3072]{2,1,0:T(8,128)(2,1)S(1)} custom-call(bf16[6,64,3072]{2,1,0:T(8,128)(2,1)} %bitcast.1), custom_call_target="tpu_custom_call" | custom-call | bytes 2359296 | tf_op jit(solution)/shard_map/pallas_call | solution.py:64
  1.9 2.5 %collective-permute-start.3 = (bf16[2,64,3072]{2,1,0:T(8,128)(2,1)S(1)}, bf16[2,64,3072]{2,1,0:T(8,128)(2,1)S(1)}, u32[]{:S(2)}, u32[]{:S(2)}) collective-permute-start(bf16[2,64,3072]{2,1,0:T(8,128)(2,1)S(1)} %shard_map.55.refs_1_.refs_0_), channel_id=1, source_target_pairs={{0,2},{1,3},{2,0},{3,1},{4,6},{5,7},{6,4},{7,5},{8,10},{9,11},{10,... | collective-permute-start | bytes 2359304 | tf_op jit(solution)/shard_map/ppermute | solution.py:23
  4.5 1.6 %shard_map.56 = (bf16[2,64,3072]{2,1,0:T(8,128)(2,1)S(1)}, bf16[1,64,3072]{2,1,0:T(8,128)(2,1)S(1)}, bf16[1,64,3072]{2,1,0:T(8,128)(2,1)S(1)}) custom-call(bf16[6,64,3072]{2,1,0:T(8,128)(2,1)} %bitcast.2, bf16[2,64,3072]{2,1,0:T(8,128)(2,1)S(1)} %shard_map.55.refs_1_.refs_0_), custom_call_target="tpu_custom_call" | custom-call | bytes 3145728 | tf_op jit(solution)/shard_map/pallas_call | solution.py:64
  6.1 0.7 collective-permute-start.7
  6.8 0.0 copy-done
  6.8 0.0 copy-done.3
  6.8 3.2 %shard_map.57 = (bf16[3,64,1024]{2,1,0:T(8,128)(2,1)S(1)}, f32[3,64,1024]{2,1,0:T(8,128)S(1)}) custom-call(bf16[2,64,3072]{2,1,0:T(8,128)(2,1)S(1)} %shard_map.55.refs_1_.refs_0_, bf16[2,64,3072]{2,1,0:T(8,128)(2,1)S(1)} %get-tuple-element.24.refs_1_.refs_6_, bf16[1,64,3072]{2,1,0:T(8,128)(2,1)S(1)} %get-tuple-element.25.refs_2_, ...), custom_call_target="tpu_custom_call" | custom-call | flops 2415919104 | bytes 9437208 | tf_op jit(solution)/shard_map/pallas_call | solution.py:64
  10.0 1.6 %collective-permute-start.1 = (bf16[3,64,1024]{2,1,0:T(8,128)(2,1)S(1)}, bf16[3,64,1024]{2,1,0:T(8,128)(2,1)S(1)}, u32[]{:S(2)}, u32[]{:S(2)}) collective-permute-start(bf16[3,64,1024]{2,1,0:T(8,128)(2,1)S(1)} %get-tuple-element.31), channel_id=1, source_target_pairs={{0,4},{4,0},{8,12},{12,8},{16,20},{20,16},{24,28},{28,24},{1,5},{5... | collective-permute-start | bytes 1179656 | tf_op jit(solution)/shard_map/ppermute | solution.py:28
  11.5 0.0 collective-permute-done.refs_4_.refs_1_.refs_0_
  11.5 3.2 %shard_map.58 = (bf16[3,64,1024]{2,1,0:T(8,128)(2,1)S(1)}, f32[3,64,1024]{2,1,0:T(8,128)S(1)}) custom-call(bf16[2,64,3072]{2,1,0:T(8,128)(2,1)S(1)} %shard_map.55.refs_1_.refs_0_, bf16[2,64,3072]{2,1,0:T(8,128)(2,1)S(1)} %get-tuple-element.24.refs_1_.refs_6_, bf16[1,64,3072]{2,1,0:T(8,128)(2,1)S(1)} %get-tuple-element.25.refs_2_, ...), custom_call_target="tpu_custom_call" | custom-call | flops 2415919104 | bytes 9437208 | tf_op jit(solution)/shard_map/pallas_call | solution.py:64
  14.7 1.9 %collective-permute-start.2 = (bf16[3,64,1024]{2,1,0:T(8,128)(2,1)S(1)}, bf16[3,64,1024]{2,1,0:T(8,128)(2,1)S(1)}, u32[]{:S(2)}, u32[]{:S(2)}) collective-permute-start(bf16[3,64,1024]{2,1,0:T(8,128)(2,1)S(1)} %get-tuple-element.32), channel_id=1, source_target_pairs={{0,4},{4,0},{8,12},{12,8},{16,20},{20,16},{24,28},{28,24},{1,5},{5... | collective-permute-start | bytes 1179656 | tf_op jit(solution)/shard_map/ppermute | solution.py:28
  16.5 6.3 %collective-permute-done.3.far_ref = bf16[2,64,3072]{2,1,0:T(8,128)(2,1)S(1)} collective-permute-done((bf16[2,64,3072]{2,1,0:T(8,128)(2,1)S(1)}, bf16[2,64,3072]{2,1,0:T(8,128)(2,1)S(1)}, u32[]{:S(2)}, u32[]{:S(2)}) %collective-permute-start.3) | collective-permute-done | bytes 786464 | tf_op jit(solution)/shard_map/ppermute | solution.py:23
  22.9 2.3 %shard_map.60.refs_4_ = bf16[2,2,64,1024]{3,2,1,0:T(8,128)(2,1)S(1)} custom-call(bf16[2,64,3072]{2,1,0:T(8,128)(2,1)S(1)} %collective-permute-done.3.far_ref, bf16[3072,1024]{1,0:T(8,128)(2,1)S(1)} %copy-done, bf16[3072,1024]{1,0:T(8,128)(2,1)S(1)} %collective-permute-done.refs_4_.refs_1_.refs_0_, s32[1,6]{1,0:T(1,128)S(1)} %copy-done.3, ...), custom_call_target="tpu_custom_call" | custom-call | flops 1610612736 | bytes 14155800 | tf_op jit(solution)/shard_map/pallas_call | solution.py:64
  25.2 2.1 %collective-permute-start.8 = (bf16[2,2,64,1024]{3,2,1,0:T(8,128)(2,1)S(1)}, bf16[2,2,64,1024]{3,2,1,0:T(8,128)(2,1)S(1)}, u32[]{:S(2)}, u32[]{:S(2)}) collective-permute-start(bf16[2,2,64,1024]{3,2,1,0:T(8,128)(2,1)S(1)} %shard_map.60.refs_4_), channel_id=1, source_target_pairs={{0,4},{4,0},{8,12},{12,8},{16,20},{20,16},{24,28},{28,24},{1,5},{5... | collective-permute-start | bytes 1572872 | tf_op jit(solution)/shard_map/ppermute | solution.py:28
  27.3 0.0 collective-permute-done.1.refs_2_.refs_0_
  27.3 3.2 %collective-permute-done.2.refs_3_.refs_1_ = bf16[3,64,1024]{2,1,0:T(8,128)(2,1)S(1)} collective-permute-done((bf16[3,64,1024]{2,1,0:T(8,128)(2,1)S(1)}, bf16[3,64,1024]{2,1,0:T(8,128)(2,1)S(1)}, u32[]{:S(2)}, u32[]{:S(2)}) %collective-permute-start.2) | collective-permute-done | bytes 393248 | tf_op jit(solution)/shard_map/ppermute | solution.py:28
  30.5 0.2 shard_map.61
  30.6 1.6 %collective-permute-start.4 = (bf16[2,64,1024]{2,1,0:T(8,128)(2,1)S(1)}, bf16[2,64,1024]{2,1,0:T(8,128)(2,1)S(1)}, u32[]{:S(2)}, u32[]{:S(2)}) collective-permute-start(bf16[2,64,1024]{2,1,0:T(8,128)(2,1)S(1)} %get-tuple-element.33), channel_id=1, source_target_pairs={{0,8},{4,12},{8,16},{12,20},{16,24},{20,28},{24,0},{28,4},{1,9},{5... | collective-permute-start | bytes 786440 | tf_op jit(solution)/shard_map/ppermute | solution.py:23
  32.2 1.4 %collective-permute-start.10 = (bf16[1,64,3072]{2,1,0:T(8,128)(2,1)S(1)}, bf16[1,64,3072]{2,1,0:T(8,128)(2,1)S(1)}, u32[]{:S(2)}, u32[]{:S(2)}) collective-permute-start(bf16[1,64,3072]{2,1,0:T(8,128)(2,1)S(1)} %get-tuple-element.25.refs_2_), channel_id=1, source_target_pairs={{0,2},{1,3},{2,0},{3,1},{4,6},{5,7},{6,4},{7,5},{8,10},{9,11},{10,... | collective-permute-start | bytes 1179656 | tf_op jit(solution)/shard_map/ppermute | solution.py:23
  33.6 2.2 %collective-permute-start.6 = (bf16[2,64,1024]{2,1,0:T(8,128)(2,1)S(1)}, bf16[2,64,1024]{2,1,0:T(8,128)(2,1)S(1)}, u32[]{:S(2)}, u32[]{:S(2)}) collective-permute-start(bf16[2,64,1024]{2,1,0:T(8,128)(2,1)S(1)} %get-tuple-element.34), channel_id=1, source_target_pairs={{0,24},{4,28},{8,0},{12,4},{16,8},{20,12},{24,16},{28,20},{1,25},{... | collective-permute-start | bytes 786440 | tf_op jit(solution)/shard_map/ppermute | solution.py:23
  35.9 5.8 %collective-permute-done.4.chained = bf16[2,64,1024]{2,1,0:T(8,128)(2,1)S(1)} collective-permute-done((bf16[2,64,1024]{2,1,0:T(8,128)(2,1)S(1)}, bf16[2,64,1024]{2,1,0:T(8,128)(2,1)S(1)}, u32[]{:S(2)}, u32[]{:S(2)}) %collective-permute-start.4) | collective-permute-done | bytes 262176 | tf_op jit(solution)/shard_map/ppermute | solution.py:23
  41.6 1.5 %collective-permute-start.13 = (bf16[1,64,3072]{2,1,0:T(8,128)(2,1)S(1)}, bf16[1,64,3072]{2,1,0:T(8,128)(2,1)S(1)}, u32[]{:S(2)}, u32[]{:S(2)}) collective-permute-start(bf16[1,64,3072]{2,1,0:T(8,128)(2,1)S(1)} %get-tuple-element.26.refs_3_), channel_id=1, source_target_pairs={{0,2},{1,3},{2,0},{3,1},{4,6},{5,7},{6,4},{7,5},{8,10},{9,11},{10,... | collective-permute-start | bytes 1179656 | tf_op jit(solution)/shard_map/ppermute | solution.py:23
  43.1 0.1 shard_map.62.refs_4_
  43.2 0.0 collective-permute-done.7.far_ref
  43.2 0.1 collective-permute-start.5
  43.3 0.0 collective-permute-done.8.refs_3_.gf
  43.3 2.5 %shard_map.63 = (bf16[2,64,1024]{2,1,0:T(8,128)(2,1)S(1)}, bf16[2,64,1024]{2,1,0:T(8,128)(2,1)S(1)}) custom-call(bf16[2,64,3072]{2,1,0:T(8,128)(2,1)S(1)} %collective-permute-done.7.far_ref, bf16[3072,1024]{1,0:T(8,128)(2,1)S(1)} %copy-done, bf16[3072,1024]{1,0:T(8,128)(2,1)S(1)} %collective-permute-done.refs_4_.refs_1_.refs_0_, s32[1,6]{1,0:T(1,128)S(1)} %copy-done.3, ...), custom_call_target="tpu_custom_call" | custom-call | flops 1610612736 | bytes 14155800 | tf_op jit(solution)/shard_map/pallas_call | solution.py:64
  45.8 4.0 %collective-permute-start.9 = (bf16[2,64,1024]{2,1,0:T(8,128)(2,1)S(1)}, bf16[2,64,1024]{2,1,0:T(8,128)(2,1)S(1)}, u32[]{:S(2)}, u32[]{:S(2)}) collective-permute-start(bf16[2,64,1024]{2,1,0:T(8,128)(2,1)S(1)} %get-tuple-element.35.refs_2_), channel_id=1, source_target_pairs={{0,8},{4,12},{8,16},{12,20},{16,24},{20,28},{24,0},{28,4},{1,9},{5... | collective-permute-start | bytes 786440 | tf_op jit(solution)/shard_map/ppermute | solution.py:23
  49.7 0.0 collective-permute-done.6.d3
  49.7 0.1 shard_map.64.refs_3_.sums
  49.8 0.0 collective-permute-done.10.far_ref
  49.8 2.9 %shard_map.65._ = bf16[1,2,64,1024]{3,2,1,0:T(8,128)(2,1)S(1)} custom-call(bf16[1,64,3072]{2,1,0:T(8,128)(2,1)S(1)} %collective-permute-done.10.far_ref, bf16[3072,1024]{1,0:T(8,128)(2,1)S(1)} %copy-done, bf16[3072,1024]{1,0:T(8,128)(2,1)S(1)} %collective-permute-done.refs_4_.refs_1_.refs_0_, s32[1,6]{1,0:T(1,128)S(1)} %copy-done.3, ...), custom_call_target="tpu_custom_call" | custom-call | flops 805306368 | bytes 13500440 | tf_op jit(solution)/shard_map/pallas_call | solution.py:64
  52.7 1.6 %collective-permute-start.11 = (bf16[1,2,64,1024]{3,2,1,0:T(8,128)(2,1)S(1)}, bf16[1,2,64,1024]{3,2,1,0:T(8,128)(2,1)S(1)}, u32[]{:S(2)}, u32[]{:S(2)}) collective-permute-start(bf16[1,2,64,1024]{3,2,1,0:T(8,128)(2,1)S(1)} %shard_map.65._), channel_id=1, source_target_pairs={{0,4},{4,0},{8,12},{12,8},{16,20},{20,16},{24,28},{28,24},{1,5},{5... | collective-permute-start | bytes 786440 | tf_op jit(solution)/shard_map/ppermute | solution.py:28
  54.3 2.4 %collective-permute-start.12 = (bf16[2,64,1024]{2,1,0:T(8,128)(2,1)S(1)}, bf16[2,64,1024]{2,1,0:T(8,128)(2,1)S(1)}, u32[]{:S(2)}, u32[]{:S(2)}) collective-permute-start(bf16[2,64,1024]{2,1,0:T(8,128)(2,1)S(1)} %get-tuple-element.38), channel_id=1, source_target_pairs={{0,24},{4,28},{8,0},{12,4},{16,8},{20,12},{24,16},{28,20},{1,25},{... | collective-permute-start | bytes 786440 | tf_op jit(solution)/shard_map/ppermute | solution.py:23
  56.7 0.0 collective-permute-done.9.d2far
  56.7 0.0 collective-permute-done.5.d1
  56.7 0.1 shard_map.66
  56.8 0.0 collective-permute-done.13.far_ref
  56.8 1.8 %shard_map.67.refs_0_.refs_1_ = f32[64,1024]{1,0:T(8,128)S(1)} custom-call(bf16[1,64,3072]{2,1,0:T(8,128)(2,1)S(1)} %collective-permute-done.13.far_ref, bf16[3072,1024]{1,0:T(8,128)(2,1)S(1)} %collective-permute-done.refs_4_.refs_1_.refs_0_, s32[1,6]{1,0:T(1,128)S(1)} %copy-done.3, f32[2,64,1024]{2,1,0:T(8,128)S(1)} %get-tuple-element.37.refs_2_.pre), custom_call_target="tpu_custom_call" | custom-call | flops 402653184 | bytes 7208984 | tf_op jit(solution)/shard_map/pallas_call | solution.py:64
  58.6 0.0 copy-start.1
  58.6 0.0 copy-start.2
  58.6 0.7 collective-permute-done.11.gl
  59.3 2.6 %collective-permute-done.12.d3far = bf16[2,64,1024]{2,1,0:T(8,128)(2,1)S(1)} collective-permute-done((bf16[2,64,1024]{2,1,0:T(8,128)(2,1)S(1)}, bf16[2,64,1024]{2,1,0:T(8,128)(2,1)S(1)}, u32[]{:S(2)}, u32[]{:S(2)}) %collective-permute-start.12) | collective-permute-done | bytes 262176 | tf_op jit(solution)/shard_map/ppermute | solution.py:23
  61.9 0.2 shard_map.68
  62.1 0.1 collective-permute-start.15
  62.2 0.7 collective-permute-start.16
  62.8 1.8 %shard_map.69.refs_3_ = bf16[64,1024]{1,0:T(8,128)(2,1)S(1)} custom-call(bf16[1,64,3072]{2,1,0:T(8,128)(2,1)S(1)} %collective-permute-done.13.far_ref, bf16[3072,1024]{1,0:T(8,128)(2,1)S(1)} %copy-done, s32[1,6]{1,0:T(1,128)S(1)} %copy-done.3, f32[64,1024]{1,0:T(8,128)S(1)} %get-tuple-element.40.refs_2_), custom_call_target="tpu_custom_call" | custom-call | flops 402653184 | bytes 6946840 | tf_op jit(solution)/shard_map/pallas_call | solution.py:64
  64.6 1.2 %collective-permute-start.14 = (bf16[64,1024]{1,0:T(8,128)(2,1)S(1)}, bf16[64,1024]{1,0:T(8,128)(2,1)S(1)}, u32[]{:S(2)}, u32[]{:S(2)}) collective-permute-start(bf16[64,1024]{1,0:T(8,128)(2,1)S(1)} %shard_map.69.refs_3_), channel_id=1, source_target_pairs={{0,8},{1,9},{2,10},{3,11},{4,12},{5,13},{6,14},{7,15},{8,16},{9,17... | collective-permute-start | bytes 393224 | tf_op jit(solution)/shard_map/ppermute | solution.py:54
  65.8 0.0 copy-done.1
  65.8 0.0 copy-done.2
  65.8 0.2 shard_map.59
  66.0 4.0 %collective-permute-done.16.refs_2_ = bf16[64,1024]{1,0:T(8,128)(2,1)S(1)} collective-permute-done((bf16[64,1024]{1,0:T(8,128)(2,1)S(1)}, bf16[64,1024]{1,0:T(8,128)(2,1)S(1)}, u32[]{:S(2)}, u32[]{:S(2)}) %collective-permute-start.16) | collective-permute-done | bytes 131104 | tf_op jit(solution)/shard_map/ppermute | solution.py:54
  70.0 0.0 collective-permute-done.15.refs_1_
  70.0 0.3 shard_map.70.part
  70.3 2.7 %collective-permute-done.14.last = bf16[64,1024]{1,0:T(8,128)(2,1)S(1)} collective-permute-done((bf16[64,1024]{1,0:T(8,128)(2,1)S(1)}, bf16[64,1024]{1,0:T(8,128)(2,1)S(1)}, u32[]{:S(2)}, u32[]{:S(2)}) %collective-permute-start.14) | collective-permute-done | bytes 131104 | tf_op jit(solution)/shard_map/ppermute | solution.py:54
  73.1 1.1 %shard_map.71 = bf16[256,1024]{1,0:T(8,128)(2,1)} custom-call(bf16[256,1024]{1,0:T(8,128)(2,1)S(1)} %get-tuple-element.29.rhs, bf16[256,256]{1,0:T(8,128)(2,1)S(1)} %get-tuple-element.30.diag, f32[2,64,1024]{2,1,0:T(8,128)S(1)} %get-tuple-element.39.refs_0_.acc, bf16[64,1024]{1,0:T(8,128)(2,1)S(1)} %collective-permute-done.14.last, ...), custom_call_target="tpu_custom_call" | custom-call | flops 33554432 | bytes 2359296 | tf_op jit(solution)/shard_map/pallas_call | solution.py:64
Async XLA Ops:
  0.0 6.8 %copy-start = (bf16[3072,1024]{1,0:T(8,128)(2,1)S(1)}, bf16[3072,1024]{1,0:T(8,128)(2,1)}, u32[]{:S(2)}) copy-start(bf16[3072,1024]{1,0:T(8,128)(2,1)} %refs_0_.7) | copy-start | bytes 18874372
  0.0 6.8 %copy-start.3 = (s32[1,6]{1,0:T(1,128)S(1)}, s32[1,6]{1,0:T(1,128)}, u32[]{:S(2)}) copy-start(s32[1,6]{1,0:T(1,128)} %refs_1_.3) | copy-start | bytes 76
  0.0 11.5 %collective-permute-start = (bf16[3072,1024]{1,0:T(8,128)(2,1)}, bf16[3072,1024]{1,0:T(8,128)(2,1)S(1)}, u32[]{:S(2)}, u32[]{:S(2)}) collective-permute-start(bf16[3072,1024]{1,0:T(8,128)(2,1)} %refs_0_.7), channel_id=1, source_target_pairs={{1,0},{0,1},{3,2},{2,3},{5,4},{4,5},{7,6},{6,7},{9,8},{8,9},{11,10... | collective-permute-start | bytes 18874376 | tf_op jit(solution)/shard_map/ppermute | solution.py:44
  1.9 20.9 %collective-permute-start.3 = (bf16[2,64,3072]{2,1,0:T(8,128)(2,1)S(1)}, bf16[2,64,3072]{2,1,0:T(8,128)(2,1)S(1)}, u32[]{:S(2)}, u32[]{:S(2)}) collective-permute-start(bf16[2,64,3072]{2,1,0:T(8,128)(2,1)S(1)} %shard_map.55.refs_1_.refs_0_), channel_id=1, source_target_pairs={{0,2},{1,3},{2,0},{3,1},{4,6},{5,7},{6,4},{7,5},{8,10},{9,11},{10,... | collective-permute-start | bytes 2359304 | tf_op jit(solution)/shard_map/ppermute | solution.py:23
  6.1 37.1 %collective-permute-start.7 = (bf16[2,64,3072]{2,1,0:T(8,128)(2,1)S(1)}, bf16[2,64,3072]{2,1,0:T(8,128)(2,1)S(1)}, u32[]{:S(2)}, u32[]{:S(2)}) collective-permute-start(bf16[2,64,3072]{2,1,0:T(8,128)(2,1)S(1)} %get-tuple-element.24.refs_1_.refs_6_), channel_id=1, source_target_pairs={{0,2},{1,3},{2,0},{3,1},{4,6},{5,7},{6,4},{7,5},{8,10},{9,11},{10,... | collective-permute-start | bytes 2359304 | tf_op jit(solution)/shard_map/ppermute | solution.py:23
  10.0 17.3 %collective-permute-start.1 = (bf16[3,64,1024]{2,1,0:T(8,128)(2,1)S(1)}, bf16[3,64,1024]{2,1,0:T(8,128)(2,1)S(1)}, u32[]{:S(2)}, u32[]{:S(2)}) collective-permute-start(bf16[3,64,1024]{2,1,0:T(8,128)(2,1)S(1)} %get-tuple-element.31), channel_id=1, source_target_pairs={{0,4},{4,0},{8,12},{12,8},{16,20},{20,16},{24,28},{28,24},{1,5},{5... | collective-permute-start | bytes 1179656 | tf_op jit(solution)/shard_map/ppermute | solution.py:28
  14.7 15.8 %collective-permute-start.2 = (bf16[3,64,1024]{2,1,0:T(8,128)(2,1)S(1)}, bf16[3,64,1024]{2,1,0:T(8,128)(2,1)S(1)}, u32[]{:S(2)}, u32[]{:S(2)}) collective-permute-start(bf16[3,64,1024]{2,1,0:T(8,128)(2,1)S(1)} %get-tuple-element.32), channel_id=1, source_target_pairs={{0,4},{4,0},{8,12},{12,8},{16,20},{20,16},{24,28},{28,24},{1,5},{5... | collective-permute-start | bytes 1179656 | tf_op jit(solution)/shard_map/ppermute | solution.py:28
  25.2 18.1 %collective-permute-start.8 = (bf16[2,2,64,1024]{3,2,1,0:T(8,128)(2,1)S(1)}, bf16[2,2,64,1024]{3,2,1,0:T(8,128)(2,1)S(1)}, u32[]{:S(2)}, u32[]{:S(2)}) collective-permute-start(bf16[2,2,64,1024]{3,2,1,0:T(8,128)(2,1)S(1)} %shard_map.60.refs_4_), channel_id=1, source_target_pairs={{0,4},{4,0},{8,12},{12,8},{16,20},{20,16},{24,28},{28,24},{1,5},{5... | collective-permute-start | bytes 1572872 | tf_op jit(solution)/shard_map/ppermute | solution.py:28
  30.6 11.0 %collective-permute-start.4 = (bf16[2,64,1024]{2,1,0:T(8,128)(2,1)S(1)}, bf16[2,64,1024]{2,1,0:T(8,128)(2,1)S(1)}, u32[]{:S(2)}, u32[]{:S(2)}) collective-permute-start(bf16[2,64,1024]{2,1,0:T(8,128)(2,1)S(1)} %get-tuple-element.33), channel_id=1, source_target_pairs={{0,8},{4,12},{8,16},{12,20},{16,24},{20,28},{24,0},{28,4},{1,9},{5... | collective-permute-start | bytes 786440 | tf_op jit(solution)/shard_map/ppermute | solution.py:23
  32.2 17.6 %collective-permute-start.10 = (bf16[1,64,3072]{2,1,0:T(8,128)(2,1)S(1)}, bf16[1,64,3072]{2,1,0:T(8,128)(2,1)S(1)}, u32[]{:S(2)}, u32[]{:S(2)}) collective-permute-start(bf16[1,64,3072]{2,1,0:T(8,128)(2,1)S(1)} %get-tuple-element.25.refs_2_), channel_id=1, source_target_pairs={{0,2},{1,3},{2,0},{3,1},{4,6},{5,7},{6,4},{7,5},{8,10},{9,11},{10,... | collective-permute-start | bytes 1179656 | tf_op jit(solution)/shard_map/ppermute | solution.py:23
  33.6 16.1 %collective-permute-start.6 = (bf16[2,64,1024]{2,1,0:T(8,128)(2,1)S(1)}, bf16[2,64,1024]{2,1,0:T(8,128)(2,1)S(1)}, u32[]{:S(2)}, u32[]{:S(2)}) collective-permute-start(bf16[2,64,1024]{2,1,0:T(8,128)(2,1)S(1)} %get-tuple-element.34), channel_id=1, source_target_pairs={{0,24},{4,28},{8,0},{12,4},{16,8},{20,12},{24,16},{28,20},{1,25},{... | collective-permute-start | bytes 786440 | tf_op jit(solution)/shard_map/ppermute | solution.py:23
  41.6 15.2 %collective-permute-start.13 = (bf16[1,64,3072]{2,1,0:T(8,128)(2,1)S(1)}, bf16[1,64,3072]{2,1,0:T(8,128)(2,1)S(1)}, u32[]{:S(2)}, u32[]{:S(2)}) collective-permute-start(bf16[1,64,3072]{2,1,0:T(8,128)(2,1)S(1)} %get-tuple-element.26.refs_3_), channel_id=1, source_target_pairs={{0,2},{1,3},{2,0},{3,1},{4,6},{5,7},{6,4},{7,5},{8,10},{9,11},{10,... | collective-permute-start | bytes 1179656 | tf_op jit(solution)/shard_map/ppermute | solution.py:23
  43.2 13.4 %collective-permute-start.5 = (bf16[2,64,1024]{2,1,0:T(8,128)(2,1)S(1)}, bf16[2,64,1024]{2,1,0:T(8,128)(2,1)S(1)}, u32[]{:S(2)}, u32[]{:S(2)}) collective-permute-start(bf16[2,64,1024]{2,1,0:T(8,128)(2,1)S(1)} %shard_map.62.refs_4_), channel_id=1, source_target_pairs={{0,8},{4,12},{8,16},{12,20},{16,24},{20,28},{24,0},{28,4},{1,9},{5... | collective-permute-start | bytes 786440 | tf_op jit(solution)/shard_map/ppermute | solution.py:23
  45.8 10.9 %collective-permute-start.9 = (bf16[2,64,1024]{2,1,0:T(8,128)(2,1)S(1)}, bf16[2,64,1024]{2,1,0:T(8,128)(2,1)S(1)}, u32[]{:S(2)}, u32[]{:S(2)}) collective-permute-start(bf16[2,64,1024]{2,1,0:T(8,128)(2,1)S(1)} %get-tuple-element.35.refs_2_), channel_id=1, source_target_pairs={{0,8},{4,12},{8,16},{12,20},{16,24},{20,28},{24,0},{28,4},{1,9},{5... | collective-permute-start | bytes 786440 | tf_op jit(solution)/shard_map/ppermute | solution.py:23
  52.7 6.6 %collective-permute-start.11 = (bf16[1,2,64,1024]{3,2,1,0:T(8,128)(2,1)S(1)}, bf16[1,2,64,1024]{3,2,1,0:T(8,128)(2,1)S(1)}, u32[]{:S(2)}, u32[]{:S(2)}) collective-permute-start(bf16[1,2,64,1024]{3,2,1,0:T(8,128)(2,1)S(1)} %shard_map.65._), channel_id=1, source_target_pairs={{0,4},{4,0},{8,12},{12,8},{16,20},{20,16},{24,28},{28,24},{1,5},{5... | collective-permute-start | bytes 786440 | tf_op jit(solution)/shard_map/ppermute | solution.py:28
  54.3 7.7 %collective-permute-start.12 = (bf16[2,64,1024]{2,1,0:T(8,128)(2,1)S(1)}, bf16[2,64,1024]{2,1,0:T(8,128)(2,1)S(1)}, u32[]{:S(2)}, u32[]{:S(2)}) collective-permute-start(bf16[2,64,1024]{2,1,0:T(8,128)(2,1)S(1)} %get-tuple-element.38), channel_id=1, source_target_pairs={{0,24},{4,28},{8,0},{12,4},{16,8},{20,12},{24,16},{28,20},{1,25},{... | collective-permute-start | bytes 786440 | tf_op jit(solution)/shard_map/ppermute | solution.py:23
  58.6 7.2 %copy-start.1 = (bf16[256,1024]{1,0:T(8,128)(2,1)S(1)}, bf16[256,1024]{1,0:T(8,128)(2,1)}, u32[]{:S(2)}) copy-start(bf16[256,1024]{1,0:T(8,128)(2,1)} %rhs.1) | copy-start | bytes 1572868
  58.6 7.2 %copy-start.2 = (bf16[1,256,256]{2,1,0:T(8,128)(2,1)S(1)}, bf16[1,256,256]{2,1,0:T(8,128)(2,1)}, u32[]{:S(2)}) copy-start(bf16[1,256,256]{2,1,0:T(8,128)(2,1)} %diag.1) | copy-start | bytes 393220
  62.1 7.9 %collective-permute-start.15 = (f32[2,64,1024]{2,1,0:T(8,128)S(1)}, f32[2,64,1024]{2,1,0:T(8,128)S(1)}, u32[]{:S(2)}, u32[]{:S(2)}) collective-permute-start(f32[2,64,1024]{2,1,0:T(8,128)S(1)} %get-tuple-element.41), channel_id=1, source_target_pairs={{0,1},{1,0},{2,3},{3,2},{4,5},{5,4},{6,7},{7,6},{8,9},{9,8},{10,11... | collective-permute-start | bytes 1572872 | tf_op jit(solution)/shard_map/ppermute | solution.py:54
  62.2 7.8 %collective-permute-start.16 = (bf16[64,1024]{1,0:T(8,128)(2,1)S(1)}, bf16[64,1024]{1,0:T(8,128)(2,1)S(1)}, u32[]{:S(2)}, u32[]{:S(2)}) collective-permute-start(bf16[64,1024]{1,0:T(8,128)(2,1)S(1)} %get-tuple-element.42), channel_id=1, source_target_pairs={{0,9},{1,8},{2,11},{3,10},{4,13},{5,12},{6,15},{7,14},{8,17},{9,16... | collective-permute-start | bytes 393224 | tf_op jit(solution)/shard_map/ppermute | solution.py:54
  64.6 8.4 %collective-permute-start.14 = (bf16[64,1024]{1,0:T(8,128)(2,1)S(1)}, bf16[64,1024]{1,0:T(8,128)(2,1)S(1)}, u32[]{:S(2)}, u32[]{:S(2)}) collective-permute-start(bf16[64,1024]{1,0:T(8,128)(2,1)S(1)} %shard_map.69.refs_3_), channel_id=1, source_target_pairs={{0,8},{1,9},{2,10},{3,11},{4,12},{5,13},{6,14},{7,15},{8,16},{9,17... | collective-permute-start | bytes 393224 | tf_op jit(solution)/shard_map/ppermute | solution.py:54

commit v4 on v0

v4 whole, which is shorter than its diff:
```python
import functools

import jax
import jax.numpy as jnp
from jax import lax
from jax.experimental import pallas as pl
from jax.experimental.pallas import tpu as pltpu
from jax.sharding import PartitionSpec as P

F32, BF16 = jnp.float32, jnp.bfloat16
VMEM = pl.BlockSpec(memory_space=pltpu.VMEM)
SMEM = pl.BlockSpec(memory_space=pltpu.SMEM)
ANY = pl.BlockSpec(memory_space=pl.ANY)
HBM = pl.BlockSpec(memory_space=pltpu.HBM)


WIDE = 256
PIECES = 4
SPLIT = 2
FIRST2 = False
DIRECT_N, DIRECT_F = False, False
ORDER = (
    "rest", "p0a", "p0b", "p1a", "p1b", "n2", "f24", "n3", "n1", "gy1",
    "a3n", "f35", "gz1", "a1n", "f0", "f1a", "a2f", "f1", "a3f", "col",
)


def shift(block, axis, distance):
    size = lax.axis_size(axis)
    return lax.ppermute(block, axis, [(i, (i + distance) % size) for i in range(size)])


def pair_swap(block, axis):
    size = lax.axis_size(axis)
    return lax.ppermute(block, axis, [(i, i ^ 1) for i in range(size)])


def across(block, axis):
    return shift(block, axis, lax.axis_size(axis) // 2)


def inner(i, j, half):
    return i // half * half + (i % half + j) % half


def half_gather(block, axis):
    size = lax.axis_size(axis)
    half = size // 2
    parts = [block]
    for j in range(1, half):
        parts.append(lax.ppermute(block, axis, [(inner(i, j, half), i) for i in range(size)]))
    return parts


def to_columns(blocks, distance):
    n, size = lax.axis_size("col"), lax.axis_size("rhs")
    out = []
    for j, block in enumerate(blocks):
        route = [(c * size + r, (c + distance) % n * size + inner(r, j, size // 2))
                 for c in range(n) for r in range(size)]
        out.append(lax.ppermute(block, ("col", "rhs"), route) if distance or j else block)
    return out


def pinned(*shape, dtype=BF16):
    return pltpu.VMEM(shape, dtype)


def call(body, outs, specs, args, flops=0, space=12, out_specs=None, **more):
    moved = sum(a.size * a.dtype.itemsize for a in args)
    return pl.pallas_call(
        body,
        out_shape=outs,
        in_specs=specs,
        out_specs=out_specs or [VMEM] * len(outs),
        compiler_params=pltpu.CompilerParams(vmem_limit_bytes=space << 20),
        cost_estimate=pl.CostEstimate(flops=flops, bytes_accessed=moved, transcendentals=0),
        **more,
    )(*args)


def take(tiles, groups, *earlier, weights=None):
    n, rows, depth = len(groups), tiles.shape[1], tiles.shape[2]
    extra = [] if weights is None else [SMEM]

    def body(*refs):
        src, dsts, sems = refs[0], refs[-1 - n - len(extra):-1], refs[-1]
        copies = []
        for group, dst in zip(groups, dsts):
            for i, (k, begin, end) in enumerate(group):
                columns = pl.ds(begin, end - begin)
                for first in range(0, rows, rows // PIECES):
                    cut = pl.ds(first, rows // PIECES)
                    copies.append(pltpu.make_async_copy(src.at[k, cut, columns], dst.at[i, cut], sems.at[len(copies)]))
        for c in copies:
            c.start()
        if extra:
            for k in range(weights.shape[1]):
                dsts[-1][k:k + 1, :] = jnp.full((1, WIDE), refs[1][0, k].astype(F32))
        for c in copies:
            c.wait()

    outs = [pinned(len(g), rows, g[0][2] - g[0][1]) for g in groups]
    if extra:
        outs.append(pinned(weights.shape[1], WIDE, dtype=F32))
    return call(body, outs, [HBM] + extra + [ANY] * len(earlier),
                [in_hbm(tiles)] + ([] if weights is None else [weights]) + [*earlier], space=2,
                scratch_shapes=[pltpu.SemaphoreType.DMA((PIECES * sum(map(len, groups)),))])


def in_hbm(array):
    return pltpu.with_memory_space_constraint(array, pltpu.HBM)


def on_odd():
    return lax.rem(lax.axis_index("col"), 2) == 1


def gate(block, *earlier):
    def body(*refs):
        pass

    return call(body, [jax.ShapeDtypeStruct(block.shape, block.dtype)], [ANY] * (1 + len(earlier)), [block, *earlier],
                space=1, out_specs=[ANY], input_output_aliases={0: 0})[0]


def column_cuts(cols):
    wide = min(WIDE, cols)
    return [slice(at, at + wide) for at in range(0, cols, wide)]


def per_device(rhs_block, solution, factor, tile_list, diag_inverse):
    hops, quarter, depth = factor.shape[1:]
    rows, cols = rhs_block.shape
    size = lax.axis_size("rhs")
    half = size // 2
    tiles = factor[0]
    gives, owns = (2, 4, 0), (3, 5, 1)
    cuts = column_cuts(cols)
    strip = (half, quarter, cols)
    one, wide_one = pinned(*strip), pinned(*strip, dtype=F32)
    flat = pinned(quarter, cols)
    v = {}

    if FIRST2:
        s2, = take(tiles, [[(2, 0, depth)]])
        s4, = take(tiles, [[(4, 0, depth)]], s2)
        s24 = [s2, s4]
    else:
        s24 = list(take(tiles, [[(2, 0, depth), (4, 0, depth)]]))
    y24 = [across(s, "rhs") for s in s24]
    others = half_gather(solution, "rhs")[1:]
    cut_at = depth * SPLIT // 4
    last_tile = [[(1, 0, cut_at)], [(1, cut_at, depth)]] if SPLIT else [[(1, 0, depth)]]
    order = (3, 5, 0, 1)
    sols = [solution, *others]
    v["token"] = s24[-1]

    def chained(body, outs, ins, flops=0):
        n = len(ins)

        def run(*refs):
            body(*refs[:n], *refs[n + 1:])

        got = call(run, outs, [VMEM] * n + [ANY], [*ins, v["token"]], flops=flops)
        v["token"] = got[0]
        return got

    y, taken = {}, []

    def rest():
        s35, s0, *s1, v["weights"] = take(tiles, [[(3, 0, depth), (5, 0, depth)], [(0, 0, depth)]] + last_tile, v["token"],
                                          weights=tile_list)
        y[35] = across(s35, "rhs")
        y[0] = s0 if "gy0" in ORDER else across(s0, "rhs")
        y[1] = [s if g in ORDER else across(s, "rhs") for g, s in zip(("gy1", "gz1"), s1)]
        taken.extend([s35, s0, *s1])
        v["token"] = s35

    def gy0():
        y[0] = across(gate(y[0], v["token"]), "rhs")

    def gy1():
        y[1][0] = across(gate(y[1][0], v["token"]), "rhs")

    def gz1():
        y[1][1] = across(gate(y[1][1], v["token"]), "rhs")

    near_got, near_own, near_give0 = [], [], []

    def near_gives(part):
        def body(*refs):
            lefts, (sol, weights, _, give) = refs[:-4], refs[-4:]
            left = jnp.concatenate([r[i] for r in lefts for i in range(r.shape[0])])
            for cut in cuts:
                total = jnp.dot(left, sol[:, cut], preferred_element_type=F32)
                for i in range(2):
                    term = total[i * quarter:(i + 1) * quarter] * weights[gives[i]:gives[i] + 1, :total.shape[1]]
                    give[i, :, cut] = term.astype(BF16)

        got = call(body, [pinned(2, quarter, cols)], [VMEM] * (len(s24) + 2) + [ANY], [*s24, sols[part], v["weights"], v["token"]],
                   flops=4 * quarter * depth * cols)
        v["token"] = got[0]
        near_got.append(pair_swap(got[0], "col"))

    def near_rest(part):
        n = len(taken)
        joins = half - 1 if part == half - 1 else 0

        def body(*refs):
            lefts, (sol, weights), outs = refs[:n], refs[n:n + 2], refs[n + 3 + joins:]
            whole = [r[i] for r in lefts[:2] for i in range(r.shape[0])]
            left = jnp.concatenate(whole + [jnp.concatenate([r[0] for r in lefts[2:]], axis=1)])
            for cut in cuts:
                total = jnp.dot(left, sol[:, cut], preferred_element_type=F32)
                for at, k in enumerate(order):
                    term = total[at * quarter:(at + 1) * quarter] * weights[k:k + 1, :total.shape[1]]
                    if k in owns:
                        outs[0][owns.index(k), :, cut] = term
                    elif joins:
                        outs[1][part, :, cut] = term.astype(BF16)
                    else:
                        outs[1][:, cut] = term.astype(BF16)
            for p in range(joins):
                outs[1][p] = refs[n + 2 + p][...]

        got = call(body, [pinned(3, quarter, cols, dtype=F32), one if joins else flat],
                   [VMEM] * (n + 2 + joins) + [ANY],
                   [*taken, sols[part], v["weights"], *near_give0[:joins], v["token"]],
                   flops=8 * quarter * depth * cols)
        v["token"] = got[0]
        near_own.append(got[0])
        if joins:
            v["got0"] = pair_swap(got[1], "col")
        else:
            near_give0.append(got[1])

    def p0a():
        near_gives(0)

    def p0b():
        near_rest(0)

    def p1a():
        for part in range(1, half):
            near_gives(part)

    def p1b():
        for part in range(1, half):
            near_rest(part)

    def zeros():
        return [v["got0"]]

    def r0(refs, part):
        return refs[0][part].astype(F32)

    def products(far, ks, epilogue, outs, extra, deep=slice(None)):
        n_extra = len(extra)

        far = far if isinstance(far, list) else [far]
        n_far = len(far)

        def body(*refs):
            far_refs, refs = refs[:n_far], refs[n_far:]
            sol_refs, weights = refs[:half], refs[half]
            more = refs[half + 1:half + 1 + n_extra]
            out = refs[len(refs) - len(outs):]
            is_odd = on_odd()
            left = jnp.concatenate([r[i] for r in far_refs for i in range(r.shape[0])])
            for part, sol_ref in enumerate(sol_refs):
                for cut in cuts:
                    total = jnp.dot(left, sol_ref[deep, cut], preferred_element_type=F32)
                    for i, k in enumerate(ks):
                        term = total[i * quarter:(i + 1) * quarter] * weights[k:k + 1, :total.shape[1]]
                        epilogue(out, more, is_odd, i, part, cut, term)

        args = [*far, *sols, v["weights"], *extra, v["token"]]
        specs = [VMEM] * (n_far + half + 1 + n_extra) + [ANY]
        got = call(body, outs, specs, args, flops=2 * len(ks) * quarter * depth * cols * half)
        v["token"] = got[0]
        return got

    def store(out, more, is_odd, i, part, cut, total):
        out[0][i, part, :, cut] = total.astype(BF16)

    def plain(out, more, is_odd, i, part, cut, total):
        out[0][part, :, cut] = total

    def added(out, more, is_odd, i, part, cut, total):
        out[0][part, :, cut] = total + more[0][part, :, cut]

    def f24():
        def each(out, more, is_odd, i, part, cut, total):
            out[i][part, :, cut] = total.astype(BF16)

        v["got_far"] = [pair_swap(g, "col") for g in products(y24, (2, 4), each, [one, one], [])]

    def stage2(refs, d2):
        for p in range(half):
            own, got = refs[p], refs[half + p]
            d2[p] = (own[0] + jnp.where(on_odd(), got[1].astype(F32), got[0].astype(F32))).astype(BF16)

    def stage3(refs, d3):
        for p in range(half):
            own, got = refs[p], refs[half + p]
            d3[p] = (own[1] + jnp.where(on_odd(), 0.0, got[1].astype(F32))).astype(BF16)

    def stage1(refs, others, arrived, d1):
        for p in range(half):
            own, got = refs[p], refs[half + p]
            r = jnp.where(on_odd(), got[0].astype(F32), r0(others, p))
            total = own[2] + r
            d1[p] = (total if arrived is None else total + arrived[p].astype(F32)).astype(BF16)

    def send2(total, direct):
        return shift(total, "col", 4 if direct else 2)

    def n2():
        d2, = chained(lambda *refs: stage2(refs, refs[-1]), [one], [*near_own, *near_got])
        v["d2n"] = send2(d2, DIRECT_N)

    def n3():
        d3, = chained(lambda *refs: stage3(refs, refs[-1]), [one], [*near_own, *near_got])
        v["d3n"] = shift(d3, "col", 6)

    def n23():
        def body(*refs):
            stage2(refs, refs[-2])
            stage3(refs, refs[-1])

        d2, d3 = chained(body, [one, one], [*near_own, *near_got])
        v["d2n"], v["d3n"] = send2(d2, DIRECT_N), shift(d3, "col", 6)

    def n1():
        n = len(zeros())
        d1, = chained(lambda *refs: stage1(refs, refs[2 * half:2 * half + n], None if DIRECT_N else refs[-2], refs[-1]),
                      [one], [*near_own, *near_got, *zeros()] + ([] if DIRECT_N else [v["d2n"]]))
        v["d1n"] = shift(d1, "col", 2)

    def n1p():
        def body(*refs):
            for p in range(half):
                refs[-1][p] = refs[p][2] + refs[half][p].astype(F32)

        v["part1"], = chained(body, [wide_one], [*near_own, v["d2n"]])

    def n1q():
        def body(part1, got0, *refs):
            for p in range(half):
                r = jnp.where(on_odd(), refs[p][0].astype(F32), got0[p].astype(F32))
                refs[-1][p] = (part1[p] + r).astype(BF16)

        d1, = chained(body, [one], [v["part1"], v["got0"], *near_got])
        v["d1n"] = shift(d1, "col", 2)

    def n13():
        n = len(zeros())

        def body(*refs):
            stage1(refs, refs[2 * half:2 * half + n], None if DIRECT_N else refs[-3], refs[-2])
            stage3(refs, refs[-1])

        d1, d3 = chained(body, [one, one], [*near_own, *near_got, *zeros()] + ([] if DIRECT_N else [v["d2n"]]))
        v["d1n"], v["d3n"] = shift(d1, "col", 2), shift(d3, "col", 6)

    def f35():
        def far35(out, more, is_odd, i, part, cut, total):
            r2, r4 = [m[part, :, cut].astype(F32) for m in more]
            if i == 0:
                total = total + jnp.where(is_odd, r4, r2)
            else:
                total = total + jnp.where(is_odd, 0.0, r4)
            out[i][part, :, cut] = total.astype(BF16)

        d2, d3 = products(y[35], (3, 5), far35, [one, one], v["got_far"])
        v["d2f"], v["d3f"] = send2(d2, DIRECT_F), shift(d3, "col", 6)

    def a3n():
        n = len(zeros())

        def body(d3, *refs):
            for p in range(half):
                refs[-1][p] = d3[p].astype(F32) + jnp.where(on_odd(), r0(refs[:n], p), 0.0)

        v["sum_n"], = chained(body, [wide_one], [v["d3n"], *zeros()])

    def a1n():
        ins = [v["d1n"]] + ([v["sum_n"]] if "sum_n" in v else [v["d3n"], *zeros()]) + ([v["d2n"]] if DIRECT_N else [])
        n = len(zeros())

        def body(d1, *refs):
            for p in range(half):
                total = d1[p].astype(F32)
                if "sum_n" in v:
                    total = total + refs[0][p]
                else:
                    total = total + refs[0][p].astype(F32) + jnp.where(on_odd(), r0(refs[1:1 + n], p), 0.0)
                refs[-1][p] = total + refs[-2][p].astype(F32) if DIRECT_N else total

        v["all_n"], = chained(body, [wide_one], ins)

    def f0():
        v["got_last"] = pair_swap(products(y[0], (0,), store, [pinned(1, *strip)], [])[0], "col")

    def f1a():
        v["first"], = products(y[1][0], (1,), plain, [wide_one], [], slice(0, cut_at))

    def a2f():
        ins = [v["got_far"][0]] + ([] if DIRECT_F else [v["d2f"]]) + [v[k] for k in ("first",) if k in v]

        def body(gf, *refs):
            for p in range(half):
                total = jnp.where(on_odd(), gf[p].astype(F32), 0.0)
                for ref in refs[:-1]:
                    total = total + ref[p].astype(F32)
                refs[-1][p] = total

        v["pre"], = chained(body, [wide_one], ins)

    def f1():
        deep = slice(cut_at, depth) if SPLIT else slice(None)
        v["added"] = "pre" in v
        if v["added"]:
            v["raw"], = products(y[1][-1], (1,), added, [wide_one], [v["pre"]], deep)
        else:
            v["raw"], = products(y[1][-1], (1,), plain, [wide_one], [], deep)

    def a3f():
        def body(d3, out):
            out[...] = d3[...].astype(F32)

        v["sum_f"], = chained(body, [wide_one], [v["d3f"]])

    def col():
        early, added = "sum_f" in v, v["added"]

        def collect(total, raw, gl, d3far, *refs):
            sums, lasts = refs[-2 * half:-half], refs[-half:]
            is_odd = on_odd()
            for part in range(half):
                r0 = gl[0, part].astype(F32)
                last = raw[part] + jnp.where(is_odd, 0.0, r0)
                lasts[part][...] = (last if added else last + refs[0][part]).astype(BF16)
                sums[part][0] = total[part]
                sums[part][1] = d3far[part].astype(F32) + jnp.where(is_odd, r0, 0.0)
                if DIRECT_F:
                    sums[part][1] += refs[0 if added else 1][part].astype(F32)

        outs = chained(collect, [pinned(2, quarter, cols, dtype=F32)] * half + [flat] * half,
                       [v["all_n"], v["raw"], v["got_last"], v["sum_f"] if early else v["d3f"]]
                       + ([] if added else [v["pre"]]) + ([v["d2f"]] if DIRECT_F else []))
        sums, v["lasts"] = outs[:half], outs[half:]
        v["sums"] = to_columns(sums, 0)
        v["last_in"] = to_columns(v["lasts"], 2)

    nodes = dict(gy0=gy0, gy1=gy1, gz1=gz1, rest=rest, p0a=p0a, p0b=p0b, p1a=p1a, p1b=p1b, n1p=n1p, n1q=n1q, f24=f24, n2=n2, n3=n3, n23=n23, n1=n1, n13=n13, f35=f35, a3n=a3n, a1n=a1n, f0=f0,
                 f1a=f1a, a2f=a2f, f1=f1, a3f=a3f, col=col)
    for name in ORDER:
        nodes[name]()

    places = [(0, j) for j in range(half)] + [(1, j) for j in range(1, half)] + [(1, 0)]

    def arrange(rhs, diag, _, rhs_out, diag_out):
        me = lax.axis_index("rhs")
        upper, mine = lax.div(me, half), lax.rem(me, half)
        column = lax.broadcasted_iota(jnp.int32, (rows, rows), 1)
        source = column
        for slot, (s, j) in enumerate(places):
            at = slot * quarter
            block = lax.rem(upper + s, 2) * half + lax.rem(mine + half - j, half)
            start = pl.multiple_of(block * quarter, quarter)
            rhs_out[at:at + quarter] = rhs[pl.ds(start, quarter)]
            source = jnp.where((column >= at) & (column < at + quarter), column - at + start, source)
        pick = (lax.broadcasted_iota(jnp.int32, (rows, rows), 0) == source).astype(BF16)
        diag_out[...] = jnp.dot(diag[0], pick, preferred_element_type=F32).astype(BF16)

    rhs_local, diag_local = call(arrange, [pinned(rows, cols), pinned(rows, rows)], [VMEM, VMEM, ANY],
                                 [rhs_block, diag_inverse, near_own[-1]], flops=2 * rows * rows * rows)

    early = rows - quarter
    sums_in, last_in = v["sums"], v["last_in"]

    def most(rhs, diag, *refs):
        acc, last, out = refs[:half], refs[half:2 * half - 1], refs[-1]
        total = jnp.concatenate([a[0] for a in acc] + [a[1] + l[...].astype(F32) for a, l in zip(acc[1:], last)])
        remaining = (rhs[:early].astype(F32) - total).astype(BF16)
        out[...] = jnp.dot(diag[:, :early], remaining, preferred_element_type=F32)

    partial, = call(most, [pinned(rows, cols, dtype=F32)], [VMEM] * (2 + 2 * half - 1) + [ANY],
                    [rhs_local, diag_local, *sums_in, *last_in[1:], v["lasts"][0]], flops=2 * rows * early * cols)

    def final(rhs, diag, acc, last, part, out, block, sems):
        total = acc[1] + last[...].astype(F32)
        remaining = (rhs[early:].astype(F32) - total).astype(BF16)
        copies = []
        for i in range(size):
            cut = slice(i * quarter, (i + 1) * quarter)
            term = jnp.dot(diag[cut, early:], remaining, preferred_element_type=F32)
            block[cut] = (part[cut] + term).astype(BF16)
            copies.append(pltpu.make_async_copy(block.at[cut], out.at[cut], sems.at[i]))
            copies[-1].start()
        for c in copies:
            c.wait()

    return call(final, [jax.ShapeDtypeStruct((rows, cols), BF16)], [VMEM] * 5,
                [rhs_local, diag_local, sums_in[0], last_in[0], partial], flops=2 * rows * quarter * cols,
                out_specs=[ANY], scratch_shapes=[pltpu.VMEM((rows, cols), BF16), pltpu.SemaphoreType.DMA((size,))])[0]

def solution(mesh):
    in_specs = (
        P("col", "rhs"),
        P("col", "rhs"),
        P("col", None, "rhs", None),
        P("col", None),
        P("col", None, None),
    )
    out_specs = P("col", "rhs")
    return jax.shard_map(
        per_device, mesh=mesh, in_specs=in_specs, out_specs=out_specs, check_vma=False
    )
```

time: 206 us -> 70.8 us (0.34)
  waiting for transfers between devices: 150 us -> 23.1 us
  matrix products: 31.1 us -> 0 us
  starting transfers between devices: 2.01 us -> 26.6 us
  Pallas kernels: 0 us -> 20 us
  between operations: 17.3 us -> 0.37 us
  local copies, waits for them, and re-layouts: 4.73 us -> 0.67 us
    ppermute x6 -> x20, waiting for transfers between devices: 112 us -> 23.1 us  [the longest x10 9.87 us: shift(): lax.ppermute(block, axis, [(i, (i + distance) % size) for i in range(size)])]
    all_gather x6 -> x0, waiting for transfers between devices: 36.8 us -> none  [per_device(): lax.all_gather(factor[0, offset], 'rhs', axis=0, tiled=True)]
    dot_general x7 -> x0, matrix products: 31.1 us -> none  [the longest x6 30.7 us: per_device(): jnp.dot(lax.all_gather(factor[0, offset], 'rhs', axis=0, tiled=True), sol...]
    ppermute x6 -> x20, starting transfers between devices: 1.81 us -> 26.6 us  [the longest x10 15.2 us: shift(): lax.ppermute(block, axis, [(i, (i + distance) % size) for i in range(size)])]
    pallas_call x0 -> x24, Pallas kernels: none -> 20 us  [call(): pl.pallas_call(body, out_shape=outs, in_specs=specs, out_specs=out_specs...]
    slice x2 -> x0, local copies, waits for them, and re-layouts: 3.71 us -> none  [the longest x1 3.04 us: per_device(): factor[0, offset]]
  transfers between devices with their start and end apart: 12 -> 20, of which waited for: 9 -> 13; matrix products, arithmetic and copies ran while one was open for 15% -> 0% of each run, Pallas kernels for 0% -> 27%
where the time goes in v4:
time: 70.8 us; the launch traced here: 70.7 us
  starting transfers between devices  26.6 us (38%)
  waiting for transfers between devices  23.1 us (33%)
  Pallas kernels  20 us (28%)
    pallas_call x24, Pallas kernels, call(): pl.pallas_call(body, out_shape=outs, in_specs=specs, out_specs=out_specs...  20 us
    ppermute x10, starting transfers between devices, shift(): lax.ppermute(block, axis, [(i, (i + distance) % size) for i in range(size)])  15.2 us
    ppermute x10, waiting for transfers between devices, shift(): lax.ppermute(block, axis, [(i, (i + distance) % size) for i in range(size)])  9.87 us
    ppermute x6, starting transfers between devices, pair_swap(): return lax.ppermute(block, axis, [(i, i ^ 1) for i in range(size)])  7.62 us
    ppermute x3, waiting for transfers between devices, to_columns(): lax.ppermute(block, ('col', 'rhs'), route)  6.74 us
    ppermute x6, waiting for transfers between devices, pair_swap(): return lax.ppermute(block, axis, [(i, i ^ 1) for i in range(size)])  6.49 us
    ppermute x3, starting transfers between devices, to_columns(): lax.ppermute(block, ('col', 'rhs'), route)  3.26 us
  transfers between devices with their start and end apart: 20, of which 13 were waited for; matrix products, arithmetic and copies ran while one was open for 0% of the time, Pallas kernels for 27%

profile of v4, /device:TPU:0, one launch (start us, length us, event | category | flops | bytes accessed | tf_op | source)
XLA Modules:
  0.0 70.7 jit_solution(14927753857296649633)
XLA Ops:
  0.0 0.5 collective-permute-start
  0.5 1.5 %shard_map.55.refs_2_.refs_0_ = bf16[2,64,3072]{2,1,0:T(8,128)(2,1)S(1)} custom-call(bf16[6,64,3072]{2,1,0:T(8,128)(2,1)} %bitcast.1), custom_call_target="tpu_custom_call" | custom-call | bytes 2359296 | tf_op jit(solution)/shard_map/pallas_call | solution.py:71
  1.9 2.5 %collective-permute-start.5 = (bf16[2,64,3072]{2,1,0:T(8,128)(2,1)S(1)}, bf16[2,64,3072]{2,1,0:T(8,128)(2,1)S(1)}, u32[]{:S(2)}, u32[]{:S(2)}) collective-permute-start(bf16[2,64,3072]{2,1,0:T(8,128)(2,1)S(1)} %shard_map.55.refs_2_.refs_0_), channel_id=1, source_target_pairs={{0,2},{1,3},{2,0},{3,1},{4,6},{5,7},{6,4},{7,5},{8,10},{9,11},{10,... | collective-permute-start | bytes 2359304 | tf_op jit(solution)/shard_map/ppermute | solution.py:30
  4.5 0.7 copy-done.3
  5.1 2.1 %shard_map.56 = (bf16[2,64,3072]{2,1,0:T(8,128)(2,1)S(1)}, bf16[1,64,3072]{2,1,0:T(8,128)(2,1)S(1)}, bf16[1,64,1536]{2,1,0:T(8,128)(2,1)S(1)}, bf16[1,64,1536]{2,1,0:T(8,128)(2,1)S(1)}, f32[6,256]{1,0:T(8,128)S(1)}) custom-call(bf16[6,64,3072]{2,1,0:T(8,128)(2,1)} %bitcast.2, s32[1,6]{1,0:T(1,128)S(1)} %copy-done.3, ...), custom_call_target="tpu_custom_call" | custom-call | bytes 3145752 | tf_op jit(solution)/shard_map/pallas_call | solution.py:71
  7.2 0.4 collective-permute-start.8
  7.6 0.0 copy-done
  7.6 1.0 %shard_map.57.refs_6_ = bf16[2,64,1024]{2,1,0:T(8,128)(2,1)S(1)} custom-call(bf16[2,64,3072]{2,1,0:T(8,128)(2,1)S(1)} %shard_map.55.refs_2_.refs_0_, bf16[3072,1024]{1,0:T(8,128)(2,1)S(1)} %copy-done, f32[6,256]{1,0:T(8,128)S(1)} %get-tuple-element.28.refs_2_.refs_5_.refs_3_, bf16[2,64,3072]{2,1,0:T(8,128)(2,1)S(1)} %get-tuple-element.24.refs_3_.refs_0_), custom_call_target="tpu_custom_call" | custom-call | flops 805306368 | bytes 7870464 | tf_op jit(solution)/shard_map/pallas_call | solution.py:71
  8.6 1.9 %collective-permute-start.1 = (bf16[2,64,1024]{2,1,0:T(8,128)(2,1)S(1)}, bf16[2,64,1024]{2,1,0:T(8,128)(2,1)S(1)}, u32[]{:S(2)}, u32[]{:S(2)}) collective-permute-start(bf16[2,64,1024]{2,1,0:T(8,128)(2,1)S(1)} %shard_map.57.refs_6_), channel_id=1, source_target_pairs={{0,4},{4,0},{8,12},{12,8},{16,20},{20,16},{24,28},{28,24},{1,5},{5... | collective-permute-start | bytes 786440 | tf_op jit(solution)/shard_map/ppermute | solution.py:35
  10.5 1.8 %shard_map.58 = (f32[3,64,1024]{2,1,0:T(8,128)S(1)}, bf16[64,1024]{1,0:T(8,128)(2,1)S(1)}) custom-call(bf16[2,64,3072]{2,1,0:T(8,128)(2,1)S(1)} %get-tuple-element.24.refs_3_.refs_0_, bf16[1,64,3072]{2,1,0:T(8,128)(2,1)S(1)} %get-tuple-element.25.refs_1_, bf16[1,64,1536]{2,1,0:T(8,128)(2,1)S(1)} %get-tuple-element.26.refs_2_.refs_0_, ...), custom_call_target="tpu_custom_call" | custom-call | flops 1610612736 | bytes 8132608 | tf_op jit(solution)/shard_map/pallas_call | solution.py:71
  12.3 0.0 collective-permute-done.refs_1_.refs_4_.refs_2_
  12.3 1.0 %shard_map.59.refs_7_ = bf16[2,64,1024]{2,1,0:T(8,128)(2,1)S(1)} custom-call(bf16[2,64,3072]{2,1,0:T(8,128)(2,1)S(1)} %shard_map.55.refs_2_.refs_0_, bf16[3072,1024]{1,0:T(8,128)(2,1)S(1)} %collective-permute-done.refs_1_.refs_4_.refs_2_, f32[6,256]{1,0:T(8,128)S(1)} %get-tuple-element.28.refs_2_.refs_5_.refs_3_, ...), custom_call_target="tpu_custom_call" | custom-call | flops 805306368 | bytes 7870464 | tf_op jit(solution)/shard_map/pallas_call | solution.py:71
  13.3 1.1 %collective-permute-start.2 = (bf16[2,64,1024]{2,1,0:T(8,128)(2,1)S(1)}, bf16[2,64,1024]{2,1,0:T(8,128)(2,1)S(1)}, u32[]{:S(2)}, u32[]{:S(2)}) collective-permute-start(bf16[2,64,1024]{2,1,0:T(8,128)(2,1)S(1)} %shard_map.59.refs_7_), channel_id=1, source_target_pairs={{0,4},{4,0},{8,12},{12,8},{16,20},{20,16},{24,28},{28,24},{1,5},{5... | collective-permute-start | bytes 786440 | tf_op jit(solution)/shard_map/ppermute | solution.py:35
  14.4 1.8 %shard_map.60 = (f32[3,64,1024]{2,1,0:T(8,128)S(1)}, bf16[2,64,1024]{2,1,0:T(8,128)(2,1)S(1)}) custom-call(bf16[2,64,3072]{2,1,0:T(8,128)(2,1)S(1)} %get-tuple-element.24.refs_3_.refs_0_, bf16[1,64,3072]{2,1,0:T(8,128)(2,1)S(1)} %get-tuple-element.25.refs_1_, bf16[1,64,1536]{2,1,0:T(8,128)(2,1)S(1)} %get-tuple-element.26.refs_2_.refs_0_, ...), custom_call_target="tpu_custom_call" | custom-call | flops 1610612736 | bytes 8263680 | tf_op jit(solution)/shard_map/pallas_call | solution.py:71
  16.2 1.1 %collective-permute-start.3 = (bf16[2,64,1024]{2,1,0:T(8,128)(2,1)S(1)}, bf16[2,64,1024]{2,1,0:T(8,128)(2,1)S(1)}, u32[]{:S(2)}, u32[]{:S(2)}) collective-permute-start(bf16[2,64,1024]{2,1,0:T(8,128)(2,1)S(1)} %get-tuple-element.34), channel_id=1, source_target_pairs={{0,4},{4,0},{8,12},{12,8},{16,20},{20,16},{24,28},{28,24},{1,5},{5... | collective-permute-start | bytes 786440 | tf_op jit(solution)/shard_map/ppermute | solution.py:35
  17.3 0.5 collective-permute-done.1.refs_2_
  17.8 5.6 %collective-permute-done.2.refs_3_ = bf16[2,64,1024]{2,1,0:T(8,128)(2,1)S(1)} collective-permute-done((bf16[2,64,1024]{2,1,0:T(8,128)(2,1)S(1)}, bf16[2,64,1024]{2,1,0:T(8,128)(2,1)S(1)}, u32[]{:S(2)}, u32[]{:S(2)}) %collective-permute-start.2) | collective-permute-done | bytes 262176 | tf_op jit(solution)/shard_map/ppermute | solution.py:35
  23.5 0.1 shard_map.62.refs_4_
  23.5 2.0 %collective-permute-start.4 = (bf16[2,64,1024]{2,1,0:T(8,128)(2,1)S(1)}, bf16[2,64,1024]{2,1,0:T(8,128)(2,1)S(1)}, u32[]{:S(2)}, u32[]{:S(2)}) collective-permute-start(bf16[2,64,1024]{2,1,0:T(8,128)(2,1)S(1)} %shard_map.62.refs_4_), channel_id=1, source_target_pairs={{0,8},{4,12},{8,16},{12,20},{16,24},{20,28},{24,0},{28,4},{1,9},{5... | collective-permute-start | bytes 786440 | tf_op jit(solution)/shard_map/ppermute | solution.py:30
  25.5 0.0 collective-permute-done.5.refs_0_
  25.5 1.9 %shard_map.63 = (bf16[2,64,1024]{2,1,0:T(8,128)(2,1)S(1)}, bf16[2,64,1024]{2,1,0:T(8,128)(2,1)S(1)}) custom-call(bf16[2,64,3072]{2,1,0:T(8,128)(2,1)S(1)} %collective-permute-done.5.refs_0_, bf16[3072,1024]{1,0:T(8,128)(2,1)S(1)} %copy-done, bf16[3072,1024]{1,0:T(8,128)(2,1)S(1)} %collective-permute-done.refs_1_.refs_4_.refs_2_, ...), custom_call_target="tpu_custom_call" | custom-call | flops 1610612736 | bytes 13637632 | tf_op jit(solution)/shard_map/pallas_call | solution.py:71
  27.4 0.1 shard_map.64.refs_6_
  27.5 2.1 %collective-permute-start.7 = (bf16[2,64,1024]{2,1,0:T(8,128)(2,1)S(1)}, bf16[2,64,1024]{2,1,0:T(8,128)(2,1)S(1)}, u32[]{:S(2)}, u32[]{:S(2)}) collective-permute-start(bf16[2,64,1024]{2,1,0:T(8,128)(2,1)S(1)} %shard_map.64.refs_6_), channel_id=1, source_target_pairs={{0,24},{4,28},{8,0},{12,4},{16,8},{20,12},{24,16},{28,20},{1,25},{... | collective-permute-start | bytes 786440 | tf_op jit(solution)/shard_map/ppermute | solution.py:30
  29.6 1.7 %collective-permute-start.10 = (bf16[2,64,1024]{2,1,0:T(8,128)(2,1)S(1)}, bf16[2,64,1024]{2,1,0:T(8,128)(2,1)S(1)}, u32[]{:S(2)}, u32[]{:S(2)}) collective-permute-start(bf16[2,64,1024]{2,1,0:T(8,128)(2,1)S(1)} %get-tuple-element.36), channel_id=1, source_target_pairs={{0,4},{4,0},{8,12},{12,8},{16,20},{20,16},{24,28},{28,24},{1,5},{5... | collective-permute-start | bytes 786440 | tf_op jit(solution)/shard_map/ppermute | solution.py:35
  31.3 0.0 collective-permute-done.3.refs_4_.refs_1_
  31.3 0.3 collective-permute-start.9
  31.6 2.6 %collective-permute-done.4.refs_5_ = bf16[2,64,1024]{2,1,0:T(8,128)(2,1)S(1)} collective-permute-done((bf16[2,64,1024]{2,1,0:T(8,128)(2,1)S(1)}, bf16[2,64,1024]{2,1,0:T(8,128)(2,1)S(1)}, u32[]{:S(2)}, u32[]{:S(2)}) %collective-permute-start.4) | collective-permute-done | bytes 262176 | tf_op jit(solution)/shard_map/ppermute | solution.py:30
  34.3 1.6 %collective-permute-start.14 = (bf16[1,64,3072]{2,1,0:T(8,128)(2,1)S(1)}, bf16[1,64,3072]{2,1,0:T(8,128)(2,1)S(1)}, u32[]{:S(2)}, u32[]{:S(2)}) collective-permute-start(bf16[1,64,3072]{2,1,0:T(8,128)(2,1)S(1)} %get-tuple-element.25.refs_1_), channel_id=1, source_target_pairs={{0,2},{1,3},{2,0},{3,1},{4,6},{5,7},{6,4},{7,5},{8,10},{9,11},{10,... | collective-permute-start | bytes 1179656 | tf_op jit(solution)/shard_map/ppermute | solution.py:30
  35.9 0.1 shard_map.65.refs_2_.refs_1_
  36.0 1.7 %collective-permute-done.7.refs_0_ = bf16[2,64,1024]{2,1,0:T(8,128)(2,1)S(1)} collective-permute-done((bf16[2,64,1024]{2,1,0:T(8,128)(2,1)S(1)}, bf16[2,64,1024]{2,1,0:T(8,128)(2,1)S(1)}, u32[]{:S(2)}, u32[]{:S(2)}) %collective-permute-start.7) | collective-permute-done | bytes 262176 | tf_op jit(solution)/shard_map/ppermute | solution.py:30
  37.7 0.6 collective-permute-start.6
  38.3 0.1 shard_map.66.refs_6_.refs_1_
  38.4 1.3 %collective-permute-done.8.refs_0_ = bf16[2,64,3072]{2,1,0:T(8,128)(2,1)S(1)} collective-permute-done((bf16[2,64,3072]{2,1,0:T(8,128)(2,1)S(1)}, bf16[2,64,3072]{2,1,0:T(8,128)(2,1)S(1)}, u32[]{:S(2)}, u32[]{:S(2)}) %collective-permute-start.8) | collective-permute-done | bytes 786464 | tf_op jit(solution)/shard_map/ppermute | solution.py:30
  39.7 2.0 %collective-permute-start.13 = (bf16[1,64,1536]{2,1,0:T(8,128)(2,1)S(1)}, bf16[1,64,1536]{2,1,0:T(8,128)(2,1)S(1)}, u32[]{:S(2)}, u32[]{:S(2)}) collective-permute-start(bf16[1,64,1536]{2,1,0:T(8,128)(2,1)S(1)} %shard_map.70), channel_id=1, source_target_pairs={{0,2},{1,3},{2,0},{3,1},{4,6},{5,7},{6,4},{7,5},{8,10},{9,11},{10,... | collective-permute-start | bytes 589832 | tf_op jit(solution)/shard_map/ppermute | solution.py:30
  41.7 0.0 collective-permute-done.10.refs_5_
  41.7 0.3 collective-permute-done.9.refs_4_.refs_0_
  42.0 1.9 %shard_map.67 = (bf16[2,64,1024]{2,1,0:T(8,128)(2,1)S(1)}, bf16[2,64,1024]{2,1,0:T(8,128)(2,1)S(1)}) custom-call(bf16[2,64,3072]{2,1,0:T(8,128)(2,1)S(1)} %collective-permute-done.8.refs_0_, bf16[3072,1024]{1,0:T(8,128)(2,1)S(1)} %copy-done, bf16[3072,1024]{1,0:T(8,128)(2,1)S(1)} %collective-permute-done.refs_1_.refs_4_.refs_2_, ...), custom_call_target="tpu_custom_call" | custom-call | flops 1610612736 | bytes 14424064 | tf_op jit(solution)/shard_map/pallas_call | solution.py:71
  43.9 1.4 %collective-permute-start.12 = (bf16[2,64,1024]{2,1,0:T(8,128)(2,1)S(1)}, bf16[2,64,1024]{2,1,0:T(8,128)(2,1)S(1)}, u32[]{:S(2)}, u32[]{:S(2)}) collective-permute-start(bf16[2,64,1024]{2,1,0:T(8,128)(2,1)S(1)} %get-tuple-element.37.refs_2_.refs_1_), channel_id=1, source_target_pairs={{0,8},{4,12},{8,16},{12,20},{16,24},{20,28},{24,0},{28,4},{1,9},{5... | collective-permute-start | bytes 786440 | tf_op jit(solution)/shard_map/ppermute | solution.py:30
  45.3 0.5 collective-permute-start.11
  45.8 1.4 %collective-permute-done.6.refs_0_ = bf16[2,64,1024]{2,1,0:T(8,128)(2,1)S(1)} collective-permute-done((bf16[2,64,1024]{2,1,0:T(8,128)(2,1)S(1)}, bf16[2,64,1024]{2,1,0:T(8,128)(2,1)S(1)}, u32[]{:S(2)}, u32[]{:S(2)}) %collective-permute-start.6) | collective-permute-done | bytes 262176 | tf_op jit(solution)/shard_map/ppermute | solution.py:30
  47.2 2.1 %collective-permute-start.16 = (bf16[2,64,1024]{2,1,0:T(8,128)(2,1)S(1)}, bf16[2,64,1024]{2,1,0:T(8,128)(2,1)S(1)}, u32[]{:S(2)}, u32[]{:S(2)}) collective-permute-start(bf16[2,64,1024]{2,1,0:T(8,128)(2,1)S(1)} %get-tuple-element.38), channel_id=1, source_target_pairs={{0,24},{4,28},{8,0},{12,4},{16,8},{20,12},{24,16},{28,20},{1,25},{... | collective-permute-start | bytes 786440 | tf_op jit(solution)/shard_map/ppermute | solution.py:30
  49.4 0.0 collective-permute-done.14.refs_0_
  49.4 2.3 %shard_map.71.refs_4_ = bf16[1,2,64,1024]{3,2,1,0:T(8,128)(2,1)S(1)} custom-call(bf16[1,64,3072]{2,1,0:T(8,128)(2,1)S(1)} %collective-permute-done.14.refs_0_, bf16[3072,1024]{1,0:T(8,128)(2,1)S(1)} %copy-done, bf16[3072,1024]{1,0:T(8,128)(2,1)S(1)} %collective-permute-done.refs_1_.refs_4_.refs_2_, f32[6,256]{1,0:T(8,128)S(1)} %get-tuple-element.28.refs_2_.refs_5_.refs_3_, ...), custom_call_target="tpu_custom_call" | custom-call | flops 805306368 | bytes 13506560 | tf_op jit(solution)/shard_map/pallas_call | solution.py:71
  51.7 1.5 %collective-permute-start.15 = (bf16[1,2,64,1024]{3,2,1,0:T(8,128)(2,1)S(1)}, bf16[1,2,64,1024]{3,2,1,0:T(8,128)(2,1)S(1)}, u32[]{:S(2)}, u32[]{:S(2)}) collective-permute-start(bf16[1,2,64,1024]{3,2,1,0:T(8,128)(2,1)S(1)} %shard_map.71.refs_4_), channel_id=1, source_target_pairs={{0,4},{4,0},{8,12},{12,8},{16,20},{20,16},{24,28},{28,24},{1,5},{5... | collective-permute-start | bytes 786440 | tf_op jit(solution)/shard_map/ppermute | solution.py:35
  53.3 0.0 collective-permute-done.13.refs_0_
  53.3 1.2 %shard_map.72.refs_2_.refs_3_ = f32[2,64,1024]{2,1,0:T(8,128)S(1)} custom-call(bf16[1,64,1536]{2,1,0:T(8,128)(2,1)S(1)} %collective-permute-done.13.refs_0_, bf16[3072,1024]{1,0:T(8,128)(2,1)S(1)} %copy-done, bf16[3072,1024]{1,0:T(8,128)(2,1)S(1)} %collective-permute-done.refs_1_.refs_4_.refs_2_, f32[6,256]{1,0:T(8,128)S(1)} %get-tuple-element.28.refs_2_.refs_5_.refs_3_, ...), custom_call_target="tpu_custom_call" | custom-call | flops 805306368 | bytes 13047808 | tf_op jit(solution)/shard_map/pallas_call | solution.py:71
  54.5 0.6 collective-permute-done.12.refs_1_
  55.1 0.1 shard_map.73.refs_4_.refs_5_
  55.2 0.0 copy-start.1
  55.2 0.0 copy-start.2
  55.2 1.3 %collective-permute-done.11.refs_0_ = bf16[1,64,1536]{2,1,0:T(8,128)(2,1)S(1)} collective-permute-done((bf16[1,64,1536]{2,1,0:T(8,128)(2,1)S(1)}, bf16[1,64,1536]{2,1,0:T(8,128)(2,1)S(1)}, u32[]{:S(2)}, u32[]{:S(2)}) %collective-permute-start.11) | collective-permute-done | bytes 196640 | tf_op jit(solution)/shard_map/ppermute | solution.py:30
  56.5 1.2 %shard_map.74.refs_1_ = f32[2,64,1024]{2,1,0:T(8,128)S(1)} custom-call(bf16[1,64,1536]{2,1,0:T(8,128)(2,1)S(1)} %collective-permute-done.11.refs_0_, bf16[3072,1024]{1,0:T(8,128)(2,1)S(1)} %copy-done, bf16[3072,1024]{1,0:T(8,128)(2,1)S(1)} %collective-permute-done.refs_1_.refs_4_.refs_2_, f32[6,256]{1,0:T(8,128)S(1)} %get-tuple-element.28.refs_2_.refs_5_.refs_3_, ...), custom_call_target="tpu_custom_call" | custom-call | flops 805306368 | bytes 13834240 | tf_op jit(solution)/shard_map/pallas_call | solution.py:71
  57.7 0.9 %collective-permute-done.16.refs_0_ = bf16[2,64,1024]{2,1,0:T(8,128)(2,1)S(1)} collective-permute-done((bf16[2,64,1024]{2,1,0:T(8,128)(2,1)S(1)}, bf16[2,64,1024]{2,1,0:T(8,128)(2,1)S(1)}, u32[]{:S(2)}, u32[]{:S(2)}) %collective-permute-start.16) | collective-permute-done | bytes 262176 | tf_op jit(solution)/shard_map/ppermute | solution.py:30
  58.7 0.1 collective-permute-done.15.refs_2_
  58.7 0.1 shard_map.76
  58.9 0.1 collective-permute-start.18
  59.0 1.6 %collective-permute-start.19 = (bf16[64,1024]{1,0:T(8,128)(2,1)S(1)}, bf16[64,1024]{1,0:T(8,128)(2,1)S(1)}, u32[]{:S(2)}, u32[]{:S(2)}) collective-permute-start(bf16[64,1024]{1,0:T(8,128)(2,1)S(1)} %get-tuple-element.42), channel_id=1, source_target_pairs={{0,9},{1,8},{2,11},{3,10},{4,13},{5,12},{6,15},{7,14},{8,17},{9,16... | collective-permute-start | bytes 393224 | tf_op jit(solution)/shard_map/ppermute | solution.py:61
  60.6 1.6 %collective-permute-start.17 = (bf16[64,1024]{1,0:T(8,128)(2,1)S(1)}, bf16[64,1024]{1,0:T(8,128)(2,1)S(1)}, u32[]{:S(2)}, u32[]{:S(2)}) collective-permute-start(bf16[64,1024]{1,0:T(8,128)(2,1)S(1)} %get-tuple-element.40.refs_3_), channel_id=1, source_target_pairs={{0,8},{1,9},{2,10},{3,11},{4,12},{5,13},{6,14},{7,15},{8,16},{9,17... | collective-permute-start | bytes 393224 | tf_op jit(solution)/shard_map/ppermute | solution.py:61
  62.2 0.2 shard_map.61
  62.4 3.7 %collective-permute-done.19.refs_2_ = bf16[64,1024]{1,0:T(8,128)(2,1)S(1)} collective-permute-done((bf16[64,1024]{1,0:T(8,128)(2,1)S(1)}, bf16[64,1024]{1,0:T(8,128)(2,1)S(1)}, u32[]{:S(2)}, u32[]{:S(2)}) %collective-permute-start.19) | collective-permute-done | bytes 131104 | tf_op jit(solution)/shard_map/ppermute | solution.py:61
  66.1 0.0 collective-permute-done.18.refs_1_
  66.1 0.3 shard_map.77.part
  66.5 3.0 %collective-permute-done.17.last = bf16[64,1024]{1,0:T(8,128)(2,1)S(1)} collective-permute-done((bf16[64,1024]{1,0:T(8,128)(2,1)S(1)}, bf16[64,1024]{1,0:T(8,128)(2,1)S(1)}, u32[]{:S(2)}, u32[]{:S(2)}) %collective-permute-start.17) | collective-permute-done | bytes 131104 | tf_op jit(solution)/shard_map/ppermute | solution.py:61
  69.5 1.0 %shard_map.78 = bf16[256,1024]{1,0:T(8,128)(2,1)} custom-call(bf16[256,1024]{1,0:T(8,128)(2,1)S(1)} %get-tuple-element.32.rhs, bf16[256,256]{1,0:T(8,128)(2,1)S(1)} %get-tuple-element.33.diag, f32[2,64,1024]{2,1,0:T(8,128)S(1)} %get-tuple-element.39.refs_0_.acc, bf16[64,1024]{1,0:T(8,128)(2,1)S(1)} %collective-permute-done.17.last, ...), custom_call_target="tpu_custom_call" | custom-call | flops 33554432 | bytes 2359296 | tf_op jit(solution)/shard_map/pallas_call | solution.py:71
  (8 shorter events, 0.1 us)
Async XLA Ops:
  0.0 7.6 %copy-start = (bf16[3072,1024]{1,0:T(8,128)(2,1)S(1)}, bf16[3072,1024]{1,0:T(8,128)(2,1)}, u32[]{:S(2)}) copy-start(bf16[3072,1024]{1,0:T(8,128)(2,1)} %refs_1_.13) | copy-start | bytes 18874372
  0.0 12.3 %collective-permute-start = (bf16[3072,1024]{1,0:T(8,128)(2,1)}, bf16[3072,1024]{1,0:T(8,128)(2,1)S(1)}, u32[]{:S(2)}, u32[]{:S(2)}) collective-permute-start(bf16[3072,1024]{1,0:T(8,128)(2,1)} %refs_1_.13), channel_id=1, source_target_pairs={{1,0},{0,1},{3,2},{2,3},{5,4},{4,5},{7,6},{6,7},{9,8},{8,9},{11,10... | collective-permute-start | bytes 18874376 | tf_op jit(solution)/shard_map/ppermute | solution.py:51
  1.9 23.6 %collective-permute-start.5 = (bf16[2,64,3072]{2,1,0:T(8,128)(2,1)S(1)}, bf16[2,64,3072]{2,1,0:T(8,128)(2,1)S(1)}, u32[]{:S(2)}, u32[]{:S(2)}) collective-permute-start(bf16[2,64,3072]{2,1,0:T(8,128)(2,1)S(1)} %shard_map.55.refs_2_.refs_0_), channel_id=1, source_target_pairs={{0,2},{1,3},{2,0},{3,1},{4,6},{5,7},{6,4},{7,5},{8,10},{9,11},{10,... | collective-permute-start | bytes 2359304 | tf_op jit(solution)/shard_map/ppermute | solution.py:30
  4.5 0.7 copy-start.3
  7.2 32.5 %collective-permute-start.8 = (bf16[2,64,3072]{2,1,0:T(8,128)(2,1)S(1)}, bf16[2,64,3072]{2,1,0:T(8,128)(2,1)S(1)}, u32[]{:S(2)}, u32[]{:S(2)}) collective-permute-start(bf16[2,64,3072]{2,1,0:T(8,128)(2,1)S(1)} %get-tuple-element.24.refs_3_.refs_0_), channel_id=1, source_target_pairs={{0,2},{1,3},{2,0},{3,1},{4,6},{5,7},{6,4},{7,5},{8,10},{9,11},{10,... | collective-permute-start | bytes 2359304 | tf_op jit(solution)/shard_map/ppermute | solution.py:30
  8.6 9.2 %collective-permute-start.1 = (bf16[2,64,1024]{2,1,0:T(8,128)(2,1)S(1)}, bf16[2,64,1024]{2,1,0:T(8,128)(2,1)S(1)}, u32[]{:S(2)}, u32[]{:S(2)}) collective-permute-start(bf16[2,64,1024]{2,1,0:T(8,128)(2,1)S(1)} %shard_map.57.refs_6_), channel_id=1, source_target_pairs={{0,4},{4,0},{8,12},{12,8},{16,20},{20,16},{24,28},{28,24},{1,5},{5... | collective-permute-start | bytes 786440 | tf_op jit(solution)/shard_map/ppermute | solution.py:35
  13.3 10.1 %collective-permute-start.2 = (bf16[2,64,1024]{2,1,0:T(8,128)(2,1)S(1)}, bf16[2,64,1024]{2,1,0:T(8,128)(2,1)S(1)}, u32[]{:S(2)}, u32[]{:S(2)}) collective-permute-start(bf16[2,64,1024]{2,1,0:T(8,128)(2,1)S(1)} %shard_map.59.refs_7_), channel_id=1, source_target_pairs={{0,4},{4,0},{8,12},{12,8},{16,20},{20,16},{24,28},{28,24},{1,5},{5... | collective-permute-start | bytes 786440 | tf_op jit(solution)/shard_map/ppermute | solution.py:35
  16.2 15.1 %collective-permute-start.3 = (bf16[2,64,1024]{2,1,0:T(8,128)(2,1)S(1)}, bf16[2,64,1024]{2,1,0:T(8,128)(2,1)S(1)}, u32[]{:S(2)}, u32[]{:S(2)}) collective-permute-start(bf16[2,64,1024]{2,1,0:T(8,128)(2,1)S(1)} %get-tuple-element.34), channel_id=1, source_target_pairs={{0,4},{4,0},{8,12},{12,8},{16,20},{20,16},{24,28},{28,24},{1,5},{5... | collective-permute-start | bytes 786440 | tf_op jit(solution)/shard_map/ppermute | solution.py:35
  23.5 10.7 %collective-permute-start.4 = (bf16[2,64,1024]{2,1,0:T(8,128)(2,1)S(1)}, bf16[2,64,1024]{2,1,0:T(8,128)(2,1)S(1)}, u32[]{:S(2)}, u32[]{:S(2)}) collective-permute-start(bf16[2,64,1024]{2,1,0:T(8,128)(2,1)S(1)} %shard_map.62.refs_4_), channel_id=1, source_target_pairs={{0,8},{4,12},{8,16},{12,20},{16,24},{20,28},{24,0},{28,4},{1,9},{5... | collective-permute-start | bytes 786440 | tf_op jit(solution)/shard_map/ppermute | solution.py:30
  27.5 10.2 %collective-permute-start.7 = (bf16[2,64,1024]{2,1,0:T(8,128)(2,1)S(1)}, bf16[2,64,1024]{2,1,0:T(8,128)(2,1)S(1)}, u32[]{:S(2)}, u32[]{:S(2)}) collective-permute-start(bf16[2,64,1024]{2,1,0:T(8,128)(2,1)S(1)} %shard_map.64.refs_6_), channel_id=1, source_target_pairs={{0,24},{4,28},{8,0},{12,4},{16,8},{20,12},{24,16},{28,20},{1,25},{... | collective-permute-start | bytes 786440 | tf_op jit(solution)/shard_map/ppermute | solution.py:30
  29.6 12.1 %collective-permute-start.10 = (bf16[2,64,1024]{2,1,0:T(8,128)(2,1)S(1)}, bf16[2,64,1024]{2,1,0:T(8,128)(2,1)S(1)}, u32[]{:S(2)}, u32[]{:S(2)}) collective-permute-start(bf16[2,64,1024]{2,1,0:T(8,128)(2,1)S(1)} %get-tuple-element.36), channel_id=1, source_target_pairs={{0,4},{4,0},{8,12},{12,8},{16,20},{20,16},{24,28},{28,24},{1,5},{5... | collective-permute-start | bytes 786440 | tf_op jit(solution)/shard_map/ppermute | solution.py:35
  31.3 10.7 %collective-permute-start.9 = (bf16[2,64,1024]{2,1,0:T(8,128)(2,1)S(1)}, bf16[2,64,1024]{2,1,0:T(8,128)(2,1)S(1)}, u32[]{:S(2)}, u32[]{:S(2)}) collective-permute-start(bf16[2,64,1024]{2,1,0:T(8,128)(2,1)S(1)} %get-tuple-element.35.refs_4_), channel_id=1, source_target_pairs={{0,4},{4,0},{8,12},{12,8},{16,20},{20,16},{24,28},{28,24},{1,5},{5... | collective-permute-start | bytes 786440 | tf_op jit(solution)/shard_map/ppermute | solution.py:35
  34.3 15.1 %collective-permute-start.14 = (bf16[1,64,3072]{2,1,0:T(8,128)(2,1)S(1)}, bf16[1,64,3072]{2,1,0:T(8,128)(2,1)S(1)}, u32[]{:S(2)}, u32[]{:S(2)}) collective-permute-start(bf16[1,64,3072]{2,1,0:T(8,128)(2,1)S(1)} %get-tuple-element.25.refs_1_), channel_id=1, source_target_pairs={{0,2},{1,3},{2,0},{3,1},{4,6},{5,7},{6,4},{7,5},{8,10},{9,11},{10,... | collective-permute-start | bytes 1179656 | tf_op jit(solution)/shard_map/ppermute | solution.py:30
  37.7 9.5 %collective-permute-start.6 = (bf16[2,64,1024]{2,1,0:T(8,128)(2,1)S(1)}, bf16[2,64,1024]{2,1,0:T(8,128)(2,1)S(1)}, u32[]{:S(2)}, u32[]{:S(2)}) collective-permute-start(bf16[2,64,1024]{2,1,0:T(8,128)(2,1)S(1)} %shard_map.65.refs_2_.refs_1_), channel_id=1, source_target_pairs={{0,8},{4,12},{8,16},{12,20},{16,24},{20,28},{24,0},{28,4},{1,9},{5... | collective-permute-start | bytes 786440 | tf_op jit(solution)/shard_map/ppermute | solution.py:30
  39.7 13.5 %collective-permute-start.13 = (bf16[1,64,1536]{2,1,0:T(8,128)(2,1)S(1)}, bf16[1,64,1536]{2,1,0:T(8,128)(2,1)S(1)}, u32[]{:S(2)}, u32[]{:S(2)}) collective-permute-start(bf16[1,64,1536]{2,1,0:T(8,128)(2,1)S(1)} %shard_map.70), channel_id=1, source_target_pairs={{0,2},{1,3},{2,0},{3,1},{4,6},{5,7},{6,4},{7,5},{8,10},{9,11},{10,... | collective-permute-start | bytes 589832 | tf_op jit(solution)/shard_map/ppermute | solution.py:30
  43.9 11.1 %collective-permute-start.12 = (bf16[2,64,1024]{2,1,0:T(8,128)(2,1)S(1)}, bf16[2,64,1024]{2,1,0:T(8,128)(2,1)S(1)}, u32[]{:S(2)}, u32[]{:S(2)}) collective-permute-start(bf16[2,64,1024]{2,1,0:T(8,128)(2,1)S(1)} %get-tuple-element.37.refs_2_.refs_1_), channel_id=1, source_target_pairs={{0,8},{4,12},{8,16},{12,20},{16,24},{20,28},{24,0},{28,4},{1,9},{5... | collective-permute-start | bytes 786440 | tf_op jit(solution)/shard_map/ppermute | solution.py:30
  45.3 11.2 %collective-permute-start.11 = (bf16[1,64,1536]{2,1,0:T(8,128)(2,1)S(1)}, bf16[1,64,1536]{2,1,0:T(8,128)(2,1)S(1)}, u32[]{:S(2)}, u32[]{:S(2)}) collective-permute-start(bf16[1,64,1536]{2,1,0:T(8,128)(2,1)S(1)} %shard_map.69), channel_id=1, source_target_pairs={{0,2},{1,3},{2,0},{3,1},{4,6},{5,7},{6,4},{7,5},{8,10},{9,11},{10,... | collective-permute-start | bytes 589832 | tf_op jit(solution)/shard_map/ppermute | solution.py:30
  47.2 11.4 %collective-permute-start.16 = (bf16[2,64,1024]{2,1,0:T(8,128)(2,1)S(1)}, bf16[2,64,1024]{2,1,0:T(8,128)(2,1)S(1)}, u32[]{:S(2)}, u32[]{:S(2)}) collective-permute-start(bf16[2,64,1024]{2,1,0:T(8,128)(2,1)S(1)} %get-tuple-element.38), channel_id=1, source_target_pairs={{0,24},{4,28},{8,0},{12,4},{16,8},{20,12},{24,16},{28,20},{1,25},{... | collective-permute-start | bytes 786440 | tf_op jit(solution)/shard_map/ppermute | solution.py:30
  51.7 7.0 %collective-permute-start.15 = (bf16[1,2,64,1024]{3,2,1,0:T(8,128)(2,1)S(1)}, bf16[1,2,64,1024]{3,2,1,0:T(8,128)(2,1)S(1)}, u32[]{:S(2)}, u32[]{:S(2)}) collective-permute-start(bf16[1,2,64,1024]{3,2,1,0:T(8,128)(2,1)S(1)} %shard_map.71.refs_4_), channel_id=1, source_target_pairs={{0,4},{4,0},{8,12},{12,8},{16,20},{20,16},{24,28},{28,24},{1,5},{5... | collective-permute-start | bytes 786440 | tf_op jit(solution)/shard_map/ppermute | solution.py:35
  55.2 7.0 %copy-start.1 = (bf16[256,1024]{1,0:T(8,128)(2,1)S(1)}, bf16[256,1024]{1,0:T(8,128)(2,1)}, u32[]{:S(2)}) copy-start(bf16[256,1024]{1,0:T(8,128)(2,1)} %rhs.1) | copy-start | bytes 1572868
  55.2 7.0 %copy-start.2 = (bf16[1,256,256]{2,1,0:T(8,128)(2,1)S(1)}, bf16[1,256,256]{2,1,0:T(8,128)(2,1)}, u32[]{:S(2)}) copy-start(bf16[1,256,256]{2,1,0:T(8,128)(2,1)} %diag.1) | copy-start | bytes 393220
  58.9 7.3 %collective-permute-start.18 = (f32[2,64,1024]{2,1,0:T(8,128)S(1)}, f32[2,64,1024]{2,1,0:T(8,128)S(1)}, u32[]{:S(2)}, u32[]{:S(2)}) collective-permute-start(f32[2,64,1024]{2,1,0:T(8,128)S(1)} %get-tuple-element.41), channel_id=1, source_target_pairs={{0,1},{1,0},{2,3},{3,2},{4,5},{5,4},{6,7},{7,6},{8,9},{9,8},{10,11... | collective-permute-start | bytes 1572872 | tf_op jit(solution)/shard_map/ppermute | solution.py:61
  59.0 7.2 %collective-permute-start.19 = (bf16[64,1024]{1,0:T(8,128)(2,1)S(1)}, bf16[64,1024]{1,0:T(8,128)(2,1)S(1)}, u32[]{:S(2)}, u32[]{:S(2)}) collective-permute-start(bf16[64,1024]{1,0:T(8,128)(2,1)S(1)} %get-tuple-element.42), channel_id=1, source_target_pairs={{0,9},{1,8},{2,11},{3,10},{4,13},{5,12},{6,15},{7,14},{8,17},{9,16... | collective-permute-start | bytes 393224 | tf_op jit(solution)/shard_map/ppermute | solution.py:61
  60.6 8.9 %collective-permute-start.17 = (bf16[64,1024]{1,0:T(8,128)(2,1)S(1)}, bf16[64,1024]{1,0:T(8,128)(2,1)S(1)}, u32[]{:S(2)}, u32[]{:S(2)}) collective-permute-start(bf16[64,1024]{1,0:T(8,128)(2,1)S(1)} %get-tuple-element.40.refs_3_), channel_id=1, source_target_pairs={{0,8},{1,9},{2,10},{3,11},{4,12},{5,13},{6,14},{7,15},{8,16},{9,17... | collective-permute-start | bytes 393224 | tf_op jit(solution)/shard_map/ppermute | solution.py:61

commit v5 on v4

--- a/solution.py
+++ b/solution.py
@@ -20,8 +20,8 @@
 FIRST2 = False
 DIRECT_N, DIRECT_F = False, False
 ORDER = (
-    "rest", "p0a", "p0b", "p1a", "p1b", "n2", "f24", "n3", "n1", "gy1",
-    "a3n", "f35", "gz1", "a1n", "f0", "f1a", "a2f", "f1", "a3f", "col",
+    "rest", "p0a", "p0b", "p1a", "p1b", "n2", "f24", "n3", "n1", "a3n",
+    "f03", "a1n", "coln", "ff", "a2f", "early", "colf", "fla", "flb",
 )
 
 
@@ -88,6 +88,7 @@
         copies = []
         for group, dst in zip(groups, dsts):
             for i, (k, begin, end) in enumerate(group):
+                k = tile_of(k, tiles.shape[0])
                 columns = pl.ds(begin, end - begin)
                 for first in range(0, rows, rows // PIECES):
                     cut = pl.ds(first, rows // PIECES)
@@ -114,6 +115,17 @@
 
 def on_odd():
     return lax.rem(lax.axis_index("col"), 2) == 1
+
+
+def on_swap():
+    if lax.axis_size("col") % 4:
+        return jnp.bool_(False)
+    return lax.rem(lax.div(lax.axis_index("col"), 2), 2) == 1
+
+
+def tile_of(k, hops):
+    low, high = (1, hops - 1) if k == "first" else (hops - 1, 1)
+    return jnp.where(on_swap(), low, high) if isinstance(k, str) else k
 
 
 def gate(block, *earlier):
@@ -151,8 +163,8 @@
     y24 = [across(s, "rhs") for s in s24]
     others = half_gather(solution, "rhs")[1:]
     cut_at = depth * SPLIT // 4
-    last_tile = [[(1, 0, cut_at)], [(1, cut_at, depth)]] if SPLIT else [[(1, 0, depth)]]
-    order = (3, 5, 0, 1)
+    last_tile = [[("last", 0, cut_at)], [("last", cut_at, depth)]] if SPLIT else [[("last", 0, depth)]]
+    order = (0, 3, "first", "last")
     sols = [solution, *others]
     v["token"] = s24[-1]
 
@@ -169,22 +181,15 @@
     y, taken = {}, []
 
     def rest():
-        s35, s0, *s1, v["weights"] = take(tiles, [[(3, 0, depth), (5, 0, depth)], [(0, 0, depth)]] + last_tile, v["token"],
-                                          weights=tile_list)
-        y[35] = across(s35, "rhs")
-        y[0] = s0 if "gy0" in ORDER else across(s0, "rhs")
-        y[1] = [s if g in ORDER else across(s, "rhs") for g, s in zip(("gy1", "gz1"), s1)]
-        taken.extend([s35, s0, *s1])
-        v["token"] = s35
-
-    def gy0():
-        y[0] = across(gate(y[0], v["token"]), "rhs")
-
-    def gy1():
-        y[1][0] = across(gate(y[1][0], v["token"]), "rhs")
-
-    def gz1():
-        y[1][1] = across(gate(y[1][1], v["token"]), "rhs")
+        groups = [[(0, 0, depth), (3, 0, depth)], [("first", 0, depth)]] + last_tile
+        *got, v["weights"] = take(tiles, groups, v["token"], weights=tile_list)
+        for name, s in zip(("g03", "gf", "gla", "glb"), got):
+            y[name] = s if name in ORDER else across(s, "rhs")
+        taken.extend(got)
+        v["token"] = got[0]
+
+    def gated(name):
+        y[name] = across(gate(y[name], v["token"]), "rhs")
 
     near_got, near_own, near_give0 = [], [], []
 
@@ -211,16 +216,19 @@
             lefts, (sol, weights), outs = refs[:n], refs[n:n + 2], refs[n + 3 + joins:]
             whole = [r[i] for r in lefts[:2] for i in range(r.shape[0])]
             left = jnp.concatenate(whole + [jnp.concatenate([r[0] for r in lefts[2:]], axis=1)])
+            swap = on_swap()
             for cut in cuts:
                 total = jnp.dot(left, sol[:, cut], preferred_element_type=F32)
-                for at, k in enumerate(order):
-                    term = total[at * quarter:(at + 1) * quarter] * weights[k:k + 1, :total.shape[1]]
-                    if k in owns:
-                        outs[0][owns.index(k), :, cut] = term
-                    elif joins:
-                        outs[1][part, :, cut] = term.astype(BF16)
-                    else:
-                        outs[1][:, cut] = term.astype(BF16)
+                zero, three, first, last = [
+                    total[at * quarter:(at + 1) * quarter] * weights[pl.ds(tile_of(k, hops), 1), :total.shape[1]]
+                    for at, k in enumerate(order)]
+                outs[0][0, :, cut] = three
+                outs[0][1, :, cut] = jnp.where(swap, last, first)
+                outs[0][2, :, cut] = jnp.where(swap, first, last)
+                if joins:
+                    outs[1][part, :, cut] = zero.astype(BF16)
+                else:
+                    outs[1][:, cut] = zero.astype(BF16)
             for p in range(joins):
                 outs[1][p] = refs[n + 2 + p][...]
 
@@ -272,7 +280,8 @@
                 for cut in cuts:
                     total = jnp.dot(left, sol_ref[deep, cut], preferred_element_type=F32)
                     for i, k in enumerate(ks):
-                        term = total[i * quarter:(i + 1) * quarter] * weights[k:k + 1, :total.shape[1]]
+                        term = total[i * quarter:(i + 1) * quarter]
+                        term = term * weights[pl.ds(tile_of(k, hops), 1), :total.shape[1]]
                         epilogue(out, more, is_odd, i, part, cut, term)
 
         args = [*far, *sols, v["weights"], *extra, v["token"]]
@@ -364,17 +373,15 @@
         d1, d3 = chained(body, [one, one], [*near_own, *near_got, *zeros()] + ([] if DIRECT_N else [v["d2n"]]))
         v["d1n"], v["d3n"] = shift(d1, "col", 2), shift(d3, "col", 6)
 
-    def f35():
-        def far35(out, more, is_odd, i, part, cut, total):
+    def f03():
+        def far03(out, more, is_odd, i, part, cut, total):
             r2, r4 = [m[part, :, cut].astype(F32) for m in more]
-            if i == 0:
+            if i == 1:
                 total = total + jnp.where(is_odd, r4, r2)
-            else:
-                total = total + jnp.where(is_odd, 0.0, r4)
             out[i][part, :, cut] = total.astype(BF16)
 
-        d2, d3 = products(y[35], (3, 5), far35, [one, one], v["got_far"])
-        v["d2f"], v["d3f"] = send2(d2, DIRECT_F), shift(d3, "col", 6)
+        give, d2 = products(y["g03"], (0, 3), far03, [one, one], v["got_far"])
+        v["got_last"], v["d2f"] = pair_swap(give, "col"), shift(d2, "col", 2)
 
     def a3n():
         n = len(zeros())
@@ -400,64 +407,76 @@
 
         v["all_n"], = chained(body, [wide_one], ins)
 
-    def f0():
-        v["got_last"] = pair_swap(products(y[0], (0,), store, [pinned(1, *strip)], [])[0], "col")
-
-    def f1a():
-        v["first"], = products(y[1][0], (1,), plain, [wide_one], [], slice(0, cut_at))
+    def ff():
+        v["raw_f"], = products(y["gf"], ("first",), plain, [wide_one], [])
+
+    def send(parts, last):
+        n = lax.axis_size("col")
+        swaps = [n % 4 == 0 and c // 2 % 2 == 1 for c in range(n)]
+        far_off = [c + (2 if last != swap else hops) for c, swap in enumerate(swaps)]
+        out = []
+        for j, part in enumerate(parts):
+            route = [(c * size + r, far_off[c] % n * size + inner(r, j, half)) for c in range(n) for r in range(size)]
+            out.append(lax.ppermute(part, ("col", "rhs"), route))
+        return out
 
     def a2f():
-        ins = [v["got_far"][0]] + ([] if DIRECT_F else [v["d2f"]]) + [v[k] for k in ("first",) if k in v]
-
-        def body(gf, *refs):
+        def body(d2, r2, out):
             for p in range(half):
-                total = jnp.where(on_odd(), gf[p].astype(F32), 0.0)
-                for ref in refs[:-1]:
-                    total = total + ref[p].astype(F32)
-                refs[-1][p] = total
-
-        v["pre"], = chained(body, [wide_one], ins)
-
-    def f1():
-        deep = slice(cut_at, depth) if SPLIT else slice(None)
-        v["added"] = "pre" in v
-        if v["added"]:
-            v["raw"], = products(y[1][-1], (1,), added, [wide_one], [v["pre"]], deep)
+                out[p] = d2[p].astype(F32) + jnp.where(on_odd(), r2[p].astype(F32), 0.0)
+
+        v["pre2"], = chained(body, [wide_one], [v["d2f"], v["got_far"][0]])
+
+    def early():
+        def body(raw, r4, r0, pre2, *refs):
+            outs, pre = refs[:half], refs[half]
+            is_odd, swap = on_odd(), on_swap()
+            for p in range(half):
+                one = pre2[p] + jnp.where(is_odd, 0.0, r0[p].astype(F32))
+                three = jnp.where(is_odd, 0.0, r4[p].astype(F32))
+                outs[p][...] = (raw[p] + jnp.where(swap, one, three)).astype(BF16)
+                pre[p] = jnp.where(swap, three, one)
+
+        *outs, v["pre"] = chained(body, [flat] * half + [wide_one],
+                                  [v["raw_f"], v["got_far"][1], v["got_last"], v["pre2"]])
+        v["early_in"] = send(outs, False)
+
+    def coln():
+        def body(total, *outs):
+            for part in range(half):
+                outs[part][...] = total[part]
+
+        v["sums_n"] = to_columns(chained(body, [pinned(quarter, cols, dtype=F32)] * half, [v["all_n"]]), 0)
+
+    def colf():
+        def body(r0, *outs):
+            for part in range(half):
+                outs[part][...] = jnp.where(on_odd(), r0[part].astype(F32), 0.0).astype(BF16)
+
+        v["sums_f"] = to_columns(chained(body, [flat] * half, [v["got_last"]]), 0)
+
+    def fla():
+        v["first"], = products(y["gla"], ("last",), plain, [wide_one], [], slice(0, cut_at))
+
+    def flb():
+        def added(out, more, is_odd, i, part, cut, total):
+            for m in more:
+                total = total + m[part, :, cut]
+            out[part][:, cut] = total.astype(BF16)
+
+        if SPLIT:
+            v["lasts"] = products(y["glb"], ("last",), added, [flat] * half, [v["first"], v["pre"]], slice(cut_at, depth))
         else:
-            v["raw"], = products(y[1][-1], (1,), plain, [wide_one], [], deep)
-
-    def a3f():
-        def body(d3, out):
-            out[...] = d3[...].astype(F32)
-
-        v["sum_f"], = chained(body, [wide_one], [v["d3f"]])
-
-    def col():
-        early, added = "sum_f" in v, v["added"]
-
-        def collect(total, raw, gl, d3far, *refs):
-            sums, lasts = refs[-2 * half:-half], refs[-half:]
-            is_odd = on_odd()
-            for part in range(half):
-                r0 = gl[0, part].astype(F32)
-                last = raw[part] + jnp.where(is_odd, 0.0, r0)
-                lasts[part][...] = (last if added else last + refs[0][part]).astype(BF16)
-                sums[part][0] = total[part]
-                sums[part][1] = d3far[part].astype(F32) + jnp.where(is_odd, r0, 0.0)
-                if DIRECT_F:
-                    sums[part][1] += refs[0 if added else 1][part].astype(F32)
-
-        outs = chained(collect, [pinned(2, quarter, cols, dtype=F32)] * half + [flat] * half,
-                       [v["all_n"], v["raw"], v["got_last"], v["sum_f"] if early else v["d3f"]]
-                       + ([] if added else [v["pre"]]) + ([v["d2f"]] if DIRECT_F else []))
-        sums, v["lasts"] = outs[:half], outs[half:]
-        v["sums"] = to_columns(sums, 0)
-        v["last_in"] = to_columns(v["lasts"], 2)
-
-    nodes = dict(gy0=gy0, gy1=gy1, gz1=gz1, rest=rest, p0a=p0a, p0b=p0b, p1a=p1a, p1b=p1b, n1p=n1p, n1q=n1q, f24=f24, n2=n2, n3=n3, n23=n23, n1=n1, n13=n13, f35=f35, a3n=a3n, a1n=a1n, f0=f0,
-                 f1a=f1a, a2f=a2f, f1=f1, a3f=a3f, col=col)
+            v["lasts"] = products(y["gla"], ("last",), added, [flat] * half, [v["pre"]])
+        v["last_in"] = send(v["lasts"], True)
+
+    nodes = dict(rest=rest, p0a=p0a, p0b=p0b, p1a=p1a, p1b=p1b, f24=f24, n2=n2, n3=n3, n23=n23, n1=n1, f03=f03, a3n=a3n,
+                 a1n=a1n, ff=ff, a2f=a2f, early=early, coln=coln, colf=colf, fla=fla, flb=flb)
     for name in ORDER:
-        nodes[name]()
+        if name in y:
+            gated(name)
+        else:
+            nodes[name]()
 
     places = [(0, j) for j in range(half)] + [(1, j) for j in range(1, half)] + [(1, 0)]
 
@@ -478,25 +497,36 @@
     rhs_local, diag_local = call(arrange, [pinned(rows, cols), pinned(rows, rows)], [VMEM, VMEM, ANY],
                                  [rhs_block, diag_inverse, near_own[-1]], flops=2 * rows * rows * rows)
 
-    early = rows - quarter
-    sums_in, last_in = v["sums"], v["last_in"]
-
-    def most(rhs, diag, *refs):
-        acc, last, out = refs[:half], refs[half:2 * half - 1], refs[-1]
-        total = jnp.concatenate([a[0] for a in acc] + [a[1] + l[...].astype(F32) for a, l in zip(acc[1:], last)])
-        remaining = (rhs[:early].astype(F32) - total).astype(BF16)
-        out[...] = jnp.dot(diag[:, :early], remaining, preferred_element_type=F32)
-
-    partial, = call(most, [pinned(rows, cols, dtype=F32)], [VMEM] * (2 + 2 * half - 1) + [ANY],
-                    [rhs_local, diag_local, *sums_in, *last_in[1:], v["lasts"][0]], flops=2 * rows * early * cols)
-
-    def final(rhs, diag, acc, last, part, out, block, sems):
-        total = acc[1] + last[...].astype(F32)
-        remaining = (rhs[early:].astype(F32) - total).astype(BF16)
+    most_rows = rows - quarter
+    early_in, last_in = v["early_in"], v["last_in"]
+
+    def gather(*refs):
+        near, stay, far, out = refs[:half], refs[half:2 * half], refs[2 * half:3 * half], refs[-1]
+        for j in range(half):
+            out[j * quarter:(j + 1) * quarter] = near[j][...]
+        for j in range(half):
+            at = (half + (j - 1) % half) * quarter
+            out[at:at + quarter] = stay[j][...].astype(F32) + far[j][...].astype(F32)
+
+    known, = chained(gather, [pinned(rows, cols, dtype=F32)], [*v["sums_n"], *v["sums_f"], *early_in])
+
+    def most(rhs, diag, known, *refs):
+        last, out = refs[:half - 1], refs[-1]
+        total = jnp.concatenate([known[:rows // 2]] + [known[(half + j) * quarter:(half + j + 1) * quarter]
+                                                      + l[...].astype(F32) for j, l in enumerate(last)])
+        remaining = (rhs[:most_rows].astype(F32) - total).astype(BF16)
+        out[...] = jnp.dot(diag[:, :most_rows], remaining, preferred_element_type=F32)
+
+    partial, = chained(most, [pinned(rows, cols, dtype=F32)], [rhs_local, diag_local, known, *last_in[1:]],
+                       flops=2 * rows * most_rows * cols)
+
+    def final(rhs, diag, known, last, part, out, block, sems):
+        total = known[most_rows:] + last[...].astype(F32)
+        remaining = (rhs[most_rows:].astype(F32) - total).astype(BF16)
         copies = []
         for i in range(size):
             cut = slice(i * quarter, (i + 1) * quarter)
-            term = jnp.dot(diag[cut, early:], remaining, preferred_element_type=F32)
+            term = jnp.dot(diag[cut, most_rows:], remaining, preferred_element_type=F32)
             block[cut] = (part[cut] + term).astype(BF16)
             copies.append(pltpu.make_async_copy(block.at[cut], out.at[cut], sems.at[i]))
             copies[-1].start()
@@ -504,7 +534,7 @@
             c.wait()
 
     return call(final, [jax.ShapeDtypeStruct((rows, cols), BF16)], [VMEM] * 5,
-                [rhs_local, diag_local, sums_in[0], last_in[0], partial], flops=2 * rows * quarter * cols,
+                [rhs_local, diag_local, known, last_in[0], partial], flops=2 * rows * quarter * cols,
                 out_specs=[ANY], scratch_shapes=[pltpu.VMEM((rows, cols), BF16), pltpu.SemaphoreType.DMA((size,))])[0]
 
 def solution(mesh):

time: 70.8 us -> 69.9 us (0.987)
  waiting for transfers between devices: 23.1 us -> 21 us
  starting transfers between devices: 26.6 us -> 27.5 us
    ppermute x3 -> x2, waiting for transfers between devices: 6.74 us -> 0.01 us  [to_columns(): lax.ppermute(block, ('col', 'rhs'), route)]
    ppermute x0 -> x4, starting transfers between devices: none -> 6.14 us  [send(): out.append(lax.ppermute(part, ('col', 'rhs'), route))]
    ppermute x0 -> x4, waiting for transfers between devices: none -> 5.86 us  [send(): out.append(lax.ppermute(part, ('col', 'rhs'), route))]
    ppermute x3 -> x2, starting transfers between devices: 3.26 us -> 0.14 us  [to_columns(): lax.ppermute(block, ('col', 'rhs'), route)]
    ppermute x10 -> x9, waiting for transfers between devices: 9.87 us -> 6.75 us  [shift(): lax.ppermute(block, axis, [(i, (i + distance) % size) for i in range(size)])]
    ppermute x10 -> x9, starting transfers between devices: 15.2 us -> 13.1 us  [shift(): lax.ppermute(block, axis, [(i, (i + distance) % size) for i in range(size)])]
    ppermute x6, waiting for transfers between devices: 6.49 us -> 8.4 us  [pair_swap(): return lax.ppermute(block, axis, [(i, i ^ 1) for i in range(size)])]
  transfers between devices with their start and end apart: 20 -> 22, of which waited for: 13 -> 11; matrix products, arithmetic and copies ran while one was open for 0% -> 0% of each run, Pallas kernels for 27% -> 27%
where the time goes in v5:
time: 69.9 us; the launch traced here: 69.7 us
  starting transfers between devices  27.5 us (39%)
  waiting for transfers between devices  21 us (30%)
  Pallas kernels  20.2 us (29%)
    pallas_call x24, Pallas kernels, call(): pl.pallas_call(body, out_shape=outs, in_specs=specs, out_specs=out_specs...  20.2 us
    ppermute x9, starting transfers between devices, shift(): lax.ppermute(block, axis, [(i, (i + distance) % size) for i in range(size)])  13.1 us
    ppermute x6, waiting for transfers between devices, pair_swap(): return lax.ppermute(block, axis, [(i, i ^ 1) for i in range(size)])  8.4 us
    ppermute x6, starting transfers between devices, pair_swap(): return lax.ppermute(block, axis, [(i, i ^ 1) for i in range(size)])  7.63 us
    ppermute x9, waiting for transfers between devices, shift(): lax.ppermute(block, axis, [(i, (i + distance) % size) for i in range(size)])  6.75 us
    ppermute x4, starting transfers between devices, send(): out.append(lax.ppermute(part, ('col', 'rhs'), route))  6.14 us
    ppermute x4, waiting for transfers between devices, send(): out.append(lax.ppermute(part, ('col', 'rhs'), route))  5.86 us
  transfers between devices with their start and end apart: 22, of which 11 were waited for; matrix products, arithmetic and copies ran while one was open for 0% of the time, Pallas kernels for 27%

profile of v5, /device:TPU:0, one launch (start us, length us, event | category | flops | bytes accessed | tf_op | source)
XLA Modules:
  0.0 69.7 jit_solution(7966903507373834750)
XLA Ops:
  0.0 0.5 collective-permute-start
  0.5 1.5 %shard_map.55.refs_2_.refs_0_ = bf16[2,64,3072]{2,1,0:T(8,128)(2,1)S(1)} custom-call(bf16[6,64,3072]{2,1,0:T(8,128)(2,1)} %bitcast.1), custom_call_target="tpu_custom_call" | custom-call | bytes 2359296 | tf_op jit(solution)/shard_map/pallas_call | solution.py:71
  1.9 2.5 %collective-permute-start.5 = (bf16[2,64,3072]{2,1,0:T(8,128)(2,1)S(1)}, bf16[2,64,3072]{2,1,0:T(8,128)(2,1)S(1)}, u32[]{:S(2)}, u32[]{:S(2)}) collective-permute-start(bf16[2,64,3072]{2,1,0:T(8,128)(2,1)S(1)} %shard_map.55.refs_2_.refs_0_), channel_id=1, source_target_pairs={{0,2},{1,3},{2,0},{3,1},{4,6},{5,7},{6,4},{7,5},{8,10},{9,11},{10,... | collective-permute-start | bytes 2359304 | tf_op jit(solution)/shard_map/ppermute | solution.py:30
  4.5 0.7 copy-done.3
  5.1 2.1 %shard_map.56 = (bf16[2,64,3072]{2,1,0:T(8,128)(2,1)S(1)}, bf16[1,64,3072]{2,1,0:T(8,128)(2,1)S(1)}, bf16[1,64,1536]{2,1,0:T(8,128)(2,1)S(1)}, bf16[1,64,1536]{2,1,0:T(8,128)(2,1)S(1)}, f32[6,256]{1,0:T(8,128)S(1)}) custom-call(bf16[6,64,3072]{2,1,0:T(8,128)(2,1)} %bitcast.2, s32[1,6]{1,0:T(1,128)S(1)} %copy-done.3, ...), custom_call_target="tpu_custom_call" | custom-call | bytes 3145752 | tf_op jit(solution)/shard_map/pallas_call | solution.py:71
  7.2 0.4 collective-permute-start.8
  7.6 1.0 %shard_map.57.refs_6_ = bf16[2,64,1024]{2,1,0:T(8,128)(2,1)S(1)} custom-call(bf16[2,64,3072]{2,1,0:T(8,128)(2,1)S(1)} %shard_map.55.refs_2_.refs_0_, bf16[3072,1024]{1,0:T(8,128)(2,1)S(1)} %copy-done, f32[6,256]{1,0:T(8,128)S(1)} %get-tuple-element.33.refs_2_.refs_5_.refs_3_, bf16[2,64,3072]{2,1,0:T(8,128)(2,1)S(1)} %get-tuple-element.29.refs_3_.refs_0_), custom_call_target="tpu_custom_call" | custom-call | flops 805306368 | bytes 7870464 | tf_op jit(solution)/shard_map/pallas_call | solution.py:71
  8.6 1.9 %collective-permute-start.1 = (bf16[2,64,1024]{2,1,0:T(8,128)(2,1)S(1)}, bf16[2,64,1024]{2,1,0:T(8,128)(2,1)S(1)}, u32[]{:S(2)}, u32[]{:S(2)}) collective-permute-start(bf16[2,64,1024]{2,1,0:T(8,128)(2,1)S(1)} %shard_map.57.refs_6_), channel_id=1, source_target_pairs={{0,4},{4,0},{8,12},{12,8},{16,20},{20,16},{24,28},{28,24},{1,5},{5... | collective-permute-start | bytes 786440 | tf_op jit(solution)/shard_map/ppermute | solution.py:35
  10.5 1.8 %shard_map.58 = (f32[3,64,1024]{2,1,0:T(8,128)S(1)}, bf16[64,1024]{1,0:T(8,128)(2,1)S(1)}) custom-call(bf16[2,64,3072]{2,1,0:T(8,128)(2,1)S(1)} %get-tuple-element.29.refs_3_.refs_0_, bf16[1,64,3072]{2,1,0:T(8,128)(2,1)S(1)} %get-tuple-element.30.refs_1_, bf16[1,64,1536]{2,1,0:T(8,128)(2,1)S(1)} %get-tuple-element.31.refs_2_, ...), custom_call_target="tpu_custom_call" | custom-call | flops 1610612736 | bytes 8132608 | tf_op jit(solution)/shard_map/pallas_call | solution.py:71
  12.3 1.0 %shard_map.59.refs_7_ = bf16[2,64,1024]{2,1,0:T(8,128)(2,1)S(1)} custom-call(bf16[2,64,3072]{2,1,0:T(8,128)(2,1)S(1)} %shard_map.55.refs_2_.refs_0_, bf16[3072,1024]{1,0:T(8,128)(2,1)S(1)} %collective-permute-done.refs_1_.refs_4_.refs_2_, f32[6,256]{1,0:T(8,128)S(1)} %get-tuple-element.33.refs_2_.refs_5_.refs_3_, ...), custom_call_target="tpu_custom_call" | custom-call | flops 805306368 | bytes 7870464 | tf_op jit(solution)/shard_map/pallas_call | solution.py:71
  13.4 1.0 %collective-permute-start.2 = (bf16[2,64,1024]{2,1,0:T(8,128)(2,1)S(1)}, bf16[2,64,1024]{2,1,0:T(8,128)(2,1)S(1)}, u32[]{:S(2)}, u32[]{:S(2)}) collective-permute-start(bf16[2,64,1024]{2,1,0:T(8,128)(2,1)S(1)} %shard_map.59.refs_7_), channel_id=1, source_target_pairs={{0,4},{4,0},{8,12},{12,8},{16,20},{20,16},{24,28},{28,24},{1,5},{5... | collective-permute-start | bytes 786440 | tf_op jit(solution)/shard_map/ppermute | solution.py:35
  14.4 1.8 %shard_map.60 = (f32[3,64,1024]{2,1,0:T(8,128)S(1)}, bf16[2,64,1024]{2,1,0:T(8,128)(2,1)S(1)}) custom-call(bf16[2,64,3072]{2,1,0:T(8,128)(2,1)S(1)} %get-tuple-element.29.refs_3_.refs_0_, bf16[1,64,3072]{2,1,0:T(8,128)(2,1)S(1)} %get-tuple-element.30.refs_1_, bf16[1,64,1536]{2,1,0:T(8,128)(2,1)S(1)} %get-tuple-element.31.refs_2_, ...), custom_call_target="tpu_custom_call" | custom-call | flops 1610612736 | bytes 8263680 | tf_op jit(solution)/shard_map/pallas_call | solution.py:71
  16.2 1.1 %collective-permute-start.3 = (bf16[2,64,1024]{2,1,0:T(8,128)(2,1)S(1)}, bf16[2,64,1024]{2,1,0:T(8,128)(2,1)S(1)}, u32[]{:S(2)}, u32[]{:S(2)}) collective-permute-start(bf16[2,64,1024]{2,1,0:T(8,128)(2,1)S(1)} %get-tuple-element.39), channel_id=1, source_target_pairs={{0,4},{4,0},{8,12},{12,8},{16,20},{20,16},{24,28},{28,24},{1,5},{5... | collective-permute-start | bytes 786440 | tf_op jit(solution)/shard_map/ppermute | solution.py:35
  17.3 0.5 collective-permute-done.1.refs_2_
  17.8 5.6 %collective-permute-done.2.refs_3_ = bf16[2,64,1024]{2,1,0:T(8,128)(2,1)S(1)} collective-permute-done((bf16[2,64,1024]{2,1,0:T(8,128)(2,1)S(1)}, bf16[2,64,1024]{2,1,0:T(8,128)(2,1)S(1)}, u32[]{:S(2)}, u32[]{:S(2)}) %collective-permute-start.2) | collective-permute-done | bytes 262176 | tf_op jit(solution)/shard_map/ppermute | solution.py:35
  23.5 0.1 shard_map.62.refs_4_
  23.5 2.0 %collective-permute-start.4 = (bf16[2,64,1024]{2,1,0:T(8,128)(2,1)S(1)}, bf16[2,64,1024]{2,1,0:T(8,128)(2,1)S(1)}, u32[]{:S(2)}, u32[]{:S(2)}) collective-permute-start(bf16[2,64,1024]{2,1,0:T(8,128)(2,1)S(1)} %shard_map.62.refs_4_), channel_id=1, source_target_pairs={{0,8},{4,12},{8,16},{12,20},{16,24},{20,28},{24,0},{28,4},{1,9},{5... | collective-permute-start | bytes 786440 | tf_op jit(solution)/shard_map/ppermute | solution.py:30
  25.5 1.9 %shard_map.63 = (bf16[2,64,1024]{2,1,0:T(8,128)(2,1)S(1)}, bf16[2,64,1024]{2,1,0:T(8,128)(2,1)S(1)}) custom-call(bf16[2,64,3072]{2,1,0:T(8,128)(2,1)S(1)} %collective-permute-done.5.refs_0_, bf16[3072,1024]{1,0:T(8,128)(2,1)S(1)} %copy-done, bf16[3072,1024]{1,0:T(8,128)(2,1)S(1)} %collective-permute-done.refs_1_.refs_4_.refs_2_, ...), custom_call_target="tpu_custom_call" | custom-call | flops 1610612736 | bytes 13637632 | tf_op jit(solution)/shard_map/pallas_call | solution.py:71
  27.4 0.1 shard_map.64.refs_6_
  27.5 2.1 %collective-permute-start.7 = (bf16[2,64,1024]{2,1,0:T(8,128)(2,1)S(1)}, bf16[2,64,1024]{2,1,0:T(8,128)(2,1)S(1)}, u32[]{:S(2)}, u32[]{:S(2)}) collective-permute-start(bf16[2,64,1024]{2,1,0:T(8,128)(2,1)S(1)} %shard_map.64.refs_6_), channel_id=1, source_target_pairs={{0,24},{4,28},{8,0},{12,4},{16,8},{20,12},{24,16},{28,20},{1,25},{... | collective-permute-start | bytes 786440 | tf_op jit(solution)/shard_map/ppermute | solution.py:30
  29.6 1.7 %collective-permute-start.10 = (bf16[2,64,1024]{2,1,0:T(8,128)(2,1)S(1)}, bf16[2,64,1024]{2,1,0:T(8,128)(2,1)S(1)}, u32[]{:S(2)}, u32[]{:S(2)}) collective-permute-start(bf16[2,64,1024]{2,1,0:T(8,128)(2,1)S(1)} %get-tuple-element.41), channel_id=1, source_target_pairs={{0,4},{4,0},{8,12},{12,8},{16,20},{20,16},{24,28},{28,24},{1,5},{5... | collective-permute-start | bytes 786440 | tf_op jit(solution)/shard_map/ppermute | solution.py:35
  31.3 0.3 collective-permute-start.9
  31.6 2.6 %collective-permute-done.4.refs_5_ = bf16[2,64,1024]{2,1,0:T(8,128)(2,1)S(1)} collective-permute-done((bf16[2,64,1024]{2,1,0:T(8,128)(2,1)S(1)}, bf16[2,64,1024]{2,1,0:T(8,128)(2,1)S(1)}, u32[]{:S(2)}, u32[]{:S(2)}) %collective-permute-start.4) | collective-permute-done | bytes 262176 | tf_op jit(solution)/shard_map/ppermute | solution.py:30
  34.3 1.6 %collective-permute-start.13 = (bf16[1,64,3072]{2,1,0:T(8,128)(2,1)S(1)}, bf16[1,64,3072]{2,1,0:T(8,128)(2,1)S(1)}, u32[]{:S(2)}, u32[]{:S(2)}) collective-permute-start(bf16[1,64,3072]{2,1,0:T(8,128)(2,1)S(1)} %get-tuple-element.30.refs_1_), channel_id=1, source_target_pairs={{0,2},{1,3},{2,0},{3,1},{4,6},{5,7},{6,4},{7,5},{8,10},{9,11},{10,... | collective-permute-start | bytes 1179656 | tf_op jit(solution)/shard_map/ppermute | solution.py:30
  35.9 0.1 shard_map.65.refs_2_
  36.0 1.7 %collective-permute-done.7.refs_0_ = bf16[2,64,1024]{2,1,0:T(8,128)(2,1)S(1)} collective-permute-done((bf16[2,64,1024]{2,1,0:T(8,128)(2,1)S(1)}, bf16[2,64,1024]{2,1,0:T(8,128)(2,1)S(1)}, u32[]{:S(2)}, u32[]{:S(2)}) %collective-permute-start.7) | collective-permute-done | bytes 262176 | tf_op jit(solution)/shard_map/ppermute | solution.py:30
  37.7 0.6 collective-permute-start.6
  38.3 0.1 shard_map.66.refs_6_.refs_1_
  38.4 1.3 %collective-permute-done.8.refs_0_ = bf16[2,64,3072]{2,1,0:T(8,128)(2,1)S(1)} collective-permute-done((bf16[2,64,3072]{2,1,0:T(8,128)(2,1)S(1)}, bf16[2,64,3072]{2,1,0:T(8,128)(2,1)S(1)}, u32[]{:S(2)}, u32[]{:S(2)}) %collective-permute-start.8) | collective-permute-done | bytes 786464 | tf_op jit(solution)/shard_map/ppermute | solution.py:30
  39.7 2.3 %collective-permute-done.9.refs_4_.refs_1_ = bf16[2,64,1024]{2,1,0:T(8,128)(2,1)S(1)} collective-permute-done((bf16[2,64,1024]{2,1,0:T(8,128)(2,1)S(1)}, bf16[2,64,1024]{2,1,0:T(8,128)(2,1)S(1)}, u32[]{:S(2)}, u32[]{:S(2)}) %collective-permute-start.9) | collective-permute-done | bytes 262176 | tf_op jit(solution)/shard_map/ppermute | solution.py:35
  42.0 1.9 %shard_map.67 = (bf16[2,64,1024]{2,1,0:T(8,128)(2,1)S(1)}, bf16[2,64,1024]{2,1,0:T(8,128)(2,1)S(1)}) custom-call(bf16[2,64,3072]{2,1,0:T(8,128)(2,1)S(1)} %collective-permute-done.8.refs_0_, bf16[3072,1024]{1,0:T(8,128)(2,1)S(1)} %copy-done, bf16[3072,1024]{1,0:T(8,128)(2,1)S(1)} %collective-permute-done.refs_1_.refs_4_.refs_2_, ...), custom_call_target="tpu_custom_call" | custom-call | flops 1610612736 | bytes 14424064 | tf_op jit(solution)/shard_map/pallas_call | solution.py:71
  43.9 0.2 collective-permute-start.14
  44.1 1.6 %collective-permute-start.12 = (bf16[2,64,1024]{2,1,0:T(8,128)(2,1)S(1)}, bf16[2,64,1024]{2,1,0:T(8,128)(2,1)S(1)}, u32[]{:S(2)}, u32[]{:S(2)}) collective-permute-start(bf16[2,64,1024]{2,1,0:T(8,128)(2,1)S(1)} %get-tuple-element.42.refs_2_), channel_id=1, source_target_pairs={{0,4},{4,0},{8,12},{12,8},{16,20},{20,16},{24,28},{28,24},{1,5},{5... | collective-permute-start | bytes 786440 | tf_op jit(solution)/shard_map/ppermute | solution.py:35
  45.7 1.5 %collective-permute-start.19 = (bf16[1,64,1536]{2,1,0:T(8,128)(2,1)S(1)}, bf16[1,64,1536]{2,1,0:T(8,128)(2,1)S(1)}, u32[]{:S(2)}, u32[]{:S(2)}) collective-permute-start(bf16[1,64,1536]{2,1,0:T(8,128)(2,1)S(1)} %get-tuple-element.31.refs_2_), channel_id=1, source_target_pairs={{0,2},{1,3},{2,0},{3,1},{4,6},{5,7},{6,4},{7,5},{8,10},{9,11},{10,... | collective-permute-start | bytes 589832 | tf_op jit(solution)/shard_map/ppermute | solution.py:30
  47.2 0.9 %collective-permute-done.6.refs_0_ = bf16[2,64,1024]{2,1,0:T(8,128)(2,1)S(1)} collective-permute-done((bf16[2,64,1024]{2,1,0:T(8,128)(2,1)S(1)}, bf16[2,64,1024]{2,1,0:T(8,128)(2,1)S(1)}, u32[]{:S(2)}, u32[]{:S(2)}) %collective-permute-start.6) | collective-permute-done | bytes 262176 | tf_op jit(solution)/shard_map/ppermute | solution.py:30
  48.1 2.1 %collective-permute-start.18 = (bf16[1,64,1536]{2,1,0:T(8,128)(2,1)S(1)}, bf16[1,64,1536]{2,1,0:T(8,128)(2,1)S(1)}, u32[]{:S(2)}, u32[]{:S(2)}) collective-permute-start(bf16[1,64,1536]{2,1,0:T(8,128)(2,1)S(1)} %get-tuple-element.32.refs_3_), channel_id=1, source_target_pairs={{0,2},{1,3},{2,0},{3,1},{4,6},{5,7},{6,4},{7,5},{8,10},{9,11},{10,... | collective-permute-start | bytes 589832 | tf_op jit(solution)/shard_map/ppermute | solution.py:30
  50.4 2.3 %shard_map.70.refs_2_.refs_0_ = f32[2,64,1024]{2,1,0:T(8,128)S(1)} custom-call(bf16[1,64,3072]{2,1,0:T(8,128)(2,1)S(1)} %collective-permute-done.13.refs_0_, bf16[3072,1024]{1,0:T(8,128)(2,1)S(1)} %copy-done, bf16[3072,1024]{1,0:T(8,128)(2,1)S(1)} %collective-permute-done.refs_1_.refs_4_.refs_2_, f32[6,256]{1,0:T(8,128)S(1)} %get-tuple-element.33.refs_2_.refs_5_.refs_3_, ...), custom_call_target="tpu_custom_call" | custom-call | flops 805306368 | bytes 13244416 | tf_op jit(solution)/shard_map/pallas_call | solution.py:71
  52.7 0.2 collective-permute-done.14.refs_0_
  52.8 0.1 shard_map.71.refs_3_.refs_4_
  52.9 0.0 collective-permute-done.12.refs_2_.refs_0_
  52.9 0.2 shard_map.72
  53.1 1.8 %collective-permute-start.16 = (bf16[64,1024]{1,0:T(8,128)(2,1)S(1)}, bf16[64,1024]{1,0:T(8,128)(2,1)S(1)}, u32[]{:S(2)}, u32[]{:S(2)}) collective-permute-start(bf16[64,1024]{1,0:T(8,128)(2,1)S(1)} %get-tuple-element.46.refs_1_), channel_id=1, source_target_pairs={{0,24},{1,25},{2,26},{3,27},{4,28},{5,29},{6,30},{7,31},{8,16},{9,... | collective-permute-start | bytes 393224 | tf_op jit(solution)/shard_map/ppermute | solution.py:420
  54.9 0.1 shard_map.73
  55.0 0.1 collective-permute-start.15
  55.1 2.2 %collective-permute-start.17 = (bf16[64,1024]{1,0:T(8,128)(2,1)S(1)}, bf16[64,1024]{1,0:T(8,128)(2,1)S(1)}, u32[]{:S(2)}, u32[]{:S(2)}) collective-permute-start(bf16[64,1024]{1,0:T(8,128)(2,1)S(1)} %get-tuple-element.49), channel_id=1, source_target_pairs={{0,25},{1,24},{2,27},{3,26},{4,29},{5,28},{6,31},{7,30},{8,17},{9,... | collective-permute-start | bytes 393224 | tf_op jit(solution)/shard_map/ppermute | solution.py:420
  57.3 0.0 collective-permute-done.19.refs_0_
  57.3 0.1 collective-permute-start.11
  57.4 1.2 %shard_map.74.refs_4_.refs_6_ = f32[2,64,1024]{2,1,0:T(8,128)S(1)} custom-call(bf16[1,64,1536]{2,1,0:T(8,128)(2,1)S(1)} %collective-permute-done.19.refs_0_, bf16[3072,1024]{1,0:T(8,128)(2,1)S(1)} %copy-done, bf16[3072,1024]{1,0:T(8,128)(2,1)S(1)} %collective-permute-done.refs_1_.refs_4_.refs_2_, f32[6,256]{1,0:T(8,128)S(1)} %get-tuple-element.33.refs_2_.refs_5_.refs_3_, ...), custom_call_target="tpu_custom_call" | custom-call | flops 805306368 | bytes 12916736 | tf_op jit(solution)/shard_map/pallas_call | solution.py:71
  58.6 0.0 collective-permute-done.18.refs_0_
  58.6 0.0 copy-start.1
  58.6 0.0 copy-start.2
  58.6 1.2 %shard_map.75 = (bf16[64,1024]{1,0:T(8,128)(2,1)S(1)}, bf16[64,1024]{1,0:T(8,128)(2,1)S(1)}) custom-call(bf16[1,64,1536]{2,1,0:T(8,128)(2,1)S(1)} %collective-permute-done.18.refs_0_, bf16[3072,1024]{1,0:T(8,128)(2,1)S(1)} %copy-done, bf16[3072,1024]{1,0:T(8,128)(2,1)S(1)} %collective-permute-done.refs_1_.refs_4_.refs_2_, ...), custom_call_target="tpu_custom_call" | custom-call | flops 805306368 | bytes 14358528 | tf_op jit(solution)/shard_map/pallas_call | solution.py:71
  59.8 0.1 collective-permute-start.21
  59.9 0.0 collective-permute-done.15.refs_3_
  59.9 2.1 %collective-permute-start.20 = (bf16[64,1024]{1,0:T(8,128)(2,1)S(1)}, bf16[64,1024]{1,0:T(8,128)(2,1)S(1)}, u32[]{:S(2)}, u32[]{:S(2)}) collective-permute-start(bf16[64,1024]{1,0:T(8,128)(2,1)S(1)} %get-tuple-element.51.refs_6_), channel_id=1, source_target_pairs={{0,8},{1,9},{2,10},{3,11},{4,12},{5,13},{6,14},{7,15},{8,0},{9,1},... | collective-permute-start | bytes 393224 | tf_op jit(solution)/shard_map/ppermute | solution.py:420
  62.0 0.2 shard_map.61
  62.2 0.0 collective-permute-done.16.refs_4_
  62.2 0.1 collective-permute-done.17.refs_5_
  62.4 0.0 collective-permute-done.11.refs_1_
  62.4 0.1 shard_map.76.refs_2_.refs_4_.known
  62.5 2.6 %collective-permute-done.21.refs_3_ = bf16[64,1024]{1,0:T(8,128)(2,1)S(1)} collective-permute-done((bf16[64,1024]{1,0:T(8,128)(2,1)S(1)}, bf16[64,1024]{1,0:T(8,128)(2,1)S(1)}, u32[]{:S(2)}, u32[]{:S(2)}) %collective-permute-start.21) | collective-permute-done | bytes 131104 | tf_op jit(solution)/shard_map/ppermute | solution.py:420
  65.1 0.3 shard_map.77.part
  65.4 3.1 %collective-permute-done.20.last = bf16[64,1024]{1,0:T(8,128)(2,1)S(1)} collective-permute-done((bf16[64,1024]{1,0:T(8,128)(2,1)S(1)}, bf16[64,1024]{1,0:T(8,128)(2,1)S(1)}, u32[]{:S(2)}, u32[]{:S(2)}) %collective-permute-start.20) | collective-permute-done | bytes 131104 | tf_op jit(solution)/shard_map/ppermute | solution.py:420
  68.5 1.1 %shard_map.78 = bf16[256,1024]{1,0:T(8,128)(2,1)} custom-call(bf16[256,1024]{1,0:T(8,128)(2,1)S(1)} %get-tuple-element.37.refs_0_.rhs, bf16[256,256]{1,0:T(8,128)(2,1)S(1)} %get-tuple-element.38.refs_1_.diag, f32[256,1024]{1,0:T(8,128)S(1)} %shard_map.76.refs_2_.refs_4_.known, bf16[64,1024]{1,0:T(8,128)(2,1)S(1)} %collective-permute-done.20.last, ...), custom_call_target="tpu_custom_call" | custom-call | flops 33554432 | bytes 2883584 | tf_op jit(solution)/shard_map/pallas_call | solution.py:71
  (12 shorter events, 0.1 us)
Async XLA Ops:
  0.0 7.6 %copy-start = (bf16[3072,1024]{1,0:T(8,128)(2,1)S(1)}, bf16[3072,1024]{1,0:T(8,128)(2,1)}, u32[]{:S(2)}) copy-start(bf16[3072,1024]{1,0:T(8,128)(2,1)} %refs_1_.13) | copy-start | bytes 18874372
  0.0 12.3 %collective-permute-start = (bf16[3072,1024]{1,0:T(8,128)(2,1)}, bf16[3072,1024]{1,0:T(8,128)(2,1)S(1)}, u32[]{:S(2)}, u32[]{:S(2)}) collective-permute-start(bf16[3072,1024]{1,0:T(8,128)(2,1)} %refs_1_.13), channel_id=1, source_target_pairs={{1,0},{0,1},{3,2},{2,3},{5,4},{4,5},{7,6},{6,7},{9,8},{8,9},{11,10... | collective-permute-start | bytes 18874376 | tf_op jit(solution)/shard_map/ppermute | solution.py:51
  1.9 23.6 %collective-permute-start.5 = (bf16[2,64,3072]{2,1,0:T(8,128)(2,1)S(1)}, bf16[2,64,3072]{2,1,0:T(8,128)(2,1)S(1)}, u32[]{:S(2)}, u32[]{:S(2)}) collective-permute-start(bf16[2,64,3072]{2,1,0:T(8,128)(2,1)S(1)} %shard_map.55.refs_2_.refs_0_), channel_id=1, source_target_pairs={{0,2},{1,3},{2,0},{3,1},{4,6},{5,7},{6,4},{7,5},{8,10},{9,11},{10,... | collective-permute-start | bytes 2359304 | tf_op jit(solution)/shard_map/ppermute | solution.py:30
  4.5 0.7 copy-start.3
  7.2 32.5 %collective-permute-start.8 = (bf16[2,64,3072]{2,1,0:T(8,128)(2,1)S(1)}, bf16[2,64,3072]{2,1,0:T(8,128)(2,1)S(1)}, u32[]{:S(2)}, u32[]{:S(2)}) collective-permute-start(bf16[2,64,3072]{2,1,0:T(8,128)(2,1)S(1)} %get-tuple-element.29.refs_3_.refs_0_), channel_id=1, source_target_pairs={{0,2},{1,3},{2,0},{3,1},{4,6},{5,7},{6,4},{7,5},{8,10},{9,11},{10,... | collective-permute-start | bytes 2359304 | tf_op jit(solution)/shard_map/ppermute | solution.py:30
  8.6 9.2 %collective-permute-start.1 = (bf16[2,64,1024]{2,1,0:T(8,128)(2,1)S(1)}, bf16[2,64,1024]{2,1,0:T(8,128)(2,1)S(1)}, u32[]{:S(2)}, u32[]{:S(2)}) collective-permute-start(bf16[2,64,1024]{2,1,0:T(8,128)(2,1)S(1)} %shard_map.57.refs_6_), channel_id=1, source_target_pairs={{0,4},{4,0},{8,12},{12,8},{16,20},{20,16},{24,28},{28,24},{1,5},{5... | collective-permute-start | bytes 786440 | tf_op jit(solution)/shard_map/ppermute | solution.py:35
  13.4 10.1 %collective-permute-start.2 = (bf16[2,64,1024]{2,1,0:T(8,128)(2,1)S(1)}, bf16[2,64,1024]{2,1,0:T(8,128)(2,1)S(1)}, u32[]{:S(2)}, u32[]{:S(2)}) collective-permute-start(bf16[2,64,1024]{2,1,0:T(8,128)(2,1)S(1)} %shard_map.59.refs_7_), channel_id=1, source_target_pairs={{0,4},{4,0},{8,12},{12,8},{16,20},{20,16},{24,28},{28,24},{1,5},{5... | collective-permute-start | bytes 786440 | tf_op jit(solution)/shard_map/ppermute | solution.py:35
  16.2 15.1 %collective-permute-start.3 = (bf16[2,64,1024]{2,1,0:T(8,128)(2,1)S(1)}, bf16[2,64,1024]{2,1,0:T(8,128)(2,1)S(1)}, u32[]{:S(2)}, u32[]{:S(2)}) collective-permute-start(bf16[2,64,1024]{2,1,0:T(8,128)(2,1)S(1)} %get-tuple-element.39), channel_id=1, source_target_pairs={{0,4},{4,0},{8,12},{12,8},{16,20},{20,16},{24,28},{28,24},{1,5},{5... | collective-permute-start | bytes 786440 | tf_op jit(solution)/shard_map/ppermute | solution.py:35
  23.5 10.7 %collective-permute-start.4 = (bf16[2,64,1024]{2,1,0:T(8,128)(2,1)S(1)}, bf16[2,64,1024]{2,1,0:T(8,128)(2,1)S(1)}, u32[]{:S(2)}, u32[]{:S(2)}) collective-permute-start(bf16[2,64,1024]{2,1,0:T(8,128)(2,1)S(1)} %shard_map.62.refs_4_), channel_id=1, source_target_pairs={{0,8},{4,12},{8,16},{12,20},{16,24},{20,28},{24,0},{28,4},{1,9},{5... | collective-permute-start | bytes 786440 | tf_op jit(solution)/shard_map/ppermute | solution.py:30
  27.5 10.2 %collective-permute-start.7 = (bf16[2,64,1024]{2,1,0:T(8,128)(2,1)S(1)}, bf16[2,64,1024]{2,1,0:T(8,128)(2,1)S(1)}, u32[]{:S(2)}, u32[]{:S(2)}) collective-permute-start(bf16[2,64,1024]{2,1,0:T(8,128)(2,1)S(1)} %shard_map.64.refs_6_), channel_id=1, source_target_pairs={{0,24},{4,28},{8,0},{12,4},{16,8},{20,12},{24,16},{28,20},{1,25},{... | collective-permute-start | bytes 786440 | tf_op jit(solution)/shard_map/ppermute | solution.py:30
  29.6 10.1 %collective-permute-start.10 = (bf16[2,64,1024]{2,1,0:T(8,128)(2,1)S(1)}, bf16[2,64,1024]{2,1,0:T(8,128)(2,1)S(1)}, u32[]{:S(2)}, u32[]{:S(2)}) collective-permute-start(bf16[2,64,1024]{2,1,0:T(8,128)(2,1)S(1)} %get-tuple-element.41), channel_id=1, source_target_pairs={{0,4},{4,0},{8,12},{12,8},{16,20},{20,16},{24,28},{28,24},{1,5},{5... | collective-permute-start | bytes 786440 | tf_op jit(solution)/shard_map/ppermute | solution.py:35
  31.3 10.7 %collective-permute-start.9 = (bf16[2,64,1024]{2,1,0:T(8,128)(2,1)S(1)}, bf16[2,64,1024]{2,1,0:T(8,128)(2,1)S(1)}, u32[]{:S(2)}, u32[]{:S(2)}) collective-permute-start(bf16[2,64,1024]{2,1,0:T(8,128)(2,1)S(1)} %get-tuple-element.40.refs_4_), channel_id=1, source_target_pairs={{0,4},{4,0},{8,12},{12,8},{16,20},{20,16},{24,28},{28,24},{1,5},{5... | collective-permute-start | bytes 786440 | tf_op jit(solution)/shard_map/ppermute | solution.py:35
  34.3 16.1 %collective-permute-start.13 = (bf16[1,64,3072]{2,1,0:T(8,128)(2,1)S(1)}, bf16[1,64,3072]{2,1,0:T(8,128)(2,1)S(1)}, u32[]{:S(2)}, u32[]{:S(2)}) collective-permute-start(bf16[1,64,3072]{2,1,0:T(8,128)(2,1)S(1)} %get-tuple-element.30.refs_1_), channel_id=1, source_target_pairs={{0,2},{1,3},{2,0},{3,1},{4,6},{5,7},{6,4},{7,5},{8,10},{9,11},{10,... | collective-permute-start | bytes 1179656 | tf_op jit(solution)/shard_map/ppermute | solution.py:30
  37.7 10.4 %collective-permute-start.6 = (bf16[2,64,1024]{2,1,0:T(8,128)(2,1)S(1)}, bf16[2,64,1024]{2,1,0:T(8,128)(2,1)S(1)}, u32[]{:S(2)}, u32[]{:S(2)}) collective-permute-start(bf16[2,64,1024]{2,1,0:T(8,128)(2,1)S(1)} %shard_map.65.refs_2_), channel_id=1, source_target_pairs={{0,8},{4,12},{8,16},{12,20},{16,24},{20,28},{24,0},{28,4},{1,9},{5... | collective-permute-start | bytes 786440 | tf_op jit(solution)/shard_map/ppermute | solution.py:30
  43.9 9.0 %collective-permute-start.14 = (bf16[2,64,1024]{2,1,0:T(8,128)(2,1)S(1)}, bf16[2,64,1024]{2,1,0:T(8,128)(2,1)S(1)}, u32[]{:S(2)}, u32[]{:S(2)}) collective-permute-start(bf16[2,64,1024]{2,1,0:T(8,128)(2,1)S(1)} %get-tuple-element.45), channel_id=1, source_target_pairs={{0,8},{4,12},{8,16},{12,20},{16,24},{20,28},{24,0},{28,4},{1,9},{5... | collective-permute-start | bytes 786440 | tf_op jit(solution)/shard_map/ppermute | solution.py:30
  44.1 8.8 %collective-permute-start.12 = (bf16[2,64,1024]{2,1,0:T(8,128)(2,1)S(1)}, bf16[2,64,1024]{2,1,0:T(8,128)(2,1)S(1)}, u32[]{:S(2)}, u32[]{:S(2)}) collective-permute-start(bf16[2,64,1024]{2,1,0:T(8,128)(2,1)S(1)} %get-tuple-element.42.refs_2_), channel_id=1, source_target_pairs={{0,4},{4,0},{8,12},{12,8},{16,20},{20,16},{24,28},{28,24},{1,5},{5... | collective-permute-start | bytes 786440 | tf_op jit(solution)/shard_map/ppermute | solution.py:35
  45.7 11.6 %collective-permute-start.19 = (bf16[1,64,1536]{2,1,0:T(8,128)(2,1)S(1)}, bf16[1,64,1536]{2,1,0:T(8,128)(2,1)S(1)}, u32[]{:S(2)}, u32[]{:S(2)}) collective-permute-start(bf16[1,64,1536]{2,1,0:T(8,128)(2,1)S(1)} %get-tuple-element.31.refs_2_), channel_id=1, source_target_pairs={{0,2},{1,3},{2,0},{3,1},{4,6},{5,7},{6,4},{7,5},{8,10},{9,11},{10,... | collective-permute-start | bytes 589832 | tf_op jit(solution)/shard_map/ppermute | solution.py:30
  48.1 10.4 %collective-permute-start.18 = (bf16[1,64,1536]{2,1,0:T(8,128)(2,1)S(1)}, bf16[1,64,1536]{2,1,0:T(8,128)(2,1)S(1)}, u32[]{:S(2)}, u32[]{:S(2)}) collective-permute-start(bf16[1,64,1536]{2,1,0:T(8,128)(2,1)S(1)} %get-tuple-element.32.refs_3_), channel_id=1, source_target_pairs={{0,2},{1,3},{2,0},{3,1},{4,6},{5,7},{6,4},{7,5},{8,10},{9,11},{10,... | collective-permute-start | bytes 589832 | tf_op jit(solution)/shard_map/ppermute | solution.py:30
  53.1 9.1 %collective-permute-start.16 = (bf16[64,1024]{1,0:T(8,128)(2,1)S(1)}, bf16[64,1024]{1,0:T(8,128)(2,1)S(1)}, u32[]{:S(2)}, u32[]{:S(2)}) collective-permute-start(bf16[64,1024]{1,0:T(8,128)(2,1)S(1)} %get-tuple-element.46.refs_1_), channel_id=1, source_target_pairs={{0,24},{1,25},{2,26},{3,27},{4,28},{5,29},{6,30},{7,31},{8,16},{9,... | collective-permute-start | bytes 393224 | tf_op jit(solution)/shard_map/ppermute | solution.py:420
  55.0 4.9 %collective-permute-start.15 = (bf16[64,1024]{1,0:T(8,128)(2,1)S(1)}, bf16[64,1024]{1,0:T(8,128)(2,1)S(1)}, u32[]{:S(2)}, u32[]{:S(2)}) collective-permute-start(bf16[64,1024]{1,0:T(8,128)(2,1)S(1)} %get-tuple-element.48), channel_id=1, source_target_pairs={{0,1},{1,0},{2,3},{3,2},{4,5},{5,4},{6,7},{7,6},{8,9},{9,8},{10,11... | collective-permute-start | bytes 393224 | tf_op jit(solution)/shard_map/ppermute | solution.py:61
  55.1 7.3 %collective-permute-start.17 = (bf16[64,1024]{1,0:T(8,128)(2,1)S(1)}, bf16[64,1024]{1,0:T(8,128)(2,1)S(1)}, u32[]{:S(2)}, u32[]{:S(2)}) collective-permute-start(bf16[64,1024]{1,0:T(8,128)(2,1)S(1)} %get-tuple-element.49), channel_id=1, source_target_pairs={{0,25},{1,24},{2,27},{3,26},{4,29},{5,28},{6,31},{7,30},{8,17},{9,... | collective-permute-start | bytes 393224 | tf_op jit(solution)/shard_map/ppermute | solution.py:420
  57.3 5.1 %collective-permute-start.11 = (f32[64,1024]{1,0:T(8,128)S(1)}, f32[64,1024]{1,0:T(8,128)S(1)}, u32[]{:S(2)}, u32[]{:S(2)}) collective-permute-start(f32[64,1024]{1,0:T(8,128)S(1)} %get-tuple-element.44), channel_id=1, source_target_pairs={{0,1},{1,0},{2,3},{3,2},{4,5},{5,4},{6,7},{7,6},{8,9},{9,8},{10,11... | collective-permute-start | bytes 786440 | tf_op jit(solution)/shard_map/ppermute | solution.py:61
  58.6 3.4 %copy-start.1 = (bf16[256,1024]{1,0:T(8,128)(2,1)S(1)}, bf16[256,1024]{1,0:T(8,128)(2,1)}, u32[]{:S(2)}) copy-start(bf16[256,1024]{1,0:T(8,128)(2,1)} %rhs.1) | copy-start | bytes 1572868
  58.6 3.4 %copy-start.2 = (bf16[1,256,256]{2,1,0:T(8,128)(2,1)S(1)}, bf16[1,256,256]{2,1,0:T(8,128)(2,1)}, u32[]{:S(2)}) copy-start(bf16[1,256,256]{2,1,0:T(8,128)(2,1)} %diag.1) | copy-start | bytes 393220
  59.8 5.3 %collective-permute-start.21 = (bf16[64,1024]{1,0:T(8,128)(2,1)S(1)}, bf16[64,1024]{1,0:T(8,128)(2,1)S(1)}, u32[]{:S(2)}, u32[]{:S(2)}) collective-permute-start(bf16[64,1024]{1,0:T(8,128)(2,1)S(1)} %get-tuple-element.52), channel_id=1, source_target_pairs={{0,9},{1,8},{2,11},{3,10},{4,13},{5,12},{6,15},{7,14},{8,1},{9,0},... | collective-permute-start | bytes 393224 | tf_op jit(solution)/shard_map/ppermute | solution.py:420
  59.9 8.6 %collective-permute-start.20 = (bf16[64,1024]{1,0:T(8,128)(2,1)S(1)}, bf16[64,1024]{1,0:T(8,128)(2,1)S(1)}, u32[]{:S(2)}, u32[]{:S(2)}) collective-permute-start(bf16[64,1024]{1,0:T(8,128)(2,1)S(1)} %get-tuple-element.51.refs_6_), channel_id=1, source_target_pairs={{0,8},{1,9},{2,10},{3,11},{4,12},{5,13},{6,14},{7,15},{8,0},{9,1},... | collective-permute-start | bytes 393224 | tf_op jit(solution)/shard_map/ppermute | solution.py:420

commit v6 on v5

v6 whole, which is shorter than its diff:
```python
import functools

import jax
import jax.numpy as jnp
from jax import lax
from jax.experimental import pallas as pl
from jax.experimental.pallas import tpu as pltpu
from jax.sharding import PartitionSpec as P

F32, BF16 = jnp.float32, jnp.bfloat16
VMEM = pl.BlockSpec(memory_space=pltpu.VMEM)
SMEM = pl.BlockSpec(memory_space=pltpu.SMEM)
ANY = pl.BlockSpec(memory_space=pl.ANY)
HBM = pl.BlockSpec(memory_space=pltpu.HBM)


WIDE = 256
PIECES = 4


def shift(block, axis, distance):
    size = lax.axis_size(axis)
    return lax.ppermute(block, axis, [(i, (i + distance) % size) for i in range(size)])


def pair_swap(block, axis):
    size = lax.axis_size(axis)
    return lax.ppermute(block, axis, [(i, i ^ 1) for i in range(size)])


def across(block, axis):
    return shift(block, axis, lax.axis_size(axis) // 2)


def inner(i, j, half):
    return i // half * half + (i % half + j) % half


def half_gather(block, axis):
    size = lax.axis_size(axis)
    half = size // 2
    parts = [block]
    for j in range(1, half):
        parts.append(lax.ppermute(block, axis, [(inner(i, j, half), i) for i in range(size)]))
    return parts


def to_columns(blocks, distance):
    n, size = lax.axis_size("col"), lax.axis_size("rhs")
    out = []
    for j, block in enumerate(blocks):
        route = [(c * size + r, (c + distance) % n * size + inner(r, j, size // 2))
                 for c in range(n) for r in range(size)]
        out.append(lax.ppermute(block, ("col", "rhs"), route) if distance or j else block)
    return out


def pinned(*shape, dtype=BF16):
    return pltpu.VMEM(shape, dtype)


def call(body, outs, specs, args, flops=0, space=12, out_specs=None, **more):
    moved = sum(a.size * a.dtype.itemsize for a in args)
    return pl.pallas_call(
        body,
        out_shape=outs,
        in_specs=specs,
        out_specs=out_specs or [VMEM] * len(outs),
        compiler_params=pltpu.CompilerParams(vmem_limit_bytes=space << 20),
        cost_estimate=pl.CostEstimate(flops=flops, bytes_accessed=moved, transcendentals=0),
        **more,
    )(*args)


def take(tiles, groups, *earlier, weights=None):
    n, rows, depth = len(groups), tiles.shape[1], tiles.shape[2]
    extra = [] if weights is None else [SMEM]

    def body(*refs):
        src, dsts, sems = refs[0], refs[-1 - n - len(extra):-1], refs[-1]
        copies = []
        for group, dst in zip(groups, dsts):
            for i, (k, begin, end) in enumerate(group):
                k = tile_of(k, tiles.shape[0])
                columns = pl.ds(begin, end - begin)
                for first in range(0, rows, rows // PIECES):
                    cut = pl.ds(first, rows // PIECES)
                    copies.append(pltpu.make_async_copy(src.at[k, cut, columns], dst.at[i, cut], sems.at[len(copies)]))
        for c in copies:
            c.start()
        if extra:
            for k in range(weights.shape[1]):
                dsts[-1][k:k + 1, :] = jnp.full((1, WIDE), refs[1][0, k].astype(F32))
        for c in copies:
            c.wait()

    outs = [pinned(len(g), rows, g[0][2] - g[0][1]) for g in groups]
    if extra:
        outs.append(pinned(weights.shape[1], WIDE, dtype=F32))
    return call(body, outs, [HBM] + extra + [ANY] * len(earlier),
                [in_hbm(tiles)] + ([] if weights is None else [weights]) + [*earlier], space=2,
                scratch_shapes=[pltpu.SemaphoreType.DMA((PIECES * sum(map(len, groups)),))])


def in_hbm(array):
    return pltpu.with_memory_space_constraint(array, pltpu.HBM)


def on_odd():
    return lax.rem(lax.axis_index("col"), 2) == 1


def on_swap():
    if lax.axis_size("col") % 4:
        return jnp.bool_(False)
    return lax.rem(lax.div(lax.axis_index("col"), 2), 2) == 1


def tile_of(k, hops):
    low, high = (1, hops - 1) if k == "first" else (hops - 1, 1)
    return jnp.where(on_swap(), low, high) if isinstance(k, str) else k


def column_cuts(cols):
    wide = min(WIDE, cols)
    return [slice(at, at + wide) for at in range(0, cols, wide)]


def per_device(rhs_block, solution, factor, tile_list, diag_inverse):
    hops, quarter, depth = factor.shape[1:]
    rows, cols = rhs_block.shape
    size = lax.axis_size("rhs")
    half = size // 2
    tiles = factor[0]
    gives, owns = (2, 4, 0), (3, 5, 1)
    cuts = column_cuts(cols)
    strip = (half, quarter, cols)
    one, wide_one = pinned(*strip), pinned(*strip, dtype=F32)
    flat = pinned(quarter, cols)
    v = {}

    s24, = take(tiles, [[(2, 0, depth), (4, 0, depth)]])
    y24 = across(s24, "rhs")
    others = half_gather(solution, "rhs")[1:]
    middle = depth // 2
    sols = [solution, *others]
    v["token"] = s24

    def chained(body, outs, ins, flops=0):
        n = len(ins)

        def run(*refs):
            body(*refs[:n], *refs[n + 1:])

        got = call(run, outs, [VMEM] * n + [ANY], [*ins, v["token"]], flops=flops)
        v["token"] = got[0]
        return got

    order = (0, 3, "first", "last")
    groups = [[(0, 0, depth), (3, 0, depth)], [("first", 0, depth)], [("last", 0, middle)], [("last", middle, depth)]]
    *taken, v["weights"] = take(tiles, groups, s24, weights=tile_list)
    y03, y_first, y_last, y_last_rest = [across(s, "rhs") for s in taken]
    v["token"] = taken[0]

    near_got, near_own, near_give0 = [], [], []

    def near_gives(part):
        def body(*refs):
            left_ref, sol, weights, _, give = refs
            left = left_ref[...].reshape(2 * quarter, depth)
            for cut in cuts:
                total = jnp.dot(left, sol[:, cut], preferred_element_type=F32)
                for i in range(2):
                    term = total[i * quarter:(i + 1) * quarter] * weights[gives[i]:gives[i] + 1, :total.shape[1]]
                    give[i, :, cut] = term.astype(BF16)

        got = call(body, [pinned(2, quarter, cols)], [VMEM] * 3 + [ANY],
                   [s24, sols[part], v["weights"], v["token"]], flops=4 * quarter * depth * cols)
        v["token"] = got[0]
        near_got.append(pair_swap(got[0], "col"))

    def near_rest(part):
        n = len(taken)
        joins = half - 1 if part == half - 1 else 0

        def body(*refs):
            lefts, (sol, weights), outs = refs[:n], refs[n:n + 2], refs[n + 3 + joins:]
            whole = [r[i] for r in lefts[:2] for i in range(r.shape[0])]
            left = jnp.concatenate(whole + [jnp.concatenate([r[0] for r in lefts[2:]], axis=1)])
            swap = on_swap()
            for cut in cuts:
                total = jnp.dot(left, sol[:, cut], preferred_element_type=F32)
                zero, three, first, last = [
                    total[at * quarter:(at + 1) * quarter] * weights[pl.ds(tile_of(k, hops), 1), :total.shape[1]]
                    for at, k in enumerate(order)]
                outs[0][0, :, cut] = three
                outs[0][1, :, cut] = jnp.where(swap, last, first)
                outs[0][2, :, cut] = jnp.where(swap, first, last)
                if joins:
                    outs[1][part, :, cut] = zero.astype(BF16)
                else:
                    outs[1][:, cut] = zero.astype(BF16)
            for p in range(joins):
                outs[1][p] = refs[n + 2 + p][...]

        got = call(body, [pinned(3, quarter, cols, dtype=F32), one if joins else flat],
                   [VMEM] * (n + 2 + joins) + [ANY],
                   [*taken, sols[part], v["weights"], *near_give0[:joins], v["token"]],
                   flops=8 * quarter * depth * cols)
        v["token"] = got[0]
        near_own.append(got[0])
        if joins:
            v["got0"] = pair_swap(got[1], "col")
        else:
            near_give0.append(got[1])

    for part in range(half):
        near_gives(part)
        near_rest(part)

    def products(far, ks, epilogue, outs, extra, deep=slice(None)):
        n_extra = len(extra)

        def body(*refs):
            far_ref, refs = refs[0], refs[1:]
            sol_refs, weights = refs[:half], refs[half]
            more = refs[half + 1:half + 1 + n_extra]
            out = refs[len(refs) - len(outs):]
            is_odd = on_odd()
            left = far_ref[...].reshape(len(ks) * quarter, far_ref.shape[2])
            for part, sol_ref in enumerate(sol_refs):
                for cut in cuts:
                    total = jnp.dot(left, sol_ref[deep, cut], preferred_element_type=F32)
                    for i, k in enumerate(ks):
                        term = total[i * quarter:(i + 1) * quarter]
                        term = term * weights[pl.ds(tile_of(k, hops), 1), :total.shape[1]]
                        epilogue(out, more, is_odd, i, part, cut, term)

        args = [far, *sols, v["weights"], *extra, v["token"]]
        specs = [VMEM] * (half + 2 + n_extra) + [ANY]
        got = call(body, outs, specs, args, flops=2 * len(ks) * quarter * depth * cols * half)
        v["token"] = got[0]
        return got

    def plain(out, more, is_odd, i, part, cut, total):
        out[0][part, :, cut] = total

    def rounded(out, more, is_odd, i, part, cut, total):
        out[i][part, :, cut] = total.astype(BF16)


    def near2(*refs):
        for p in range(half):
            own, got = refs[p], refs[half + p]
            refs[-1][p] = (own[0] + jnp.where(on_odd(), got[1].astype(F32), got[0].astype(F32))).astype(BF16)

    d2n, = chained(near2, [one], [*near_own, *near_got])
    d2n_in = shift(d2n, "col", 2)

    got_far = [pair_swap(g, "col") for g in products(y24, (2, 4), rounded, [one, one], [])]

    def near3(*refs):
        for p in range(half):
            own, got = refs[p], refs[half + p]
            refs[-1][p] = (own[1] + jnp.where(on_odd(), 0.0, got[1].astype(F32))).astype(BF16)

    d3n, = chained(near3, [one], [*near_own, *near_got])
    d3n_in = shift(d3n, "col", hops)

    def near1(*refs):
        got0, arrived, d1 = refs[2 * half:]
        for p in range(half):
            own, got = refs[p], refs[half + p]
            r = jnp.where(on_odd(), got[0].astype(F32), got0[p].astype(F32))
            d1[p] = (own[2] + r + arrived[p].astype(F32)).astype(BF16)

    d1n, = chained(near1, [one], [*near_own, *near_got, v["got0"], d2n_in])
    d1n_in = shift(d1n, "col", 2)

    def near3_in(d3, got0, out):
        for p in range(half):
            out[p] = d3[p].astype(F32) + jnp.where(on_odd(), got0[p].astype(F32), 0.0)

    near_sum, = chained(near3_in, [wide_one], [d3n_in, v["got0"]])

    def far03(out, more, is_odd, i, part, cut, total):
        r2, r4 = [m[part, :, cut].astype(F32) for m in more]
        if i == 1:
            total = total + jnp.where(is_odd, r4, r2)
        out[i][part, :, cut] = total.astype(BF16)

    last_give, d2f = products(y03, (0, 3), far03, [one, one], got_far)
    got_last, d2f_in = pair_swap(last_give, "col"), shift(d2f, "col", 2)

    def near1_in(d1, sums, *outs):
        for p in range(half):
            outs[p][...] = d1[p].astype(F32) + sums[p]

    sums_n = chained(near1_in, [pinned(quarter, cols, dtype=F32)] * half, [d1n_in, near_sum])
    sums_n = to_columns(sums_n, 0)

    raw, = products(y_first, ("first",), plain, [wide_one], [])

    def send(parts, last):
        n = lax.axis_size("col")
        swaps = [n % 4 == 0 and c // 2 % 2 == 1 for c in range(n)]
        far_off = [c + (2 if last != swap else hops) for c, swap in enumerate(swaps)]
        out = []
        for j, part in enumerate(parts):
            route = [(c * size + r, far_off[c] % n * size + inner(r, j, half)) for c in range(n) for r in range(size)]
            out.append(lax.ppermute(part, ("col", "rhs"), route))
        return out

    def far2_in(d2, r2, out):
        for p in range(half):
            out[p] = d2[p].astype(F32) + jnp.where(on_odd(), r2[p].astype(F32), 0.0)

    chain, = chained(far2_in, [wide_one], [d2f_in, got_far[0]])

    def far_first(raw, r4, r0, chain, *refs):
        outs, pre = refs[:half], refs[half]
        is_odd, swap = on_odd(), on_swap()
        for p in range(half):
            one = chain[p] + jnp.where(is_odd, 0.0, r0[p].astype(F32))
            three = jnp.where(is_odd, 0.0, r4[p].astype(F32))
            outs[p][...] = (raw[p] + jnp.where(swap, one, three)).astype(BF16)
            pre[p] = jnp.where(swap, three, one)

    *firsts, pre = chained(far_first, [flat] * half + [wide_one], [raw, got_far[1], got_last, chain])
    first_in = send(firsts, False)

    def far_stay(r0, *outs):
        for p in range(half):
            outs[p][...] = jnp.where(on_odd(), r0[p].astype(F32), 0.0).astype(BF16)

    sums_f = to_columns(chained(far_stay, [flat] * half, [got_last]), 0)

    part1, = products(y_last, ("last",), plain, [wide_one], [], slice(0, middle))

    def added(out, more, is_odd, i, part, cut, total):
        for m in more:
            total = total + m[part, :, cut]
        out[part][:, cut] = total.astype(BF16)

    lasts = products(y_last_rest, ("last",), added, [flat] * half, [part1, pre], slice(middle, depth))
    last_in = send(lasts, True)

    places = [(0, j) for j in range(half)] + [(1, j) for j in range(1, half)] + [(1, 0)]

    def arrange(rhs, diag, _, rhs_out, diag_out):
        me = lax.axis_index("rhs")
        upper, mine = lax.div(me, half), lax.rem(me, half)
        column = lax.broadcasted_iota(jnp.int32, (rows, rows), 1)
        source = column
        for slot, (s, j) in enumerate(places):
            at = slot * quarter
            block = lax.rem(upper + s, 2) * half + lax.rem(mine + half - j, half)
            start = pl.multiple_of(block * quarter, quarter)
            rhs_out[at:at + quarter] = rhs[pl.ds(start, quarter)]
            source = jnp.where((column >= at) & (column < at + quarter), column - at + start, source)
        pick = (lax.broadcasted_iota(jnp.int32, (rows, rows), 0) == source).astype(BF16)
        diag_out[...] = jnp.dot(diag[0], pick, preferred_element_type=F32).astype(BF16)

    rhs_local, diag_local = call(arrange, [pinned(rows, cols), pinned(rows, rows)], [VMEM, VMEM, ANY],
                                 [rhs_block, diag_inverse, near_own[-1]], flops=2 * rows * rows * rows)

    most_rows = rows - quarter

    def gather(*refs):
        near, stay, far, out = refs[:half], refs[half:2 * half], refs[2 * half:3 * half], refs[-1]
        for j in range(half):
            out[j * quarter:(j + 1) * quarter] = near[j][...]
        for j in range(half):
            at = (half + (j - 1) % half) * quarter
            out[at:at + quarter] = stay[j][...].astype(F32) + far[j][...].astype(F32)

    known, = chained(gather, [pinned(rows, cols, dtype=F32)], [*sums_n, *sums_f, *first_in])

    def most(rhs, diag, known, *refs):
        last, out = refs[:half - 1], refs[-1]
        total = jnp.concatenate([known[:rows // 2]] + [known[(half + j) * quarter:(half + j + 1) * quarter]
                                                      + l[...].astype(F32) for j, l in enumerate(last)])
        remaining = (rhs[:most_rows].astype(F32) - total).astype(BF16)
        out[...] = jnp.dot(diag[:, :most_rows], remaining, preferred_element_type=F32)

    partial, = chained(most, [pinned(rows, cols, dtype=F32)], [rhs_local, diag_local, known, *last_in[1:]],
                       flops=2 * rows * most_rows * cols)

    def final(rhs, diag, known, last, part, out, block, sems):
        total = known[most_rows:] + last[...].astype(F32)
        remaining = (rhs[most_rows:].astype(F32) - total).astype(BF16)
        copies = []
        for i in range(size):
            cut = slice(i * quarter, (i + 1) * quarter)
            term = jnp.dot(diag[cut, most_rows:], remaining, preferred_element_type=F32)
            block[cut] = (part[cut] + term).astype(BF16)
            copies.append(pltpu.make_async_copy(block.at[cut], out.at[cut], sems.at[i]))
            copies[-1].start()
        for c in copies:
            c.wait()

    return call(final, [jax.ShapeDtypeStruct((rows, cols), BF16)], [VMEM] * 5,
                [rhs_local, diag_local, known, last_in[0], partial], flops=2 * rows * quarter * cols,
                out_specs=[ANY], scratch_shapes=[pltpu.VMEM((rows, cols), BF16), pltpu.SemaphoreType.DMA((size,))])[0]


def solution(mesh):
    in_specs = (
        P("col", "rhs"),
        P("col", "rhs"),
        P("col", None, "rhs", None),
        P("col", None),
        P("col", None, None),
    )
    out_specs = P("col", "rhs")
    return jax.shard_map(
        per_device, mesh=mesh, in_specs=in_specs, out_specs=out_specs, check_vma=False
    )
```

time: 69.9 us -> 69.9 us (level)
    pallas_call x24 -> x23, Pallas kernels: 20.2 us -> 20.2 us  [call(): pl.pallas_call(body, out_shape=outs, in_specs=specs, out_specs=out_specs...]
where the time goes in v6:
time: 69.9 us; the launch traced here: 69.7 us
  starting transfers between devices  27.4 us (39%)
  waiting for transfers between devices  21.1 us (30%)
  Pallas kernels  20.2 us (29%)
    pallas_call x23, Pallas kernels, call(): pl.pallas_call(body, out_shape=outs, in_specs=specs, out_specs=out_specs...  20.2 us
    ppermute x9, starting transfers between devices, shift(): lax.ppermute(block, axis, [(i, (i + distance) % size) for i in range(size)])  13.1 us
    ppermute x6, waiting for transfers between devices, pair_swap(): return lax.ppermute(block, axis, [(i, i ^ 1) for i in range(size)])  8.44 us
    ppermute x6, starting transfers between devices, pair_swap(): return lax.ppermute(block, axis, [(i, i ^ 1) for i in range(size)])  7.63 us
    ppermute x9, waiting for transfers between devices, shift(): lax.ppermute(block, axis, [(i, (i + distance) % size) for i in range(size)])  6.75 us
    ppermute x4, starting transfers between devices, send(): out.append(lax.ppermute(part, ('col', 'rhs'), route))  6.13 us
    ppermute x4, waiting for transfers between devices, send(): out.append(lax.ppermute(part, ('col', 'rhs'), route))  5.86 us
  transfers between devices with their start and end apart: 22, of which 11 were waited for; matrix products, arithmetic and copies ran while one was open for 0% of the time, Pallas kernels for 27%

profile of v6, /device:TPU:0, one launch (start us, length us, event | category | flops | bytes accessed | tf_op | source)
XLA Modules:
  0.0 69.7 jit_solution(16090425726386415896)
XLA Ops:
  0.0 0.5 collective-permute-start
  0.5 1.5 %shard_map.55.refs_2_.refs_0_ = bf16[2,64,3072]{2,1,0:T(8,128)(2,1)S(1)} custom-call(bf16[6,64,3072]{2,1,0:T(8,128)(2,1)} %bitcast.1), custom_call_target="tpu_custom_call" | custom-call | bytes 2359296 | tf_op jit(solution)/shard_map/pallas_call | solution.py:64
  1.9 2.5 %collective-permute-start.5 = (bf16[2,64,3072]{2,1,0:T(8,128)(2,1)S(1)}, bf16[2,64,3072]{2,1,0:T(8,128)(2,1)S(1)}, u32[]{:S(2)}, u32[]{:S(2)}) collective-permute-start(bf16[2,64,3072]{2,1,0:T(8,128)(2,1)S(1)} %shard_map.55.refs_2_.refs_0_), channel_id=1, source_target_pairs={{0,2},{1,3},{2,0},{3,1},{4,6},{5,7},{6,4},{7,5},{8,10},{9,11},{10,... | collective-permute-start | bytes 2359304 | tf_op jit(solution)/shard_map/ppermute | solution.py:23
  4.5 0.7 copy-done.3
  5.1 2.1 %shard_map.56 = (bf16[2,64,3072]{2,1,0:T(8,128)(2,1)S(1)}, bf16[1,64,3072]{2,1,0:T(8,128)(2,1)S(1)}, bf16[1,64,1536]{2,1,0:T(8,128)(2,1)S(1)}, bf16[1,64,1536]{2,1,0:T(8,128)(2,1)S(1)}, f32[6,256]{1,0:T(8,128)S(1)}) custom-call(bf16[6,64,3072]{2,1,0:T(8,128)(2,1)} %bitcast.2, s32[1,6]{1,0:T(1,128)S(1)} %copy-done.3, ...), custom_call_target="tpu_custom_call" | custom-call | bytes 3145752 | tf_op jit(solution)/shard_map/pallas_call | solution.py:64
  7.2 0.4 collective-permute-start.8
  7.6 1.0 %shard_map.57.refs_6_ = bf16[2,64,1024]{2,1,0:T(8,128)(2,1)S(1)} custom-call(bf16[2,64,3072]{2,1,0:T(8,128)(2,1)S(1)} %shard_map.55.refs_2_.refs_0_, bf16[3072,1024]{1,0:T(8,128)(2,1)S(1)} %copy-done, f32[6,256]{1,0:T(8,128)S(1)} %get-tuple-element.33.refs_2_.refs_5_.refs_3_, bf16[2,64,3072]{2,1,0:T(8,128)(2,1)S(1)} %get-tuple-element.29.refs_3_.refs_0_), custom_call_target="tpu_custom_call" | custom-call | flops 805306368 | bytes 7870464 | tf_op jit(solution)/shard_map/pallas_call | solution.py:64
  8.6 1.9 %collective-permute-start.1 = (bf16[2,64,1024]{2,1,0:T(8,128)(2,1)S(1)}, bf16[2,64,1024]{2,1,0:T(8,128)(2,1)S(1)}, u32[]{:S(2)}, u32[]{:S(2)}) collective-permute-start(bf16[2,64,1024]{2,1,0:T(8,128)(2,1)S(1)} %shard_map.57.refs_6_), channel_id=1, source_target_pairs={{0,4},{4,0},{8,12},{12,8},{16,20},{20,16},{24,28},{28,24},{1,5},{5... | collective-permute-start | bytes 786440 | tf_op jit(solution)/shard_map/ppermute | solution.py:28
  10.5 1.8 %shard_map.58 = (f32[3,64,1024]{2,1,0:T(8,128)S(1)}, bf16[64,1024]{1,0:T(8,128)(2,1)S(1)}) custom-call(bf16[2,64,3072]{2,1,0:T(8,128)(2,1)S(1)} %get-tuple-element.29.refs_3_.refs_0_, bf16[1,64,3072]{2,1,0:T(8,128)(2,1)S(1)} %get-tuple-element.30.refs_1_, bf16[1,64,1536]{2,1,0:T(8,128)(2,1)S(1)} %get-tuple-element.31.refs_2_, ...), custom_call_target="tpu_custom_call" | custom-call | flops 1610612736 | bytes 8132608 | tf_op jit(solution)/shard_map/pallas_call | solution.py:64
  12.3 0.0 collective-permute-done.refs_1_.refs_4_.refs_2_
  12.3 1.0 %shard_map.59.refs_7_ = bf16[2,64,1024]{2,1,0:T(8,128)(2,1)S(1)} custom-call(bf16[2,64,3072]{2,1,0:T(8,128)(2,1)S(1)} %shard_map.55.refs_2_.refs_0_, bf16[3072,1024]{1,0:T(8,128)(2,1)S(1)} %collective-permute-done.refs_1_.refs_4_.refs_2_, f32[6,256]{1,0:T(8,128)S(1)} %get-tuple-element.33.refs_2_.refs_5_.refs_3_, ...), custom_call_target="tpu_custom_call" | custom-call | flops 805306368 | bytes 7870464 | tf_op jit(solution)/shard_map/pallas_call | solution.py:64
  13.4 1.0 %collective-permute-start.2 = (bf16[2,64,1024]{2,1,0:T(8,128)(2,1)S(1)}, bf16[2,64,1024]{2,1,0:T(8,128)(2,1)S(1)}, u32[]{:S(2)}, u32[]{:S(2)}) collective-permute-start(bf16[2,64,1024]{2,1,0:T(8,128)(2,1)S(1)} %shard_map.59.refs_7_), channel_id=1, source_target_pairs={{0,4},{4,0},{8,12},{12,8},{16,20},{20,16},{24,28},{28,24},{1,5},{5... | collective-permute-start | bytes 786440 | tf_op jit(solution)/shard_map/ppermute | solution.py:28
  14.4 1.8 %shard_map.60 = (f32[3,64,1024]{2,1,0:T(8,128)S(1)}, bf16[2,64,1024]{2,1,0:T(8,128)(2,1)S(1)}) custom-call(bf16[2,64,3072]{2,1,0:T(8,128)(2,1)S(1)} %get-tuple-element.29.refs_3_.refs_0_, bf16[1,64,3072]{2,1,0:T(8,128)(2,1)S(1)} %get-tuple-element.30.refs_1_, bf16[1,64,1536]{2,1,0:T(8,128)(2,1)S(1)} %get-tuple-element.31.refs_2_, ...), custom_call_target="tpu_custom_call" | custom-call | flops 1610612736 | bytes 8263680 | tf_op jit(solution)/shard_map/pallas_call | solution.py:64
  16.2 1.1 %collective-permute-start.3 = (bf16[2,64,1024]{2,1,0:T(8,128)(2,1)S(1)}, bf16[2,64,1024]{2,1,0:T(8,128)(2,1)S(1)}, u32[]{:S(2)}, u32[]{:S(2)}) collective-permute-start(bf16[2,64,1024]{2,1,0:T(8,128)(2,1)S(1)} %get-tuple-element.39), channel_id=1, source_target_pairs={{0,4},{4,0},{8,12},{12,8},{16,20},{20,16},{24,28},{28,24},{1,5},{5... | collective-permute-start | bytes 786440 | tf_op jit(solution)/shard_map/ppermute | solution.py:28
  17.3 0.5 collective-permute-done.1.refs_2_
  17.8 5.6 %collective-permute-done.2.refs_3_ = bf16[2,64,1024]{2,1,0:T(8,128)(2,1)S(1)} collective-permute-done((bf16[2,64,1024]{2,1,0:T(8,128)(2,1)S(1)}, bf16[2,64,1024]{2,1,0:T(8,128)(2,1)S(1)}, u32[]{:S(2)}, u32[]{:S(2)}) %collective-permute-start.2) | collective-permute-done | bytes 262176 | tf_op jit(solution)/shard_map/ppermute | solution.py:28
  23.5 0.1 shard_map.62.refs_4_
  23.5 2.0 %collective-permute-start.4 = (bf16[2,64,1024]{2,1,0:T(8,128)(2,1)S(1)}, bf16[2,64,1024]{2,1,0:T(8,128)(2,1)S(1)}, u32[]{:S(2)}, u32[]{:S(2)}) collective-permute-start(bf16[2,64,1024]{2,1,0:T(8,128)(2,1)S(1)} %shard_map.62.refs_4_), channel_id=1, source_target_pairs={{0,8},{4,12},{8,16},{12,20},{16,24},{20,28},{24,0},{28,4},{1,9},{5... | collective-permute-start | bytes 786440 | tf_op jit(solution)/shard_map/ppermute | solution.py:23
  25.5 1.9 %shard_map.63 = (bf16[2,64,1024]{2,1,0:T(8,128)(2,1)S(1)}, bf16[2,64,1024]{2,1,0:T(8,128)(2,1)S(1)}) custom-call(bf16[2,64,3072]{2,1,0:T(8,128)(2,1)S(1)} %collective-permute-done.5.refs_0_, bf16[3072,1024]{1,0:T(8,128)(2,1)S(1)} %copy-done, bf16[3072,1024]{1,0:T(8,128)(2,1)S(1)} %collective-permute-done.refs_1_.refs_4_.refs_2_, ...), custom_call_target="tpu_custom_call" | custom-call | flops 1610612736 | bytes 13637632 | tf_op jit(solution)/shard_map/pallas_call | solution.py:64
  27.5 0.1 shard_map.64.refs_6_
  27.5 2.1 %collective-permute-start.7 = (bf16[2,64,1024]{2,1,0:T(8,128)(2,1)S(1)}, bf16[2,64,1024]{2,1,0:T(8,128)(2,1)S(1)}, u32[]{:S(2)}, u32[]{:S(2)}) collective-permute-start(bf16[2,64,1024]{2,1,0:T(8,128)(2,1)S(1)} %shard_map.64.refs_6_), channel_id=1, source_target_pairs={{0,24},{4,28},{8,0},{12,4},{16,8},{20,12},{24,16},{28,20},{1,25},{... | collective-permute-start | bytes 786440 | tf_op jit(solution)/shard_map/ppermute | solution.py:23
  29.6 1.7 %collective-permute-start.10 = (bf16[2,64,1024]{2,1,0:T(8,128)(2,1)S(1)}, bf16[2,64,1024]{2,1,0:T(8,128)(2,1)S(1)}, u32[]{:S(2)}, u32[]{:S(2)}) collective-permute-start(bf16[2,64,1024]{2,1,0:T(8,128)(2,1)S(1)} %get-tuple-element.41), channel_id=1, source_target_pairs={{0,4},{4,0},{8,12},{12,8},{16,20},{20,16},{24,28},{28,24},{1,5},{5... | collective-permute-start | bytes 786440 | tf_op jit(solution)/shard_map/ppermute | solution.py:28
  31.3 0.0 collective-permute-done.3.refs_4_.refs_1_
  31.3 0.3 collective-permute-start.9
  31.7 2.6 %collective-permute-done.4.refs_5_ = bf16[2,64,1024]{2,1,0:T(8,128)(2,1)S(1)} collective-permute-done((bf16[2,64,1024]{2,1,0:T(8,128)(2,1)S(1)}, bf16[2,64,1024]{2,1,0:T(8,128)(2,1)S(1)}, u32[]{:S(2)}, u32[]{:S(2)}) %collective-permute-start.4) | collective-permute-done | bytes 262176 | tf_op jit(solution)/shard_map/ppermute | solution.py:23
  34.2 1.6 %collective-permute-start.13 = (bf16[1,64,3072]{2,1,0:T(8,128)(2,1)S(1)}, bf16[1,64,3072]{2,1,0:T(8,128)(2,1)S(1)}, u32[]{:S(2)}, u32[]{:S(2)}) collective-permute-start(bf16[1,64,3072]{2,1,0:T(8,128)(2,1)S(1)} %get-tuple-element.30.refs_1_), channel_id=1, source_target_pairs={{0,2},{1,3},{2,0},{3,1},{4,6},{5,7},{6,4},{7,5},{8,10},{9,11},{10,... | collective-permute-start | bytes 1179656 | tf_op jit(solution)/shard_map/ppermute | solution.py:23
  35.9 0.1 shard_map.65.refs_2_
  36.0 1.7 %collective-permute-done.7.refs_0_ = bf16[2,64,1024]{2,1,0:T(8,128)(2,1)S(1)} collective-permute-done((bf16[2,64,1024]{2,1,0:T(8,128)(2,1)S(1)}, bf16[2,64,1024]{2,1,0:T(8,128)(2,1)S(1)}, u32[]{:S(2)}, u32[]{:S(2)}) %collective-permute-start.7) | collective-permute-done | bytes 262176 | tf_op jit(solution)/shard_map/ppermute | solution.py:23
  37.7 0.6 collective-permute-start.6
  38.3 0.1 shard_map.66.refs_6_.refs_1_
  38.4 1.3 %collective-permute-done.8.refs_0_ = bf16[2,64,3072]{2,1,0:T(8,128)(2,1)S(1)} collective-permute-done((bf16[2,64,3072]{2,1,0:T(8,128)(2,1)S(1)}, bf16[2,64,3072]{2,1,0:T(8,128)(2,1)S(1)}, u32[]{:S(2)}, u32[]{:S(2)}) %collective-permute-start.8) | collective-permute-done | bytes 786464 | tf_op jit(solution)/shard_map/ppermute | solution.py:23
  39.7 2.3 %collective-permute-done.9.refs_4_.refs_1_ = bf16[2,64,1024]{2,1,0:T(8,128)(2,1)S(1)} collective-permute-done((bf16[2,64,1024]{2,1,0:T(8,128)(2,1)S(1)}, bf16[2,64,1024]{2,1,0:T(8,128)(2,1)S(1)}, u32[]{:S(2)}, u32[]{:S(2)}) %collective-permute-start.9) | collective-permute-done | bytes 262176 | tf_op jit(solution)/shard_map/ppermute | solution.py:28
  42.0 1.9 %shard_map.67 = (bf16[2,64,1024]{2,1,0:T(8,128)(2,1)S(1)}, bf16[2,64,1024]{2,1,0:T(8,128)(2,1)S(1)}) custom-call(bf16[2,64,3072]{2,1,0:T(8,128)(2,1)S(1)} %collective-permute-done.8.refs_0_, bf16[3072,1024]{1,0:T(8,128)(2,1)S(1)} %copy-done, bf16[3072,1024]{1,0:T(8,128)(2,1)S(1)} %collective-permute-done.refs_1_.refs_4_.refs_2_, ...), custom_call_target="tpu_custom_call" | custom-call | flops 1610612736 | bytes 14424064 | tf_op jit(solution)/shard_map/pallas_call | solution.py:64
  43.9 0.2 collective-permute-start.14
  44.1 1.5 %collective-permute-start.12 = (bf16[2,64,1024]{2,1,0:T(8,128)(2,1)S(1)}, bf16[2,64,1024]{2,1,0:T(8,128)(2,1)S(1)}, u32[]{:S(2)}, u32[]{:S(2)}) collective-permute-start(bf16[2,64,1024]{2,1,0:T(8,128)(2,1)S(1)} %get-tuple-element.42.refs_2_), channel_id=1, source_target_pairs={{0,4},{4,0},{8,12},{12,8},{16,20},{20,16},{24,28},{28,24},{1,5},{5... | collective-permute-start | bytes 786440 | tf_op jit(solution)/shard_map/ppermute | solution.py:28
  45.7 1.5 %collective-permute-start.19 = (bf16[1,64,1536]{2,1,0:T(8,128)(2,1)S(1)}, bf16[1,64,1536]{2,1,0:T(8,128)(2,1)S(1)}, u32[]{:S(2)}, u32[]{:S(2)}) collective-permute-start(bf16[1,64,1536]{2,1,0:T(8,128)(2,1)S(1)} %get-tuple-element.31.refs_2_), channel_id=1, source_target_pairs={{0,2},{1,3},{2,0},{3,1},{4,6},{5,7},{6,4},{7,5},{8,10},{9,11},{10,... | collective-permute-start | bytes 589832 | tf_op jit(solution)/shard_map/ppermute | solution.py:23
  47.2 0.9 %collective-permute-done.6.refs_0_ = bf16[2,64,1024]{2,1,0:T(8,128)(2,1)S(1)} collective-permute-done((bf16[2,64,1024]{2,1,0:T(8,128)(2,1)S(1)}, bf16[2,64,1024]{2,1,0:T(8,128)(2,1)S(1)}, u32[]{:S(2)}, u32[]{:S(2)}) %collective-permute-start.6) | collective-permute-done | bytes 262176 | tf_op jit(solution)/shard_map/ppermute | solution.py:23
  48.1 2.1 %collective-permute-start.18 = (bf16[1,64,1536]{2,1,0:T(8,128)(2,1)S(1)}, bf16[1,64,1536]{2,1,0:T(8,128)(2,1)S(1)}, u32[]{:S(2)}, u32[]{:S(2)}) collective-permute-start(bf16[1,64,1536]{2,1,0:T(8,128)(2,1)S(1)} %get-tuple-element.32.refs_3_), channel_id=1, source_target_pairs={{0,2},{1,3},{2,0},{3,1},{4,6},{5,7},{6,4},{7,5},{8,10},{9,11},{10,... | collective-permute-start | bytes 589832 | tf_op jit(solution)/shard_map/ppermute | solution.py:23
  50.3 2.3 %shard_map.69.refs_2_.refs_0_ = f32[2,64,1024]{2,1,0:T(8,128)S(1)} custom-call(bf16[1,64,3072]{2,1,0:T(8,128)(2,1)S(1)} %collective-permute-done.13.refs_0_, bf16[3072,1024]{1,0:T(8,128)(2,1)S(1)} %copy-done, bf16[3072,1024]{1,0:T(8,128)(2,1)S(1)} %collective-permute-done.refs_1_.refs_4_.refs_2_, f32[6,256]{1,0:T(8,128)S(1)} %get-tuple-element.33.refs_2_.refs_5_.refs_3_, ...), custom_call_target="tpu_custom_call" | custom-call | flops 805306368 | bytes 13244416 | tf_op jit(solution)/shard_map/pallas_call | solution.py:64
  52.6 0.2 collective-permute-done.14.refs_0_
  52.8 0.1 shard_map.70.refs_3_.refs_4_
  52.9 0.0 collective-permute-done.12.refs_2_.refs_0_
  52.9 0.2 shard_map.71
  53.1 1.8 %collective-permute-start.16 = (bf16[64,1024]{1,0:T(8,128)(2,1)S(1)}, bf16[64,1024]{1,0:T(8,128)(2,1)S(1)}, u32[]{:S(2)}, u32[]{:S(2)}) collective-permute-start(bf16[64,1024]{1,0:T(8,128)(2,1)S(1)} %get-tuple-element.46.refs_1_), channel_id=1, source_target_pairs={{0,24},{1,25},{2,26},{3,27},{4,28},{5,29},{6,30},{7,31},{8,16},{9,... | collective-permute-start | bytes 393224 | tf_op jit(solution)/shard_map/ppermute | solution.py:311
  54.9 0.1 shard_map.72
  55.0 0.1 collective-permute-start.15
  55.1 2.2 %collective-permute-start.17 = (bf16[64,1024]{1,0:T(8,128)(2,1)S(1)}, bf16[64,1024]{1,0:T(8,128)(2,1)S(1)}, u32[]{:S(2)}, u32[]{:S(2)}) collective-permute-start(bf16[64,1024]{1,0:T(8,128)(2,1)S(1)} %get-tuple-element.49), channel_id=1, source_target_pairs={{0,25},{1,24},{2,27},{3,26},{4,29},{5,28},{6,31},{7,30},{8,17},{9,... | collective-permute-start | bytes 393224 | tf_op jit(solution)/shard_map/ppermute | solution.py:311
  57.3 0.0 collective-permute-done.19.refs_0_
  57.3 0.1 collective-permute-start.11
  57.4 1.2 %shard_map.73.refs_4_.refs_6_ = f32[2,64,1024]{2,1,0:T(8,128)S(1)} custom-call(bf16[1,64,1536]{2,1,0:T(8,128)(2,1)S(1)} %collective-permute-done.19.refs_0_, bf16[3072,1024]{1,0:T(8,128)(2,1)S(1)} %copy-done, bf16[3072,1024]{1,0:T(8,128)(2,1)S(1)} %collective-permute-done.refs_1_.refs_4_.refs_2_, f32[6,256]{1,0:T(8,128)S(1)} %get-tuple-element.33.refs_2_.refs_5_.refs_3_, ...), custom_call_target="tpu_custom_call" | custom-call | flops 805306368 | bytes 12916736 | tf_op jit(solution)/shard_map/pallas_call | solution.py:64
  58.6 0.0 copy-start.1
  58.6 0.0 copy-start.2
  58.6 1.2 %shard_map.74 = (bf16[64,1024]{1,0:T(8,128)(2,1)S(1)}, bf16[64,1024]{1,0:T(8,128)(2,1)S(1)}) custom-call(bf16[1,64,1536]{2,1,0:T(8,128)(2,1)S(1)} %collective-permute-done.18.refs_0_, bf16[3072,1024]{1,0:T(8,128)(2,1)S(1)} %copy-done, bf16[3072,1024]{1,0:T(8,128)(2,1)S(1)} %collective-permute-done.refs_1_.refs_4_.refs_2_, ...), custom_call_target="tpu_custom_call" | custom-call | flops 805306368 | bytes 14358528 | tf_op jit(solution)/shard_map/pallas_call | solution.py:64
  59.8 0.1 collective-permute-start.21
  59.9 0.0 collective-permute-done.15.refs_3_
  59.9 2.1 %collective-permute-start.20 = (bf16[64,1024]{1,0:T(8,128)(2,1)S(1)}, bf16[64,1024]{1,0:T(8,128)(2,1)S(1)}, u32[]{:S(2)}, u32[]{:S(2)}) collective-permute-start(bf16[64,1024]{1,0:T(8,128)(2,1)S(1)} %get-tuple-element.51.refs_6_), channel_id=1, source_target_pairs={{0,8},{1,9},{2,10},{3,11},{4,12},{5,13},{6,14},{7,15},{8,0},{9,1},... | collective-permute-start | bytes 393224 | tf_op jit(solution)/shard_map/ppermute | solution.py:311
  62.0 0.2 shard_map.61
  62.2 0.0 collective-permute-done.16.refs_4_
  62.2 0.1 collective-permute-done.17.refs_5_
  62.4 0.1 shard_map.75.refs_2_.refs_4_.known
  62.5 2.7 %collective-permute-done.21.refs_3_ = bf16[64,1024]{1,0:T(8,128)(2,1)S(1)} collective-permute-done((bf16[64,1024]{1,0:T(8,128)(2,1)S(1)}, bf16[64,1024]{1,0:T(8,128)(2,1)S(1)}, u32[]{:S(2)}, u32[]{:S(2)}) %collective-permute-start.21) | collective-permute-done | bytes 131104 | tf_op jit(solution)/shard_map/ppermute | solution.py:311
  65.1 0.3 shard_map.76.part
  65.4 3.1 %collective-permute-done.20.last = bf16[64,1024]{1,0:T(8,128)(2,1)S(1)} collective-permute-done((bf16[64,1024]{1,0:T(8,128)(2,1)S(1)}, bf16[64,1024]{1,0:T(8,128)(2,1)S(1)}, u32[]{:S(2)}, u32[]{:S(2)}) %collective-permute-start.20) | collective-permute-done | bytes 131104 | tf_op jit(solution)/shard_map/ppermute | solution.py:311
  68.5 1.1 %shard_map.77 = bf16[256,1024]{1,0:T(8,128)(2,1)} custom-call(bf16[256,1024]{1,0:T(8,128)(2,1)S(1)} %get-tuple-element.37.refs_0_.rhs, bf16[256,256]{1,0:T(8,128)(2,1)S(1)} %get-tuple-element.38.refs_1_.diag, f32[256,1024]{1,0:T(8,128)S(1)} %shard_map.75.refs_2_.refs_4_.known, bf16[64,1024]{1,0:T(8,128)(2,1)S(1)} %collective-permute-done.20.last, ...), custom_call_target="tpu_custom_call" | custom-call | flops 33554432 | bytes 2883584 | tf_op jit(solution)/shard_map/pallas_call | solution.py:64
  (11 shorter events, 0.1 us)
Async XLA Ops:
  0.0 7.6 %copy-start = (bf16[3072,1024]{1,0:T(8,128)(2,1)S(1)}, bf16[3072,1024]{1,0:T(8,128)(2,1)}, u32[]{:S(2)}) copy-start(bf16[3072,1024]{1,0:T(8,128)(2,1)} %refs_1_.13) | copy-start | bytes 18874372
  0.0 12.3 %collective-permute-start = (bf16[3072,1024]{1,0:T(8,128)(2,1)}, bf16[3072,1024]{1,0:T(8,128)(2,1)S(1)}, u32[]{:S(2)}, u32[]{:S(2)}) collective-permute-start(bf16[3072,1024]{1,0:T(8,128)(2,1)} %refs_1_.13), channel_id=1, source_target_pairs={{1,0},{0,1},{3,2},{2,3},{5,4},{4,5},{7,6},{6,7},{9,8},{8,9},{11,10... | collective-permute-start | bytes 18874376 | tf_op jit(solution)/shard_map/ppermute | solution.py:44
  1.9 23.6 %collective-permute-start.5 = (bf16[2,64,3072]{2,1,0:T(8,128)(2,1)S(1)}, bf16[2,64,3072]{2,1,0:T(8,128)(2,1)S(1)}, u32[]{:S(2)}, u32[]{:S(2)}) collective-permute-start(bf16[2,64,3072]{2,1,0:T(8,128)(2,1)S(1)} %shard_map.55.refs_2_.refs_0_), channel_id=1, source_target_pairs={{0,2},{1,3},{2,0},{3,1},{4,6},{5,7},{6,4},{7,5},{8,10},{9,11},{10,... | collective-permute-start | bytes 2359304 | tf_op jit(solution)/shard_map/ppermute | solution.py:23
  4.5 0.7 copy-start.3
  7.2 32.5 %collective-permute-start.8 = (bf16[2,64,3072]{2,1,0:T(8,128)(2,1)S(1)}, bf16[2,64,3072]{2,1,0:T(8,128)(2,1)S(1)}, u32[]{:S(2)}, u32[]{:S(2)}) collective-permute-start(bf16[2,64,3072]{2,1,0:T(8,128)(2,1)S(1)} %get-tuple-element.29.refs_3_.refs_0_), channel_id=1, source_target_pairs={{0,2},{1,3},{2,0},{3,1},{4,6},{5,7},{6,4},{7,5},{8,10},{9,11},{10,... | collective-permute-start | bytes 2359304 | tf_op jit(solution)/shard_map/ppermute | solution.py:23
  8.6 9.2 %collective-permute-start.1 = (bf16[2,64,1024]{2,1,0:T(8,128)(2,1)S(1)}, bf16[2,64,1024]{2,1,0:T(8,128)(2,1)S(1)}, u32[]{:S(2)}, u32[]{:S(2)}) collective-permute-start(bf16[2,64,1024]{2,1,0:T(8,128)(2,1)S(1)} %shard_map.57.refs_6_), channel_id=1, source_target_pairs={{0,4},{4,0},{8,12},{12,8},{16,20},{20,16},{24,28},{28,24},{1,5},{5... | collective-permute-start | bytes 786440 | tf_op jit(solution)/shard_map/ppermute | solution.py:28
  13.4 10.1 %collective-permute-start.2 = (bf16[2,64,1024]{2,1,0:T(8,128)(2,1)S(1)}, bf16[2,64,1024]{2,1,0:T(8,128)(2,1)S(1)}, u32[]{:S(2)}, u32[]{:S(2)}) collective-permute-start(bf16[2,64,1024]{2,1,0:T(8,128)(2,1)S(1)} %shard_map.59.refs_7_), channel_id=1, source_target_pairs={{0,4},{4,0},{8,12},{12,8},{16,20},{20,16},{24,28},{28,24},{1,5},{5... | collective-permute-start | bytes 786440 | tf_op jit(solution)/shard_map/ppermute | solution.py:28
  16.2 15.1 %collective-permute-start.3 = (bf16[2,64,1024]{2,1,0:T(8,128)(2,1)S(1)}, bf16[2,64,1024]{2,1,0:T(8,128)(2,1)S(1)}, u32[]{:S(2)}, u32[]{:S(2)}) collective-permute-start(bf16[2,64,1024]{2,1,0:T(8,128)(2,1)S(1)} %get-tuple-element.39), channel_id=1, source_target_pairs={{0,4},{4,0},{8,12},{12,8},{16,20},{20,16},{24,28},{28,24},{1,5},{5... | collective-permute-start | bytes 786440 | tf_op jit(solution)/shard_map/ppermute | solution.py:28
  23.5 10.7 %collective-permute-start.4 = (bf16[2,64,1024]{2,1,0:T(8,128)(2,1)S(1)}, bf16[2,64,1024]{2,1,0:T(8,128)(2,1)S(1)}, u32[]{:S(2)}, u32[]{:S(2)}) collective-permute-start(bf16[2,64,1024]{2,1,0:T(8,128)(2,1)S(1)} %shard_map.62.refs_4_), channel_id=1, source_target_pairs={{0,8},{4,12},{8,16},{12,20},{16,24},{20,28},{24,0},{28,4},{1,9},{5... | collective-permute-start | bytes 786440 | tf_op jit(solution)/shard_map/ppermute | solution.py:23
  27.5 10.2 %collective-permute-start.7 = (bf16[2,64,1024]{2,1,0:T(8,128)(2,1)S(1)}, bf16[2,64,1024]{2,1,0:T(8,128)(2,1)S(1)}, u32[]{:S(2)}, u32[]{:S(2)}) collective-permute-start(bf16[2,64,1024]{2,1,0:T(8,128)(2,1)S(1)} %shard_map.64.refs_6_), channel_id=1, source_target_pairs={{0,24},{4,28},{8,0},{12,4},{16,8},{20,12},{24,16},{28,20},{1,25},{... | collective-permute-start | bytes 786440 | tf_op jit(solution)/shard_map/ppermute | solution.py:23
  29.6 10.1 %collective-permute-start.10 = (bf16[2,64,1024]{2,1,0:T(8,128)(2,1)S(1)}, bf16[2,64,1024]{2,1,0:T(8,128)(2,1)S(1)}, u32[]{:S(2)}, u32[]{:S(2)}) collective-permute-start(bf16[2,64,1024]{2,1,0:T(8,128)(2,1)S(1)} %get-tuple-element.41), channel_id=1, source_target_pairs={{0,4},{4,0},{8,12},{12,8},{16,20},{20,16},{24,28},{28,24},{1,5},{5... | collective-permute-start | bytes 786440 | tf_op jit(solution)/shard_map/ppermute | solution.py:28
  31.3 10.7 %collective-permute-start.9 = (bf16[2,64,1024]{2,1,0:T(8,128)(2,1)S(1)}, bf16[2,64,1024]{2,1,0:T(8,128)(2,1)S(1)}, u32[]{:S(2)}, u32[]{:S(2)}) collective-permute-start(bf16[2,64,1024]{2,1,0:T(8,128)(2,1)S(1)} %get-tuple-element.40.refs_4_), channel_id=1, source_target_pairs={{0,4},{4,0},{8,12},{12,8},{16,20},{20,16},{24,28},{28,24},{1,5},{5... | collective-permute-start | bytes 786440 | tf_op jit(solution)/shard_map/ppermute | solution.py:28
  34.2 16.1 %collective-permute-start.13 = (bf16[1,64,3072]{2,1,0:T(8,128)(2,1)S(1)}, bf16[1,64,3072]{2,1,0:T(8,128)(2,1)S(1)}, u32[]{:S(2)}, u32[]{:S(2)}) collective-permute-start(bf16[1,64,3072]{2,1,0:T(8,128)(2,1)S(1)} %get-tuple-element.30.refs_1_), channel_id=1, source_target_pairs={{0,2},{1,3},{2,0},{3,1},{4,6},{5,7},{6,4},{7,5},{8,10},{9,11},{10,... | collective-permute-start | bytes 1179656 | tf_op jit(solution)/shard_map/ppermute | solution.py:23
  37.7 10.4 %collective-permute-start.6 = (bf16[2,64,1024]{2,1,0:T(8,128)(2,1)S(1)}, bf16[2,64,1024]{2,1,0:T(8,128)(2,1)S(1)}, u32[]{:S(2)}, u32[]{:S(2)}) collective-permute-start(bf16[2,64,1024]{2,1,0:T(8,128)(2,1)S(1)} %shard_map.65.refs_2_), channel_id=1, source_target_pairs={{0,8},{4,12},{8,16},{12,20},{16,24},{20,28},{24,0},{28,4},{1,9},{5... | collective-permute-start | bytes 786440 | tf_op jit(solution)/shard_map/ppermute | solution.py:23
  43.9 8.9 %collective-permute-start.14 = (bf16[2,64,1024]{2,1,0:T(8,128)(2,1)S(1)}, bf16[2,64,1024]{2,1,0:T(8,128)(2,1)S(1)}, u32[]{:S(2)}, u32[]{:S(2)}) collective-permute-start(bf16[2,64,1024]{2,1,0:T(8,128)(2,1)S(1)} %get-tuple-element.45), channel_id=1, source_target_pairs={{0,8},{4,12},{8,16},{12,20},{16,24},{20,28},{24,0},{28,4},{1,9},{5... | collective-permute-start | bytes 786440 | tf_op jit(solution)/shard_map/ppermute | solution.py:23
  44.1 8.8 %collective-permute-start.12 = (bf16[2,64,1024]{2,1,0:T(8,128)(2,1)S(1)}, bf16[2,64,1024]{2,1,0:T(8,128)(2,1)S(1)}, u32[]{:S(2)}, u32[]{:S(2)}) collective-permute-start(bf16[2,64,1024]{2,1,0:T(8,128)(2,1)S(1)} %get-tuple-element.42.refs_2_), channel_id=1, source_target_pairs={{0,4},{4,0},{8,12},{12,8},{16,20},{20,16},{24,28},{28,24},{1,5},{5... | collective-permute-start | bytes 786440 | tf_op jit(solution)/shard_map/ppermute | solution.py:28
  45.7 11.6 %collective-permute-start.19 = (bf16[1,64,1536]{2,1,0:T(8,128)(2,1)S(1)}, bf16[1,64,1536]{2,1,0:T(8,128)(2,1)S(1)}, u32[]{:S(2)}, u32[]{:S(2)}) collective-permute-start(bf16[1,64,1536]{2,1,0:T(8,128)(2,1)S(1)} %get-tuple-element.31.refs_2_), channel_id=1, source_target_pairs={{0,2},{1,3},{2,0},{3,1},{4,6},{5,7},{6,4},{7,5},{8,10},{9,11},{10,... | collective-permute-start | bytes 589832 | tf_op jit(solution)/shard_map/ppermute | solution.py:23
  48.1 10.4 %collective-permute-start.18 = (bf16[1,64,1536]{2,1,0:T(8,128)(2,1)S(1)}, bf16[1,64,1536]{2,1,0:T(8,128)(2,1)S(1)}, u32[]{:S(2)}, u32[]{:S(2)}) collective-permute-start(bf16[1,64,1536]{2,1,0:T(8,128)(2,1)S(1)} %get-tuple-element.32.refs_3_), channel_id=1, source_target_pairs={{0,2},{1,3},{2,0},{3,1},{4,6},{5,7},{6,4},{7,5},{8,10},{9,11},{10,... | collective-permute-start | bytes 589832 | tf_op jit(solution)/shard_map/ppermute | solution.py:23
  53.1 9.1 %collective-permute-start.16 = (bf16[64,1024]{1,0:T(8,128)(2,1)S(1)}, bf16[64,1024]{1,0:T(8,128)(2,1)S(1)}, u32[]{:S(2)}, u32[]{:S(2)}) collective-permute-start(bf16[64,1024]{1,0:T(8,128)(2,1)S(1)} %get-tuple-element.46.refs_1_), channel_id=1, source_target_pairs={{0,24},{1,25},{2,26},{3,27},{4,28},{5,29},{6,30},{7,31},{8,16},{9,... | collective-permute-start | bytes 393224 | tf_op jit(solution)/shard_map/ppermute | solution.py:311
  55.0 4.9 %collective-permute-start.15 = (bf16[64,1024]{1,0:T(8,128)(2,1)S(1)}, bf16[64,1024]{1,0:T(8,128)(2,1)S(1)}, u32[]{:S(2)}, u32[]{:S(2)}) collective-permute-start(bf16[64,1024]{1,0:T(8,128)(2,1)S(1)} %get-tuple-element.48), channel_id=1, source_target_pairs={{0,1},{1,0},{2,3},{3,2},{4,5},{5,4},{6,7},{7,6},{8,9},{9,8},{10,11... | collective-permute-start | bytes 393224 | tf_op jit(solution)/shard_map/ppermute | solution.py:54
  55.1 7.3 %collective-permute-start.17 = (bf16[64,1024]{1,0:T(8,128)(2,1)S(1)}, bf16[64,1024]{1,0:T(8,128)(2,1)S(1)}, u32[]{:S(2)}, u32[]{:S(2)}) collective-permute-start(bf16[64,1024]{1,0:T(8,128)(2,1)S(1)} %get-tuple-element.49), channel_id=1, source_target_pairs={{0,25},{1,24},{2,27},{3,26},{4,29},{5,28},{6,31},{7,30},{8,17},{9,... | collective-permute-start | bytes 393224 | tf_op jit(solution)/shard_map/ppermute | solution.py:311
  57.3 5.1 %collective-permute-start.11 = (f32[64,1024]{1,0:T(8,128)S(1)}, f32[64,1024]{1,0:T(8,128)S(1)}, u32[]{:S(2)}, u32[]{:S(2)}) collective-permute-start(f32[64,1024]{1,0:T(8,128)S(1)} %get-tuple-element.44), channel_id=1, source_target_pairs={{0,1},{1,0},{2,3},{3,2},{4,5},{5,4},{6,7},{7,6},{8,9},{9,8},{10,11... | collective-permute-start | bytes 786440 | tf_op jit(solution)/shard_map/ppermute | solution.py:54
  58.6 3.4 %copy-start.1 = (bf16[256,1024]{1,0:T(8,128)(2,1)S(1)}, bf16[256,1024]{1,0:T(8,128)(2,1)}, u32[]{:S(2)}) copy-start(bf16[256,1024]{1,0:T(8,128)(2,1)} %rhs.1) | copy-start | bytes 1572868
  58.6 3.4 %copy-start.2 = (bf16[1,256,256]{2,1,0:T(8,128)(2,1)S(1)}, bf16[1,256,256]{2,1,0:T(8,128)(2,1)}, u32[]{:S(2)}) copy-start(bf16[1,256,256]{2,1,0:T(8,128)(2,1)} %diag.1) | copy-start | bytes 393220
  59.8 5.3 %collective-permute-start.21 = (bf16[64,1024]{1,0:T(8,128)(2,1)S(1)}, bf16[64,1024]{1,0:T(8,128)(2,1)S(1)}, u32[]{:S(2)}, u32[]{:S(2)}) collective-permute-start(bf16[64,1024]{1,0:T(8,128)(2,1)S(1)} %get-tuple-element.52), channel_id=1, source_target_pairs={{0,9},{1,8},{2,11},{3,10},{4,13},{5,12},{6,15},{7,14},{8,1},{9,0},... | collective-permute-start | bytes 393224 | tf_op jit(solution)/shard_map/ppermute | solution.py:311
  59.9 8.6 %collective-permute-start.20 = (bf16[64,1024]{1,0:T(8,128)(2,1)S(1)}, bf16[64,1024]{1,0:T(8,128)(2,1)S(1)}, u32[]{:S(2)}, u32[]{:S(2)}) collective-permute-start(bf16[64,1024]{1,0:T(8,128)(2,1)S(1)} %get-tuple-element.51.refs_6_), channel_id=1, source_target_pairs={{0,8},{1,9},{2,10},{3,11},{4,12},{5,13},{6,14},{7,15},{8,0},{9,1},... | collective-permute-start | bytes 393224 | tf_op jit(solution)/shard_map/ppermute | solution.py:311

commit v7 on v6

--- a/solution.py
+++ b/solution.py
@@ -292,12 +292,17 @@
     last_give, d2f = products(y03, (0, 3), far03, [one, one], got_far)
     got_last, d2f_in = pair_swap(last_give, "col"), shift(d2f, "col", 2)
 
-    def near1_in(d1, sums, *outs):
-        for p in range(half):
-            outs[p][...] = d1[p].astype(F32) + sums[p]
-
-    sums_n = chained(near1_in, [pinned(quarter, cols, dtype=F32)] * half, [d1n_in, near_sum])
-    sums_n = to_columns(sums_n, 0)
+    def near1_in(d1, sums, out):
+        for p in range(half):
+            out[p] = d1[p].astype(F32) + sums[p]
+
+    near_all, = chained(near1_in, [wide_one], [d1n_in, near_sum])
+
+    def by_columns(total, *outs):
+        for p in range(half):
+            outs[p][...] = total[p]
+
+    sums_n = to_columns(chained(by_columns, [pinned(quarter, cols, dtype=F32)] * half, [near_all]), 0)
 
     raw, = products(y_first, ("first",), plain, [wide_one], [])
 

time: 69.9 us -> 69.9 us (level)
    pallas_call x23 -> x24, Pallas kernels: 20.2 us -> 20.2 us  [call(): pl.pallas_call(body, out_shape=outs, in_specs=specs, out_specs=out_specs...]
where the time goes in v7:
time: 69.9 us; the launch traced here: 69.7 us
  starting transfers between devices  27.5 us (39%)
  waiting for transfers between devices  21 us (30%)
  Pallas kernels  20.2 us (29%)
    pallas_call x24, Pallas kernels, call(): pl.pallas_call(body, out_shape=outs, in_specs=specs, out_specs=out_specs...  20.2 us
    ppermute x9, starting transfers between devices, shift(): lax.ppermute(block, axis, [(i, (i + distance) % size) for i in range(size)])  13.1 us
    ppermute x6, waiting for transfers between devices, pair_swap(): return lax.ppermute(block, axis, [(i, i ^ 1) for i in range(size)])  8.4 us
    ppermute x6, starting transfers between devices, pair_swap(): return lax.ppermute(block, axis, [(i, i ^ 1) for i in range(size)])  7.63 us
    ppermute x9, waiting for transfers between devices, shift(): lax.ppermute(block, axis, [(i, (i + distance) % size) for i in range(size)])  6.75 us
    ppermute x4, starting transfers between devices, send(): out.append(lax.ppermute(part, ('col', 'rhs'), route))  6.14 us
    ppermute x4, waiting for transfers between devices, send(): out.append(lax.ppermute(part, ('col', 'rhs'), route))  5.86 us
  transfers between devices with their start and end apart: 22, of which 11 were waited for; matrix products, arithmetic and copies ran while one was open for 0% of the time, Pallas kernels for 27%

profile of v7, /device:TPU:0, one launch (start us, length us, event | category | flops | bytes accessed | tf_op | source)
XLA Modules:
  0.0 69.7 jit_solution(7966903507373834750)
XLA Ops:
  0.0 0.5 collective-permute-start
  0.5 1.5 %shard_map.55.refs_2_.refs_0_ = bf16[2,64,3072]{2,1,0:T(8,128)(2,1)S(1)} custom-call(bf16[6,64,3072]{2,1,0:T(8,128)(2,1)} %bitcast.1), custom_call_target="tpu_custom_call" | custom-call | bytes 2359296 | tf_op jit(solution)/shard_map/pallas_call | solution.py:64
  1.9 2.5 %collective-permute-start.5 = (bf16[2,64,3072]{2,1,0:T(8,128)(2,1)S(1)}, bf16[2,64,3072]{2,1,0:T(8,128)(2,1)S(1)}, u32[]{:S(2)}, u32[]{:S(2)}) collective-permute-start(bf16[2,64,3072]{2,1,0:T(8,128)(2,1)S(1)} %shard_map.55.refs_2_.refs_0_), channel_id=1, source_target_pairs={{0,2},{1,3},{2,0},{3,1},{4,6},{5,7},{6,4},{7,5},{8,10},{9,11},{10,... | collective-permute-start | bytes 2359304 | tf_op jit(solution)/shard_map/ppermute | solution.py:23
  4.5 0.7 copy-done.3
  5.1 2.1 %shard_map.56 = (bf16[2,64,3072]{2,1,0:T(8,128)(2,1)S(1)}, bf16[1,64,3072]{2,1,0:T(8,128)(2,1)S(1)}, bf16[1,64,1536]{2,1,0:T(8,128)(2,1)S(1)}, bf16[1,64,1536]{2,1,0:T(8,128)(2,1)S(1)}, f32[6,256]{1,0:T(8,128)S(1)}) custom-call(bf16[6,64,3072]{2,1,0:T(8,128)(2,1)} %bitcast.2, s32[1,6]{1,0:T(1,128)S(1)} %copy-done.3, ...), custom_call_target="tpu_custom_call" | custom-call | bytes 3145752 | tf_op jit(solution)/shard_map/pallas_call | solution.py:64
  7.2 0.4 collective-permute-start.8
  7.6 1.0 %shard_map.57.refs_6_ = bf16[2,64,1024]{2,1,0:T(8,128)(2,1)S(1)} custom-call(bf16[2,64,3072]{2,1,0:T(8,128)(2,1)S(1)} %shard_map.55.refs_2_.refs_0_, bf16[3072,1024]{1,0:T(8,128)(2,1)S(1)} %copy-done, f32[6,256]{1,0:T(8,128)S(1)} %get-tuple-element.33.refs_2_.refs_5_.refs_3_, bf16[2,64,3072]{2,1,0:T(8,128)(2,1)S(1)} %get-tuple-element.29.refs_3_.refs_0_), custom_call_target="tpu_custom_call" | custom-call | flops 805306368 | bytes 7870464 | tf_op jit(solution)/shard_map/pallas_call | solution.py:64
  8.6 1.9 %collective-permute-start.1 = (bf16[2,64,1024]{2,1,0:T(8,128)(2,1)S(1)}, bf16[2,64,1024]{2,1,0:T(8,128)(2,1)S(1)}, u32[]{:S(2)}, u32[]{:S(2)}) collective-permute-start(bf16[2,64,1024]{2,1,0:T(8,128)(2,1)S(1)} %shard_map.57.refs_6_), channel_id=1, source_target_pairs={{0,4},{4,0},{8,12},{12,8},{16,20},{20,16},{24,28},{28,24},{1,5},{5... | collective-permute-start | bytes 786440 | tf_op jit(solution)/shard_map/ppermute | solution.py:28
  10.5 1.8 %shard_map.58 = (f32[3,64,1024]{2,1,0:T(8,128)S(1)}, bf16[64,1024]{1,0:T(8,128)(2,1)S(1)}) custom-call(bf16[2,64,3072]{2,1,0:T(8,128)(2,1)S(1)} %get-tuple-element.29.refs_3_.refs_0_, bf16[1,64,3072]{2,1,0:T(8,128)(2,1)S(1)} %get-tuple-element.30.refs_1_, bf16[1,64,1536]{2,1,0:T(8,128)(2,1)S(1)} %get-tuple-element.31.refs_2_, ...), custom_call_target="tpu_custom_call" | custom-call | flops 1610612736 | bytes 8132608 | tf_op jit(solution)/shard_map/pallas_call | solution.py:64
  12.3 1.0 %shard_map.59.refs_7_ = bf16[2,64,1024]{2,1,0:T(8,128)(2,1)S(1)} custom-call(bf16[2,64,3072]{2,1,0:T(8,128)(2,1)S(1)} %shard_map.55.refs_2_.refs_0_, bf16[3072,1024]{1,0:T(8,128)(2,1)S(1)} %collective-permute-done.refs_1_.refs_4_.refs_2_, f32[6,256]{1,0:T(8,128)S(1)} %get-tuple-element.33.refs_2_.refs_5_.refs_3_, ...), custom_call_target="tpu_custom_call" | custom-call | flops 805306368 | bytes 7870464 | tf_op jit(solution)/shard_map/pallas_call | solution.py:64
  13.4 1.0 %collective-permute-start.2 = (bf16[2,64,1024]{2,1,0:T(8,128)(2,1)S(1)}, bf16[2,64,1024]{2,1,0:T(8,128)(2,1)S(1)}, u32[]{:S(2)}, u32[]{:S(2)}) collective-permute-start(bf16[2,64,1024]{2,1,0:T(8,128)(2,1)S(1)} %shard_map.59.refs_7_), channel_id=1, source_target_pairs={{0,4},{4,0},{8,12},{12,8},{16,20},{20,16},{24,28},{28,24},{1,5},{5... | collective-permute-start | bytes 786440 | tf_op jit(solution)/shard_map/ppermute | solution.py:28
  14.4 1.8 %shard_map.60 = (f32[3,64,1024]{2,1,0:T(8,128)S(1)}, bf16[2,64,1024]{2,1,0:T(8,128)(2,1)S(1)}) custom-call(bf16[2,64,3072]{2,1,0:T(8,128)(2,1)S(1)} %get-tuple-element.29.refs_3_.refs_0_, bf16[1,64,3072]{2,1,0:T(8,128)(2,1)S(1)} %get-tuple-element.30.refs_1_, bf16[1,64,1536]{2,1,0:T(8,128)(2,1)S(1)} %get-tuple-element.31.refs_2_, ...), custom_call_target="tpu_custom_call" | custom-call | flops 1610612736 | bytes 8263680 | tf_op jit(solution)/shard_map/pallas_call | solution.py:64
  16.2 1.1 %collective-permute-start.3 = (bf16[2,64,1024]{2,1,0:T(8,128)(2,1)S(1)}, bf16[2,64,1024]{2,1,0:T(8,128)(2,1)S(1)}, u32[]{:S(2)}, u32[]{:S(2)}) collective-permute-start(bf16[2,64,1024]{2,1,0:T(8,128)(2,1)S(1)} %get-tuple-element.39), channel_id=1, source_target_pairs={{0,4},{4,0},{8,12},{12,8},{16,20},{20,16},{24,28},{28,24},{1,5},{5... | collective-permute-start | bytes 786440 | tf_op jit(solution)/shard_map/ppermute | solution.py:28
  17.3 0.5 collective-permute-done.1.refs_2_
  17.8 5.6 %collective-permute-done.2.refs_3_ = bf16[2,64,1024]{2,1,0:T(8,128)(2,1)S(1)} collective-permute-done((bf16[2,64,1024]{2,1,0:T(8,128)(2,1)S(1)}, bf16[2,64,1024]{2,1,0:T(8,128)(2,1)S(1)}, u32[]{:S(2)}, u32[]{:S(2)}) %collective-permute-start.2) | collective-permute-done | bytes 262176 | tf_op jit(solution)/shard_map/ppermute | solution.py:28
  23.5 0.1 shard_map.62.refs_4_
  23.5 2.0 %collective-permute-start.4 = (bf16[2,64,1024]{2,1,0:T(8,128)(2,1)S(1)}, bf16[2,64,1024]{2,1,0:T(8,128)(2,1)S(1)}, u32[]{:S(2)}, u32[]{:S(2)}) collective-permute-start(bf16[2,64,1024]{2,1,0:T(8,128)(2,1)S(1)} %shard_map.62.refs_4_), channel_id=1, source_target_pairs={{0,8},{4,12},{8,16},{12,20},{16,24},{20,28},{24,0},{28,4},{1,9},{5... | collective-permute-start | bytes 786440 | tf_op jit(solution)/shard_map/ppermute | solution.py:23
  25.5 1.9 %shard_map.63 = (bf16[2,64,1024]{2,1,0:T(8,128)(2,1)S(1)}, bf16[2,64,1024]{2,1,0:T(8,128)(2,1)S(1)}) custom-call(bf16[2,64,3072]{2,1,0:T(8,128)(2,1)S(1)} %collective-permute-done.5.refs_0_, bf16[3072,1024]{1,0:T(8,128)(2,1)S(1)} %copy-done, bf16[3072,1024]{1,0:T(8,128)(2,1)S(1)} %collective-permute-done.refs_1_.refs_4_.refs_2_, ...), custom_call_target="tpu_custom_call" | custom-call | flops 1610612736 | bytes 13637632 | tf_op jit(solution)/shard_map/pallas_call | solution.py:64
  27.4 0.1 shard_map.64.refs_6_
  27.5 2.1 %collective-permute-start.7 = (bf16[2,64,1024]{2,1,0:T(8,128)(2,1)S(1)}, bf16[2,64,1024]{2,1,0:T(8,128)(2,1)S(1)}, u32[]{:S(2)}, u32[]{:S(2)}) collective-permute-start(bf16[2,64,1024]{2,1,0:T(8,128)(2,1)S(1)} %shard_map.64.refs_6_), channel_id=1, source_target_pairs={{0,24},{4,28},{8,0},{12,4},{16,8},{20,12},{24,16},{28,20},{1,25},{... | collective-permute-start | bytes 786440 | tf_op jit(solution)/shard_map/ppermute | solution.py:23
  29.6 1.7 %collective-permute-start.10 = (bf16[2,64,1024]{2,1,0:T(8,128)(2,1)S(1)}, bf16[2,64,1024]{2,1,0:T(8,128)(2,1)S(1)}, u32[]{:S(2)}, u32[]{:S(2)}) collective-permute-start(bf16[2,64,1024]{2,1,0:T(8,128)(2,1)S(1)} %get-tuple-element.41), channel_id=1, source_target_pairs={{0,4},{4,0},{8,12},{12,8},{16,20},{20,16},{24,28},{28,24},{1,5},{5... | collective-permute-start | bytes 786440 | tf_op jit(solution)/shard_map/ppermute | solution.py:28
  31.3 0.3 collective-permute-start.9
  31.6 2.6 %collective-permute-done.4.refs_5_ = bf16[2,64,1024]{2,1,0:T(8,128)(2,1)S(1)} collective-permute-done((bf16[2,64,1024]{2,1,0:T(8,128)(2,1)S(1)}, bf16[2,64,1024]{2,1,0:T(8,128)(2,1)S(1)}, u32[]{:S(2)}, u32[]{:S(2)}) %collective-permute-start.4) | collective-permute-done | bytes 262176 | tf_op jit(solution)/shard_map/ppermute | solution.py:23
  34.3 1.6 %collective-permute-start.13 = (bf16[1,64,3072]{2,1,0:T(8,128)(2,1)S(1)}, bf16[1,64,3072]{2,1,0:T(8,128)(2,1)S(1)}, u32[]{:S(2)}, u32[]{:S(2)}) collective-permute-start(bf16[1,64,3072]{2,1,0:T(8,128)(2,1)S(1)} %get-tuple-element.30.refs_1_), channel_id=1, source_target_pairs={{0,2},{1,3},{2,0},{3,1},{4,6},{5,7},{6,4},{7,5},{8,10},{9,11},{10,... | collective-permute-start | bytes 1179656 | tf_op jit(solution)/shard_map/ppermute | solution.py:23
  35.9 0.1 shard_map.65.refs_2_
  36.0 1.7 %collective-permute-done.7.refs_0_ = bf16[2,64,1024]{2,1,0:T(8,128)(2,1)S(1)} collective-permute-done((bf16[2,64,1024]{2,1,0:T(8,128)(2,1)S(1)}, bf16[2,64,1024]{2,1,0:T(8,128)(2,1)S(1)}, u32[]{:S(2)}, u32[]{:S(2)}) %collective-permute-start.7) | collective-permute-done | bytes 262176 | tf_op jit(solution)/shard_map/ppermute | solution.py:23
  37.7 0.6 collective-permute-start.6
  38.3 0.1 shard_map.66.refs_6_.refs_1_
  38.4 1.3 %collective-permute-done.8.refs_0_ = bf16[2,64,3072]{2,1,0:T(8,128)(2,1)S(1)} collective-permute-done((bf16[2,64,3072]{2,1,0:T(8,128)(2,1)S(1)}, bf16[2,64,3072]{2,1,0:T(8,128)(2,1)S(1)}, u32[]{:S(2)}, u32[]{:S(2)}) %collective-permute-start.8) | collective-permute-done | bytes 786464 | tf_op jit(solution)/shard_map/ppermute | solution.py:23
  39.7 2.3 %collective-permute-done.9.refs_4_.refs_1_ = bf16[2,64,1024]{2,1,0:T(8,128)(2,1)S(1)} collective-permute-done((bf16[2,64,1024]{2,1,0:T(8,128)(2,1)S(1)}, bf16[2,64,1024]{2,1,0:T(8,128)(2,1)S(1)}, u32[]{:S(2)}, u32[]{:S(2)}) %collective-permute-start.9) | collective-permute-done | bytes 262176 | tf_op jit(solution)/shard_map/ppermute | solution.py:28
  42.0 1.9 %shard_map.67 = (bf16[2,64,1024]{2,1,0:T(8,128)(2,1)S(1)}, bf16[2,64,1024]{2,1,0:T(8,128)(2,1)S(1)}) custom-call(bf16[2,64,3072]{2,1,0:T(8,128)(2,1)S(1)} %collective-permute-done.8.refs_0_, bf16[3072,1024]{1,0:T(8,128)(2,1)S(1)} %copy-done, bf16[3072,1024]{1,0:T(8,128)(2,1)S(1)} %collective-permute-done.refs_1_.refs_4_.refs_2_, ...), custom_call_target="tpu_custom_call" | custom-call | flops 1610612736 | bytes 14424064 | tf_op jit(solution)/shard_map/pallas_call | solution.py:64
  43.9 0.2 collective-permute-start.14
  44.1 1.6 %collective-permute-start.12 = (bf16[2,64,1024]{2,1,0:T(8,128)(2,1)S(1)}, bf16[2,64,1024]{2,1,0:T(8,128)(2,1)S(1)}, u32[]{:S(2)}, u32[]{:S(2)}) collective-permute-start(bf16[2,64,1024]{2,1,0:T(8,128)(2,1)S(1)} %get-tuple-element.42.refs_2_), channel_id=1, source_target_pairs={{0,4},{4,0},{8,12},{12,8},{16,20},{20,16},{24,28},{28,24},{1,5},{5... | collective-permute-start | bytes 786440 | tf_op jit(solution)/shard_map/ppermute | solution.py:28
  45.7 1.5 %collective-permute-start.19 = (bf16[1,64,1536]{2,1,0:T(8,128)(2,1)S(1)}, bf16[1,64,1536]{2,1,0:T(8,128)(2,1)S(1)}, u32[]{:S(2)}, u32[]{:S(2)}) collective-permute-start(bf16[1,64,1536]{2,1,0:T(8,128)(2,1)S(1)} %get-tuple-element.31.refs_2_), channel_id=1, source_target_pairs={{0,2},{1,3},{2,0},{3,1},{4,6},{5,7},{6,4},{7,5},{8,10},{9,11},{10,... | collective-permute-start | bytes 589832 | tf_op jit(solution)/shard_map/ppermute | solution.py:23
  47.2 0.9 %collective-permute-done.6.refs_0_ = bf16[2,64,1024]{2,1,0:T(8,128)(2,1)S(1)} collective-permute-done((bf16[2,64,1024]{2,1,0:T(8,128)(2,1)S(1)}, bf16[2,64,1024]{2,1,0:T(8,128)(2,1)S(1)}, u32[]{:S(2)}, u32[]{:S(2)}) %collective-permute-start.6) | collective-permute-done | bytes 262176 | tf_op jit(solution)/shard_map/ppermute | solution.py:23
  48.1 2.1 %collective-permute-start.18 = (bf16[1,64,1536]{2,1,0:T(8,128)(2,1)S(1)}, bf16[1,64,1536]{2,1,0:T(8,128)(2,1)S(1)}, u32[]{:S(2)}, u32[]{:S(2)}) collective-permute-start(bf16[1,64,1536]{2,1,0:T(8,128)(2,1)S(1)} %get-tuple-element.32.refs_3_), channel_id=1, source_target_pairs={{0,2},{1,3},{2,0},{3,1},{4,6},{5,7},{6,4},{7,5},{8,10},{9,11},{10,... | collective-permute-start | bytes 589832 | tf_op jit(solution)/shard_map/ppermute | solution.py:23
  50.4 2.3 %shard_map.70.refs_2_.refs_0_ = f32[2,64,1024]{2,1,0:T(8,128)S(1)} custom-call(bf16[1,64,3072]{2,1,0:T(8,128)(2,1)S(1)} %collective-permute-done.13.refs_0_, bf16[3072,1024]{1,0:T(8,128)(2,1)S(1)} %copy-done, bf16[3072,1024]{1,0:T(8,128)(2,1)S(1)} %collective-permute-done.refs_1_.refs_4_.refs_2_, f32[6,256]{1,0:T(8,128)S(1)} %get-tuple-element.33.refs_2_.refs_5_.refs_3_, ...), custom_call_target="tpu_custom_call" | custom-call | flops 805306368 | bytes 13244416 | tf_op jit(solution)/shard_map/pallas_call | solution.py:64
  52.7 0.2 collective-permute-done.14.refs_0_
  52.8 0.1 shard_map.71.refs_3_.refs_4_
  52.9 0.0 collective-permute-done.12.refs_2_.refs_0_
  52.9 0.2 shard_map.72
  53.1 1.8 %collective-permute-start.16 = (bf16[64,1024]{1,0:T(8,128)(2,1)S(1)}, bf16[64,1024]{1,0:T(8,128)(2,1)S(1)}, u32[]{:S(2)}, u32[]{:S(2)}) collective-permute-start(bf16[64,1024]{1,0:T(8,128)(2,1)S(1)} %get-tuple-element.46.refs_1_), channel_id=1, source_target_pairs={{0,24},{1,25},{2,26},{3,27},{4,28},{5,29},{6,30},{7,31},{8,16},{9,... | collective-permute-start | bytes 393224 | tf_op jit(solution)/shard_map/ppermute | solution.py:316
  54.9 0.1 shard_map.73
  55.0 0.1 collective-permute-start.15
  55.1 2.2 %collective-permute-start.17 = (bf16[64,1024]{1,0:T(8,128)(2,1)S(1)}, bf16[64,1024]{1,0:T(8,128)(2,1)S(1)}, u32[]{:S(2)}, u32[]{:S(2)}) collective-permute-start(bf16[64,1024]{1,0:T(8,128)(2,1)S(1)} %get-tuple-element.49), channel_id=1, source_target_pairs={{0,25},{1,24},{2,27},{3,26},{4,29},{5,28},{6,31},{7,30},{8,17},{9,... | collective-permute-start | bytes 393224 | tf_op jit(solution)/shard_map/ppermute | solution.py:316
  57.3 0.0 collective-permute-done.19.refs_0_
  57.3 0.1 collective-permute-start.11
  57.4 1.2 %shard_map.74.refs_4_.refs_6_ = f32[2,64,1024]{2,1,0:T(8,128)S(1)} custom-call(bf16[1,64,1536]{2,1,0:T(8,128)(2,1)S(1)} %collective-permute-done.19.refs_0_, bf16[3072,1024]{1,0:T(8,128)(2,1)S(1)} %copy-done, bf16[3072,1024]{1,0:T(8,128)(2,1)S(1)} %collective-permute-done.refs_1_.refs_4_.refs_2_, f32[6,256]{1,0:T(8,128)S(1)} %get-tuple-element.33.refs_2_.refs_5_.refs_3_, ...), custom_call_target="tpu_custom_call" | custom-call | flops 805306368 | bytes 12916736 | tf_op jit(solution)/shard_map/pallas_call | solution.py:64
  58.6 0.0 collective-permute-done.18.refs_0_
  58.6 0.0 copy-start.1
  58.6 0.0 copy-start.2
  58.6 1.2 %shard_map.75 = (bf16[64,1024]{1,0:T(8,128)(2,1)S(1)}, bf16[64,1024]{1,0:T(8,128)(2,1)S(1)}) custom-call(bf16[1,64,1536]{2,1,0:T(8,128)(2,1)S(1)} %collective-permute-done.18.refs_0_, bf16[3072,1024]{1,0:T(8,128)(2,1)S(1)} %copy-done, bf16[3072,1024]{1,0:T(8,128)(2,1)S(1)} %collective-permute-done.refs_1_.refs_4_.refs_2_, ...), custom_call_target="tpu_custom_call" | custom-call | flops 805306368 | bytes 14358528 | tf_op jit(solution)/shard_map/pallas_call | solution.py:64
  59.8 0.1 collective-permute-start.21
  59.9 0.0 collective-permute-done.15.refs_3_
  59.9 2.1 %collective-permute-start.20 = (bf16[64,1024]{1,0:T(8,128)(2,1)S(1)}, bf16[64,1024]{1,0:T(8,128)(2,1)S(1)}, u32[]{:S(2)}, u32[]{:S(2)}) collective-permute-start(bf16[64,1024]{1,0:T(8,128)(2,1)S(1)} %get-tuple-element.51.refs_6_), channel_id=1, source_target_pairs={{0,8},{1,9},{2,10},{3,11},{4,12},{5,13},{6,14},{7,15},{8,0},{9,1},... | collective-permute-start | bytes 393224 | tf_op jit(solution)/shard_map/ppermute | solution.py:316
  62.0 0.2 shard_map.61
  62.2 0.0 collective-permute-done.16.refs_4_
  62.2 0.1 collective-permute-done.17.refs_5_
  62.4 0.0 collective-permute-done.11.refs_1_
  62.4 0.1 shard_map.76.refs_2_.refs_4_.known
  62.5 2.6 %collective-permute-done.21.refs_3_ = bf16[64,1024]{1,0:T(8,128)(2,1)S(1)} collective-permute-done((bf16[64,1024]{1,0:T(8,128)(2,1)S(1)}, bf16[64,1024]{1,0:T(8,128)(2,1)S(1)}, u32[]{:S(2)}, u32[]{:S(2)}) %collective-permute-start.21) | collective-permute-done | bytes 131104 | tf_op jit(solution)/shard_map/ppermute | solution.py:316
  65.1 0.3 shard_map.77.part
  65.4 3.1 %collective-permute-done.20.last = bf16[64,1024]{1,0:T(8,128)(2,1)S(1)} collective-permute-done((bf16[64,1024]{1,0:T(8,128)(2,1)S(1)}, bf16[64,1024]{1,0:T(8,128)(2,1)S(1)}, u32[]{:S(2)}, u32[]{:S(2)}) %collective-permute-start.20) | collective-permute-done | bytes 131104 | tf_op jit(solution)/shard_map/ppermute | solution.py:316
  68.5 1.1 %shard_map.78 = bf16[256,1024]{1,0:T(8,128)(2,1)} custom-call(bf16[256,1024]{1,0:T(8,128)(2,1)S(1)} %get-tuple-element.37.refs_0_.rhs, bf16[256,256]{1,0:T(8,128)(2,1)S(1)} %get-tuple-element.38.refs_1_.diag, f32[256,1024]{1,0:T(8,128)S(1)} %shard_map.76.refs_2_.refs_4_.known, bf16[64,1024]{1,0:T(8,128)(2,1)S(1)} %collective-permute-done.20.last, ...), custom_call_target="tpu_custom_call" | custom-call | flops 33554432 | bytes 2883584 | tf_op jit(solution)/shard_map/pallas_call | solution.py:64
  (12 shorter events, 0.1 us)
Async XLA Ops:
  0.0 7.6 %copy-start = (bf16[3072,1024]{1,0:T(8,128)(2,1)S(1)}, bf16[3072,1024]{1,0:T(8,128)(2,1)}, u32[]{:S(2)}) copy-start(bf16[3072,1024]{1,0:T(8,128)(2,1)} %refs_1_.13) | copy-start | bytes 18874372
  0.0 12.3 %collective-permute-start = (bf16[3072,1024]{1,0:T(8,128)(2,1)}, bf16[3072,1024]{1,0:T(8,128)(2,1)S(1)}, u32[]{:S(2)}, u32[]{:S(2)}) collective-permute-start(bf16[3072,1024]{1,0:T(8,128)(2,1)} %refs_1_.13), channel_id=1, source_target_pairs={{1,0},{0,1},{3,2},{2,3},{5,4},{4,5},{7,6},{6,7},{9,8},{8,9},{11,10... | collective-permute-start | bytes 18874376 | tf_op jit(solution)/shard_map/ppermute | solution.py:44
  1.9 23.6 %collective-permute-start.5 = (bf16[2,64,3072]{2,1,0:T(8,128)(2,1)S(1)}, bf16[2,64,3072]{2,1,0:T(8,128)(2,1)S(1)}, u32[]{:S(2)}, u32[]{:S(2)}) collective-permute-start(bf16[2,64,3072]{2,1,0:T(8,128)(2,1)S(1)} %shard_map.55.refs_2_.refs_0_), channel_id=1, source_target_pairs={{0,2},{1,3},{2,0},{3,1},{4,6},{5,7},{6,4},{7,5},{8,10},{9,11},{10,... | collective-permute-start | bytes 2359304 | tf_op jit(solution)/shard_map/ppermute | solution.py:23
  4.5 0.7 copy-start.3
  7.2 32.5 %collective-permute-start.8 = (bf16[2,64,3072]{2,1,0:T(8,128)(2,1)S(1)}, bf16[2,64,3072]{2,1,0:T(8,128)(2,1)S(1)}, u32[]{:S(2)}, u32[]{:S(2)}) collective-permute-start(bf16[2,64,3072]{2,1,0:T(8,128)(2,1)S(1)} %get-tuple-element.29.refs_3_.refs_0_), channel_id=1, source_target_pairs={{0,2},{1,3},{2,0},{3,1},{4,6},{5,7},{6,4},{7,5},{8,10},{9,11},{10,... | collective-permute-start | bytes 2359304 | tf_op jit(solution)/shard_map/ppermute | solution.py:23
  8.6 9.2 %collective-permute-start.1 = (bf16[2,64,1024]{2,1,0:T(8,128)(2,1)S(1)}, bf16[2,64,1024]{2,1,0:T(8,128)(2,1)S(1)}, u32[]{:S(2)}, u32[]{:S(2)}) collective-permute-start(bf16[2,64,1024]{2,1,0:T(8,128)(2,1)S(1)} %shard_map.57.refs_6_), channel_id=1, source_target_pairs={{0,4},{4,0},{8,12},{12,8},{16,20},{20,16},{24,28},{28,24},{1,5},{5... | collective-permute-start | bytes 786440 | tf_op jit(solution)/shard_map/ppermute | solution.py:28
  13.4 10.1 %collective-permute-start.2 = (bf16[2,64,1024]{2,1,0:T(8,128)(2,1)S(1)}, bf16[2,64,1024]{2,1,0:T(8,128)(2,1)S(1)}, u32[]{:S(2)}, u32[]{:S(2)}) collective-permute-start(bf16[2,64,1024]{2,1,0:T(8,128)(2,1)S(1)} %shard_map.59.refs_7_), channel_id=1, source_target_pairs={{0,4},{4,0},{8,12},{12,8},{16,20},{20,16},{24,28},{28,24},{1,5},{5... | collective-permute-start | bytes 786440 | tf_op jit(solution)/shard_map/ppermute | solution.py:28
  16.2 15.1 %collective-permute-start.3 = (bf16[2,64,1024]{2,1,0:T(8,128)(2,1)S(1)}, bf16[2,64,1024]{2,1,0:T(8,128)(2,1)S(1)}, u32[]{:S(2)}, u32[]{:S(2)}) collective-permute-start(bf16[2,64,1024]{2,1,0:T(8,128)(2,1)S(1)} %get-tuple-element.39), channel_id=1, source_target_pairs={{0,4},{4,0},{8,12},{12,8},{16,20},{20,16},{24,28},{28,24},{1,5},{5... | collective-permute-start | bytes 786440 | tf_op jit(solution)/shard_map/ppermute | solution.py:28
  23.5 10.7 %collective-permute-start.4 = (bf16[2,64,1024]{2,1,0:T(8,128)(2,1)S(1)}, bf16[2,64,1024]{2,1,0:T(8,128)(2,1)S(1)}, u32[]{:S(2)}, u32[]{:S(2)}) collective-permute-start(bf16[2,64,1024]{2,1,0:T(8,128)(2,1)S(1)} %shard_map.62.refs_4_), channel_id=1, source_target_pairs={{0,8},{4,12},{8,16},{12,20},{16,24},{20,28},{24,0},{28,4},{1,9},{5... | collective-permute-start | bytes 786440 | tf_op jit(solution)/shard_map/ppermute | solution.py:23
  27.5 10.2 %collective-permute-start.7 = (bf16[2,64,1024]{2,1,0:T(8,128)(2,1)S(1)}, bf16[2,64,1024]{2,1,0:T(8,128)(2,1)S(1)}, u32[]{:S(2)}, u32[]{:S(2)}) collective-permute-start(bf16[2,64,1024]{2,1,0:T(8,128)(2,1)S(1)} %shard_map.64.refs_6_), channel_id=1, source_target_pairs={{0,24},{4,28},{8,0},{12,4},{16,8},{20,12},{24,16},{28,20},{1,25},{... | collective-permute-start | bytes 786440 | tf_op jit(solution)/shard_map/ppermute | solution.py:23
  29.6 10.1 %collective-permute-start.10 = (bf16[2,64,1024]{2,1,0:T(8,128)(2,1)S(1)}, bf16[2,64,1024]{2,1,0:T(8,128)(2,1)S(1)}, u32[]{:S(2)}, u32[]{:S(2)}) collective-permute-start(bf16[2,64,1024]{2,1,0:T(8,128)(2,1)S(1)} %get-tuple-element.41), channel_id=1, source_target_pairs={{0,4},{4,0},{8,12},{12,8},{16,20},{20,16},{24,28},{28,24},{1,5},{5... | collective-permute-start | bytes 786440 | tf_op jit(solution)/shard_map/ppermute | solution.py:28
  31.3 10.7 %collective-permute-start.9 = (bf16[2,64,1024]{2,1,0:T(8,128)(2,1)S(1)}, bf16[2,64,1024]{2,1,0:T(8,128)(2,1)S(1)}, u32[]{:S(2)}, u32[]{:S(2)}) collective-permute-start(bf16[2,64,1024]{2,1,0:T(8,128)(2,1)S(1)} %get-tuple-element.40.refs_4_), channel_id=1, source_target_pairs={{0,4},{4,0},{8,12},{12,8},{16,20},{20,16},{24,28},{28,24},{1,5},{5... | collective-permute-start | bytes 786440 | tf_op jit(solution)/shard_map/ppermute | solution.py:28
  34.3 16.1 %collective-permute-start.13 = (bf16[1,64,3072]{2,1,0:T(8,128)(2,1)S(1)}, bf16[1,64,3072]{2,1,0:T(8,128)(2,1)S(1)}, u32[]{:S(2)}, u32[]{:S(2)}) collective-permute-start(bf16[1,64,3072]{2,1,0:T(8,128)(2,1)S(1)} %get-tuple-element.30.refs_1_), channel_id=1, source_target_pairs={{0,2},{1,3},{2,0},{3,1},{4,6},{5,7},{6,4},{7,5},{8,10},{9,11},{10,... | collective-permute-start | bytes 1179656 | tf_op jit(solution)/shard_map/ppermute | solution.py:23
  37.7 10.4 %collective-permute-start.6 = (bf16[2,64,1024]{2,1,0:T(8,128)(2,1)S(1)}, bf16[2,64,1024]{2,1,0:T(8,128)(2,1)S(1)}, u32[]{:S(2)}, u32[]{:S(2)}) collective-permute-start(bf16[2,64,1024]{2,1,0:T(8,128)(2,1)S(1)} %shard_map.65.refs_2_), channel_id=1, source_target_pairs={{0,8},{4,12},{8,16},{12,20},{16,24},{20,28},{24,0},{28,4},{1,9},{5... | collective-permute-start | bytes 786440 | tf_op jit(solution)/shard_map/ppermute | solution.py:23
  43.9 9.0 %collective-permute-start.14 = (bf16[2,64,1024]{2,1,0:T(8,128)(2,1)S(1)}, bf16[2,64,1024]{2,1,0:T(8,128)(2,1)S(1)}, u32[]{:S(2)}, u32[]{:S(2)}) collective-permute-start(bf16[2,64,1024]{2,1,0:T(8,128)(2,1)S(1)} %get-tuple-element.45), channel_id=1, source_target_pairs={{0,8},{4,12},{8,16},{12,20},{16,24},{20,28},{24,0},{28,4},{1,9},{5... | collective-permute-start | bytes 786440 | tf_op jit(solution)/shard_map/ppermute | solution.py:23
  44.1 8.8 %collective-permute-start.12 = (bf16[2,64,1024]{2,1,0:T(8,128)(2,1)S(1)}, bf16[2,64,1024]{2,1,0:T(8,128)(2,1)S(1)}, u32[]{:S(2)}, u32[]{:S(2)}) collective-permute-start(bf16[2,64,1024]{2,1,0:T(8,128)(2,1)S(1)} %get-tuple-element.42.refs_2_), channel_id=1, source_target_pairs={{0,4},{4,0},{8,12},{12,8},{16,20},{20,16},{24,28},{28,24},{1,5},{5... | collective-permute-start | bytes 786440 | tf_op jit(solution)/shard_map/ppermute | solution.py:28
  45.7 11.6 %collective-permute-start.19 = (bf16[1,64,1536]{2,1,0:T(8,128)(2,1)S(1)}, bf16[1,64,1536]{2,1,0:T(8,128)(2,1)S(1)}, u32[]{:S(2)}, u32[]{:S(2)}) collective-permute-start(bf16[1,64,1536]{2,1,0:T(8,128)(2,1)S(1)} %get-tuple-element.31.refs_2_), channel_id=1, source_target_pairs={{0,2},{1,3},{2,0},{3,1},{4,6},{5,7},{6,4},{7,5},{8,10},{9,11},{10,... | collective-permute-start | bytes 589832 | tf_op jit(solution)/shard_map/ppermute | solution.py:23
  48.1 10.4 %collective-permute-start.18 = (bf16[1,64,1536]{2,1,0:T(8,128)(2,1)S(1)}, bf16[1,64,1536]{2,1,0:T(8,128)(2,1)S(1)}, u32[]{:S(2)}, u32[]{:S(2)}) collective-permute-start(bf16[1,64,1536]{2,1,0:T(8,128)(2,1)S(1)} %get-tuple-element.32.refs_3_), channel_id=1, source_target_pairs={{0,2},{1,3},{2,0},{3,1},{4,6},{5,7},{6,4},{7,5},{8,10},{9,11},{10,... | collective-permute-start | bytes 589832 | tf_op jit(solution)/shard_map/ppermute | solution.py:23
  53.1 9.1 %collective-permute-start.16 = (bf16[64,1024]{1,0:T(8,128)(2,1)S(1)}, bf16[64,1024]{1,0:T(8,128)(2,1)S(1)}, u32[]{:S(2)}, u32[]{:S(2)}) collective-permute-start(bf16[64,1024]{1,0:T(8,128)(2,1)S(1)} %get-tuple-element.46.refs_1_), channel_id=1, source_target_pairs={{0,24},{1,25},{2,26},{3,27},{4,28},{5,29},{6,30},{7,31},{8,16},{9,... | collective-permute-start | bytes 393224 | tf_op jit(solution)/shard_map/ppermute | solution.py:316
  55.0 4.9 %collective-permute-start.15 = (bf16[64,1024]{1,0:T(8,128)(2,1)S(1)}, bf16[64,1024]{1,0:T(8,128)(2,1)S(1)}, u32[]{:S(2)}, u32[]{:S(2)}) collective-permute-start(bf16[64,1024]{1,0:T(8,128)(2,1)S(1)} %get-tuple-element.48), channel_id=1, source_target_pairs={{0,1},{1,0},{2,3},{3,2},{4,5},{5,4},{6,7},{7,6},{8,9},{9,8},{10,11... | collective-permute-start | bytes 393224 | tf_op jit(solution)/shard_map/ppermute | solution.py:54
  55.1 7.3 %collective-permute-start.17 = (bf16[64,1024]{1,0:T(8,128)(2,1)S(1)}, bf16[64,1024]{1,0:T(8,128)(2,1)S(1)}, u32[]{:S(2)}, u32[]{:S(2)}) collective-permute-start(bf16[64,1024]{1,0:T(8,128)(2,1)S(1)} %get-tuple-element.49), channel_id=1, source_target_pairs={{0,25},{1,24},{2,27},{3,26},{4,29},{5,28},{6,31},{7,30},{8,17},{9,... | collective-permute-start | bytes 393224 | tf_op jit(solution)/shard_map/ppermute | solution.py:316
  57.3 5.1 %collective-permute-start.11 = (f32[64,1024]{1,0:T(8,128)S(1)}, f32[64,1024]{1,0:T(8,128)S(1)}, u32[]{:S(2)}, u32[]{:S(2)}) collective-permute-start(f32[64,1024]{1,0:T(8,128)S(1)} %get-tuple-element.44), channel_id=1, source_target_pairs={{0,1},{1,0},{2,3},{3,2},{4,5},{5,4},{6,7},{7,6},{8,9},{9,8},{10,11... | collective-permute-start | bytes 786440 | tf_op jit(solution)/shard_map/ppermute | solution.py:54
  58.6 3.4 %copy-start.1 = (bf16[256,1024]{1,0:T(8,128)(2,1)S(1)}, bf16[256,1024]{1,0:T(8,128)(2,1)}, u32[]{:S(2)}) copy-start(bf16[256,1024]{1,0:T(8,128)(2,1)} %rhs.1) | copy-start | bytes 1572868
  58.6 3.4 %copy-start.2 = (bf16[1,256,256]{2,1,0:T(8,128)(2,1)S(1)}, bf16[1,256,256]{2,1,0:T(8,128)(2,1)}, u32[]{:S(2)}) copy-start(bf16[1,256,256]{2,1,0:T(8,128)(2,1)} %diag.1) | copy-start | bytes 393220
  59.8 5.3 %collective-permute-start.21 = (bf16[64,1024]{1,0:T(8,128)(2,1)S(1)}, bf16[64,1024]{1,0:T(8,128)(2,1)S(1)}, u32[]{:S(2)}, u32[]{:S(2)}) collective-permute-start(bf16[64,1024]{1,0:T(8,128)(2,1)S(1)} %get-tuple-element.52), channel_id=1, source_target_pairs={{0,9},{1,8},{2,11},{3,10},{4,13},{5,12},{6,15},{7,14},{8,1},{9,0},... | collective-permute-start | bytes 393224 | tf_op jit(solution)/shard_map/ppermute | solution.py:316
  59.9 8.6 %collective-permute-start.20 = (bf16[64,1024]{1,0:T(8,128)(2,1)S(1)}, bf16[64,1024]{1,0:T(8,128)(2,1)S(1)}, u32[]{:S(2)}, u32[]{:S(2)}) collective-permute-start(bf16[64,1024]{1,0:T(8,128)(2,1)S(1)} %get-tuple-element.51.refs_6_), channel_id=1, source_target_pairs={{0,8},{1,9},{2,10},{3,11},{4,12},{5,13},{6,14},{7,15},{8,0},{9,1},... | collective-permute-start | bytes 393224 | tf_op jit(solution)/shard_map/ppermute | solution.py:316

commit v8 on v7

--- a/solution.py
+++ b/solution.py
@@ -98,7 +98,7 @@
     if extra:
         outs.append(pinned(weights.shape[1], WIDE, dtype=F32))
     return call(body, outs, [HBM] + extra + [ANY] * len(earlier),
-                [in_hbm(tiles)] + ([] if weights is None else [weights]) + [*earlier], space=2,
+                [in_hbm(tiles)] + ([] if weights is None else [in_hbm(weights)]) + [*earlier], space=2,
                 scratch_shapes=[pltpu.SemaphoreType.DMA((PIECES * sum(map(len, groups)),))])
 
 

time: 69.9 us -> 69.8 us (level)
  waiting for transfers between devices: 21 us -> 22 us
    ppermute x9, waiting for transfers between devices: 6.75 us -> 7.68 us  [shift(): lax.ppermute(block, axis, [(i, (i + distance) % size) for i in range(size)])]
    ppermute x9, starting transfers between devices: 13.1 us -> 12.4 us  [shift(): lax.ppermute(block, axis, [(i, (i + distance) % size) for i in range(size)])]
  transfers between devices with their start and end apart: 22 -> 22, of which waited for: 11 -> 10; matrix products, arithmetic and copies ran while one was open for 0% -> 0% of each run, Pallas kernels for 27% -> 28%
where the time goes in v8:
time: 69.8 us; the launch traced here: 69.6 us
  starting transfers between devices  26.9 us (39%)
  waiting for transfers between devices  22 us (32%)
  Pallas kernels  20.3 us (29%)
    pallas_call x24, Pallas kernels, call(): pl.pallas_call(body, out_shape=outs, in_specs=specs, out_specs=out_specs...  20.3 us
    ppermute x9, starting transfers between devices, shift(): lax.ppermute(block, axis, [(i, (i + distance) % size) for i in range(size)])  12.4 us
    ppermute x6, waiting for transfers between devices, pair_swap(): return lax.ppermute(block, axis, [(i, i ^ 1) for i in range(size)])  8.23 us
    ppermute x6, starting transfers between devices, pair_swap(): return lax.ppermute(block, axis, [(i, i ^ 1) for i in range(size)])  7.8 us
    ppermute x9, waiting for transfers between devices, shift(): lax.ppermute(block, axis, [(i, (i + distance) % size) for i in range(size)])  7.68 us
    ppermute x4, starting transfers between devices, send(): out.append(lax.ppermute(part, ('col', 'rhs'), route))  6.13 us
    ppermute x4, waiting for transfers between devices, send(): out.append(lax.ppermute(part, ('col', 'rhs'), route))  6.12 us
  transfers between devices with their start and end apart: 22, of which 10 were waited for; matrix products, arithmetic and copies ran while one was open for 0% of the time, Pallas kernels for 28%

profile of v8, /device:TPU:0, one launch (start us, length us, event | category | flops | bytes accessed | tf_op | source)
XLA Modules:
  0.0 69.6 jit_solution(5257486099875959122)
XLA Ops:
  0.0 0.5 collective-permute-start
  0.5 1.5 %shard_map.55.refs_2_.refs_0_ = bf16[2,64,3072]{2,1,0:T(8,128)(2,1)S(1)} custom-call(bf16[6,64,3072]{2,1,0:T(8,128)(2,1)} %bitcast.1), custom_call_target="tpu_custom_call" | custom-call | bytes 2359296 | tf_op jit(solution)/shard_map/pallas_call | solution.py:64
  1.9 2.5 %collective-permute-start.5 = (bf16[2,64,3072]{2,1,0:T(8,128)(2,1)S(1)}, bf16[2,64,3072]{2,1,0:T(8,128)(2,1)S(1)}, u32[]{:S(2)}, u32[]{:S(2)}) collective-permute-start(bf16[2,64,3072]{2,1,0:T(8,128)(2,1)S(1)} %shard_map.55.refs_2_.refs_0_), channel_id=1, source_target_pairs={{0,2},{1,3},{2,0},{3,1},{4,6},{5,7},{6,4},{7,5},{8,10},{9,11},{10,... | collective-permute-start | bytes 2359304 | tf_op jit(solution)/shard_map/ppermute | solution.py:23
  4.5 2.2 %shard_map.56 = (bf16[2,64,3072]{2,1,0:T(8,128)(2,1)S(1)}, bf16[1,64,3072]{2,1,0:T(8,128)(2,1)S(1)}, bf16[1,64,1536]{2,1,0:T(8,128)(2,1)S(1)}, bf16[1,64,1536]{2,1,0:T(8,128)(2,1)S(1)}, f32[6,256]{1,0:T(8,128)S(1)}) custom-call(bf16[6,64,3072]{2,1,0:T(8,128)(2,1)} %bitcast.2, s32[1,6]{1,0:T(1,128)} %refs_1_.7, bf16[2,64,3072]{2,1,0:T(8,128)(2,1)S(1)} %shard_map.55.refs_2_.refs_0_), custom_call_target="tpu_custom_call" | custom-call | bytes 3145752 | tf_op jit(solution)/shard_map/pallas_call | solution.py:64
  6.7 0.2 collective-permute-start.8
  6.9 1.0 %shard_map.57.refs_6_ = bf16[2,64,1024]{2,1,0:T(8,128)(2,1)S(1)} custom-call(bf16[2,64,3072]{2,1,0:T(8,128)(2,1)S(1)} %shard_map.55.refs_2_.refs_0_, bf16[3072,1024]{1,0:T(8,128)(2,1)S(1)} %copy-done, f32[6,256]{1,0:T(8,128)S(1)} %get-tuple-element.33.refs_2_.refs_5_.refs_3_, bf16[2,64,3072]{2,1,0:T(8,128)(2,1)S(1)} %get-tuple-element.29.refs_3_.refs_0_), custom_call_target="tpu_custom_call" | custom-call | flops 805306368 | bytes 7870464 | tf_op jit(solution)/shard_map/pallas_call | solution.py:64
  7.9 2.1 %collective-permute-start.1 = (bf16[2,64,1024]{2,1,0:T(8,128)(2,1)S(1)}, bf16[2,64,1024]{2,1,0:T(8,128)(2,1)S(1)}, u32[]{:S(2)}, u32[]{:S(2)}) collective-permute-start(bf16[2,64,1024]{2,1,0:T(8,128)(2,1)S(1)} %shard_map.57.refs_6_), channel_id=1, source_target_pairs={{0,4},{4,0},{8,12},{12,8},{16,20},{20,16},{24,28},{28,24},{1,5},{5... | collective-permute-start | bytes 786440 | tf_op jit(solution)/shard_map/ppermute | solution.py:28
  10.0 1.8 %shard_map.58 = (f32[3,64,1024]{2,1,0:T(8,128)S(1)}, bf16[64,1024]{1,0:T(8,128)(2,1)S(1)}) custom-call(bf16[2,64,3072]{2,1,0:T(8,128)(2,1)S(1)} %get-tuple-element.29.refs_3_.refs_0_, bf16[1,64,3072]{2,1,0:T(8,128)(2,1)S(1)} %get-tuple-element.30.refs_1_, bf16[1,64,1536]{2,1,0:T(8,128)(2,1)S(1)} %get-tuple-element.31.refs_2_, ...), custom_call_target="tpu_custom_call" | custom-call | flops 1610612736 | bytes 8132608 | tf_op jit(solution)/shard_map/pallas_call | solution.py:64
  11.8 0.0 collective-permute-done.refs_1_.refs_4_.refs_2_
  11.8 1.0 %shard_map.59.refs_7_ = bf16[2,64,1024]{2,1,0:T(8,128)(2,1)S(1)} custom-call(bf16[2,64,3072]{2,1,0:T(8,128)(2,1)S(1)} %shard_map.55.refs_2_.refs_0_, bf16[3072,1024]{1,0:T(8,128)(2,1)S(1)} %collective-permute-done.refs_1_.refs_4_.refs_2_, f32[6,256]{1,0:T(8,128)S(1)} %get-tuple-element.33.refs_2_.refs_5_.refs_3_, ...), custom_call_target="tpu_custom_call" | custom-call | flops 805306368 | bytes 7870464 | tf_op jit(solution)/shard_map/pallas_call | solution.py:64
  12.8 1.6 %collective-permute-start.2 = (bf16[2,64,1024]{2,1,0:T(8,128)(2,1)S(1)}, bf16[2,64,1024]{2,1,0:T(8,128)(2,1)S(1)}, u32[]{:S(2)}, u32[]{:S(2)}) collective-permute-start(bf16[2,64,1024]{2,1,0:T(8,128)(2,1)S(1)} %shard_map.59.refs_7_), channel_id=1, source_target_pairs={{0,4},{4,0},{8,12},{12,8},{16,20},{20,16},{24,28},{28,24},{1,5},{5... | collective-permute-start | bytes 786440 | tf_op jit(solution)/shard_map/ppermute | solution.py:28
  14.4 1.8 %shard_map.60 = (f32[3,64,1024]{2,1,0:T(8,128)S(1)}, bf16[2,64,1024]{2,1,0:T(8,128)(2,1)S(1)}) custom-call(bf16[2,64,3072]{2,1,0:T(8,128)(2,1)S(1)} %get-tuple-element.29.refs_3_.refs_0_, bf16[1,64,3072]{2,1,0:T(8,128)(2,1)S(1)} %get-tuple-element.30.refs_1_, bf16[1,64,1536]{2,1,0:T(8,128)(2,1)S(1)} %get-tuple-element.31.refs_2_, ...), custom_call_target="tpu_custom_call" | custom-call | flops 1610612736 | bytes 8263680 | tf_op jit(solution)/shard_map/pallas_call | solution.py:64
  16.2 0.6 collective-permute-start.3
  16.8 0.3 collective-permute-done.1.refs_2_
  17.1 5.6 %collective-permute-done.2.refs_3_ = bf16[2,64,1024]{2,1,0:T(8,128)(2,1)S(1)} collective-permute-done((bf16[2,64,1024]{2,1,0:T(8,128)(2,1)S(1)}, bf16[2,64,1024]{2,1,0:T(8,128)(2,1)S(1)}, u32[]{:S(2)}, u32[]{:S(2)}) %collective-permute-start.2) | collective-permute-done | bytes 262176 | tf_op jit(solution)/shard_map/ppermute | solution.py:28
  22.7 0.1 shard_map.62.refs_4_
  22.8 2.1 %collective-permute-start.4 = (bf16[2,64,1024]{2,1,0:T(8,128)(2,1)S(1)}, bf16[2,64,1024]{2,1,0:T(8,128)(2,1)S(1)}, u32[]{:S(2)}, u32[]{:S(2)}) collective-permute-start(bf16[2,64,1024]{2,1,0:T(8,128)(2,1)S(1)} %shard_map.62.refs_4_), channel_id=1, source_target_pairs={{0,8},{4,12},{8,16},{12,20},{16,24},{20,28},{24,0},{28,4},{1,9},{5... | collective-permute-start | bytes 786440 | tf_op jit(solution)/shard_map/ppermute | solution.py:23
  24.9 0.0 collective-permute-done.5.refs_0_
  24.9 1.9 %shard_map.63 = (bf16[2,64,1024]{2,1,0:T(8,128)(2,1)S(1)}, bf16[2,64,1024]{2,1,0:T(8,128)(2,1)S(1)}) custom-call(bf16[2,64,3072]{2,1,0:T(8,128)(2,1)S(1)} %collective-permute-done.5.refs_0_, bf16[3072,1024]{1,0:T(8,128)(2,1)S(1)} %copy-done, bf16[3072,1024]{1,0:T(8,128)(2,1)S(1)} %collective-permute-done.refs_1_.refs_4_.refs_2_, ...), custom_call_target="tpu_custom_call" | custom-call | flops 1610612736 | bytes 13637632 | tf_op jit(solution)/shard_map/pallas_call | solution.py:64
  26.8 0.1 shard_map.64.refs_6_
  26.9 2.1 %collective-permute-start.7 = (bf16[2,64,1024]{2,1,0:T(8,128)(2,1)S(1)}, bf16[2,64,1024]{2,1,0:T(8,128)(2,1)S(1)}, u32[]{:S(2)}, u32[]{:S(2)}) collective-permute-start(bf16[2,64,1024]{2,1,0:T(8,128)(2,1)S(1)} %shard_map.64.refs_6_), channel_id=1, source_target_pairs={{0,24},{4,28},{8,0},{12,4},{16,8},{20,12},{24,16},{28,20},{1,25},{... | collective-permute-start | bytes 786440 | tf_op jit(solution)/shard_map/ppermute | solution.py:23
  29.0 1.7 %collective-permute-start.10 = (bf16[2,64,1024]{2,1,0:T(8,128)(2,1)S(1)}, bf16[2,64,1024]{2,1,0:T(8,128)(2,1)S(1)}, u32[]{:S(2)}, u32[]{:S(2)}) collective-permute-start(bf16[2,64,1024]{2,1,0:T(8,128)(2,1)S(1)} %get-tuple-element.41), channel_id=1, source_target_pairs={{0,4},{4,0},{8,12},{12,8},{16,20},{20,16},{24,28},{28,24},{1,5},{5... | collective-permute-start | bytes 786440 | tf_op jit(solution)/shard_map/ppermute | solution.py:28
  30.7 0.0 collective-permute-done.3.refs_4_.refs_1_
  30.7 0.3 collective-permute-start.9
  31.0 2.8 %collective-permute-done.4.refs_5_ = bf16[2,64,1024]{2,1,0:T(8,128)(2,1)S(1)} collective-permute-done((bf16[2,64,1024]{2,1,0:T(8,128)(2,1)S(1)}, bf16[2,64,1024]{2,1,0:T(8,128)(2,1)S(1)}, u32[]{:S(2)}, u32[]{:S(2)}) %collective-permute-start.4) | collective-permute-done | bytes 262176 | tf_op jit(solution)/shard_map/ppermute | solution.py:23
  33.8 1.6 %collective-permute-start.13 = (bf16[1,64,3072]{2,1,0:T(8,128)(2,1)S(1)}, bf16[1,64,3072]{2,1,0:T(8,128)(2,1)S(1)}, u32[]{:S(2)}, u32[]{:S(2)}) collective-permute-start(bf16[1,64,3072]{2,1,0:T(8,128)(2,1)S(1)} %get-tuple-element.30.refs_1_), channel_id=1, source_target_pairs={{0,2},{1,3},{2,0},{3,1},{4,6},{5,7},{6,4},{7,5},{8,10},{9,11},{10,... | collective-permute-start | bytes 1179656 | tf_op jit(solution)/shard_map/ppermute | solution.py:23
  35.4 0.1 shard_map.65.refs_2_
  35.5 1.8 %collective-permute-done.7.refs_0_ = bf16[2,64,1024]{2,1,0:T(8,128)(2,1)S(1)} collective-permute-done((bf16[2,64,1024]{2,1,0:T(8,128)(2,1)S(1)}, bf16[2,64,1024]{2,1,0:T(8,128)(2,1)S(1)}, u32[]{:S(2)}, u32[]{:S(2)}) %collective-permute-start.7) | collective-permute-done | bytes 262176 | tf_op jit(solution)/shard_map/ppermute | solution.py:23
  37.3 0.6 collective-permute-start.6
  37.8 0.1 shard_map.66.refs_6_.refs_1_
  37.9 1.8 %collective-permute-done.8.refs_0_ = bf16[2,64,3072]{2,1,0:T(8,128)(2,1)S(1)} collective-permute-done((bf16[2,64,3072]{2,1,0:T(8,128)(2,1)S(1)}, bf16[2,64,3072]{2,1,0:T(8,128)(2,1)S(1)}, u32[]{:S(2)}, u32[]{:S(2)}) %collective-permute-start.8) | collective-permute-done | bytes 786464 | tf_op jit(solution)/shard_map/ppermute | solution.py:23
  39.7 0.0 collective-permute-done.10.refs_5_.refs_1_
  39.7 2.3 %collective-permute-done.9.refs_4_.refs_1_ = bf16[2,64,1024]{2,1,0:T(8,128)(2,1)S(1)} collective-permute-done((bf16[2,64,1024]{2,1,0:T(8,128)(2,1)S(1)}, bf16[2,64,1024]{2,1,0:T(8,128)(2,1)S(1)}, u32[]{:S(2)}, u32[]{:S(2)}) %collective-permute-start.9) | collective-permute-done | bytes 262176 | tf_op jit(solution)/shard_map/ppermute | solution.py:28
  42.0 1.9 %shard_map.67 = (bf16[2,64,1024]{2,1,0:T(8,128)(2,1)S(1)}, bf16[2,64,1024]{2,1,0:T(8,128)(2,1)S(1)}) custom-call(bf16[2,64,3072]{2,1,0:T(8,128)(2,1)S(1)} %collective-permute-done.8.refs_0_, bf16[3072,1024]{1,0:T(8,128)(2,1)S(1)} %copy-done, bf16[3072,1024]{1,0:T(8,128)(2,1)S(1)} %collective-permute-done.refs_1_.refs_4_.refs_2_, ...), custom_call_target="tpu_custom_call" | custom-call | flops 1610612736 | bytes 14424064 | tf_op jit(solution)/shard_map/pallas_call | solution.py:64
  43.9 0.2 collective-permute-start.14
  44.1 1.6 %collective-permute-start.12 = (bf16[2,64,1024]{2,1,0:T(8,128)(2,1)S(1)}, bf16[2,64,1024]{2,1,0:T(8,128)(2,1)S(1)}, u32[]{:S(2)}, u32[]{:S(2)}) collective-permute-start(bf16[2,64,1024]{2,1,0:T(8,128)(2,1)S(1)} %get-tuple-element.42.refs_2_), channel_id=1, source_target_pairs={{0,4},{4,0},{8,12},{12,8},{16,20},{20,16},{24,28},{28,24},{1,5},{5... | collective-permute-start | bytes 786440 | tf_op jit(solution)/shard_map/ppermute | solution.py:28
  45.7 1.5 %collective-permute-start.19 = (bf16[1,64,1536]{2,1,0:T(8,128)(2,1)S(1)}, bf16[1,64,1536]{2,1,0:T(8,128)(2,1)S(1)}, u32[]{:S(2)}, u32[]{:S(2)}) collective-permute-start(bf16[1,64,1536]{2,1,0:T(8,128)(2,1)S(1)} %get-tuple-element.31.refs_2_), channel_id=1, source_target_pairs={{0,2},{1,3},{2,0},{3,1},{4,6},{5,7},{6,4},{7,5},{8,10},{9,11},{10,... | collective-permute-start | bytes 589832 | tf_op jit(solution)/shard_map/ppermute | solution.py:23
  47.2 0.0 collective-permute-done.6.refs_0_
  47.2 1.5 %collective-permute-start.18 = (bf16[1,64,1536]{2,1,0:T(8,128)(2,1)S(1)}, bf16[1,64,1536]{2,1,0:T(8,128)(2,1)S(1)}, u32[]{:S(2)}, u32[]{:S(2)}) collective-permute-start(bf16[1,64,1536]{2,1,0:T(8,128)(2,1)S(1)} %get-tuple-element.32.refs_3_), channel_id=1, source_target_pairs={{0,2},{1,3},{2,0},{3,1},{4,6},{5,7},{6,4},{7,5},{8,10},{9,11},{10,... | collective-permute-start | bytes 589832 | tf_op jit(solution)/shard_map/ppermute | solution.py:23
  48.8 0.0 collective-permute-done.13.refs_0_
  48.8 2.3 %shard_map.70.refs_2_.refs_0_ = f32[2,64,1024]{2,1,0:T(8,128)S(1)} custom-call(bf16[1,64,3072]{2,1,0:T(8,128)(2,1)S(1)} %collective-permute-done.13.refs_0_, bf16[3072,1024]{1,0:T(8,128)(2,1)S(1)} %copy-done, bf16[3072,1024]{1,0:T(8,128)(2,1)S(1)} %collective-permute-done.refs_1_.refs_4_.refs_2_, f32[6,256]{1,0:T(8,128)S(1)} %get-tuple-element.33.refs_2_.refs_5_.refs_3_, ...), custom_call_target="tpu_custom_call" | custom-call | flops 805306368 | bytes 13244416 | tf_op jit(solution)/shard_map/pallas_call | solution.py:64
  51.1 1.3 %collective-permute-done.14.refs_0_ = bf16[2,64,1024]{2,1,0:T(8,128)(2,1)S(1)} collective-permute-done((bf16[2,64,1024]{2,1,0:T(8,128)(2,1)S(1)}, bf16[2,64,1024]{2,1,0:T(8,128)(2,1)S(1)}, u32[]{:S(2)}, u32[]{:S(2)}) %collective-permute-start.14) | collective-permute-done | bytes 262176 | tf_op jit(solution)/shard_map/ppermute | solution.py:23
  52.5 0.1 shard_map.71.refs_3_.refs_4_
  52.6 0.2 shard_map.72
  52.8 2.2 %collective-permute-start.16 = (bf16[64,1024]{1,0:T(8,128)(2,1)S(1)}, bf16[64,1024]{1,0:T(8,128)(2,1)S(1)}, u32[]{:S(2)}, u32[]{:S(2)}) collective-permute-start(bf16[64,1024]{1,0:T(8,128)(2,1)S(1)} %get-tuple-element.46.refs_1_), channel_id=1, source_target_pairs={{0,24},{1,25},{2,26},{3,27},{4,28},{5,29},{6,30},{7,31},{8,16},{9,... | collective-permute-start | bytes 393224 | tf_op jit(solution)/shard_map/ppermute | solution.py:316
  54.9 0.1 shard_map.73
  55.0 0.1 collective-permute-start.15
  55.1 1.8 %collective-permute-start.17 = (bf16[64,1024]{1,0:T(8,128)(2,1)S(1)}, bf16[64,1024]{1,0:T(8,128)(2,1)S(1)}, u32[]{:S(2)}, u32[]{:S(2)}) collective-permute-start(bf16[64,1024]{1,0:T(8,128)(2,1)S(1)} %get-tuple-element.49), channel_id=1, source_target_pairs={{0,25},{1,24},{2,27},{3,26},{4,29},{5,28},{6,31},{7,30},{8,17},{9,... | collective-permute-start | bytes 393224 | tf_op jit(solution)/shard_map/ppermute | solution.py:316
  56.9 0.1 collective-permute-start.11
  57.0 1.2 %shard_map.74.refs_4_.refs_6_ = f32[2,64,1024]{2,1,0:T(8,128)S(1)} custom-call(bf16[1,64,1536]{2,1,0:T(8,128)(2,1)S(1)} %collective-permute-done.19.refs_0_, bf16[3072,1024]{1,0:T(8,128)(2,1)S(1)} %copy-done, bf16[3072,1024]{1,0:T(8,128)(2,1)S(1)} %collective-permute-done.refs_1_.refs_4_.refs_2_, f32[6,256]{1,0:T(8,128)S(1)} %get-tuple-element.33.refs_2_.refs_5_.refs_3_, ...), custom_call_target="tpu_custom_call" | custom-call | flops 805306368 | bytes 12916736 | tf_op jit(solution)/shard_map/pallas_call | solution.py:64
  58.2 0.0 copy-start.1
  58.2 0.0 copy-start.2
  58.2 1.2 %shard_map.75 = (bf16[64,1024]{1,0:T(8,128)(2,1)S(1)}, bf16[64,1024]{1,0:T(8,128)(2,1)S(1)}) custom-call(bf16[1,64,1536]{2,1,0:T(8,128)(2,1)S(1)} %collective-permute-done.18.refs_0_, bf16[3072,1024]{1,0:T(8,128)(2,1)S(1)} %copy-done, bf16[3072,1024]{1,0:T(8,128)(2,1)S(1)} %collective-permute-done.refs_1_.refs_4_.refs_2_, ...), custom_call_target="tpu_custom_call" | custom-call | flops 805306368 | bytes 14358528 | tf_op jit(solution)/shard_map/pallas_call | solution.py:64
  59.5 0.1 collective-permute-start.21
  59.6 0.0 collective-permute-done.15.refs_3_
  59.6 2.1 %collective-permute-start.20 = (bf16[64,1024]{1,0:T(8,128)(2,1)S(1)}, bf16[64,1024]{1,0:T(8,128)(2,1)S(1)}, u32[]{:S(2)}, u32[]{:S(2)}) collective-permute-start(bf16[64,1024]{1,0:T(8,128)(2,1)S(1)} %get-tuple-element.51.refs_6_), channel_id=1, source_target_pairs={{0,8},{1,9},{2,10},{3,11},{4,12},{5,13},{6,14},{7,15},{8,0},{9,1},... | collective-permute-start | bytes 393224 | tf_op jit(solution)/shard_map/ppermute | solution.py:316
  61.6 0.2 shard_map.61
  61.9 0.0 collective-permute-done.16.refs_4_
  61.9 0.3 collective-permute-done.17.refs_5_
  62.2 0.1 shard_map.76.refs_2_.refs_4_.known
  62.3 3.0 %collective-permute-done.21.refs_3_ = bf16[64,1024]{1,0:T(8,128)(2,1)S(1)} collective-permute-done((bf16[64,1024]{1,0:T(8,128)(2,1)S(1)}, bf16[64,1024]{1,0:T(8,128)(2,1)S(1)}, u32[]{:S(2)}, u32[]{:S(2)}) %collective-permute-start.21) | collective-permute-done | bytes 131104 | tf_op jit(solution)/shard_map/ppermute | solution.py:316
  65.3 0.3 shard_map.77.part
  65.6 2.8 %collective-permute-done.20.last = bf16[64,1024]{1,0:T(8,128)(2,1)S(1)} collective-permute-done((bf16[64,1024]{1,0:T(8,128)(2,1)S(1)}, bf16[64,1024]{1,0:T(8,128)(2,1)S(1)}, u32[]{:S(2)}, u32[]{:S(2)}) %collective-permute-start.20) | collective-permute-done | bytes 131104 | tf_op jit(solution)/shard_map/ppermute | solution.py:316
  68.4 1.1 %shard_map.78 = bf16[256,1024]{1,0:T(8,128)(2,1)} custom-call(bf16[256,1024]{1,0:T(8,128)(2,1)S(1)} %get-tuple-element.37.refs_0_.rhs, bf16[256,256]{1,0:T(8,128)(2,1)S(1)} %get-tuple-element.38.refs_1_.diag, f32[256,1024]{1,0:T(8,128)S(1)} %shard_map.76.refs_2_.refs_4_.known, bf16[64,1024]{1,0:T(8,128)(2,1)S(1)} %collective-permute-done.20.last, ...), custom_call_target="tpu_custom_call" | custom-call | flops 33554432 | bytes 2883584 | tf_op jit(solution)/shard_map/pallas_call | solution.py:64
  (10 shorter events, 0.1 us)
Async XLA Ops:
  0.0 6.9 %copy-start = (bf16[3072,1024]{1,0:T(8,128)(2,1)S(1)}, bf16[3072,1024]{1,0:T(8,128)(2,1)}, u32[]{:S(2)}) copy-start(bf16[3072,1024]{1,0:T(8,128)(2,1)} %refs_1_.13) | copy-start | bytes 18874372
  0.0 11.8 %collective-permute-start = (bf16[3072,1024]{1,0:T(8,128)(2,1)}, bf16[3072,1024]{1,0:T(8,128)(2,1)S(1)}, u32[]{:S(2)}, u32[]{:S(2)}) collective-permute-start(bf16[3072,1024]{1,0:T(8,128)(2,1)} %refs_1_.13), channel_id=1, source_target_pairs={{1,0},{0,1},{3,2},{2,3},{5,4},{4,5},{7,6},{6,7},{9,8},{8,9},{11,10... | collective-permute-start | bytes 18874376 | tf_op jit(solution)/shard_map/ppermute | solution.py:44
  1.9 23.0 %collective-permute-start.5 = (bf16[2,64,3072]{2,1,0:T(8,128)(2,1)S(1)}, bf16[2,64,3072]{2,1,0:T(8,128)(2,1)S(1)}, u32[]{:S(2)}, u32[]{:S(2)}) collective-permute-start(bf16[2,64,3072]{2,1,0:T(8,128)(2,1)S(1)} %shard_map.55.refs_2_.refs_0_), channel_id=1, source_target_pairs={{0,2},{1,3},{2,0},{3,1},{4,6},{5,7},{6,4},{7,5},{8,10},{9,11},{10,... | collective-permute-start | bytes 2359304 | tf_op jit(solution)/shard_map/ppermute | solution.py:23
  6.7 33.0 %collective-permute-start.8 = (bf16[2,64,3072]{2,1,0:T(8,128)(2,1)S(1)}, bf16[2,64,3072]{2,1,0:T(8,128)(2,1)S(1)}, u32[]{:S(2)}, u32[]{:S(2)}) collective-permute-start(bf16[2,64,3072]{2,1,0:T(8,128)(2,1)S(1)} %get-tuple-element.29.refs_3_.refs_0_), channel_id=1, source_target_pairs={{0,2},{1,3},{2,0},{3,1},{4,6},{5,7},{6,4},{7,5},{8,10},{9,11},{10,... | collective-permute-start | bytes 2359304 | tf_op jit(solution)/shard_map/ppermute | solution.py:23
  7.9 9.2 %collective-permute-start.1 = (bf16[2,64,1024]{2,1,0:T(8,128)(2,1)S(1)}, bf16[2,64,1024]{2,1,0:T(8,128)(2,1)S(1)}, u32[]{:S(2)}, u32[]{:S(2)}) collective-permute-start(bf16[2,64,1024]{2,1,0:T(8,128)(2,1)S(1)} %shard_map.57.refs_6_), channel_id=1, source_target_pairs={{0,4},{4,0},{8,12},{12,8},{16,20},{20,16},{24,28},{28,24},{1,5},{5... | collective-permute-start | bytes 786440 | tf_op jit(solution)/shard_map/ppermute | solution.py:28
  12.8 9.9 %collective-permute-start.2 = (bf16[2,64,1024]{2,1,0:T(8,128)(2,1)S(1)}, bf16[2,64,1024]{2,1,0:T(8,128)(2,1)S(1)}, u32[]{:S(2)}, u32[]{:S(2)}) collective-permute-start(bf16[2,64,1024]{2,1,0:T(8,128)(2,1)S(1)} %shard_map.59.refs_7_), channel_id=1, source_target_pairs={{0,4},{4,0},{8,12},{12,8},{16,20},{20,16},{24,28},{28,24},{1,5},{5... | collective-permute-start | bytes 786440 | tf_op jit(solution)/shard_map/ppermute | solution.py:28
  16.2 14.5 %collective-permute-start.3 = (bf16[2,64,1024]{2,1,0:T(8,128)(2,1)S(1)}, bf16[2,64,1024]{2,1,0:T(8,128)(2,1)S(1)}, u32[]{:S(2)}, u32[]{:S(2)}) collective-permute-start(bf16[2,64,1024]{2,1,0:T(8,128)(2,1)S(1)} %get-tuple-element.39), channel_id=1, source_target_pairs={{0,4},{4,0},{8,12},{12,8},{16,20},{20,16},{24,28},{28,24},{1,5},{5... | collective-permute-start | bytes 786440 | tf_op jit(solution)/shard_map/ppermute | solution.py:28
  22.8 11.0 %collective-permute-start.4 = (bf16[2,64,1024]{2,1,0:T(8,128)(2,1)S(1)}, bf16[2,64,1024]{2,1,0:T(8,128)(2,1)S(1)}, u32[]{:S(2)}, u32[]{:S(2)}) collective-permute-start(bf16[2,64,1024]{2,1,0:T(8,128)(2,1)S(1)} %shard_map.62.refs_4_), channel_id=1, source_target_pairs={{0,8},{4,12},{8,16},{12,20},{16,24},{20,28},{24,0},{28,4},{1,9},{5... | collective-permute-start | bytes 786440 | tf_op jit(solution)/shard_map/ppermute | solution.py:23
  26.9 10.4 %collective-permute-start.7 = (bf16[2,64,1024]{2,1,0:T(8,128)(2,1)S(1)}, bf16[2,64,1024]{2,1,0:T(8,128)(2,1)S(1)}, u32[]{:S(2)}, u32[]{:S(2)}) collective-permute-start(bf16[2,64,1024]{2,1,0:T(8,128)(2,1)S(1)} %shard_map.64.refs_6_), channel_id=1, source_target_pairs={{0,24},{4,28},{8,0},{12,4},{16,8},{20,12},{24,16},{28,20},{1,25},{... | collective-permute-start | bytes 786440 | tf_op jit(solution)/shard_map/ppermute | solution.py:23
  29.0 10.7 %collective-permute-start.10 = (bf16[2,64,1024]{2,1,0:T(8,128)(2,1)S(1)}, bf16[2,64,1024]{2,1,0:T(8,128)(2,1)S(1)}, u32[]{:S(2)}, u32[]{:S(2)}) collective-permute-start(bf16[2,64,1024]{2,1,0:T(8,128)(2,1)S(1)} %get-tuple-element.41), channel_id=1, source_target_pairs={{0,4},{4,0},{8,12},{12,8},{16,20},{20,16},{24,28},{28,24},{1,5},{5... | collective-permute-start | bytes 786440 | tf_op jit(solution)/shard_map/ppermute | solution.py:28
  30.7 11.3 %collective-permute-start.9 = (bf16[2,64,1024]{2,1,0:T(8,128)(2,1)S(1)}, bf16[2,64,1024]{2,1,0:T(8,128)(2,1)S(1)}, u32[]{:S(2)}, u32[]{:S(2)}) collective-permute-start(bf16[2,64,1024]{2,1,0:T(8,128)(2,1)S(1)} %get-tuple-element.40.refs_4_), channel_id=1, source_target_pairs={{0,4},{4,0},{8,12},{12,8},{16,20},{20,16},{24,28},{28,24},{1,5},{5... | collective-permute-start | bytes 786440 | tf_op jit(solution)/shard_map/ppermute | solution.py:28
  33.8 15.0 %collective-permute-start.13 = (bf16[1,64,3072]{2,1,0:T(8,128)(2,1)S(1)}, bf16[1,64,3072]{2,1,0:T(8,128)(2,1)S(1)}, u32[]{:S(2)}, u32[]{:S(2)}) collective-permute-start(bf16[1,64,3072]{2,1,0:T(8,128)(2,1)S(1)} %get-tuple-element.30.refs_1_), channel_id=1, source_target_pairs={{0,2},{1,3},{2,0},{3,1},{4,6},{5,7},{6,4},{7,5},{8,10},{9,11},{10,... | collective-permute-start | bytes 1179656 | tf_op jit(solution)/shard_map/ppermute | solution.py:23
  37.3 9.9 %collective-permute-start.6 = (bf16[2,64,1024]{2,1,0:T(8,128)(2,1)S(1)}, bf16[2,64,1024]{2,1,0:T(8,128)(2,1)S(1)}, u32[]{:S(2)}, u32[]{:S(2)}) collective-permute-start(bf16[2,64,1024]{2,1,0:T(8,128)(2,1)S(1)} %shard_map.65.refs_2_), channel_id=1, source_target_pairs={{0,8},{4,12},{8,16},{12,20},{16,24},{20,28},{24,0},{28,4},{1,9},{5... | collective-permute-start | bytes 786440 | tf_op jit(solution)/shard_map/ppermute | solution.py:23
  43.9 8.6 %collective-permute-start.14 = (bf16[2,64,1024]{2,1,0:T(8,128)(2,1)S(1)}, bf16[2,64,1024]{2,1,0:T(8,128)(2,1)S(1)}, u32[]{:S(2)}, u32[]{:S(2)}) collective-permute-start(bf16[2,64,1024]{2,1,0:T(8,128)(2,1)S(1)} %get-tuple-element.45), channel_id=1, source_target_pairs={{0,8},{4,12},{8,16},{12,20},{16,24},{20,28},{24,0},{28,4},{1,9},{5... | collective-permute-start | bytes 786440 | tf_op jit(solution)/shard_map/ppermute | solution.py:23
  44.1 8.4 %collective-permute-start.12 = (bf16[2,64,1024]{2,1,0:T(8,128)(2,1)S(1)}, bf16[2,64,1024]{2,1,0:T(8,128)(2,1)S(1)}, u32[]{:S(2)}, u32[]{:S(2)}) collective-permute-start(bf16[2,64,1024]{2,1,0:T(8,128)(2,1)S(1)} %get-tuple-element.42.refs_2_), channel_id=1, source_target_pairs={{0,4},{4,0},{8,12},{12,8},{16,20},{20,16},{24,28},{28,24},{1,5},{5... | collective-permute-start | bytes 786440 | tf_op jit(solution)/shard_map/ppermute | solution.py:28
  45.7 11.3 %collective-permute-start.19 = (bf16[1,64,1536]{2,1,0:T(8,128)(2,1)S(1)}, bf16[1,64,1536]{2,1,0:T(8,128)(2,1)S(1)}, u32[]{:S(2)}, u32[]{:S(2)}) collective-permute-start(bf16[1,64,1536]{2,1,0:T(8,128)(2,1)S(1)} %get-tuple-element.31.refs_2_), channel_id=1, source_target_pairs={{0,2},{1,3},{2,0},{3,1},{4,6},{5,7},{6,4},{7,5},{8,10},{9,11},{10,... | collective-permute-start | bytes 589832 | tf_op jit(solution)/shard_map/ppermute | solution.py:23
  47.2 11.0 %collective-permute-start.18 = (bf16[1,64,1536]{2,1,0:T(8,128)(2,1)S(1)}, bf16[1,64,1536]{2,1,0:T(8,128)(2,1)S(1)}, u32[]{:S(2)}, u32[]{:S(2)}) collective-permute-start(bf16[1,64,1536]{2,1,0:T(8,128)(2,1)S(1)} %get-tuple-element.32.refs_3_), channel_id=1, source_target_pairs={{0,2},{1,3},{2,0},{3,1},{4,6},{5,7},{6,4},{7,5},{8,10},{9,11},{10,... | collective-permute-start | bytes 589832 | tf_op jit(solution)/shard_map/ppermute | solution.py:23
  52.8 9.1 %collective-permute-start.16 = (bf16[64,1024]{1,0:T(8,128)(2,1)S(1)}, bf16[64,1024]{1,0:T(8,128)(2,1)S(1)}, u32[]{:S(2)}, u32[]{:S(2)}) collective-permute-start(bf16[64,1024]{1,0:T(8,128)(2,1)S(1)} %get-tuple-element.46.refs_1_), channel_id=1, source_target_pairs={{0,24},{1,25},{2,26},{3,27},{4,28},{5,29},{6,30},{7,31},{8,16},{9,... | collective-permute-start | bytes 393224 | tf_op jit(solution)/shard_map/ppermute | solution.py:316
  55.0 4.6 %collective-permute-start.15 = (bf16[64,1024]{1,0:T(8,128)(2,1)S(1)}, bf16[64,1024]{1,0:T(8,128)(2,1)S(1)}, u32[]{:S(2)}, u32[]{:S(2)}) collective-permute-start(bf16[64,1024]{1,0:T(8,128)(2,1)S(1)} %get-tuple-element.48), channel_id=1, source_target_pairs={{0,1},{1,0},{2,3},{3,2},{4,5},{5,4},{6,7},{7,6},{8,9},{9,8},{10,11... | collective-permute-start | bytes 393224 | tf_op jit(solution)/shard_map/ppermute | solution.py:54
  55.1 7.1 %collective-permute-start.17 = (bf16[64,1024]{1,0:T(8,128)(2,1)S(1)}, bf16[64,1024]{1,0:T(8,128)(2,1)S(1)}, u32[]{:S(2)}, u32[]{:S(2)}) collective-permute-start(bf16[64,1024]{1,0:T(8,128)(2,1)S(1)} %get-tuple-element.49), channel_id=1, source_target_pairs={{0,25},{1,24},{2,27},{3,26},{4,29},{5,28},{6,31},{7,30},{8,17},{9,... | collective-permute-start | bytes 393224 | tf_op jit(solution)/shard_map/ppermute | solution.py:316
  56.9 5.3 %collective-permute-start.11 = (f32[64,1024]{1,0:T(8,128)S(1)}, f32[64,1024]{1,0:T(8,128)S(1)}, u32[]{:S(2)}, u32[]{:S(2)}) collective-permute-start(f32[64,1024]{1,0:T(8,128)S(1)} %get-tuple-element.44), channel_id=1, source_target_pairs={{0,1},{1,0},{2,3},{3,2},{4,5},{5,4},{6,7},{7,6},{8,9},{9,8},{10,11... | collective-permute-start | bytes 786440 | tf_op jit(solution)/shard_map/ppermute | solution.py:54
  58.2 3.4 %copy-start.1 = (bf16[256,1024]{1,0:T(8,128)(2,1)S(1)}, bf16[256,1024]{1,0:T(8,128)(2,1)}, u32[]{:S(2)}) copy-start(bf16[256,1024]{1,0:T(8,128)(2,1)} %rhs.1) | copy-start | bytes 1572868
  58.2 3.4 %copy-start.2 = (bf16[1,256,256]{2,1,0:T(8,128)(2,1)S(1)}, bf16[1,256,256]{2,1,0:T(8,128)(2,1)}, u32[]{:S(2)}) copy-start(bf16[1,256,256]{2,1,0:T(8,128)(2,1)} %diag.1) | copy-start | bytes 393220
  59.5 5.8 %collective-permute-start.21 = (bf16[64,1024]{1,0:T(8,128)(2,1)S(1)}, bf16[64,1024]{1,0:T(8,128)(2,1)S(1)}, u32[]{:S(2)}, u32[]{:S(2)}) collective-permute-start(bf16[64,1024]{1,0:T(8,128)(2,1)S(1)} %get-tuple-element.52), channel_id=1, source_target_pairs={{0,9},{1,8},{2,11},{3,10},{4,13},{5,12},{6,15},{7,14},{8,1},{9,0},... | collective-permute-start | bytes 393224 | tf_op jit(solution)/shard_map/ppermute | solution.py:316
  59.6 8.8 %collective-permute-start.20 = (bf16[64,1024]{1,0:T(8,128)(2,1)S(1)}, bf16[64,1024]{1,0:T(8,128)(2,1)S(1)}, u32[]{:S(2)}, u32[]{:S(2)}) collective-permute-start(bf16[64,1024]{1,0:T(8,128)(2,1)S(1)} %get-tuple-element.51.refs_6_), channel_id=1, source_target_pairs={{0,8},{1,9},{2,10},{3,11},{4,12},{5,13},{6,14},{7,15},{8,0},{9,1},... | collective-permute-start | bytes 393224 | tf_op jit(solution)/shard_map/ppermute | solution.py:316
